TPU v7x, 32 devices: a whole 2x2x4 slice. The times are simulated.
32 devices in a mesh: dp: 8 (over z, y), tensor: 4 (over x, core).
Axes of the slice: x: 2, y: 2, z: 4, core: 2. Of those that a mesh axis runs over, the one named last changes fastest.
Arguments:
- inputs: bfloat16 [16384, 1024], P(('dp', 'tensor')), may hold values from -6 to 6
- out_grad: bfloat16 [16384, 1024], P(('dp', 'tensor')), may hold values from -6 to 6
- owners: int32 [4, 4], replicated, may hold values from 0 to 7, as said below
- master_slots: float32 [8, 4096, 1024], P('dp', 'tensor'), may hold values from -0.1875 to 0.1875
- momentum_slots: float32 [8, 4096, 1024], P('dp', 'tensor'), may hold values from -224 to 224
- small_master: float32 [12288], P(('dp', 'tensor')), may hold values from -0.8 to 1.4, as said below
- small_first: float32 [12288], P(('dp', 'tensor')), may hold values from -80 to 80
- small_second: float32 [12288], P(('dp', 'tensor')), may hold values from 245.76 to 2457.6
Outputs:
- block_out: bfloat16 [16384, 1024], P(('dp', 'tensor'))
- input_grad: float32 [16384, 1024], P(('dp', 'tensor'))
- grad_slots: float32 [8, 4096, 1024], P('dp', 'tensor')
- momentum_new: float32 [8, 4096, 1024], P('dp', 'tensor')
- master_new: float32 [8, 4096, 1024], P('dp', 'tensor')
- small_grad: float32 [12288], P(('dp', 'tensor'))
- small_second_new: float32 [12288], P(('dp', 'tensor'))
- small_new: float32 [12288], P(('dp', 'tensor'))
Inputs may be any that keep to these rules, and one draw needn't show every extreme that they name: For each tensor index t, owners[t, 0..3] name the devices of dp owning the query-key-value, output, feed-forward-in and feed-forward-out matrices of shard t; the four are different. Slots of devices that own nothing, and entries of a slot outside its matrix's shape, are not read. `small_master`: entries 0 to 1023 and 5120 to 6143 are LayerNorm gains, the rest biases.
All inputs are finite; a program needn't handle non-finite values.
Results may differ from a plain program's by a relative error of at most 0.017.
Values may be sent and summed in bfloat16 or wider, within the bound.
No kernel may reach another device: no remote copies, remote signals or barrier semaphores. Data moves between devices by JAX's collectives and lax.ppermute only.
A program may use at most 192 MiB of HBM per device.

v0:
```python
from functools import partial

import jax
import jax.numpy as jnp
from jax import lax
from jax.sharding import PartitionSpec as P

HEADS = 16
FF = 4096
SEQ = 1024
NS_STEPS = 5
STEP = 10


ln_eps = 1e-05
mom_decay = 0.95
ns_a = 3.4445
ns_b = -4.775
ns_c = 2.0315
muon_rate = 0.5
muon_decay = 0.01
beta_one = 0.9
beta_two = 0.95
adam_rate = 0.2
adam_eps = 1e-08
masked_score = -1e30


def layer_norm(values, gain_vec, shift_vec):
    row_mean = jnp.mean(values, axis=-1, keepdims=True)
    centred = values - row_mean
    spread = jnp.mean(centred * centred, axis=-1, keepdims=True)
    return centred * lax.rsqrt(spread + ln_eps) * gain_vec + shift_vec


def newton_schulz(matrix):
    scaled = matrix / (jnp.sqrt(jnp.sum(matrix * matrix)) + 1e-07)
    iterate = scaled.astype(jnp.bfloat16)
    for ns_turn in range(NS_STEPS):
        gram_mat = jnp.einsum(
            "ij,kj->ik", iterate, iterate, preferred_element_type=jnp.float32
        ).astype(jnp.bfloat16)
        square = jnp.dot(gram_mat, gram_mat, preferred_element_type=jnp.float32)
        poly_mat = (ns_b * gram_mat.astype(jnp.float32) + ns_c * square).astype(jnp.bfloat16)
        iterate = (
            ns_a * iterate.astype(jnp.float32)
            + jnp.dot(poly_mat, iterate, preferred_element_type=jnp.float32)
        ).astype(jnp.bfloat16)
    return iterate.astype(jnp.float32)


def muon_update(grad_slot, mom_slot, master_slot, valid):
    momentum = valid * (mom_decay * mom_slot + grad_slot)
    ortho = newton_schulz(momentum)
    fresh = valid * (master_slot * (1.0 - muon_rate * muon_decay) - muon_rate * ortho)
    return (grad_slot * valid, momentum, fresh)


def attention_forward(queries, keys_low, values_low, seq_count, local_heads, head_dim):
    length = queries.shape[0] // seq_count
    block_rows = min(512, length)
    block_count = length // block_rows
    score_scale = head_dim ** (-0.5)
    four_dims = (seq_count, length, local_heads, head_dim)
    query_all = queries.reshape(four_dims)
    key_all = keys_low.reshape(four_dims)
    value_all = values_low.reshape(four_dims)

    def one_block(blk_index):
        seq_index = blk_index // block_count
        first_row = blk_index % block_count * block_rows
        query_seq = lax.dynamic_index_in_dim(query_all, seq_index, 0, keepdims=False)
        query_blk = lax.dynamic_slice_in_dim(query_seq, first_row, block_rows, 0)
        key_seq = lax.dynamic_index_in_dim(key_all, seq_index, 0, keepdims=False)
        value_seq = lax.dynamic_index_in_dim(value_all, seq_index, 0, keepdims=False)
        scores = (
            jnp.einsum("qhd,khd->hqk", query_blk, key_seq, preferred_element_type=jnp.float32)
            * score_scale
        )
        causal = (first_row + jnp.arange(block_rows))[:, None] >= jnp.arange(length)[None, :]
        scores = jnp.where(causal[None], scores, masked_score)
        row_top = jnp.max(scores, axis=-1, keepdims=True)
        shifted = jnp.exp(scores - row_top)
        totals = jnp.sum(shifted, axis=-1, keepdims=True)
        probs_low = (shifted / totals).astype(jnp.bfloat16)
        mixed_out = jnp.einsum(
            "hqk,khd->qhd", probs_low, value_seq, preferred_element_type=jnp.float32
        )
        return (mixed_out.astype(jnp.bfloat16), row_top[..., 0] + jnp.log(totals[..., 0]))

    mixed_all, log_sums = lax.map(one_block, jnp.arange(seq_count * block_count))
    return (mixed_all.reshape(queries.shape), log_sums)


def attention_backward(
    queries, keys_low, values_low, log_sums, back_mixed, seq_count, local_heads, head_dim
):
    length = queries.shape[0] // seq_count
    block_rows = min(512, length)
    block_count = length // block_rows
    score_scale = head_dim ** (-0.5)
    four_dims = (seq_count, length, local_heads, head_dim)
    query_all = queries.reshape(four_dims)
    key_all = keys_low.reshape(four_dims)
    value_all = values_low.reshape(four_dims)
    back_all = back_mixed.reshape(four_dims)
    sums_all = log_sums.reshape(seq_count, block_count, local_heads, block_rows)

    def one_sequence(seq_index):
        query_seq = lax.dynamic_index_in_dim(query_all, seq_index, 0, keepdims=False)
        key_seq = lax.dynamic_index_in_dim(key_all, seq_index, 0, keepdims=False)
        value_seq = lax.dynamic_index_in_dim(value_all, seq_index, 0, keepdims=False)
        back_seq = lax.dynamic_index_in_dim(back_all, seq_index, 0, keepdims=False)
        sums_seq = lax.dynamic_index_in_dim(sums_all, seq_index, 0, keepdims=False)

        def one_step(carried, blk_index):
            key_acc, value_acc = carried
            first_row = blk_index * block_rows
            query_blk = lax.dynamic_slice_in_dim(query_seq, first_row, block_rows, 0)
            back_blk = lax.dynamic_slice_in_dim(back_seq, first_row, block_rows, 0)
            sums_blk = lax.dynamic_index_in_dim(sums_seq, blk_index, 0, keepdims=False)
            scores = (
                jnp.einsum("qhd,khd->hqk", query_blk, key_seq, preferred_element_type=jnp.float32)
                * score_scale
            )
            causal = (first_row + jnp.arange(block_rows))[:, None] >= jnp.arange(length)[None, :]
            scores = jnp.where(causal[None], scores, masked_score)
            probs = jnp.exp(scores - sums_blk[..., None])
            probs_low = probs.astype(jnp.bfloat16)
            back_probs = jnp.einsum(
                "qhd,khd->hqk", back_blk, value_seq, preferred_element_type=jnp.float32
            )
            inner = jnp.sum(probs * back_probs, axis=-1, keepdims=True)
            back_scores = (probs * (back_probs - inner)).astype(jnp.bfloat16)
            query_grad = (
                jnp.einsum("hqk,khd->qhd", back_scores, key_seq, preferred_element_type=jnp.float32)
                * score_scale
            )
            key_acc = (
                key_acc
                + jnp.einsum(
                    "hqk,qhd->khd", back_scores, query_blk, preferred_element_type=jnp.float32
                )
                * score_scale
            )
            value_acc = value_acc + jnp.einsum(
                "hqk,qhd->khd", probs_low, back_blk, preferred_element_type=jnp.float32
            )
            return ((key_acc, value_acc), query_grad.astype(jnp.bfloat16))

        zeros_acc = jnp.zeros((length, local_heads, head_dim), jnp.float32)
        (key_acc, value_acc), query_grads = lax.scan(
            one_step, (zeros_acc, zeros_acc), jnp.arange(block_count)
        )
        return (
            query_grads.reshape(length, local_heads, head_dim),
            key_acc.astype(jnp.bfloat16),
            value_acc.astype(jnp.bfloat16),
        )

    query_grad, key_grad, value_grad = lax.map(one_sequence, jnp.arange(seq_count))
    return (
        query_grad.reshape(queries.shape),
        key_grad.reshape(queries.shape),
        value_grad.reshape(queries.shape),
    )


def pad_blocks(qkv_grad, out_grad_rows, fc_grad, proj_grad, width, head_width):
    return (
        jnp.pad(qkv_grad, ((0, 0), (0, width - 3 * head_width))),
        jnp.pad(out_grad_rows, ((0, width - head_width), (0, 0))),
        fc_grad,
        proj_grad,
    )


def per_device(
    inputs, out_grad, owners, master_slots, momentum_slots, small_master, small_first, small_second
):
    width = inputs.shape[1]
    tensor_count = lax.axis_size("tensor")
    tensor_idx = lax.axis_index("tensor")
    data_idx = lax.axis_index("dp")
    head_width = width // tensor_count
    ff_width = FF // tensor_count
    head_dim = width // HEADS
    local_heads = head_width // head_dim
    owner_row = lax.dynamic_index_in_dim(owners, tensor_idx, 0, keepdims=False)
    owned = owner_row == data_idx
    slot_value = master_slots[0]
    slot_low = slot_value.astype(jnp.bfloat16).astype(jnp.float32)
    offer_qkv = jnp.where(owned[0], slot_low[:, : 3 * head_width], 0.0)
    offer_out = jnp.where(owned[1], slot_low[:head_width, :], 0.0)
    offer_fc = jnp.where(owned[2], slot_low, 0.0)
    offer_proj = jnp.where(owned[3], slot_low, 0.0)
    sum_qkv, sum_out, sum_fc, sum_proj = lax.psum(
        (offer_qkv, offer_out, offer_fc, offer_proj), "dp"
    )
    w_qkv = sum_qkv.astype(jnp.bfloat16)
    w_out = sum_out.astype(jnp.bfloat16)
    w_fc = sum_fc.astype(jnp.bfloat16)
    w_proj = sum_proj.astype(jnp.bfloat16)
    params = lax.all_gather(small_master, ("dp", "tensor"), axis=0, tiled=True)
    gain_one = params[0:width]
    shift_one = params[width : 2 * width]
    bias_query = lax.dynamic_slice_in_dim(
        params, 2 * width + tensor_idx * head_width, head_width, 0
    )
    bias_value = lax.dynamic_slice_in_dim(
        params, 3 * width + tensor_idx * head_width, head_width, 0
    )
    bias_out = params[4 * width : 5 * width]
    gain_two = params[5 * width : 6 * width]
    shift_two = params[6 * width : 7 * width]
    bias_fc = lax.dynamic_slice_in_dim(params, 7 * width + tensor_idx * ff_width, ff_width, 0)
    bias_proj = params[7 * width + FF :]
    rows_in = inputs.astype(jnp.float32)
    normed = layer_norm(rows_in, gain_one, shift_one).astype(jnp.bfloat16)
    normed_all = lax.all_gather(normed, "tensor", axis=0, tiled=True)
    projected = jnp.dot(normed_all, w_qkv, preferred_element_type=jnp.float32)
    queries = (projected[:, :head_width] + bias_query).astype(jnp.bfloat16)
    keys_low = projected[:, head_width : 2 * head_width].astype(jnp.bfloat16)
    values_low = (projected[:, 2 * head_width :] + bias_value).astype(jnp.bfloat16)
    seq_count = normed_all.shape[0] // SEQ
    mixed_low, log_sums = attention_forward(
        queries, keys_low, values_low, seq_count, local_heads, head_dim
    )
    part_rows = mixed_low
    branch = lax.psum_scatter(
        jnp.dot(part_rows, w_out, preferred_element_type=jnp.float32).astype(jnp.bfloat16),
        "tensor",
        scatter_dimension=0,
        tiled=True,
    ).astype(jnp.float32)
    middle = rows_in + branch + bias_out
    normed_two = layer_norm(middle, gain_two, shift_two).astype(jnp.bfloat16)
    normed_two_all = lax.all_gather(normed_two, "tensor", axis=0, tiled=True)
    hidden_pre = jnp.dot(normed_two_all, w_fc, preferred_element_type=jnp.float32) + bias_fc
    hidden_act = jax.nn.gelu(hidden_pre, approximate=True).astype(jnp.bfloat16)
    part_rows = hidden_act
    branch_two = lax.psum_scatter(
        jnp.dot(part_rows, w_proj, preferred_element_type=jnp.float32).astype(jnp.bfloat16),
        "tensor",
        scatter_dimension=0,
        tiled=True,
    ).astype(jnp.float32)
    block_out = (middle + branch_two + bias_proj).astype(jnp.bfloat16)
    back_all = lax.all_gather(out_grad, "tensor", axis=0, tiled=True)
    grad_proj = jnp.einsum("gf,gd->fd", hidden_act, back_all, preferred_element_type=jnp.float32)
    back_act = jnp.einsum("gd,fd->gf", back_all, w_proj, preferred_element_type=jnp.float32)
    gelu_out, gelu_pull = jax.vjp(partial(jax.nn.gelu, approximate=True), hidden_pre)
    back_pre = gelu_pull(back_act)[0].astype(jnp.bfloat16)
    grad_fc = jnp.einsum("gd,gf->df", normed_two_all, back_pre, preferred_element_type=jnp.float32)
    fc_bias_grad = jnp.sum(back_pre, axis=0, dtype=jnp.float32)
    part_rows = back_pre
    back_normed_two = lax.psum_scatter(
        jnp.einsum("gf,df->gd", part_rows, w_fc, preferred_element_type=jnp.float32).astype(
            jnp.bfloat16
        ),
        "tensor",
        scatter_dimension=0,
        tiled=True,
    ).astype(jnp.float32)
    norm_out, norm_pull = jax.vjp(layer_norm, middle, gain_two, shift_two)
    back_middle_ln, gain_two_grad, shift_two_grad = norm_pull(back_normed_two)
    back_middle = out_grad.astype(jnp.float32) + back_middle_ln
    proj_bias_grad = jnp.sum(out_grad, axis=0, dtype=jnp.float32)
    out_bias_grad = jnp.sum(back_middle, axis=0)
    back_branch_all = lax.all_gather(back_middle.astype(jnp.bfloat16), "tensor", axis=0, tiled=True)
    grad_out = jnp.einsum(
        "ge,gd->ed", mixed_low, back_branch_all, preferred_element_type=jnp.float32
    )
    back_mixed = jnp.einsum(
        "gd,ed->ge", back_branch_all, w_out, preferred_element_type=jnp.float32
    ).astype(jnp.bfloat16)
    back_query, back_key, back_value = attention_backward(
        queries, keys_low, values_low, log_sums, back_mixed, seq_count, local_heads, head_dim
    )
    back_proj = jnp.concatenate([back_query, back_key, back_value], axis=1)
    grad_qkv = jnp.einsum("gd,ge->de", normed_all, back_proj, preferred_element_type=jnp.float32)
    query_bias_grad = jnp.sum(back_query, axis=0, dtype=jnp.float32)
    value_bias_grad = jnp.sum(back_value, axis=0, dtype=jnp.float32)
    part_rows = back_proj
    back_normed = lax.psum_scatter(
        jnp.einsum("ge,de->gd", part_rows, w_qkv, preferred_element_type=jnp.float32).astype(
            jnp.bfloat16
        ),
        "tensor",
        scatter_dimension=0,
        tiled=True,
    ).astype(jnp.float32)
    first_out, first_pull = jax.vjp(layer_norm, rows_in, gain_one, shift_one)
    back_in_ln, gain_one_grad, shift_one_grad = first_pull(back_normed)
    input_grad = back_middle + back_in_ln
    col_ids = jnp.arange(width)
    mask_qkv = jnp.broadcast_to((col_ids < 3 * head_width)[None, :], (width, width)).astype(
        jnp.float32
    )
    mask_out = jnp.broadcast_to((col_ids < head_width)[:, None], (width, width)).astype(jnp.float32)
    full_mask = jnp.ones((width, width), jnp.float32)
    masks = (mask_qkv, mask_out, full_mask, full_mask)
    qkv_sum, out_sum, fc_sum, proj_sum = lax.psum((grad_qkv, grad_out, grad_fc, grad_proj), "dp")
    padded = pad_blocks(qkv_sum, out_sum, fc_sum, proj_sum, width, head_width)
    chosen = jnp.zeros((width, width), jnp.float32)
    for kind in range(4):
        chosen = chosen + jnp.where(owned[kind], padded[kind], 0.0)
    full_grad = jnp.concatenate(
        [
            gain_one_grad,
            shift_one_grad,
            jnp.zeros((2 * width,), jnp.float32),
            out_bias_grad,
            gain_two_grad,
            shift_two_grad,
            jnp.zeros((FF,), jnp.float32),
            proj_bias_grad,
        ]
    )
    full_grad = lax.dynamic_update_slice_in_dim(
        full_grad, query_bias_grad, 2 * width + tensor_idx * head_width, 0
    )
    full_grad = lax.dynamic_update_slice_in_dim(
        full_grad, value_bias_grad, 3 * width + tensor_idx * head_width, 0
    )
    full_grad = lax.dynamic_update_slice_in_dim(
        full_grad, fc_bias_grad, 7 * width + tensor_idx * ff_width, 0
    )
    small_grad = lax.psum_scatter(full_grad, ("dp", "tensor"), scatter_dimension=0, tiled=True)
    first_new = beta_one * small_first + (1.0 - beta_one) * small_grad
    second_new = beta_two * small_second + (1.0 - beta_two) * small_grad * small_grad
    first_hat = first_new / (1.0 - beta_one**STEP)
    second_hat = second_new / (1.0 - beta_two**STEP)
    small_new = small_master - adam_rate * first_hat / (jnp.sqrt(second_hat) + adam_eps)
    valid = jnp.zeros((width, width), jnp.float32)
    for kind in range(4):
        valid = valid + jnp.where(owned[kind], masks[kind], 0.0)

    def run_owner(packed):
        return muon_update(packed[0], packed[1], packed[2], packed[3])

    def skip_owner(packed):
        blank_slot = jnp.zeros_like(packed[0])
        return (blank_slot, blank_slot, blank_slot)

    grad_slot, mom_slot, fresh_slot = lax.cond(
        jnp.any(owned), run_owner, skip_owner, (chosen, momentum_slots[0], slot_value, valid)
    )
    return (
        block_out,
        input_grad,
        grad_slot[None],
        mom_slot[None],
        fresh_slot[None],
        small_grad,
        second_new,
        small_new,
    )


def solution(mesh):
    return jax.shard_map(
        per_device,
        mesh=mesh,
        in_specs=(
            P(("dp", "tensor"), None),
            P(("dp", "tensor"), None),
            P(),
            P("dp", "tensor", None),
            P("dp", "tensor", None),
            P(("dp", "tensor")),
            P(("dp", "tensor")),
            P(("dp", "tensor")),
        ),
        out_specs=(
            P(("dp", "tensor"), None),
            P(("dp", "tensor"), None),
            P("dp", "tensor", None),
            P("dp", "tensor", None),
            P("dp", "tensor", None),
            P(("dp", "tensor")),
            P(("dp", "tensor")),
            P(("dp", "tensor")),
        ),
        check_vma=False,
    )
```

profile of v0, /device:TPU:8, one launch (start us, length us, event | category | flops | bytes accessed | tf_op | source)
XLA Modules:
  0.0 1586.4 jit_solution(6755935395835183061)
XLA Ops:
  11.0 35.5 %all-gather = f32[32,1,384]{2,1,0:T(1,128)S(1)} all-gather(f32[1,1,384]{2,1,0:T(1,128)S(1)} %reshape.235), channel_id=1, replica_groups=mesh['dp'=8,'tensor'=4] {'dp','tensor'}, dimensions={0}, use_global_device_ids=true | all-gather | bytes 50688 | tf_op jit(solution)/shard_map/all_gather | solution.py:204
  63.8 489.1 %all-reduce.9 = (bf16[1024,1024]{1,0:T(8,128)(2,1)}, bf16[1024,768]{1,0:T(8,128)(2,1)S(1)}, bf16[256,1024]{1,0:T(8,128)(2,1)}, bf16[1024,1024]{1,0:T(8,128)(2,1)}) all-reduce(f32[1024,1024]{1,0:T(8,128)} %get-tuple-element.573, f32[1024,768]{1,0:T(8,128)} %slice_select_fusion, ...), channel_id=1, replica_groups=mesh['dp'=8,'tensor'=4] {'dp'}, use_global_device_ids=true, to_apply=%region_12.13 | all-reduce | flops 3145728 | bytes 18874368 | tf_op jit(solution)/shard_map/psum | solution.py:197
  574.0 53.3 %while.44 = (s32[]{:T(128)}, bf16[4,512,4,64]{1,3,2,0:T(8,128)(2,1)}, f32[4,4,512]{2,1,0:T(4,128)S(1)}, s32[4]{0:T(128)S(1)}, bf16[2,1024,4,64]{1,3,2,0:T(8,128)...) while((s32[]{:T(128)}, ...), condition=%wide.region_6.7_spmd, body=%wide.region_3.6_spmd.sunk | while | flops 562690560 | bytes 28905944 | solution.py:91
  634.1 55.9 %reduce-scatter.5.cloned.1.call-done = bf16[512,1024]{1,0:T(8,128)(2,1)} async-done(((bf16[2048,1024]{1,0:T(8,128)(2,1)}), bf16[512,1024]{1,0:T(8,128)(2,1)}) %reduce-scatter.5.cloned.1.call-update) | async-done | bytes 1048592 | tf_op jit(solution)/shard_map/reduce_scatter | solution.py:230
  695.7 34.0 %all-gather.8.cloned.1.call-done = bf16[2048,1024]{1,0:T(8,128)(2,1)} async-done(((bf16[512,1024]{1,0:T(8,128)(2,1)}), bf16[2048,1024]{1,0:T(8,128)(2,1)}) %all-gather.8.cloned.1.call-update) | async-done | bytes 4194320 | tf_op jit(solution)/shard_map/all_gather | solution.py:238
  729.8 11.4 fusion.134
  741.2 24.6 %all-gather.10.cloned.1.call-done = bf16[2048,1024]{1,0:T(8,128)(2,1)} async-done(((bf16[512,1024]{1,0:T(8,128)(2,1)}), bf16[2048,1024]{1,0:T(8,128)(2,1)}) %all-gather.10.cloned.1.call-update) | async-done | bytes 4194320 | tf_op jit(solution)/shard_map/all_gather | solution.py:249
  765.8 13.8 convert_reduce_fusion
  781.6 6.2 convolution_convert_fusion.2
  788.1 11.8 convolution_convert_fusion.3
  800.0 32.5 %reduce-scatter.9.cloned.1.call-done = bf16[512,1024]{1,0:T(8,128)(2,1)} async-done(((bf16[2048,1024]{1,0:T(8,128)(2,1)}), bf16[512,1024]{1,0:T(8,128)(2,1)}) %reduce-scatter.9.cloned.1.call-update) | async-done | bytes 1048592 | tf_op jit(solution)/shard_map/reduce_scatter | solution.py:257
  838.4 41.6 %reduce-scatter.7.cloned.1.call-done = bf16[512,1024]{1,0:T(8,128)(2,1)} async-done(((bf16[2048,1024]{1,0:T(8,128)(2,1)}), bf16[512,1024]{1,0:T(8,128)(2,1)}) %reduce-scatter.7.cloned.1.call-update) | async-done | bytes 1048592 | tf_op jit(solution)/shard_map/reduce_scatter | solution.py:242
  886.9 34.5 %all-gather.12.cloned.1.call-done = bf16[2048,1024]{1,0:T(8,128)(2,1)} async-done(((bf16[512,1024]{1,0:T(8,128)(2,1)}), bf16[2048,1024]{1,0:T(8,128)(2,1)}) %all-gather.12.cloned.1.call-update) | async-done | bytes 4194320 | tf_op jit(solution)/shard_map/all_gather | solution.py:270
  931.5 83.5 %while.46 = (s32[]{:T(128)}, bf16[2,1024,4,64]{3,2,1,0:T(4,128)(2,1)}, bf16[2,1024,4,64]{1,3,2,0:T(8,128)(2,1)}, bf16[2,1024,4,64]{1,3,2,0:T(8,128)(2,1)}, s32[2...) while((s32[]{:T(128)}, ...), condition=%wide.region_21.22_spmd, body=%wide.region_17.21_spmd.sunk | while | flops 1376254464 | bytes 103117632 | solution.py:161
  937.5 30.3 %while.47 = (s32[]{:T(128)}, f32[1024,4,64]{0,2,1:T(8,128)S(1)}, f32[1024,4,64]{0,2,1:T(8,128)}, bf16[2,512,4,64]{1,3,2,0:T(8,128)(2,1)}, s32[2]{0:T(128)S(1)}, ...) while((s32[]{:T(128)}, f32[1024,4,64]{0,2,1:T(8,128)S(1)}, ...), condition=%wide.region_20.20_spmd.clone, body=%wide.region_18.19_spmd.clone.sunk | while | flops 1375730176 | bytes 84734344 | solution.py:152
  979.0 30.3 %while.47 = (s32[]{:T(128)}, f32[1024,4,64]{0,2,1:T(8,128)S(1)}, f32[1024,4,64]{0,2,1:T(8,128)}, bf16[2,512,4,64]{1,3,2,0:T(8,128)(2,1)}, s32[2]{0:T(128)S(1)}, ...) while((s32[]{:T(128)}, f32[1024,4,64]{0,2,1:T(8,128)S(1)}, ...), condition=%wide.region_20.20_spmd.clone, body=%wide.region_18.19_spmd.clone.sunk | while | flops 1375730176 | bytes 84734344 | solution.py:152
  1023.1 7.6 convolution_convert_fusion.1
  1030.9 10.2 fusion.133
  1041.1 11.8 fusion.120
  1068.2 7.0 reduce-scatter.11.cloned.1.call-done
  1080.5 44.4 %all-reduce.2 = f32[12288]{0:T(1024)S(1)} all-reduce(f32[12288]{0:T(1024)S(1)} %dynamic_update_slice.41), channel_id=6, replica_groups=mesh['dp'=8,'tensor'=4] {'dp','tensor'}, use_global_device_ids=true, to_apply=%region_42.43.clone | all-reduce | flops 12288 | bytes 98304
  1128.9 351.4 %all-reduce.8.cloned.1.call-done = (f32[1024,768]{1,0:T(8,128)}, f32[256,1024]{1,0:T(8,128)}, f32[1024,1024]{1,0:T(8,128)}, f32[1024,1024]{1,0:T(8,128)}) async-done(((f32[1024,768]{1,0:T(8,128)}, f32[256,1024]{1,0:T(8,128)}, f32[1024,1024]{1,0:T(8,128)}, f32[1024,1024]{1,0:T(8,128)}), (f32[1024,768]{1,0:T(8,128)}, f32[256,1024]{1,0:T(8,128)}, f32[1024,1024]{1,0:T(8,128)}, ...) | async-done | bytes 12582928 | tf_op jit(solution)/shard_map/psum | solution.py:303
  1484.8 94.8 %conditional.1 = (f32[1,1024,1024]{2,1,0:T(8,128)}, f32[1,1024,1024]{2,1,0:T(8,128)}, f32[1,1024,1024]{2,1,0:T(8,128)}) conditional(s32[]{:T(128)} %convert_element_type.281, () %tuple.51, (pred[]{:T(512)}, f32[1024,768]{1,0:T(8,128)}, f32[1024,1024]{1,0:T(8,128)}, pred[]{:T(512)}, f32[256,1024]{1,0:T(8,128)S(1)}, ...), branch_computations={%region_30.31_spmd, %region_31.33_spmd} | conditional | flops 32294049792 | bytes 111190160 | solution.py:346
  1487.3 12.6 multiply_reduce_fusion
  1505.5 7.2 fusion.43
  1512.7 9.9 add_convert_fusion.8
  1526.2 8.8 add_convert_fusion.6
  1535.0 6.3 fusion.129
  1541.3 8.8 add_convert_fusion.4
  1550.2 5.9 fusion.130
  1556.1 8.7 add_convert_fusion.2
  1568.5 10.9 multiply_bitcast_fusion
  (321 shorter events, 241.3 us)
Async XLA Ops:
  7.2 545.7 %all-gather.6.cloned.1.call-start = ((), (), s32[]{:S(2)}) async-start(), calls=%async_computation.4 | async-start | bytes 5242880 | tf_op jit(solution)/shard_map/all_gather | solution.py:220
  9.3 45.0 %copy-start.23 = (f32[512]{0:T(512)}, f32[512]{0:T(512)S(1)}, u32[]{:S(2)}) copy-start(f32[512]{0:T(512)S(1)} %broadcast_multiply_fusion.1) | copy-start | bytes 6148
  11.0 35.5 %copy-start.27 = (f32[512]{0:T(512)}, f32[512]{0:T(512)S(1)}, u32[]{:S(2)}) copy-start(f32[512]{0:T(512)S(1)} %fusion.92) | copy-start | bytes 6148
  11.0 43.4 %copy-start.25 = (f32[512]{0:T(512)}, f32[512]{0:T(512)S(1)}, u32[]{:S(2)}) copy-start(f32[512]{0:T(512)S(1)} %fusion.114) | copy-start | bytes 6148
  47.1 740.9 %copy-start.35 = (f32[1024]{0:T(1024)}, f32[1024]{0:T(1024)S(1)}, u32[]{:S(2)}) copy-start(f32[1024]{0:T(1024)S(1)} %get-tuple-element.577) | copy-start | bytes 12292
  49.8 640.2 %reduce-scatter.5.cloned.1.call-start = ((), (), s32[]{:S(2)}) async-start(), calls=%async_computation.5 | async-start | bytes 5242880 | tf_op jit(solution)/shard_map/reduce_scatter | solution.py:230
  634.0 56.0 %copy-start = (bf16[512,1024]{1,0:T(8,128)(2,1)S(1)}, bf16[512,1024]{1,0:T(8,128)(2,1)}, u32[]{:S(2)}) copy-start(bf16[512,1024]{1,0:T(8,128)(2,1)} %param.16) | copy-start | bytes 3145732
  634.0 95.8 %all-gather.8.cloned.1.call-start = ((), (), s32[]{:S(2)}) async-start(), calls=%async_computation.6 | async-start | bytes 5242880 | tf_op jit(solution)/shard_map/all_gather | solution.py:238
  695.1 70.7 %all-gather.10.cloned.1.call-start = ((), (), s32[]{:S(2)}) async-start(), calls=%async_computation.8 | async-start | bytes 5242880 | tf_op jit(solution)/shard_map/all_gather | solution.py:249
  695.7 136.8 %reduce-scatter.9.cloned.1.call-start = ((), (), s32[]{:S(2)}) async-start(), calls=%async_computation.9 | async-start | bytes 5242880 | tf_op jit(solution)/shard_map/reduce_scatter | solution.py:257
  765.8 15.8 copy-start.43
  787.8 92.1 %reduce-scatter.7.cloned.1.call-start = ((), (), s32[]{:S(2)}) async-start(), calls=%async_computation.7 | async-start | bytes 5242880 | tf_op jit(solution)/shard_map/reduce_scatter | solution.py:242
  799.9 80.1 %copy-start.29 = (f32[1024]{0:T(1024)S(1)}, f32[1024]{0:T(1024)}, u32[]{:S(2)}) copy-start(f32[1024]{0:T(1024)} %get-tuple-element.576) | copy-start | bytes 12292
  799.9 121.5 %all-gather.12.cloned.1.call-start = ((), (), s32[]{:S(2)}) async-start(), calls=%async_computation.10 | async-start | bytes 5242880 | tf_op jit(solution)/shard_map/all_gather | solution.py:270
  884.3 37.1 %copy-start.20 = (bf16[256,1024]{1,0:T(8,128)(2,1)S(1)}, bf16[256,1024]{1,0:T(8,128)(2,1)}, u32[]{:S(2)}) copy-start(bf16[256,1024]{1,0:T(8,128)(2,1)} %get-tuple-element.548) | copy-start | bytes 1572868
  886.8 188.5 %reduce-scatter.11.cloned.1.call-start = ((), (), s32[]{:S(2)}) async-start(), calls=%async_computation.11 | async-start | bytes 5242880 | tf_op jit(solution)/shard_map/reduce_scatter | solution.py:285
  1030.7 449.6 %all-reduce.8.cloned.1.call-start = ((), (), s32[]{:S(2)}) async-start(), calls=%async_computation.12 | async-start | bytes 25165824 | tf_op jit(solution)/shard_map/psum | solution.py:303
  1041.1 11.8 copy-start.14
  1061.8 13.4 copy-start.1
  1061.8 13.4 copy-start.22
  1061.8 13.4 copy-start.24
  1061.8 15.3 copy-start.28
  1061.9 15.3 copy-start.26
  1061.9 17.8 %copy-start.33 = (f32[1024]{0:T(1024)S(1)}, f32[1024]{0:T(1024)}, u32[]{:S(2)}) copy-start(f32[1024]{0:T(1024)} %get-tuple-element.560) | copy-start | bytes 12292
  1061.9 17.8 %copy-start.31 = (f32[1024]{0:T(1024)S(1)}, f32[1024]{0:T(1024)}, u32[]{:S(2)}) copy-start(f32[1024]{0:T(1024)} %get-tuple-element.484) | copy-start | bytes 12292
  1061.9 17.8 %copy-start.30 = (f32[1024]{0:T(1024)S(1)}, f32[1024]{0:T(1024)}, u32[]{:S(2)}) copy-start(f32[1024]{0:T(1024)} %get-tuple-element.488) | copy-start | bytes 12292
  1061.9 17.8 %copy-start.32 = (f32[1024]{0:T(1024)S(1)}, f32[1024]{0:T(1024)}, u32[]{:S(2)}) copy-start(f32[1024]{0:T(1024)} %get-tuple-element.575) | copy-start | bytes 12292
  1061.9 18.4 %copy-start.37 = (f32[1024]{0:T(1024)S(1)}, f32[1024]{0:T(1024)}, u32[]{:S(2)}) copy-start(f32[1024]{0:T(1024)} %get-tuple-element.589) | copy-start | bytes 12292
  1061.9 63.0 %copy-start.34 = (f32[384]{0:T(512)S(1)}, f32[384]{0:T(512)}, u32[]{:S(2)}) copy-start(f32[384]{0:T(512)} %param.21) | copy-start | bytes 4612
  1061.9 63.0 %copy-start.38 = (f32[384]{0:T(512)S(1)}, f32[384]{0:T(512)}, u32[]{:S(2)}) copy-start(f32[384]{0:T(512)} %param.22) | copy-start | bytes 4612
  1061.9 63.0 %copy-start.39 = (f32[384]{0:T(512)S(1)}, f32[384]{0:T(512)}, u32[]{:S(2)}) copy-start(f32[384]{0:T(512)} %param.23) | copy-start | bytes 4612
  1062.0 63.7 %copy-start.8 = (f32[512,1024]{1,0:T(8,128)S(1)}, f32[512,1024]{1,0:T(8,128)}, u32[]{:S(2)}) copy-start(f32[512,1024]{1,0:T(8,128)} %copy-done.7) | copy-start | bytes 6291460
  (38 other events, 138.0 us)
Sparse Core Ops, SparseCore 0:
  49.9 36.8 all-gather.5
  634.1 55.8 reduce-scatter.4
  695.2 34.4 all-gather.7
  731.2 34.4 all-gather.9
  788.0 44.4 reduce-scatter.8
  835.4 44.4 reduce-scatter.6
  886.9 34.4 all-gather.11
  1030.8 44.3 reduce-scatter.10
  1080.6 399.6 all-reduce.7
where the time goes:
time: 1590 us
  waiting for transfers between devices  582 us (37%)
  blocking collectives  569 us (36%)
  matrix products  235 us (15%)
  other arithmetic  95.8 us (6%)
  local copies, waits for them, and re-layouts  61.4 us (4%)
  loops' own time  27.1 us (2%)
    psum x1, blocking collectives, per_device(): lax.psum((offer_qkv, offer_out, offer_fc, offer_proj), 'dp')  489 us
    psum x1, waiting for transfers between devices, per_device(): lax.psum((grad_qkv, grad_out, grad_fc, grad_proj), 'dp')  351 us
    reduce_scatter x1, waiting for transfers between devices, per_device(): lax.psum_scatter(jnp.dot(part_rows, w_out, preferred_element_type=jnp.flo...  55.9 us
    dot_general x5, matrix products, newton_schulz(): jnp.dot(poly_mat, iterate, preferred_element_type=jnp.float32)  47.1 us
    unnamed x1, blocking collectives  44.4 us
    reduce_scatter x1, waiting for transfers between devices, per_device(): lax.psum_scatter(jnp.dot(part_rows, w_proj, preferred_element_type=jnp.fl...  41.6 us
    all_gather x1, blocking collectives, per_device(): params = lax.all_gather(small_master, ('dp', 'tensor'), axis=0, tiled=True)  35.5 us
    all_gather x1, waiting for transfers between devices, per_device(): lax.all_gather(back_middle.astype(jnp.bfloat16), 'tensor', axis=0, tiled=...  34.5 us
  transfers between devices with their start and end apart: 9, of which 8 were waited for; matrix products, arithmetic and copies ran while one was open for 6% of the time, Pallas kernels for 0%

commit v1 on v0

v1 whole, which is shorter than its diff:
```python
from functools import partial

import jax
import jax.numpy as jnp
from jax import lax
from jax.experimental import pallas as pl
from jax.experimental.pallas import tpu as pltpu
from jax.sharding import PartitionSpec as P

HEADS = 16
FF = 4096
SEQ = 1024
NS_STEPS = 5
STEP = 10
HEAD_DIM = 64

ln_eps = 1e-05
mom_decay = 0.95
ns_a = 3.4445
ns_b = -4.775
ns_c = 2.0315
muon_rate = 0.5
muon_decay = 0.01
beta_one = 0.9
beta_two = 0.95
adam_rate = 0.2
adam_eps = 1e-08
masked_score = -1e30
gelu_in = 0.7978845608028654
gelu_cube = 0.044715

CHUNKS = 2
TILE = 256
VMEM_GRANT = 48 * 1024 * 1024
BF16 = jnp.bfloat16
F32 = jnp.float32

NN = (((1,), (0,)), ((), ()))
NT = (((1,), (1,)), ((), ()))
TN = (((0,), (0,)), ((), ()))


def mm(left, right, dims=NN):
    return lax.dot_general(left, right, dims, preferred_element_type=F32)


def rows2(value):
    return value.reshape(-1, value.shape[-1])


def head_ids(shape):
    return lax.broadcasted_iota(jnp.int32, shape, 1) // HEAD_DIM


def causal_tile(tile):
    row = lax.broadcasted_iota(jnp.int32, (tile, tile), 0)
    col = lax.broadcasted_iota(jnp.int32, (tile, tile), 1)
    return row >= col


def attend_kernel(core_ref, q_ref, k_ref, v_ref, o_ref, lse_ref, *, subs, heads):
    core = core_ref[0]
    place = (core, 1 - core)
    width = q_ref.shape[-1]
    col_head = head_ids((TILE, width))
    lane = lax.broadcasted_iota(jnp.int32, (TILE, 128), 1)
    causal = causal_tile(TILE)
    per_half = k_ref.shape[2] // TILE
    for half in range(2):
        for at, sub in enumerate(subs):
            blk = per_half * half + sub
            rows = slice(at * TILE, (at + 1) * TILE)
            q_blk = q_ref[place[half], 0, rows, :]
            acc = jnp.zeros((TILE, width), F32)
            lse = jnp.zeros((TILE, 128), F32)
            for head in range(heads):
                q_one = jnp.where(col_head == head, q_blk, jnp.zeros_like(q_blk))
                scores = []
                for j in range(blk + 1):
                    cols = slice((j % per_half) * TILE, (j % per_half + 1) * TILE)
                    s = mm(q_one, k_ref[place[j // per_half], 0, cols, :], NT)
                    if j == blk:
                        s = jnp.where(causal, s, masked_score)
                    scores.append(s)
                top = scores[0]
                for s in scores[1:]:
                    top = jnp.maximum(top, s)
                top = jnp.max(top, axis=1, keepdims=True)
                total = jnp.zeros((TILE, TILE), F32)
                out = jnp.zeros((TILE, width), F32)
                for j in range(blk + 1):
                    cols = slice((j % per_half) * TILE, (j % per_half + 1) * TILE)
                    p = jnp.exp(scores[j] - top)
                    total = total + p
                    out = out + mm(p.astype(BF16), v_ref[place[j // per_half], 0, cols, :])
                total = jnp.sum(total, axis=1, keepdims=True)
                acc = jnp.where(col_head == head, out * (1.0 / total), acc)
                lse = jnp.where(lane == head, top + jnp.log(total), lse)
            o_ref[place[half], 0, rows, :] = acc.astype(BF16)
            lse_ref[place[half], 0, rows, :] = lse


def attend(core, qkv, chunk, chunks):
    _, seqs, rows, triple = qkv.shape
    width = triple // 3
    part = rows // chunks
    per = part // TILE
    subs = tuple(range(chunk * per, (chunk + 1) * per))
    return pl.pallas_call(
        partial(attend_kernel, subs=subs, heads=width // HEAD_DIM),
        grid_spec=pltpu.PrefetchScalarGridSpec(
            num_scalar_prefetch=1,
            grid=(seqs,),
            in_specs=[
                pl.BlockSpec((2, 1, part, width), lambda s, c: (0, s, chunk, 0)),
                pl.BlockSpec((2, 1, rows, width), lambda s, c: (0, s, 0, 1)),
                pl.BlockSpec((2, 1, rows, width), lambda s, c: (0, s, 0, 2)),
            ],
            out_specs=[
                pl.BlockSpec((2, 1, part, width), lambda s, c: (0, s, 0, 0)),
                pl.BlockSpec((2, 1, part, 128), lambda s, c: (0, s, 0, 0)),
            ],
        ),
        out_shape=[
            jax.ShapeDtypeStruct((2, seqs, part, width), BF16),
            jax.ShapeDtypeStruct((2, seqs, part, 128), F32),
        ],
        compiler_params=pltpu.CompilerParams(vmem_limit_bytes=VMEM_GRANT),
        cost_estimate=pl.CostEstimate(
            flops=10 * 10**9 // chunks, bytes_accessed=6 * 10**6, transcendentals=0
        ),
    )(core, qkv, qkv, qkv)


def attend_back_kernel(
    core_ref, q_ref, k_ref, v_ref, *refs, heads, chunks
):
    o_refs = refs[0:chunks]
    lse_refs = refs[chunks : 2 * chunks]
    do_ref = refs[2 * chunks]
    out_ref, dk_acc, dv_acc = refs[2 * chunks + 1 :]
    core = core_ref[0]
    place = (core, 1 - core)
    width = q_ref.shape[-1]
    col_head = head_ids((TILE, width))
    causal = causal_tile(TILE)
    per_half = k_ref.shape[2] // TILE
    per_chunk = per_half // chunks
    dk_acc[...] = jnp.zeros_like(dk_acc)
    dv_acc[...] = jnp.zeros_like(dv_acc)
    for half in range(2):
        for sub in range(per_half):
            blk = per_half * half + sub
            rows = slice(sub * TILE, (sub + 1) * TILE)
            inner = slice((sub % per_chunk) * TILE, (sub % per_chunk + 1) * TILE)
            q_blk = q_ref[place[half], 0, rows, :]
            do_blk = do_ref[place[half], 0, rows, :]
            o_blk = o_refs[sub // per_chunk][place[half], 0, inner, :]
            lse_blk = lse_refs[sub // per_chunk][place[half], 0, inner, :]
            overlap = do_blk.astype(F32) * o_blk.astype(F32)
            q_all, do_all, lse_all, delta_all = [], [], [], []
            for head in range(heads):
                mine = col_head == head
                q_all.append(jnp.where(mine, q_blk, jnp.zeros_like(q_blk)))
                do_all.append(jnp.where(mine, do_blk, jnp.zeros_like(do_blk)))
                lse_all.append(lse_blk[:, head : head + 1])
                delta_all.append(jnp.sum(jnp.where(mine, overlap, 0.0), axis=1, keepdims=True))
            q_cat = jnp.concatenate(q_all, axis=0)
            do_cat = jnp.concatenate(do_all, axis=0)
            dq = [jnp.zeros((TILE, width), F32) for _ in range(heads)]
            for j in range(blk + 1):
                cols = slice((j % per_half) * TILE, (j % per_half + 1) * TILE)
                k_blk = k_ref[place[j // per_half], 0, cols, :]
                v_blk = v_ref[place[j // per_half], 0, cols, :]
                p_all, ds_all = [], []
                for head in range(heads):
                    p = jnp.exp(mm(q_all[head], k_blk, NT) - lse_all[head])
                    if j == blk:
                        p = jnp.where(causal, p, 0.0)
                    dp = mm(do_all[head], v_blk, NT)
                    ds = (p * (dp - delta_all[head])).astype(BF16)
                    dq[head] = dq[head] + mm(ds, k_blk)
                    p_all.append(p.astype(BF16))
                    ds_all.append(ds)
                dk_acc[j] += mm(jnp.concatenate(ds_all, axis=0), q_cat, TN)
                dv_acc[j] += mm(jnp.concatenate(p_all, axis=0), do_cat, TN)
            total = dq[0]
            for head in range(1, heads):
                total = jnp.where(col_head == head, dq[head], total)
            out_ref[place[half], 0, rows, 0:width] = (total * HEAD_DIM**-0.5).astype(BF16)
    for j in range(2 * per_half):
        rows = slice((j % per_half) * TILE, (j % per_half + 1) * TILE)
        out_ref[place[j // per_half], 0, rows, width : 2 * width] = dk_acc[j].astype(BF16)
        out_ref[place[j // per_half], 0, rows, 2 * width :] = dv_acc[j].astype(BF16)


def attend_back(core, qkv, outs, lses, back):
    _, seqs, rows, triple = qkv.shape
    width = triple // 3
    chunks = len(outs)
    part = rows // chunks

    def block(size, cols, at):
        return pl.BlockSpec((2, 1, size, cols), lambda s, c: (0, s, 0, at))

    return pl.pallas_call(
        partial(attend_back_kernel, heads=width // HEAD_DIM, chunks=chunks),
        grid_spec=pltpu.PrefetchScalarGridSpec(
            num_scalar_prefetch=1,
            grid=(seqs,),
            in_specs=[block(rows, width, 0), block(rows, width, 1), block(rows, width, 2)]
            + [block(part, width, 0)] * chunks
            + [block(part, 128, 0)] * chunks
            + [block(rows, width, 0)],
            out_specs=block(rows, triple, 0),
            scratch_shapes=[pltpu.VMEM((2 * rows // TILE, TILE, width), F32)] * 2,
        ),
        out_shape=jax.ShapeDtypeStruct(qkv.shape, BF16),
        compiler_params=pltpu.CompilerParams(vmem_limit_bytes=VMEM_GRANT),
        cost_estimate=pl.CostEstimate(
            flops=25 * 10**9, bytes_accessed=12 * 10**6, transcendentals=0
        ),
    )(core, qkv, qkv, qkv, *outs, *lses, back)


def schulz_kernel(x_ref, o_ref, x_buf, gram, poly):
    size = x_ref.shape[0]
    tiles = size // TILE
    x_buf[0] = x_ref[...]

    def one_turn(turn, carry):
        now = lax.rem(turn, 2)
        later = 1 - now

        def gram_rows(r, c):
            rows = pl.ds(pl.multiple_of(r * TILE, TILE), TILE)
            gram[rows, :] = mm(x_buf[now, rows, :], x_buf[now], NT).astype(BF16)
            return c

        lax.fori_loop(0, tiles, gram_rows, 0)

        def poly_rows(r, c):
            rows = pl.ds(pl.multiple_of(r * TILE, TILE), TILE)
            mine = gram[rows, :]
            poly[rows, :] = (ns_b * mine.astype(F32) + ns_c * mm(mine, gram[...])).astype(BF16)
            return c

        lax.fori_loop(0, tiles, poly_rows, 0)

        def next_rows(r, c):
            rows = pl.ds(pl.multiple_of(r * TILE, TILE), TILE)
            x_buf[later, rows, :] = (
                ns_a * x_buf[now, rows, :].astype(F32) + mm(poly[rows, :], x_buf[now])
            ).astype(BF16)
            return c

        lax.fori_loop(0, tiles, next_rows, 0)
        return carry

    lax.fori_loop(0, NS_STEPS, one_turn, 0)
    o_ref[...] = x_buf[NS_STEPS % 2]


def newton_schulz(start):
    size = start.shape[0]
    return pl.pallas_call(
        schulz_kernel,
        in_specs=[pl.BlockSpec(memory_space=pltpu.VMEM)],
        out_specs=pl.BlockSpec(memory_space=pltpu.VMEM),
        out_shape=jax.ShapeDtypeStruct(start.shape, BF16),
        scratch_shapes=[
            pltpu.VMEM((2, size, size), BF16),
            pltpu.VMEM((size, size), BF16),
            pltpu.VMEM((size, size), BF16),
        ],
        compiler_params=pltpu.CompilerParams(vmem_limit_bytes=VMEM_GRANT),
        cost_estimate=pl.CostEstimate(
            flops=6 * NS_STEPS * size**3, bytes_accessed=4 * size * size, transcendentals=0
        ),
    )(start)


def swap(value, bit):
    count = lax.axis_size("tensor")
    return lax.ppermute(value, "tensor", [(i, i ^ bit) for i in range(count)])


def gather_pair(value):
    mine = jnp.stack([value, swap(value, 2)])
    return mine, swap(mine, 1)


def scatter_sum(keep_in, send_in, weight, dims):
    shape = keep_in.shape[:-1] + (-1,)
    send = mm(rows2(send_in), weight, dims).astype(BF16).reshape(shape)
    arrived = swap(send, 1)
    keep = mm(rows2(keep_in), weight, dims).reshape(shape)
    part = keep + arrived.astype(F32)
    far = swap(part[1].astype(BF16), 2)
    return part[0] + far.astype(F32)


def axis_bits(name):
    count = lax.axis_size(name)
    bits = []
    bit = 1
    while bit < count:
        bits.append(bit)
        bit *= 2
    return bits


def small_gather(value):
    piece = value.reshape(1, -1)
    for name in ("tensor", "dp"):
        index = lax.axis_index(name)
        count = lax.axis_size(name)
        for bit in axis_bits(name):
            other = lax.ppermute(piece, name, [(i, i ^ bit) for i in range(count)])
            upper = (index & bit) != 0
            piece = jnp.where(
                upper,
                jnp.concatenate([other, piece], axis=0),
                jnp.concatenate([piece, other], axis=0),
            )
    return piece.reshape(-1)


def small_scatter(value):
    for name in ("dp", "tensor"):
        index = lax.axis_index(name)
        count = lax.axis_size(name)
        for bit in reversed(axis_bits(name)):
            low, high = jnp.split(value, 2)
            upper = (index & bit) != 0
            give = jnp.where(upper, low, high)
            keep = jnp.where(upper, high, low)
            value = keep + lax.ppermute(give, name, [(i, i ^ bit) for i in range(count)])
    return value


def norm_parts(values):
    centred = values - jnp.mean(values, axis=-1, keepdims=True)
    spread = jnp.mean(centred * centred, axis=-1, keepdims=True)
    scale = lax.rsqrt(spread + ln_eps)
    return centred * scale, scale


def norm_back(unit, scale, gain_vec, grad):
    inner = grad * gain_vec
    return scale * (
        inner
        - jnp.mean(inner, axis=-1, keepdims=True)
        - unit * jnp.mean(inner * unit, axis=-1, keepdims=True)
    )


def per_device(
    inputs, out_grad, owners, master_slots, momentum_slots, small_master, small_first, small_second
):
    rows_dev, width = inputs.shape
    tensor_count = lax.axis_size("tensor")
    data_count = lax.axis_size("dp")
    tensor_idx = lax.axis_index("tensor")
    data_idx = lax.axis_index("dp")
    head_width = width // tensor_count
    ff_width = FF // tensor_count
    share = width // data_count
    share_out = head_width // data_count
    core = jnp.reshape(tensor_idx & 1, (1,)).astype(jnp.int32)
    owner_row = lax.dynamic_index_in_dim(owners, tensor_idx, 0, keepdims=False)
    owned = owner_row == data_idx
    slot_value = master_slots[0]

    slot_low = slot_value.astype(BF16)
    offer_out = jnp.pad(
        slot_low[:head_width].reshape(data_count, share_out, width),
        ((0, 0), (0, share - share_out), (0, 0)),
    )
    offer = jnp.where(owned[1], offer_out, slot_low.reshape(data_count, share, width))
    shares = lax.all_to_all(offer, "dp", 0, 0)

    def share_of(kind):
        return lax.dynamic_index_in_dim(shares, owner_row[kind], 0, keepdims=False)

    def gather_rows(value):
        return lax.all_gather(value, "dp", axis=0, tiled=True)

    w_qkv = gather_rows(share_of(0)[:, : 3 * head_width])
    w_out = gather_rows(share_of(1)[:share_out])
    w_proj = gather_rows(share_of(3))
    w_fc = gather_rows(share_of(2))

    params = small_gather(small_master)

    def own_slice(start, size):
        return lax.dynamic_slice_in_dim(params, start + tensor_idx * size, size, 0)

    gain_one = params[0:width]
    shift_one = params[width : 2 * width]
    bias_query = own_slice(2 * width, head_width)
    bias_value = own_slice(3 * width, head_width)
    bias_out = params[4 * width : 5 * width]
    gain_two = params[5 * width : 6 * width]
    shift_two = params[6 * width : 7 * width]
    bias_fc = own_slice(7 * width, ff_width)
    bias_proj = params[7 * width + FF :]

    rows_in = inputs.astype(F32)
    unit_one, scale_one = norm_parts(rows_in)
    normed = (unit_one * gain_one + shift_one).astype(BF16)
    normed_all = jnp.stack(gather_pair(normed))
    dy_pair = gather_pair(out_grad)
    bias_qkv = jnp.concatenate([bias_query, jnp.zeros_like(bias_query), bias_value])
    scale_qkv = jnp.where(jnp.arange(3 * head_width) < head_width, HEAD_DIM**-0.5, 1.0)
    qkv = ((mm(rows2(normed_all), w_qkv) + bias_qkv) * scale_qkv).astype(BF16)
    qkv = qkv.reshape(2, 2, rows_dev, 3 * head_width)
    back_act = [mm(rows2(dy), w_proj, NT).astype(BF16) for dy in dy_pair]

    part = rows_dev // CHUNKS
    mixed, log_sums = [], []
    for chunk in range(CHUNKS):
        mixed_one, sums_one = attend(core, qkv, chunk, CHUNKS)
        mixed.append(mixed_one)
        log_sums.append(sums_one)
    middles, branches, grad_proj, grad_fc, fc_bias_grad = [], [], 0.0, 0.0, 0.0
    back_normed_two, mine_two = [], []
    for chunk in range(CHUNKS):
        rows = slice(chunk * part, (chunk + 1) * part)
        branch = scatter_sum(mixed[chunk][0], mixed[chunk][1], w_out, NN)
        middle = rows_in[rows] + branch + bias_out
        unit_two, scale_two = norm_parts(middle)
        normed_two = (unit_two * gain_two + shift_two).astype(BF16)
        pair = gather_pair(normed_two)
        acts, backs = [], []
        for side in range(2):
            hidden = mm(rows2(pair[side]), w_fc) + bias_fc
            bent = jnp.tanh(gelu_in * (hidden + gelu_cube * hidden * hidden * hidden))
            act = (0.5 * hidden * (1.0 + bent)).astype(BF16)
            slope = 0.5 * (1.0 + bent) + 0.5 * hidden * (1.0 - bent * bent) * (
                gelu_in * (1.0 + 3.0 * gelu_cube * hidden * hidden)
            )
            dact = back_act[side].reshape(2, rows_dev, ff_width)[:, rows]
            back = (rows2(dact).astype(F32) * slope).astype(BF16)
            fc_bias_grad = fc_bias_grad + jnp.sum(back, axis=0, dtype=F32)
            acts.append(act)
            backs.append(back)
        shape = (2, part, ff_width)
        back_normed_two.append(
            scatter_sum(backs[0].reshape(shape), backs[1].reshape(shape), w_fc, NT)
        )
        branches.append(scatter_sum(acts[0].reshape(shape), acts[1].reshape(shape), w_proj, NN))
        for side in range(2):
            dy = dy_pair[side][:, rows]
            grad_proj = grad_proj + mm(acts[side], rows2(dy), TN)
            grad_fc = grad_fc + mm(rows2(pair[side]), backs[side], TN)
        middles.append(middle)
        mine_two.append((unit_two, scale_two))
    middle = jnp.concatenate(middles)
    block_out = (middle + jnp.concatenate(branches) + bias_proj).astype(BF16)

    def scatter_grad(value):
        return lax.psum_scatter(value.astype(BF16), "dp", scatter_dimension=0, tiled=True)

    share_proj = scatter_grad(grad_proj)
    share_fc = scatter_grad(grad_fc)

    back_middles, mid_pairs, gain_two_grad, shift_two_grad = [], [], 0.0, 0.0
    for chunk in range(CHUNKS):
        rows = slice(chunk * part, (chunk + 1) * part)
        unit_two, scale_two = mine_two[chunk]
        grad = back_normed_two[chunk]
        back_middle = out_grad[rows].astype(F32) + norm_back(unit_two, scale_two, gain_two, grad)
        gain_two_grad = gain_two_grad + jnp.sum(grad * unit_two, axis=0)
        shift_two_grad = shift_two_grad + jnp.sum(grad, axis=0)
        mid_pairs.append(gather_pair(back_middle.astype(BF16)))
        back_middles.append(back_middle)
    back_middle = jnp.concatenate(back_middles)
    proj_bias_grad = jnp.sum(out_grad, axis=0, dtype=F32)
    out_bias_grad = jnp.sum(back_middle, axis=0)
    back_mixed, grad_out = [], 0.0
    for side in range(2):
        sides = []
        for chunk in range(CHUNKS):
            mid = rows2(mid_pairs[chunk][side])
            sides.append(mm(mid, w_out, NT).astype(BF16).reshape(2, part, head_width))
            grad_out = grad_out + mm(rows2(mixed[chunk][side]), mid, TN)
        back_mixed.append(jnp.concatenate(sides, axis=1))
    back_qkv = attend_back(core, qkv, mixed, log_sums, jnp.stack(back_mixed))
    grad_qkv = mm(rows2(normed_all), rows2(back_qkv), TN)
    qkv_bias_grad = jnp.sum(back_qkv, axis=(0, 1, 2), dtype=F32)

    share_out_grad = scatter_grad(grad_out)
    share_qkv = scatter_grad(grad_qkv)
    back_normed = scatter_sum(back_qkv[0], back_qkv[1], w_qkv, NT)
    input_grad = back_middle + norm_back(unit_one, scale_one, gain_one, back_normed)
    gain_one_grad = jnp.sum(back_normed * unit_one, axis=0)
    shift_one_grad = jnp.sum(back_normed, axis=0)

    bundle = jnp.zeros((data_count, share, width), BF16)
    pieces = (
        jnp.pad(share_qkv, ((0, 0), (0, width - 3 * head_width))),
        jnp.pad(share_out_grad, ((0, share - share_out), (0, 0))),
        share_fc,
        share_proj,
    )
    for kind in range(4):
        bundle = lax.dynamic_update_index_in_dim(bundle, pieces[kind], owner_row[kind], 0)
    landed = lax.all_to_all(bundle, "dp", 0, 0)
    landed_out = jnp.pad(
        landed[:, :share_out].reshape(head_width, width), ((0, width - head_width), (0, 0))
    )
    chosen = jnp.where(owned[1], landed_out, landed.reshape(width, width)).astype(F32)

    full_grad = jnp.concatenate(
        [
            gain_one_grad,
            shift_one_grad,
            jnp.zeros((2 * width,), F32),
            out_bias_grad,
            gain_two_grad,
            shift_two_grad,
            jnp.zeros((FF,), F32),
            proj_bias_grad,
        ]
    )
    for grad, start, size in (
        (qkv_bias_grad[:head_width], 2 * width, head_width),
        (qkv_bias_grad[2 * head_width :], 3 * width, head_width),
        (fc_bias_grad, 7 * width, ff_width),
    ):
        full_grad = lax.dynamic_update_slice_in_dim(full_grad, grad, start + tensor_idx * size, 0)
    small_grad = small_scatter(full_grad)
    first_new = beta_one * small_first + (1.0 - beta_one) * small_grad
    second_new = beta_two * small_second + (1.0 - beta_two) * small_grad * small_grad
    first_hat = first_new / (1.0 - beta_one**STEP)
    second_hat = second_new / (1.0 - beta_two**STEP)
    small_new = small_master - adam_rate * first_hat / (jnp.sqrt(second_hat) + adam_eps)

    any_owned = jnp.any(owned)
    row_limit = jnp.where(owned[1], head_width, jnp.where(any_owned, width, 0))
    col_limit = jnp.where(owned[0], 3 * head_width, width)
    row_ids = lax.broadcasted_iota(jnp.int32, (width, width), 0)
    col_ids = lax.broadcasted_iota(jnp.int32, (width, width), 1)
    valid = (row_ids < row_limit) & (col_ids < col_limit)
    mom_slot = jnp.where(valid, mom_decay * momentum_slots[0] + chosen, 0.0)

    def run_owner(packed):
        momentum, master, keep = packed
        start = (momentum / (jnp.sqrt(jnp.sum(momentum * momentum)) + 1e-07)).astype(BF16)
        ortho = newton_schulz(start).astype(F32)
        return jnp.where(keep, master * (1.0 - muon_rate * muon_decay) - muon_rate * ortho, 0.0)

    def skip_owner(packed):
        return jnp.zeros_like(packed[1])

    fresh_slot = lax.cond(any_owned, run_owner, skip_owner, (mom_slot, slot_value, valid))
    return (
        block_out,
        input_grad,
        chosen[None],
        mom_slot[None],
        fresh_slot[None],
        small_grad,
        second_new,
        small_new,
    )


def solution(mesh):
    return jax.shard_map(
        per_device,
        mesh=mesh,
        in_specs=(
            P(("dp", "tensor"), None),
            P(("dp", "tensor"), None),
            P(),
            P("dp", "tensor", None),
            P("dp", "tensor", None),
            P(("dp", "tensor")),
            P(("dp", "tensor")),
            P(("dp", "tensor")),
        ),
        out_specs=(
            P(("dp", "tensor"), None),
            P(("dp", "tensor"), None),
            P("dp", "tensor", None),
            P("dp", "tensor", None),
            P("dp", "tensor", None),
            P(("dp", "tensor")),
            P(("dp", "tensor")),
            P(("dp", "tensor")),
        ),
        check_vma=False,
    )
```

time: 1590 us -> 776 us (0.49)
  blocking collectives: 569 us -> 30.7 us
  waiting for transfers between devices: 582 us -> 403 us
  matrix products: 235 us -> 95 us
  Pallas kernels: 0 us -> 74.1 us
  starting transfers between devices: 0.72 us -> 43 us
  local copies, waits for them, and re-layouts: 61.4 us -> 29.8 us
  other arithmetic: 95.8 us -> 64.4 us
  loops' own time: 27.1 us -> 0.92 us
    psum x1 -> x0, blocking collectives: 489 us -> none  [per_device(): lax.psum((offer_qkv, offer_out, offer_fc, offer_proj), 'dp')]
    psum x1 -> x0, waiting for transfers between devices: 351 us -> none  [per_device(): lax.psum((grad_qkv, grad_out, grad_fc, grad_proj), 'dp')]
    ppermute x0 -> x36, waiting for transfers between devices: none -> 204 us  [the longest x26 121 us: swap(): return lax.ppermute(value, 'tensor', [(i, i ^ bit) for i in range(count)])]
    dot_general x50 -> x38, matrix products: 235 us -> 95 us  [mm(): return lax.dot_general(left, right, dims, preferred_element_type=F32)]
    all_gather x4 -> x3, waiting for transfers between devices: 93.2 us -> 0.01 us  [gather_rows(): return lax.all_gather(value, 'dp', axis=0, tiled=True)]
    pallas_call x0 -> x4, Pallas kernels: none -> 74.1 us  [the longest x1 44.2 us: newton_schulz(): pl.pallas_call(schulz_kernel, in_specs=[pl.BlockSpec(memory_space=pltpu.V...]
    reduce_scatter x4, waiting for transfers between devices: 137 us -> 198 us  [scatter_grad(): lax.psum_scatter(value.astype(BF16), 'dp', scatter_dimension=0, tiled=True)]
    unnamed x1 -> x0, blocking collectives: 44.4 us -> none
  transfers between devices with their start and end apart: 9 -> 45, of which waited for: 8 -> 24; matrix products, arithmetic and copies ran while one was open for 6% -> 17% of each run, Pallas kernels for 0% -> 1%
where the time goes in v1:
time: 776 us; the launch traced here: 767 us
  waiting for transfers between devices  403 us (52%)
  matrix products  95 us (12%)
  Pallas kernels  74.1 us (10%)
  other arithmetic  64.4 us (8%)
  starting transfers between devices  43 us (6%)
  blocking collectives  30.7 us (4%)
  local copies, waits for them, and re-layouts  29.8 us (4%)
  between operations  25.9 us (3%)
    reduce_scatter x4, waiting for transfers between devices, scatter_grad(): lax.psum_scatter(value.astype(BF16), 'dp', scatter_dimension=0, tiled=True)  198 us
    ppermute x26, waiting for transfers between devices, swap(): return lax.ppermute(value, 'tensor', [(i, i ^ bit) for i in range(count)])  121 us
    dot_general x38, matrix products, mm(): return lax.dot_general(left, right, dims, preferred_element_type=F32)  95 us
    pallas_call x1, Pallas kernels, newton_schulz(): pl.pallas_call(schulz_kernel, in_specs=[pl.BlockSpec(memory_space=pltpu.V...  44.2 us
    ppermute x5, waiting for transfers between devices, small_gather(): other = lax.ppermute(piece, name, [(i, i ^ bit) for i in range(count)])  41.8 us
    ppermute x5, waiting for transfers between devices, small_scatter(): lax.ppermute(give, name, [(i, i ^ bit) for i in range(count)])  41.6 us
    all_gather x1, blocking collectives, gather_rows(): return lax.all_gather(value, 'dp', axis=0, tiled=True)  30.7 us
    pallas_call x1, Pallas kernels, attend_back(): pl.pallas_call(partial(attend_back_kernel, heads=width // HEAD_DIM, chunk...  19.9 us
  transfers between devices with their start and end apart: 45, of which 24 were waited for; matrix products, arithmetic and copies ran while one was open for 17% of the time, Pallas kernels for 1%

profile of v1, /device:TPU:8, one launch (start us, length us, event | category | flops | bytes accessed | tf_op | source)
XLA Modules:
  0.0 766.5 jit_solution(8367101461179922748)
XLA Ops:
  15.7 6.4 all-to-all-start
  28.6 10.4 %collective-permute-done.2 = f32[4,384]{1,0:T(4,128)S(1)} collective-permute-done((f32[4,384]{1,0:T(4,128)S(1)}, f32[4,384]{1,0:T(4,128)S(1)}, u32[]{:S(2)}, u32[]{:S(2)}) %collective-permute-start.2) | collective-permute-done | bytes 6176 | tf_op jit(solution)/shard_map/ppermute | solution.py:319
  39.8 18.0 %collective-permute-done.3 = f32[8,384]{1,0:T(8,128)S(1)} collective-permute-done((f32[8,384]{1,0:T(8,128)S(1)}, f32[8,384]{1,0:T(8,128)S(1)}, u32[]{:S(2)}, u32[]{:S(2)}) %collective-permute-start.3) | collective-permute-done | bytes 12320 | tf_op jit(solution)/shard_map/ppermute | solution.py:319
  58.5 10.4 %collective-permute-done.4 = f32[16,384]{1,0:T(8,128)S(1)} collective-permute-done((f32[16,384]{1,0:T(8,128)S(1)}, f32[16,384]{1,0:T(8,128)S(1)}, u32[]{:S(2)}, u32[]{:S(2)}) %collective-permute-start.4) | collective-permute-done | bytes 24608 | tf_op jit(solution)/shard_map/ppermute | solution.py:319
  81.0 15.3 %collective-permute-done.5 = bf16[512,1024]{1,0:T(8,128)(2,1)} collective-permute-done((bf16[512,1024]{1,0:T(8,128)(2,1)}, bf16[512,1024]{1,0:T(8,128)(2,1)}, u32[]{:S(2)}, u32[]{:S(2)}) %collective-permute-start.5) | collective-permute-done | bytes 1048608 | tf_op jit(solution)/shard_map/ppermute | solution.py:285
  103.2 22.3 %collective-permute-done.19 = bf16[512,1024]{1,0:T(8,128)(2,1)S(1)} collective-permute-done((bf16[512,1024]{1,0:T(8,128)(2,1)S(1)}, bf16[512,1024]{1,0:T(8,128)(2,1)S(1)}, u32[]{:S(2)}, u32[]{:S(2)}) %collective-permute-start.19) | collective-permute-done | bytes 1048608 | tf_op jit(solution)/shard_map/ppermute | solution.py:285
  132.7 30.7 %all-gather = bf16[1,256,1024]{2,1,0:T(8,128)(2,1)S(1)} all-gather(bf16[1,32,1024]{2,1,0:T(8,128)(2,1)S(1)} %constant_dynamic-slice_fusion.2), channel_id=2, replica_groups=mesh['dp'=8,'tensor'=4] {'dp'}, dimensions={1}, use_global_device_ids=true | all-gather | bytes 589824 | tf_op jit(solution)/shard_map/all_gather | solution.py:387
  163.5 6.3 multiply_convert_fusion
  176.5 5.5 shard_map.144
  193.7 4.7 fusion.67
  198.4 5.1 collective-permute-done.8
  203.5 10.3 %collective-permute-done.10 = bf16[256,1024]{1,0:T(8,128)(2,1)} collective-permute-done((bf16[256,1024]{1,0:T(8,128)(2,1)S(1)}, bf16[256,1024]{1,0:T(8,128)(2,1)}, u32[]{:S(2)}, u32[]{:S(2)}) %collective-permute-start.10) | collective-permute-done | bytes 524320 | tf_op jit(solution)/shard_map/ppermute | solution.py:285
  222.5 8.9 %collective-permute-done.15 = bf16[256,1024]{1,0:T(8,128)(2,1)S(1)} collective-permute-done((bf16[256,1024]{1,0:T(8,128)(2,1)S(1)}, bf16[256,1024]{1,0:T(8,128)(2,1)S(1)}, u32[]{:S(2)}, u32[]{:S(2)}) %collective-permute-start.15) | collective-permute-done | bytes 524320 | tf_op jit(solution)/shard_map/ppermute | solution.py:285
  234.6 6.1 collective-permute-done.11
  251.9 10.1 %convert_reduce_fusion.3 = (f32[1024]{0:T(1024)S(1)}, bf16[512,1024]{1,0:T(8,128)(2,1)S(1)}, f32[1024]{0:T(1024)S(1)}, bf16[512,1024]{1,0:T(8,128)(2,1)S(1)}, f3...) fusion(f32[1024]{0:T(1024)S(1)} %get-tuple-element.85, ...), kind=kOutput, calls=%fused_computation.97 | convolution fusion | flops 1121972224 | bytes 19943424 | tf_op jit(solution)/shard_map/dot_general | solution.py:44
  270.9 12.2 %collective-permute-done.22 = bf16[256,1024]{1,0:T(8,128)(2,1)S(1)} collective-permute-done((bf16[256,1024]{1,0:T(8,128)(2,1)S(1)}, bf16[256,1024]{1,0:T(8,128)(2,1)S(1)}, u32[]{:S(2)}, u32[]{:S(2)}) %collective-permute-start.22) | collective-permute-done | bytes 524320 | tf_op jit(solution)/shard_map/ppermute | solution.py:285
  283.1 10.8 %collective-permute-done.24 = bf16[256,1024]{1,0:T(8,128)(2,1)S(1)} collective-permute-done((bf16[256,1024]{1,0:T(8,128)(2,1)S(1)}, bf16[256,1024]{1,0:T(8,128)(2,1)S(1)}, u32[]{:S(2)}, u32[]{:S(2)}) %collective-permute-start.24) | collective-permute-done | bytes 524320 | tf_op jit(solution)/shard_map/ppermute | solution.py:285
  298.8 12.6 %collective-permute-done.26 = bf16[256,1024]{1,0:T(8,128)(2,1)S(1)} collective-permute-done((bf16[256,1024]{1,0:T(8,128)(2,1)S(1)}, bf16[256,1024]{1,0:T(8,128)(2,1)S(1)}, u32[]{:S(2)}, u32[]{:S(2)}) %collective-permute-start.26) | collective-permute-done | bytes 524320 | tf_op jit(solution)/shard_map/ppermute | solution.py:285
  311.7 9.7 %collective-permute-done.25 = bf16[256,1024]{1,0:T(8,128)(2,1)S(1)} collective-permute-done((bf16[256,1024]{1,0:T(8,128)(2,1)S(1)}, bf16[256,1024]{1,0:T(8,128)(2,1)S(1)}, u32[]{:S(2)}, u32[]{:S(2)}) %collective-permute-start.25) | collective-permute-done | bytes 524320 | tf_op jit(solution)/shard_map/ppermute | solution.py:285
  325.3 19.9 %shard_map.145 = bf16[2,2,512,768]{3,2,1,0:T(8,128)(2,1)} custom-call(s32[1]{0:T(128)} %bitcast.1.core_ref, bf16[2,2,512,768]{3,2,1,0:T(8,128)(2,1)} %bitcast.325, bf16[2,2,512,768]{3,2,1,0:T(8,128)(2,1)} %bitcast.326, bf16[2,2,512,768]{3,2,1,0:T(8,128)(2,1)} %bitcast.327, bf16[2,2,256,256]{3,2,1,0:T(8,128)(2,1)S(1)} %get-tuple-element.25.refs_0_, ...), custom_call_target="tpu_custom_call" | custom-call | flops 24999999488 | bytes 12000000 | tf_op jit(solution)/shard_map/pallas_call | solution.py:206
  345.2 7.3 bitcast_convert_fusion
  371.3 5.7 add_convert_fusion.1
  412.4 6.7 collective-permute-done.18
  423.1 61.8 %reduce-scatter.7.cloned.1.call-done = bf16[32,1024]{1,0:T(8,128)(2,1)} async-done(((bf16[256,1024]{1,0:T(8,128)(2,1)}), bf16[32,1024]{1,0:T(8,128)(2,1)}) %reduce-scatter.7.cloned.1.call-update) | async-done | bytes 65552 | tf_op jit(solution)/shard_map/reduce_scatter | solution.py:463
  486.4 67.9 %reduce-scatter.9.cloned.1.call-done = bf16[128,1024]{1,0:T(8,128)(2,1)} async-done(((bf16[1024,1024]{1,0:T(8,128)(2,1)}), bf16[128,1024]{1,0:T(8,128)(2,1)}) %reduce-scatter.9.cloned.1.call-update) | async-done | bytes 262160 | tf_op jit(solution)/shard_map/reduce_scatter | solution.py:463
  556.0 68.6 %reduce-scatter.11.cloned.1.call-done = bf16[128,1024]{1,0:T(8,128)(2,1)} async-done(((bf16[1024,1024]{1,0:T(8,128)(2,1)}), bf16[128,1024]{1,0:T(8,128)(2,1)}) %reduce-scatter.11.cloned.1.call-update) | async-done | bytes 262160 | tf_op jit(solution)/shard_map/reduce_scatter | solution.py:463
  626.3 5.6 all-to-all-start.1
  638.9 37.0 %collective-permute-done.31 = f32[6144]{0:T(1024)S(1)} collective-permute-done((f32[6144]{0:T(1024)S(1)}, f32[6144]{0:T(1024)S(1)}, u32[]{:S(2)}, u32[]{:S(2)}) %collective-permute-start.31) | collective-permute-done | bytes 24608 | tf_op jit(solution)/shard_map/ppermute | solution.py:338
  692.9 6.6 fusion
  699.6 55.0 %conditional.1 = (f32[1,1024,1024]{2,1,0:T(8,128)}) conditional(s32[]{:T(128)} %convert_element_type.314, () %tuple.16, (f32[1024,1024]{1,0:T(8,128)}, f32[1024,1024]{1,0:T(8,128)}, pred[1024,1024]{1,0:T(8,128)(4,1)S(1)}) %tuple.96), branch_computations={%region_17.18_spmd, %region_18.20_spmd} | conditional | flops 32221691904 | bytes 42991680 | solution.py:557
  707.1 44.2 %branch_1_fun.1 = bf16[1024,1024]{1,0:T(8,128)(2,1)S(1)} custom-call(bf16[1024,1024]{1,0:T(8,128)(2,1)S(1)} %divide_convert_fusion.x_ref), custom_call_target="tpu_custom_call" | custom-call | flops 32212254720 | bytes 4194304 | tf_op jit(solution)/shard_map/cond/branch_1_fun/pallas_call | solution.py:266
  754.6 4.9 convert_bitcast_fusion
  (396 shorter events, 187.7 us)
Async XLA Ops:
  15.7 63.1 %all-to-all-start = ((bf16[8,128,1024]{2,1,0:T(8,128)(2,1)}), bf16[8,128,1024]{2,1,0:T(8,128)(2,1)S(1)}, u32[]{:S(2)}, u32[]{:S(2)}) async-start(bf16[8,128,1024]{2,1,0:T(8,128)(2,1)} %pad_select_fusion), calls=%async_computation | async-start | bytes 4194304 | tf_op jit(solution)/shard_map/all_to_all | solution.py:381
  22.1 141.3 %all-gather.7.cloned.1.call-start = ((), (), s32[]{:S(2)}) async-start(), calls=%async_computation.6 | async-start | bytes 1769472 | tf_op jit(solution)/shard_map/all_gather | solution.py:387
  27.1 12.0 %collective-permute-start.2 = (f32[4,384]{1,0:T(4,128)S(1)}, f32[4,384]{1,0:T(4,128)S(1)}, u32[]{:S(2)}, u32[]{:S(2)}) collective-permute-start(f32[4,384]{1,0:T(4,128)S(1)} %maximum_select_fusion.3), channel_id=1, source_target_pairs={{0,4},{4,0},{8,12},{12,8},{16,20},{20,16},{24,28},{28,24},{1,5},{5... | collective-permute-start | bytes 18440 | tf_op jit(solution)/shard_map/ppermute | solution.py:319
  39.1 18.8 %collective-permute-start.3 = (f32[8,384]{1,0:T(8,128)S(1)}, f32[8,384]{1,0:T(8,128)S(1)}, u32[]{:S(2)}, u32[]{:S(2)}) collective-permute-start(f32[8,384]{1,0:T(8,128)S(1)} %maximum_select_fusion.2), channel_id=1, source_target_pairs={{0,8},{4,12},{8,0},{12,4},{16,24},{20,28},{24,16},{28,20},{1,9},{5... | collective-permute-start | bytes 36872 | tf_op jit(solution)/shard_map/ppermute | solution.py:319
  57.8 11.0 %collective-permute-start.4 = (f32[16,384]{1,0:T(8,128)S(1)}, f32[16,384]{1,0:T(8,128)S(1)}, u32[]{:S(2)}, u32[]{:S(2)}) collective-permute-start(f32[16,384]{1,0:T(8,128)S(1)} %maximum_select_fusion.1), channel_id=1, source_target_pairs={{0,16},{4,20},{8,24},{12,28},{16,0},{20,4},{24,8},{28,12},{1,17},{... | collective-permute-start | bytes 73736 | tf_op jit(solution)/shard_map/ppermute | solution.py:319
  70.9 25.4 %collective-permute-start.5 = (bf16[512,1024]{1,0:T(8,128)(2,1)}, bf16[512,1024]{1,0:T(8,128)(2,1)}, u32[]{:S(2)}, u32[]{:S(2)}) collective-permute-start(bf16[512,1024]{1,0:T(8,128)(2,1)} %add_convert_fusion.2), channel_id=1, source_target_pairs={{0,2},{1,3},{2,0},{3,1},{4,6},{5,7},{6,4},{7,5},{8,10},{9,11},{10,... | collective-permute-start | bytes 3145736 | tf_op jit(solution)/shard_map/ppermute | solution.py:285
  80.5 113.2 %all-gather.11.cloned.1.call-start = ((), (), s32[]{:S(2)}) async-start(), calls=%async_computation.12 | async-start | bytes 2359296 | tf_op jit(solution)/shard_map/all_gather | solution.py:387
  99.9 27.4 %collective-permute-start.6 = (bf16[2,512,1024]{2,1,0:T(8,128)(2,1)}, bf16[2,512,1024]{2,1,0:T(8,128)(2,1)}, u32[]{:S(2)}, u32[]{:S(2)}) collective-permute-start(bf16[2,512,1024]{2,1,0:T(8,128)(2,1)} %get-tuple-element.77), channel_id=1, source_target_pairs={{0,1},{1,0},{2,3},{3,2},{4,5},{5,4},{6,7},{7,6},{8,9},{9,8},{10,11... | collective-permute-start | bytes 6291464 | tf_op jit(solution)/shard_map/ppermute | solution.py:285
  99.9 25.6 %collective-permute-start.19 = (bf16[512,1024]{1,0:T(8,128)(2,1)S(1)}, bf16[512,1024]{1,0:T(8,128)(2,1)S(1)}, u32[]{:S(2)}, u32[]{:S(2)}) collective-permute-start(bf16[512,1024]{1,0:T(8,128)(2,1)S(1)} %copy-done.12), channel_id=1, source_target_pairs={{0,2},{1,3},{2,0},{3,1},{4,6},{5,7},{6,4},{7,5},{8,10},{9,11},{10,... | collective-permute-start | bytes 3145736 | tf_op jit(solution)/shard_map/ppermute | solution.py:285
  127.2 66.5 %collective-permute-start.20 = (bf16[2,512,1024]{2,1,0:T(8,128)(2,1)}, bf16[2,512,1024]{2,1,0:T(8,128)(2,1)}, u32[]{:S(2)}, u32[]{:S(2)}) collective-permute-start(bf16[2,512,1024]{2,1,0:T(8,128)(2,1)} %pad_maximum_fusion.1), channel_id=1, source_target_pairs={{0,1},{1,0},{2,3},{3,2},{4,5},{5,4},{6,7},{7,6},{8,9},{9,8},{10,11... | collective-permute-start | bytes 6291464 | tf_op jit(solution)/shard_map/ppermute | solution.py:285
  127.2 114.7 %all-gather.9.cloned.1.call-start = ((), (), s32[]{:S(2)}) async-start(), calls=%async_computation.11 | async-start | bytes 2359296 | tf_op jit(solution)/shard_map/all_gather | solution.py:387
  176.5 10.1 %collective-permute-start.7 = (bf16[2,256,1024]{2,1,0:T(8,128)(2,1)}, bf16[2,256,1024]{2,1,0:T(8,128)(2,1)}, u32[]{:S(2)}, u32[]{:S(2)}) collective-permute-start(bf16[2,256,1024]{2,1,0:T(8,128)(2,1)} %bitcast.19), channel_id=1, source_target_pairs={{0,1},{1,0},{2,3},{3,2},{4,5},{5,4},{6,7},{7,6},{8,9},{9,8},{10,11... | collective-permute-start | bytes 3145736 | tf_op jit(solution)/shard_map/ppermute | solution.py:285
  186.3 234.5 %reduce-scatter.5.cloned.1.call-start = ((), (), s32[]{:S(2)}) async-start(), calls=%async_computation.7 | async-start | bytes 1769472 | tf_op jit(solution)/shard_map/reduce_scatter | solution.py:463
  188.5 15.0 %collective-permute-start.8 = (bf16[256,1024]{1,0:T(8,128)(2,1)S(1)}, bf16[256,1024]{1,0:T(8,128)(2,1)}, u32[]{:S(2)}, u32[]{:S(2)}) collective-permute-start(bf16[256,1024]{1,0:T(8,128)(2,1)S(1)} %fusion.99), channel_id=1, source_target_pairs={{0,2},{1,3},{2,0},{3,1},{4,6},{5,7},{6,4},{7,5},{8,10},{9,11},{10,... | collective-permute-start | bytes 1572872 | tf_op jit(solution)/shard_map/ppermute | solution.py:285
  193.1 20.7 %collective-permute-start.10 = (bf16[256,1024]{1,0:T(8,128)(2,1)S(1)}, bf16[256,1024]{1,0:T(8,128)(2,1)}, u32[]{:S(2)}, u32[]{:S(2)}) collective-permute-start(bf16[256,1024]{1,0:T(8,128)(2,1)S(1)} %fusion.100), channel_id=1, source_target_pairs={{0,2},{1,3},{2,0},{3,1},{4,6},{5,7},{6,4},{7,5},{8,10},{9,11},{10,... | collective-permute-start | bytes 1572872 | tf_op jit(solution)/shard_map/ppermute | solution.py:285
  216.4 14.9 %collective-permute-start.15 = (bf16[256,1024]{1,0:T(8,128)(2,1)S(1)}, bf16[256,1024]{1,0:T(8,128)(2,1)S(1)}, u32[]{:S(2)}, u32[]{:S(2)}) collective-permute-start(bf16[256,1024]{1,0:T(8,128)(2,1)S(1)} %get-tuple-element.94), channel_id=1, source_target_pairs={{0,2},{1,3},{2,0},{3,1},{4,6},{5,7},{6,4},{7,5},{8,10},{9,11},{10,... | collective-permute-start | bytes 1572872 | tf_op jit(solution)/shard_map/ppermute | solution.py:285
  218.0 22.8 %collective-permute-start.11 = (bf16[256,1024]{1,0:T(8,128)(2,1)S(1)}, bf16[256,1024]{1,0:T(8,128)(2,1)S(1)}, u32[]{:S(2)}, u32[]{:S(2)}) collective-permute-start(bf16[256,1024]{1,0:T(8,128)(2,1)S(1)} %get-tuple-element.93), channel_id=1, source_target_pairs={{0,2},{1,3},{2,0},{3,1},{4,6},{5,7},{6,4},{7,5},{8,10},{9,11},{10,... | collective-permute-start | bytes 1572872 | tf_op jit(solution)/shard_map/ppermute | solution.py:285
  232.4 16.0 %collective-permute-start.16 = (bf16[2,256,1024]{2,1,0:T(8,128)(2,1)}, bf16[2,256,1024]{2,1,0:T(8,128)(2,1)}, u32[]{:S(2)}, u32[]{:S(2)}) collective-permute-start(bf16[2,256,1024]{2,1,0:T(8,128)(2,1)} %pad_maximum_fusion.4), channel_id=1, source_target_pairs={{0,1},{1,0},{2,3},{3,2},{4,5},{5,4},{6,7},{7,6},{8,9},{9,8},{10,11... | collective-permute-start | bytes 3145736 | tf_op jit(solution)/shard_map/ppermute | solution.py:285
  268.3 14.8 %collective-permute-start.22 = (bf16[256,1024]{1,0:T(8,128)(2,1)S(1)}, bf16[256,1024]{1,0:T(8,128)(2,1)S(1)}, u32[]{:S(2)}, u32[]{:S(2)}) collective-permute-start(bf16[256,1024]{1,0:T(8,128)(2,1)S(1)} %fusion.103), channel_id=1, source_target_pairs={{0,2},{1,3},{2,0},{3,1},{4,6},{5,7},{6,4},{7,5},{8,10},{9,11},{10,... | collective-permute-start | bytes 1572872 | tf_op jit(solution)/shard_map/ppermute | solution.py:285
  270.3 23.6 %collective-permute-start.24 = (bf16[256,1024]{1,0:T(8,128)(2,1)S(1)}, bf16[256,1024]{1,0:T(8,128)(2,1)S(1)}, u32[]{:S(2)}, u32[]{:S(2)}) collective-permute-start(bf16[256,1024]{1,0:T(8,128)(2,1)S(1)} %fusion.104), channel_id=1, source_target_pairs={{0,2},{1,3},{2,0},{3,1},{4,6},{5,7},{6,4},{7,5},{8,10},{9,11},{10,... | collective-permute-start | bytes 1572872 | tf_op jit(solution)/shard_map/ppermute | solution.py:285
  296.5 14.9 %collective-permute-start.26 = (bf16[256,1024]{1,0:T(8,128)(2,1)S(1)}, bf16[256,1024]{1,0:T(8,128)(2,1)S(1)}, u32[]{:S(2)}, u32[]{:S(2)}) collective-permute-start(bf16[256,1024]{1,0:T(8,128)(2,1)S(1)} %convert_element_type.301), channel_id=1, source_target_pairs={{0,2},{1,3},{2,0},{3,1},{4,6},{5,7},{6,4},{7,5},{8,10},{9,11},{10,... | collective-permute-start | bytes 1572872 | tf_op jit(solution)/shard_map/ppermute | solution.py:285
  298.1 23.2 %collective-permute-start.25 = (bf16[256,1024]{1,0:T(8,128)(2,1)S(1)}, bf16[256,1024]{1,0:T(8,128)(2,1)S(1)}, u32[]{:S(2)}, u32[]{:S(2)}) collective-permute-start(bf16[256,1024]{1,0:T(8,128)(2,1)S(1)} %convert_element_type.299), channel_id=1, source_target_pairs={{0,2},{1,3},{2,0},{3,1},{4,6},{5,7},{6,4},{7,5},{8,10},{9,11},{10,... | collective-permute-start | bytes 1572872 | tf_op jit(solution)/shard_map/ppermute | solution.py:285
  311.5 11.1 %collective-permute-start.28 = (bf16[2,256,1024]{2,1,0:T(8,128)(2,1)S(1)}, bf16[2,256,1024]{2,1,0:T(8,128)(2,1)S(1)}, u32[]{:S(2)}, u32[]{:S(2)}) collective-permute-start(bf16[2,256,1024]{2,1,0:T(8,128)(2,1)S(1)} %pad_maximum_fusion.6), channel_id=1, source_target_pairs={{0,1},{1,0},{2,3},{3,2},{4,5},{5,4},{6,7},{7,6},{8,9},{9,8},{10,11... | collective-permute-start | bytes 3145736 | tf_op jit(solution)/shard_map/ppermute | solution.py:285
  352.5 132.4 %reduce-scatter.7.cloned.1.call-start = ((), (), s32[]{:S(2)}) async-start(), calls=%async_computation.8 | async-start | bytes 589824 | tf_op jit(solution)/shard_map/reduce_scatter | solution.py:463
  368.4 185.9 %reduce-scatter.9.cloned.1.call-start = ((), (), s32[]{:S(2)}) async-start(), calls=%async_computation.9 | async-start | bytes 2359296 | tf_op jit(solution)/shard_map/reduce_scatter | solution.py:463
  377.0 247.6 %reduce-scatter.11.cloned.1.call-start = ((), (), s32[]{:S(2)}) async-start(), calls=%async_computation.10 | async-start | bytes 2359296 | tf_op jit(solution)/shard_map/reduce_scatter | solution.py:463
  389.7 12.9 %collective-permute-start.17 = (bf16[2,256,1024]{2,1,0:T(8,128)(2,1)}, bf16[2,256,1024]{2,1,0:T(8,128)(2,1)}, u32[]{:S(2)}, u32[]{:S(2)}) collective-permute-start(bf16[2,256,1024]{2,1,0:T(8,128)(2,1)} %bitcast.44), channel_id=1, source_target_pairs={{0,1},{1,0},{2,3},{3,2},{4,5},{5,4},{6,7},{7,6},{8,9},{9,8},{10,11... | collective-permute-start | bytes 3145736 | tf_op jit(solution)/shard_map/ppermute | solution.py:285
  404.3 14.8 %collective-permute-start.18 = (bf16[256,1024]{1,0:T(8,128)(2,1)S(1)}, bf16[256,1024]{1,0:T(8,128)(2,1)S(1)}, u32[]{:S(2)}, u32[]{:S(2)}) collective-permute-start(bf16[256,1024]{1,0:T(8,128)(2,1)S(1)} %fusion.102), channel_id=1, source_target_pairs={{0,2},{1,3},{2,0},{3,1},{4,6},{5,7},{6,4},{7,5},{8,10},{9,11},{10,... | collective-permute-start | bytes 1572872 | tf_op jit(solution)/shard_map/ppermute | solution.py:285
  407.0 230.6 %collective-permute-start.14 = (bf16[256,1024]{1,0:T(8,128)(2,1)}, bf16[256,1024]{1,0:T(8,128)(2,1)}, u32[]{:S(2)}, u32[]{:S(2)}) collective-permute-start(bf16[256,1024]{1,0:T(8,128)(2,1)} %fusion.101), channel_id=1, source_target_pairs={{0,2},{1,3},{2,0},{3,1},{4,6},{5,7},{6,4},{7,5},{8,10},{9,11},{10,... | collective-permute-start | bytes 1572872 | tf_op jit(solution)/shard_map/ppermute | solution.py:285
  411.8 220.2 %collective-permute-start.30 = (bf16[512,1024]{1,0:T(8,128)(2,1)}, bf16[512,1024]{1,0:T(8,128)(2,1)S(1)}, u32[]{:S(2)}, u32[]{:S(2)}) collective-permute-start(bf16[512,1024]{1,0:T(8,128)(2,1)} %fusion.86), channel_id=1, source_target_pairs={{0,2},{1,3},{2,0},{3,1},{4,6},{5,7},{6,4},{7,5},{8,10},{9,11},{10,... | collective-permute-start | bytes 3145736 | tf_op jit(solution)/shard_map/ppermute | solution.py:285
  626.3 65.6 %all-to-all-start.1 = ((bf16[8,128,1024]{2,1,0:T(8,128)(2,1)}), bf16[8,128,1024]{2,1,0:T(8,128)(2,1)}, u32[]{:S(2)}, u32[]{:S(2)}) async-start(bf16[8,128,1024]{2,1,0:T(8,128)(2,1)} %bitcast_dynamic-update-slice_fusion), calls=%async_computation.5 | async-start | bytes 4194304 | tf_op jit(solution)/shard_map/all_to_all | solution.py:509
  635.1 40.8 %collective-permute-start.31 = (f32[6144]{0:T(1024)S(1)}, f32[6144]{0:T(1024)S(1)}, u32[]{:S(2)}, u32[]{:S(2)}) collective-permute-start(f32[6144]{0:T(1024)S(1)} %slice_select_fusion), channel_id=1, source_target_pairs={{0,16},{4,20},{8,24},{12,28},{16,0},{20,4},{24,8},{28,12},{1,17},{... | collective-permute-start | bytes 73736 | tf_op jit(solution)/shard_map/ppermute | solution.py:338
  (99 other events, 798.8 us)
Sparse Core Ops, SparseCore 0:
  80.6 44.3 all-gather.6
  127.3 53.2 all-gather.10
  186.4 52.2 all-gather.8
  352.6 67.4 reduce-scatter.4
  423.7 61.1 reduce-scatter.6
  488.3 65.9 reduce-scatter.8
  557.8 66.7 reduce-scatter.10

commit v2 on v1

--- a/solution.py
+++ b/solution.py
@@ -137,8 +137,8 @@
 ):
     o_refs = refs[0:chunks]
     lse_refs = refs[chunks : 2 * chunks]
-    do_ref = refs[2 * chunks]
-    out_ref, dk_acc, dv_acc = refs[2 * chunks + 1 :]
+    do_refs = refs[2 * chunks : 3 * chunks]
+    out_ref, dk_acc, dv_acc = refs[3 * chunks :]
     core = core_ref[0]
     place = (core, 1 - core)
     width = q_ref.shape[-1]
@@ -154,7 +154,7 @@
             rows = slice(sub * TILE, (sub + 1) * TILE)
             inner = slice((sub % per_chunk) * TILE, (sub % per_chunk + 1) * TILE)
             q_blk = q_ref[place[half], 0, rows, :]
-            do_blk = do_ref[place[half], 0, rows, :]
+            do_blk = do_refs[sub // per_chunk][place[half], 0, inner, :]
             o_blk = o_refs[sub // per_chunk][place[half], 0, inner, :]
             lse_blk = lse_refs[sub // per_chunk][place[half], 0, inner, :]
             overlap = do_blk.astype(F32) * o_blk.astype(F32)
@@ -211,7 +211,7 @@
             in_specs=[block(rows, width, 0), block(rows, width, 1), block(rows, width, 2)]
             + [block(part, width, 0)] * chunks
             + [block(part, 128, 0)] * chunks
-            + [block(rows, width, 0)],
+            + [block(part, width, 0)] * chunks,
             out_specs=block(rows, triple, 0),
             scratch_shapes=[pltpu.VMEM((2 * rows // TILE, TILE, width), F32)] * 2,
         ),
@@ -220,27 +220,164 @@
         cost_estimate=pl.CostEstimate(
             flops=25 * 10**9, bytes_accessed=12 * 10**6, transcendentals=0
         ),
-    )(core, qkv, qkv, qkv, *outs, *lses, back)
-
-
-def schulz_kernel(x_ref, o_ref, x_buf, gram, poly):
-    size = x_ref.shape[0]
-    tiles = size // TILE
-    x_buf[0] = x_ref[...]
+    )(core, qkv, qkv, qkv, *outs, *lses, *back)
+
+
+def hidden_kernel(*refs):
+    blocks = refs[0:4]
+    w_ref, bias_ref, dact_ref, act_ref, back_ref, sum_ref, all_ref = refs[4:]
+    rows = blocks[0].shape[0]
+    value = jnp.concatenate([block[...] for block in blocks], axis=0)
+    hidden = mm(value, w_ref[...]) + bias_ref[...]
+    square = hidden * hidden
+    bent = jnp.tanh(gelu_in * hidden * (1.0 + gelu_cube * square))
+    half = 0.5 * (1.0 + bent)
+    act_ref[...] = (hidden * half).astype(BF16)
+    slope = half + 0.5 * hidden * (1.0 - bent * bent) * (
+        gelu_in * (1.0 + 3.0 * gelu_cube * square)
+    )
+    back = (dact_ref[...].astype(F32) * slope).astype(BF16)
+    back_ref[...] = back
+    sum_ref[...] = jnp.sum(back.astype(F32), axis=0, keepdims=True)
+
+    @pl.when(pl.program_id(0) == 0)
+    def _():
+        for at in range(4):
+            all_ref[at * rows : (at + 1) * rows, :] = blocks[at][...]
+
+
+def hidden_layer(blocks, weight, bias, dact):
+    rows, width = blocks[0].shape
+    cols = weight.shape[1]
+    tile = min(256, cols)
+    whole = pl.BlockSpec((rows, width), lambda n: (0, 0))
+    column = pl.BlockSpec((4 * rows, tile), lambda n: (0, n))
+    return pl.pallas_call(
+        hidden_kernel,
+        grid=(cols // tile,),
+        in_specs=[whole] * 4
+        + [
+            pl.BlockSpec((width, tile), lambda n: (0, n)),
+            pl.BlockSpec((1, tile), lambda n: (0, n)),
+            column,
+        ],
+        out_specs=[
+            column,
+            column,
+            pl.BlockSpec((1, tile), lambda n: (0, n)),
+            pl.BlockSpec((4 * rows, width), lambda n: (0, 0)),
+        ],
+        out_shape=[
+            jax.ShapeDtypeStruct((4 * rows, cols), BF16),
+            jax.ShapeDtypeStruct((4 * rows, cols), BF16),
+            jax.ShapeDtypeStruct((1, cols), F32),
+            jax.ShapeDtypeStruct((4 * rows, width), BF16),
+        ],
+        compiler_params=pltpu.CompilerParams(vmem_limit_bytes=VMEM_GRANT),
+        cost_estimate=pl.CostEstimate(
+            flops=8 * rows * width * cols, bytes_accessed=12 * 10**6, transcendentals=0
+        ),
+    )(*blocks, weight, bias.reshape(1, -1), dact)
+
+
+def reversed_bits(index, count):
+    out = 0
+    bit = 1
+    while bit < count:
+        out = 2 * out + (index & 1)
+        index //= 2
+        bit *= 2
+    return out
+
+
+def muon_kernel(
+    limit_ref,
+    landed_ref,
+    mom_hbm,
+    master_hbm,
+    grad_out,
+    mom_out,
+    master_out,
+    grad_buf,
+    mom_buf,
+    master_buf,
+    x_buf,
+    gram,
+    poly,
+    sems,
+    *,
+    out_rows,
+):
+    count, share, size = landed_ref.shape
+    tile = 512
+    tiles = size // tile
+    load_mom = pltpu.make_async_copy(mom_hbm, mom_buf, sems.at[0])
+    load_master = pltpu.make_async_copy(master_hbm, master_buf, sems.at[1])
+    store_grad = pltpu.make_async_copy(grad_buf, grad_out, sems.at[2])
+    store_mom = pltpu.make_async_copy(mom_buf, mom_out, sems.at[3])
+    store_master = pltpu.make_async_copy(master_buf, master_out, sems.at[4])
+    load_mom.start()
+    load_master.start()
+    row_limit = limit_ref[0]
+    col_limit = limit_ref[1]
+    is_out = limit_ref[2] == 1
+
+    @pl.when(is_out)
+    def _():
+        grad_buf[...] = jnp.zeros_like(grad_buf)
+        for src in range(count):
+            at = reversed_bits(src, count)
+            piece = landed_ref[src].astype(F32)
+            grad_buf[at * out_rows : (at + 1) * out_rows, :] = piece[:out_rows]
+
+    @pl.when(jnp.logical_not(is_out))
+    def _():
+        for src in range(count):
+            at = reversed_bits(src, count)
+            grad_buf[at * share : (at + 1) * share, :] = landed_ref[src].astype(F32)
+
+    store_grad.start()
+    load_mom.wait()
+    block = 128
+
+    def valid(r):
+        row = lax.broadcasted_iota(jnp.int32, (block, size), 0) + r * block
+        col = lax.broadcasted_iota(jnp.int32, (block, size), 1)
+        return (row < row_limit) & (col < col_limit)
+
+    def at_rows(r, step):
+        return pl.ds(pl.multiple_of(r * step, step), step)
+
+    def momentum_rows(r, total):
+        rows = at_rows(r, block)
+        value = jnp.where(valid(r), mom_decay * mom_buf[rows, :] + grad_buf[rows, :], 0.0)
+        mom_buf[rows, :] = value
+        return total + value * value
+
+    total = lax.fori_loop(0, size // block, momentum_rows, jnp.zeros((block, size), F32))
+    store_mom.start()
+    scale = 1.0 / (jnp.sqrt(jnp.sum(total)) + 1e-07)
+
+    def first_rows(r, carry):
+        rows = at_rows(r, block)
+        x_buf[0, rows, :] = (mom_buf[rows, :] * scale).astype(BF16)
+        return carry
+
+    lax.fori_loop(0, size // block, first_rows, 0)
 
     def one_turn(turn, carry):
         now = lax.rem(turn, 2)
         later = 1 - now
 
         def gram_rows(r, c):
-            rows = pl.ds(pl.multiple_of(r * TILE, TILE), TILE)
+            rows = at_rows(r, tile)
             gram[rows, :] = mm(x_buf[now, rows, :], x_buf[now], NT).astype(BF16)
             return c
 
         lax.fori_loop(0, tiles, gram_rows, 0)
 
         def poly_rows(r, c):
-            rows = pl.ds(pl.multiple_of(r * TILE, TILE), TILE)
+            rows = at_rows(r, tile)
             mine = gram[rows, :]
             poly[rows, :] = (ns_b * mine.astype(F32) + ns_c * mm(mine, gram[...])).astype(BF16)
             return c
@@ -248,7 +385,7 @@
         lax.fori_loop(0, tiles, poly_rows, 0)
 
         def next_rows(r, c):
-            rows = pl.ds(pl.multiple_of(r * TILE, TILE), TILE)
+            rows = at_rows(r, tile)
             x_buf[later, rows, :] = (
                 ns_a * x_buf[now, rows, :].astype(F32) + mm(poly[rows, :], x_buf[now])
             ).astype(BF16)
@@ -257,27 +394,51 @@
         lax.fori_loop(0, tiles, next_rows, 0)
         return carry
 
-    lax.fori_loop(0, NS_STEPS, one_turn, 0)
-    o_ref[...] = x_buf[NS_STEPS % 2]
-
-
-def newton_schulz(start):
-    size = start.shape[0]
+    lax.fori_loop(0, jnp.where(row_limit > 0, NS_STEPS, 0), one_turn, 0)
+    load_master.wait()
+
+    def master_rows(r, carry):
+        rows = at_rows(r, block)
+        ortho = x_buf[NS_STEPS % 2, rows, :].astype(F32)
+        fresh = master_buf[rows, :] * (1.0 - muon_rate * muon_decay) - muon_rate * ortho
+        master_buf[rows, :] = jnp.where(valid(r), fresh, 0.0)
+        return carry
+
+    lax.fori_loop(0, size // block, master_rows, 0)
+    store_master.start()
+    store_grad.wait()
+    store_mom.wait()
+    store_master.wait()
+
+
+def muon_update(limits, landed, momentum, master, out_rows):
+    size = momentum.shape[0]
+    shape = jax.ShapeDtypeStruct((size, size), F32)
+    anywhere = pl.BlockSpec(memory_space=pl.ANY)
     return pl.pallas_call(
-        schulz_kernel,
-        in_specs=[pl.BlockSpec(memory_space=pltpu.VMEM)],
-        out_specs=pl.BlockSpec(memory_space=pltpu.VMEM),
-        out_shape=jax.ShapeDtypeStruct(start.shape, BF16),
+        partial(muon_kernel, out_rows=out_rows),
+        in_specs=[
+            pl.BlockSpec(memory_space=pltpu.SMEM),
+            pl.BlockSpec(memory_space=pltpu.VMEM),
+            anywhere,
+            anywhere,
+        ],
+        out_specs=[anywhere] * 3,
+        out_shape=[shape] * 3,
         scratch_shapes=[
+            pltpu.VMEM((size, size), F32),
+            pltpu.VMEM((size, size), F32),
+            pltpu.VMEM((size, size), F32),
             pltpu.VMEM((2, size, size), BF16),
             pltpu.VMEM((size, size), BF16),
             pltpu.VMEM((size, size), BF16),
+            pltpu.SemaphoreType.DMA((5,)),
         ],
         compiler_params=pltpu.CompilerParams(vmem_limit_bytes=VMEM_GRANT),
         cost_estimate=pl.CostEstimate(
-            flops=6 * NS_STEPS * size**3, bytes_accessed=4 * size * size, transcendentals=0
+            flops=6 * NS_STEPS * size**3, bytes_accessed=22 * size * size, transcendentals=0
         ),
-    )(start)
+    )(limits, landed, momentum, master)
 
 
 def swap(value, bit):
@@ -285,19 +446,65 @@
     return lax.ppermute(value, "tensor", [(i, i ^ bit) for i in range(count)])
 
 
-def gather_pair(value):
-    mine = jnp.stack([value, swap(value, 2)])
-    return mine, swap(mine, 1)
-
-
-def scatter_sum(keep_in, send_in, weight, dims):
-    shape = keep_in.shape[:-1] + (-1,)
-    send = mm(rows2(send_in), weight, dims).astype(BF16).reshape(shape)
+def gather_four(value):
+    core_block = swap(value, 1)
+    far_block = swap(value, 2)
+    return value, far_block, core_block, swap(far_block, 1)
+
+
+def scatter_sum(value, weight, dims):
+    size = value.shape[0] // 4
+    send = mm(value[2 * size :], weight, dims).astype(BF16)
     arrived = swap(send, 1)
-    keep = mm(rows2(keep_in), weight, dims).reshape(shape)
+    keep = mm(value[: 2 * size], weight, dims)
     part = keep + arrived.astype(F32)
-    far = swap(part[1].astype(BF16), 2)
-    return part[0] + far.astype(F32)
+    far = swap(part[size:].astype(BF16), 2)
+    return part[:size] + far.astype(F32)
+
+
+def data_swap(value, bit):
+    count = lax.axis_size("dp")
+    return lax.ppermute(value, "dp", [(i, i ^ bit) for i in range(count)])
+
+
+def after(value, *others):
+    return lax.optimization_barrier((value, *others))[0]
+
+
+def gather_kinds(pieces):
+    index = lax.axis_index("dp")
+    before = []
+    results = []
+    for piece in pieces:
+        done = []
+        for at, bit in enumerate(reversed(axis_bits("dp"))):
+            if before:
+                piece = after(piece, before[at])
+            other = data_swap(piece, bit)
+            upper = (index & bit) != 0
+            piece = jnp.where(
+                upper,
+                jnp.concatenate([other, piece], axis=0),
+                jnp.concatenate([piece, other], axis=0),
+            )
+            done.append(other)
+        before = done
+        results.append(piece)
+    return results
+
+
+def halve(value, bit):
+    half = value.shape[0] // 2
+    upper = ((lax.axis_index("dp") & bit) != 0).astype(jnp.int32)
+    give = lax.dynamic_slice_in_dim(value, (1 - upper) * half, half, 0)
+    keep = lax.dynamic_slice_in_dim(value, upper * half, half, 0)
+    return (keep.astype(F32) + data_swap(give, bit).astype(F32)).astype(BF16)
+
+
+def halve_rest(value, done=1):
+    for bit in axis_bits("dp")[done:]:
+        value = halve(value, bit)
+    return value
 
 
 def axis_bits(name):
@@ -372,24 +579,21 @@
     owned = owner_row == data_idx
     slot_value = master_slots[0]
 
+    order = [reversed_bits(i, data_count) for i in range(data_count)]
     slot_low = slot_value.astype(BF16)
     offer_out = jnp.pad(
         slot_low[:head_width].reshape(data_count, share_out, width),
         ((0, 0), (0, share - share_out), (0, 0)),
     )
     offer = jnp.where(owned[1], offer_out, slot_low.reshape(data_count, share, width))
-    shares = lax.all_to_all(offer, "dp", 0, 0)
+    shares = lax.all_to_all(jnp.concatenate([offer[i : i + 1] for i in order]), "dp", 0, 0)
 
     def share_of(kind):
         return lax.dynamic_index_in_dim(shares, owner_row[kind], 0, keepdims=False)
 
-    def gather_rows(value):
-        return lax.all_gather(value, "dp", axis=0, tiled=True)
-
-    w_qkv = gather_rows(share_of(0)[:, : 3 * head_width])
-    w_out = gather_rows(share_of(1)[:share_out])
-    w_proj = gather_rows(share_of(3))
-    w_fc = gather_rows(share_of(2))
+    w_qkv, w_out, w_proj, w_fc = gather_kinds(
+        (share_of(0)[:, : 3 * head_width], share_of(1)[:share_out], share_of(3), share_of(2))
+    )
 
     params = small_gather(small_master)
 
@@ -406,18 +610,19 @@
     bias_fc = own_slice(7 * width, ff_width)
     bias_proj = params[7 * width + FF :]
 
+    part = rows_dev // CHUNKS
+    rows_of = [slice(chunk * part, (chunk + 1) * part) for chunk in range(CHUNKS)]
     rows_in = inputs.astype(F32)
     unit_one, scale_one = norm_parts(rows_in)
-    normed = (unit_one * gain_one + shift_one).astype(BF16)
-    normed_all = jnp.stack(gather_pair(normed))
-    dy_pair = gather_pair(out_grad)
+    unit_all, _ = norm_parts(jnp.concatenate(gather_four(inputs)).astype(F32))
+    normed_all = (unit_all * gain_one + shift_one).astype(BF16)
+    dy_all = [jnp.concatenate(gather_four(out_grad[rows])) for rows in rows_of]
     bias_qkv = jnp.concatenate([bias_query, jnp.zeros_like(bias_query), bias_value])
     scale_qkv = jnp.where(jnp.arange(3 * head_width) < head_width, HEAD_DIM**-0.5, 1.0)
-    qkv = ((mm(rows2(normed_all), w_qkv) + bias_qkv) * scale_qkv).astype(BF16)
+    qkv = ((mm(normed_all, w_qkv) + bias_qkv) * scale_qkv).astype(BF16)
     qkv = qkv.reshape(2, 2, rows_dev, 3 * head_width)
-    back_act = [mm(rows2(dy), w_proj, NT).astype(BF16) for dy in dy_pair]
-
-    part = rows_dev // CHUNKS
+    back_act = [mm(dy, w_proj, NT).astype(BF16) for dy in dy_all]
+
     mixed, log_sums = [], []
     for chunk in range(CHUNKS):
         mixed_one, sums_one = attend(core, qkv, chunk, CHUNKS)
@@ -425,74 +630,59 @@
         log_sums.append(sums_one)
     middles, branches, grad_proj, grad_fc, fc_bias_grad = [], [], 0.0, 0.0, 0.0
     back_normed_two, mine_two = [], []
+    normed_two = None
     for chunk in range(CHUNKS):
-        rows = slice(chunk * part, (chunk + 1) * part)
-        branch = scatter_sum(mixed[chunk][0], mixed[chunk][1], w_out, NN)
-        middle = rows_in[rows] + branch + bias_out
+        branch = scatter_sum(rows2(mixed[chunk]), w_out, NN)
+        if chunk > 0:
+            branch = after(branch, normed_two)
+        middle = rows_in[rows_of[chunk]] + branch + bias_out
         unit_two, scale_two = norm_parts(middle)
         normed_two = (unit_two * gain_two + shift_two).astype(BF16)
-        pair = gather_pair(normed_two)
-        acts, backs = [], []
-        for side in range(2):
-            hidden = mm(rows2(pair[side]), w_fc) + bias_fc
-            bent = jnp.tanh(gelu_in * (hidden + gelu_cube * hidden * hidden * hidden))
-            act = (0.5 * hidden * (1.0 + bent)).astype(BF16)
-            slope = 0.5 * (1.0 + bent) + 0.5 * hidden * (1.0 - bent * bent) * (
-                gelu_in * (1.0 + 3.0 * gelu_cube * hidden * hidden)
-            )
-            dact = back_act[side].reshape(2, rows_dev, ff_width)[:, rows]
-            back = (rows2(dact).astype(F32) * slope).astype(BF16)
-            fc_bias_grad = fc_bias_grad + jnp.sum(back, axis=0, dtype=F32)
-            acts.append(act)
-            backs.append(back)
-        shape = (2, part, ff_width)
-        back_normed_two.append(
-            scatter_sum(backs[0].reshape(shape), backs[1].reshape(shape), w_fc, NT)
+        acts, backs, sums, normed_two_all = hidden_layer(
+            gather_four(normed_two), w_fc, bias_fc, back_act[chunk]
         )
-        branches.append(scatter_sum(acts[0].reshape(shape), acts[1].reshape(shape), w_proj, NN))
-        for side in range(2):
-            dy = dy_pair[side][:, rows]
-            grad_proj = grad_proj + mm(acts[side], rows2(dy), TN)
-            grad_fc = grad_fc + mm(rows2(pair[side]), backs[side], TN)
+        fc_bias_grad = fc_bias_grad + sums[0]
+        back_normed_two.append(scatter_sum(backs, w_fc, NT))
+        branches.append(scatter_sum(acts, w_proj, NN))
+        grad_proj = grad_proj + mm(acts, dy_all[chunk], TN)
+        grad_fc = grad_fc + mm(normed_two_all, backs, TN)
         middles.append(middle)
         mine_two.append((unit_two, scale_two))
     middle = jnp.concatenate(middles)
     block_out = (middle + jnp.concatenate(branches) + bias_proj).astype(BF16)
-
-    def scatter_grad(value):
-        return lax.psum_scatter(value.astype(BF16), "dp", scatter_dimension=0, tiled=True)
-
-    share_proj = scatter_grad(grad_proj)
-    share_fc = scatter_grad(grad_fc)
-
-    back_middles, mid_pairs, gain_two_grad, shift_two_grad = [], [], 0.0, 0.0
+    half_proj = halve(halve(grad_proj.astype(BF16), 1), 2)
+    half_fc = halve(grad_fc.astype(BF16), 1)
+
+    back_middles, back_mixed = [], []
+    gain_two_grad, shift_two_grad, grad_out = 0.0, 0.0, 0.0
+    back_low = None
     for chunk in range(CHUNKS):
-        rows = slice(chunk * part, (chunk + 1) * part)
         unit_two, scale_two = mine_two[chunk]
         grad = back_normed_two[chunk]
-        back_middle = out_grad[rows].astype(F32) + norm_back(unit_two, scale_two, gain_two, grad)
+        if chunk > 0:
+            grad = after(grad, back_low)
+        back_middle = out_grad[rows_of[chunk]].astype(F32) + norm_back(
+            unit_two, scale_two, gain_two, grad
+        )
+        back_low = back_middle.astype(BF16)
+        mid = jnp.concatenate(gather_four(back_low))
+        back_mixed.append(mm(mid, w_out, NT).astype(BF16).reshape(2, 2, part, head_width))
+        grad_out = grad_out + mm(rows2(mixed[chunk]), mid, TN)
         gain_two_grad = gain_two_grad + jnp.sum(grad * unit_two, axis=0)
         shift_two_grad = shift_two_grad + jnp.sum(grad, axis=0)
-        mid_pairs.append(gather_pair(back_middle.astype(BF16)))
         back_middles.append(back_middle)
     back_middle = jnp.concatenate(back_middles)
     proj_bias_grad = jnp.sum(out_grad, axis=0, dtype=F32)
     out_bias_grad = jnp.sum(back_middle, axis=0)
-    back_mixed, grad_out = [], 0.0
-    for side in range(2):
-        sides = []
-        for chunk in range(CHUNKS):
-            mid = rows2(mid_pairs[chunk][side])
-            sides.append(mm(mid, w_out, NT).astype(BF16).reshape(2, part, head_width))
-            grad_out = grad_out + mm(rows2(mixed[chunk][side]), mid, TN)
-        back_mixed.append(jnp.concatenate(sides, axis=1))
-    back_qkv = attend_back(core, qkv, mixed, log_sums, jnp.stack(back_mixed))
-    grad_qkv = mm(rows2(normed_all), rows2(back_qkv), TN)
+    back_mixed, half_proj, half_fc = lax.optimization_barrier((back_mixed, half_proj, half_fc))
+    share_proj = halve_rest(half_proj, 2)
+    share_fc = halve_rest(half_fc)
+    back_qkv = attend_back(core, qkv, mixed, log_sums, back_mixed)
+    grad_qkv = mm(normed_all, rows2(back_qkv), TN).astype(BF16)
     qkv_bias_grad = jnp.sum(back_qkv, axis=(0, 1, 2), dtype=F32)
-
-    share_out_grad = scatter_grad(grad_out)
-    share_qkv = scatter_grad(grad_qkv)
-    back_normed = scatter_sum(back_qkv[0], back_qkv[1], w_qkv, NT)
+    share_out_grad = halve_rest(halve(grad_out.astype(BF16), 1))
+    share_qkv = halve_rest(halve(grad_qkv, 1))
+    back_normed = scatter_sum(rows2(after(back_qkv, grad_qkv)), w_qkv, NT)
     input_grad = back_middle + norm_back(unit_one, scale_one, gain_one, back_normed)
     gain_one_grad = jnp.sum(back_normed * unit_one, axis=0)
     shift_one_grad = jnp.sum(back_normed, axis=0)
@@ -507,11 +697,6 @@
     for kind in range(4):
         bundle = lax.dynamic_update_index_in_dim(bundle, pieces[kind], owner_row[kind], 0)
     landed = lax.all_to_all(bundle, "dp", 0, 0)
-    landed_out = jnp.pad(
-        landed[:, :share_out].reshape(head_width, width), ((0, width - head_width), (0, 0))
-    )
-    chosen = jnp.where(owned[1], landed_out, landed.reshape(width, width)).astype(F32)
-
     full_grad = jnp.concatenate(
         [
             gain_one_grad,
@@ -537,28 +722,16 @@
     second_hat = second_new / (1.0 - beta_two**STEP)
     small_new = small_master - adam_rate * first_hat / (jnp.sqrt(second_hat) + adam_eps)
 
-    any_owned = jnp.any(owned)
-    row_limit = jnp.where(owned[1], head_width, jnp.where(any_owned, width, 0))
+    row_limit = jnp.where(owned[1], head_width, jnp.where(jnp.any(owned), width, 0))
     col_limit = jnp.where(owned[0], 3 * head_width, width)
-    row_ids = lax.broadcasted_iota(jnp.int32, (width, width), 0)
-    col_ids = lax.broadcasted_iota(jnp.int32, (width, width), 1)
-    valid = (row_ids < row_limit) & (col_ids < col_limit)
-    mom_slot = jnp.where(valid, mom_decay * momentum_slots[0] + chosen, 0.0)
-
-    def run_owner(packed):
-        momentum, master, keep = packed
-        start = (momentum / (jnp.sqrt(jnp.sum(momentum * momentum)) + 1e-07)).astype(BF16)
-        ortho = newton_schulz(start).astype(F32)
-        return jnp.where(keep, master * (1.0 - muon_rate * muon_decay) - muon_rate * ortho, 0.0)
-
-    def skip_owner(packed):
-        return jnp.zeros_like(packed[1])
-
-    fresh_slot = lax.cond(any_owned, run_owner, skip_owner, (mom_slot, slot_value, valid))
+    limits = jnp.stack([row_limit, col_limit, owned[1].astype(jnp.int32)]).astype(jnp.int32)
+    grad_slot, mom_slot, fresh_slot = muon_update(
+        limits, landed, momentum_slots[0], slot_value, share_out
+    )
     return (
         block_out,
         input_grad,
-        chosen[None],
+        grad_slot[None],
         mom_slot[None],
         fresh_slot[None],
         small_grad,

time: 776 us -> 575 us (0.74)
  the two profiles are of different devices: /device:TPU:8 before, /device:TPU:13 now
where the time goes in v2:
time: 575 us; the launch traced here: 565 us
  waiting for transfers between devices  224 us (39%)
  Pallas kernels  97.2 us (17%)
  starting transfers between devices  96.4 us (17%)
  matrix products  67.3 us (12%)
  other arithmetic  39.6 us (7%)
  local copies, waits for them, and re-layouts  26.7 us (5%)
  between operations  13.2 us (2%)
    ppermute x24, waiting for transfers between devices, data_swap(): return lax.ppermute(value, 'dp', [(i, i ^ bit) for i in range(count)])  116 us
    dot_general x26, matrix products, mm(): return lax.dot_general(left, right, dims, preferred_element_type=F32)  67.3 us
    pallas_call x1, Pallas kernels, muon_update(): pl.pallas_call(partial(muon_kernel, out_rows=out_rows), in_specs=[pl.Bloc...  49.1 us
    ppermute x5, waiting for transfers between devices, small_scatter(): lax.ppermute(give, name, [(i, i ^ bit) for i in range(count)])  43.3 us
    ppermute x35, starting transfers between devices, swap(): return lax.ppermute(value, 'tensor', [(i, i ^ bit) for i in range(count)])  41.7 us
    ppermute x35, waiting for transfers between devices, swap(): return lax.ppermute(value, 'tensor', [(i, i ^ bit) for i in range(count)])  38 us
    ppermute x24, starting transfers between devices, data_swap(): return lax.ppermute(value, 'dp', [(i, i ^ bit) for i in range(count)])  29 us
    ppermute x5, waiting for transfers between devices, small_gather(): other = lax.ppermute(piece, name, [(i, i ^ bit) for i in range(count)])  27.3 us
  transfers between devices with their start and end apart: 71, of which 28 were waited for; matrix products, arithmetic and copies ran while one was open for 20% of the time, Pallas kernels for 9%

profile of v2, /device:TPU:13, one launch (start us, length us, event | category | flops | bytes accessed | tf_op | source)
XLA Modules:
  0.0 564.7 jit_solution(9384709235468622617)
XLA Ops:
  13.5 5.8 %all-to-all-start = ((bf16[8,128,1024]{2,1,0:T(8,128)(2,1)}), bf16[8,128,1024]{2,1,0:T(8,128)(2,1)}, u32[]{:S(2)}, u32[]{:S(2)}) async-start(bf16[8,128,1024]{2,1,0:T(8,128)(2,1)} %slice_dynamic-update-slice_fusion), calls=%async_computation | async-start | bytes 4194304 | tf_op jit(solution)/shard_map/all_to_all | solution.py:589
  23.8 19.1 %collective-permute-done.4 = f32[2,384]{1,0:T(2,128)S(1)} collective-permute-done((f32[2,384]{1,0:T(2,128)S(1)}, f32[2,384]{1,0:T(2,128)S(1)}, u32[]{:S(2)}, u32[]{:S(2)}) %collective-permute-start.4) | collective-permute-done | bytes 3104 | tf_op jit(solution)/shard_map/ppermute | solution.py:526
  49.6 4.6 collective-permute-done.6
  71.0 7.1 %collective-permute-done.8 = bf16[128,768]{1,0:T(8,128)(2,1)S(1)} collective-permute-done((bf16[128,768]{1,0:T(8,128)(2,1)S(1)}, bf16[128,768]{1,0:T(8,128)(2,1)S(1)}, u32[]{:S(2)}, u32[]{:S(2)}) %collective-permute-start.8) | collective-permute-done | bytes 196640 | tf_op jit(solution)/shard_map/ppermute | solution.py:467
  85.4 5.3 collective-permute-done.9
  97.0 11.2 %collective-permute-done.21 = bf16[128,1024]{1,0:T(8,128)(2,1)S(1)} collective-permute-done((bf16[128,1024]{1,0:T(8,128)(2,1)S(1)}, bf16[128,1024]{1,0:T(8,128)(2,1)S(1)}, u32[]{:S(2)}, u32[]{:S(2)}) %collective-permute-start.21) | collective-permute-done | bytes 262176 | tf_op jit(solution)/shard_map/ppermute | solution.py:467
  113.0 5.6 multiply_convert_fusion
  118.6 4.9 shard_map.143
  132.2 5.5 shard_map.144
  143.5 10.3 %collective-permute-done.25 = bf16[512,1024]{1,0:T(8,128)(2,1)S(1)} collective-permute-done((bf16[512,1024]{1,0:T(8,128)(2,1)S(1)}, bf16[512,1024]{1,0:T(8,128)(2,1)S(1)}, u32[]{:S(2)}, u32[]{:S(2)}) %collective-permute-start.25) | collective-permute-done | bytes 1048608 | tf_op jit(solution)/shard_map/ppermute | solution.py:467
  167.5 6.9 %collective-permute-start.20 = (bf16[256,1024]{1,0:T(8,128)(2,1)S(1)}, bf16[256,1024]{1,0:T(8,128)(2,1)S(1)}, u32[]{:S(2)}, u32[]{:S(2)}) collective-permute-start(bf16[256,1024]{1,0:T(8,128)(2,1)S(1)} %collective-permute-done.18.refs_1_), channel_id=1, source_target_pairs={{0,1},{1,0},{2,3},{3,2},{4,5},{5,4},{6,7},{7,6},{8,9},{9,8},{10,11... | collective-permute-start | bytes 1572872 | tf_op jit(solution)/shard_map/ppermute | solution.py:446
  174.4 5.0 convolution_convert_fusion.1.refs_6_
  183.0 8.9 %shard_map.145 = (bf16[1024,1024]{1,0:T(8,128)(2,1)S(1)}, bf16[1024,1024]{1,0:T(8,128)(2,1)}, f32[1,1024]{1,0:T(1,128)S(1)}, bf16[1024,1024]{1,0:T(8,128)(2,1)}) custom-call(bf16[256,1024]{1,0:T(8,128)(2,1)S(1)} %add_convert_fusion.8.refs_0_, bf16[256,1024]{1,0:T(8,128)(2,1)S(1)} %collective-permute-done.18.refs_1_, ...), custom_call_target="tpu_custom_call" | custom-call | flops 2147483648 | bytes 12000000 | tf_op jit(solution)/shard_map/pallas_call | solution.py:255
  191.9 4.3 convolution_convert_fusion.5
  209.7 10.1 %collective-permute-done.41 = bf16[256,1024]{1,0:T(8,128)(2,1)S(1)} collective-permute-done((bf16[256,1024]{1,0:T(8,128)(2,1)S(1)}, bf16[256,1024]{1,0:T(8,128)(2,1)S(1)}, u32[]{:S(2)}, u32[]{:S(2)}) %collective-permute-start.41) | collective-permute-done | bytes 524320 | tf_op jit(solution)/shard_map/ppermute | solution.py:446
  221.5 4.5 convert_add_fusion.4
  237.1 5.2 convolution_convert_fusion.refs_6_
  245.8 10.2 %collective-permute-done.44 = bf16[256,1024]{1,0:T(8,128)(2,1)} collective-permute-done((bf16[256,1024]{1,0:T(8,128)(2,1)}, bf16[256,1024]{1,0:T(8,128)(2,1)}, u32[]{:S(2)}, u32[]{:S(2)}) %collective-permute-start.44) | collective-permute-done | bytes 524320 | tf_op jit(solution)/shard_map/ppermute | solution.py:446
  258.1 9.0 %shard_map.146 = (bf16[1024,1024]{1,0:T(8,128)(2,1)S(1)}, bf16[1024,1024]{1,0:T(8,128)(2,1)}, f32[1,1024]{1,0:T(1,128)S(1)}, bf16[1024,1024]{1,0:T(8,128)(2,1)}) custom-call(bf16[256,1024]{1,0:T(8,128)(2,1)S(1)} %get-tuple-element.116.refs_0_, bf16[256,1024]{1,0:T(8,128)(2,1)S(1)} %collective-permute-done.32.refs_1_, ...), custom_call_target="tpu_custom_call" | custom-call | flops 2147483648 | bytes 12000000 | tf_op jit(solution)/shard_map/pallas_call | solution.py:255
  276.3 4.1 fusion.20
  291.2 31.1 %collective-permute-done.50 = bf16[512,1024]{1,0:T(8,128)(2,1)S(1)} collective-permute-done((bf16[512,1024]{1,0:T(8,128)(2,1)S(1)}, bf16[512,1024]{1,0:T(8,128)(2,1)S(1)}, u32[]{:S(2)}, u32[]{:S(2)}) %collective-permute-start.50) | collective-permute-done | bytes 1048608 | tf_op jit(solution)/shard_map/ppermute | solution.py:467
  330.5 7.2 %collective-permute-done.47 = bf16[256,1024]{1,0:T(8,128)(2,1)S(1)} collective-permute-done((bf16[256,1024]{1,0:T(8,128)(2,1)S(1)}, bf16[256,1024]{1,0:T(8,128)(2,1)S(1)}, u32[]{:S(2)}, u32[]{:S(2)}) %collective-permute-start.47) | collective-permute-done | bytes 524320 | tf_op jit(solution)/shard_map/ppermute | solution.py:446
  343.1 19.9 %shard_map.147 = bf16[2,2,512,768]{3,2,1,0:T(8,128)(2,1)} custom-call(s32[1]{0:T(128)} %bitcast.core_ref, bf16[2,2,512,768]{3,2,1,0:T(8,128)(2,1)} %bitcast.79, bf16[2,2,512,768]{3,2,1,0:T(8,128)(2,1)} %bitcast.80, bf16[2,2,512,768]{3,2,1,0:T(8,128)(2,1)} %bitcast.81, bf16[2,2,256,256]{3,2,1,0:T(8,128)(2,1)S(1)} %get-tuple-element.39.refs_0_, ...), custom_call_target="tpu_custom_call" | custom-call | flops 24999999488 | bytes 12000000 | tf_op jit(solution)/shard_map/pallas_call | solution.py:206
  363.0 6.3 %convolution_convert_fusion.3 = bf16[1024,768]{1,0:T(8,128)(2,1)S(1)} fusion(bf16[2048,768]{1,0:T(8,128)(2,1)} %bitcast.84, f32[1024]{0:T(1024)S(1)} %get-tuple-element.112, f32[1024]{0:T(1024)S(1)} %get-tuple-element.113, f32[2048]{0:T(1024)S(1)} %add_rsqrt_fusion, f32[2048]{0:T(1024)S(1)} %broadcast_multiply_fusion, bf16[512,1024]{1,0:T(8,128)(2,1)S(1)} %copy-done.33, ...), kind=kOutput, calls=%fused_computation.44 | convolution fusion | flops 3249274880 | bytes 8937472 | tf_op jit(solution)/shard_map/dot_general | solution.py:44
  378.2 5.8 %collective-permute-done.58 = bf16[128,1024]{1,0:T(8,128)(2,1)S(1)} collective-permute-done((bf16[128,1024]{1,0:T(8,128)(2,1)S(1)}, bf16[128,1024]{1,0:T(8,128)(2,1)S(1)}, u32[]{:S(2)}, u32[]{:S(2)}) %collective-permute-start.58) | collective-permute-done | bytes 262176 | tf_op jit(solution)/shard_map/ppermute | solution.py:467
  388.4 12.4 %collective-permute-done.55 = bf16[512,768]{1,0:T(8,128)(2,1)S(1)} collective-permute-done((bf16[512,768]{1,0:T(8,128)(2,1)S(1)}, bf16[512,768]{1,0:T(8,128)(2,1)S(1)}, u32[]{:S(2)}, u32[]{:S(2)}) %collective-permute-start.55) | collective-permute-done | bytes 786464 | tf_op jit(solution)/shard_map/ppermute | solution.py:467
  401.0 6.4 %collective-permute-done.60 = bf16[32,1024]{1,0:T(8,128)(2,1)S(1)} collective-permute-done((bf16[32,1024]{1,0:T(8,128)(2,1)S(1)}, bf16[32,1024]{1,0:T(8,128)(2,1)S(1)}, u32[]{:S(2)}, u32[]{:S(2)}) %collective-permute-start.60) | collective-permute-done | bytes 65568 | tf_op jit(solution)/shard_map/ppermute | solution.py:467
  410.7 8.8 %collective-permute-done.56 = bf16[256,768]{1,0:T(8,128)(2,1)S(1)} collective-permute-done((bf16[256,768]{1,0:T(8,128)(2,1)S(1)}, bf16[256,768]{1,0:T(8,128)(2,1)S(1)}, u32[]{:S(2)}, u32[]{:S(2)}) %collective-permute-start.56) | collective-permute-done | bytes 393248 | tf_op jit(solution)/shard_map/ppermute | solution.py:467
  425.6 9.5 %collective-permute-done.57 = bf16[128,768]{1,0:T(8,128)(2,1)S(1)} collective-permute-done((bf16[128,768]{1,0:T(8,128)(2,1)S(1)}, bf16[128,768]{1,0:T(8,128)(2,1)S(1)}, u32[]{:S(2)}, u32[]{:S(2)}) %collective-permute-start.57) | collective-permute-done | bytes 196640 | tf_op jit(solution)/shard_map/ppermute | solution.py:467
  442.2 7.9 %all-to-all-start.1 = ((bf16[8,128,1024]{2,1,0:T(8,128)(2,1)}), bf16[8,128,1024]{2,1,0:T(8,128)(2,1)S(1)}, u32[]{:S(2)}, u32[]{:S(2)}) async-start(bf16[8,128,1024]{2,1,0:T(8,128)(2,1)} %fusion.25), calls=%async_computation.1 | async-start | bytes 4194304 | tf_op jit(solution)/shard_map/all_to_all | solution.py:699
  457.9 38.9 %collective-permute-done.64 = f32[6144]{0:T(1024)S(1)} collective-permute-done((f32[6144]{0:T(1024)S(1)}, f32[6144]{0:T(1024)S(1)}, u32[]{:S(2)}, u32[]{:S(2)}) %collective-permute-start.64) | collective-permute-done | bytes 24608 | tf_op jit(solution)/shard_map/ppermute | solution.py:545
  515.2 49.1 %shard_map.148 = (f32[1024,1024]{1,0:T(8,128)}, f32[1024,1024]{1,0:T(8,128)}, f32[1024,1024]{1,0:T(8,128)}) custom-call(s32[3]{0:T(128)S(1)} %pad_add_fusion.limit_ref, bf16[8,128,1024]{2,1,0:T(8,128)(2,1)S(1)} %all-to-all-done.1.landed_ref, f32[1024,1024]{1,0:T(8,128)} %bitcast.96, f32[1024,1024]{1,0:T(8,128)} %bitcast.87), custom_call_target="tpu_custom_call" | custom-call | flops 32212254720 | bytes 23068672 | tf_op jit(solution)/shard_map/pallas_call | solution.py:418
  (425 shorter events, 200.9 us)
Async XLA Ops:
  13.5 52.6 %all-to-all-start = ((bf16[8,128,1024]{2,1,0:T(8,128)(2,1)}), bf16[8,128,1024]{2,1,0:T(8,128)(2,1)}, u32[]{:S(2)}, u32[]{:S(2)}) async-start(bf16[8,128,1024]{2,1,0:T(8,128)(2,1)} %slice_dynamic-update-slice_fusion), calls=%async_computation | async-start | bytes 4194304 | tf_op jit(solution)/shard_map/all_to_all | solution.py:589
  19.3 29.0 %collective-permute-start = (bf16[512,1024]{1,0:T(8,128)(2,1)S(1)}, bf16[512,1024]{1,0:T(8,128)(2,1)S(1)}, u32[]{:S(2)}, u32[]{:S(2)}) collective-permute-start(bf16[512,1024]{1,0:T(8,128)(2,1)S(1)} %copy-done.7), channel_id=1, source_target_pairs={{0,2},{1,3},{2,0},{3,1},{4,6},{5,7},{6,4},{7,5},{8,10},{9,11},{10,... | collective-permute-start | bytes 3145736 | tf_op jit(solution)/shard_map/ppermute | solution.py:446
  22.8 20.0 %collective-permute-start.4 = (f32[2,384]{1,0:T(2,128)S(1)}, f32[2,384]{1,0:T(2,128)S(1)}, u32[]{:S(2)}, u32[]{:S(2)}) collective-permute-start(f32[2,384]{1,0:T(2,128)S(1)} %maximum_select_fusion.16), channel_id=1, source_target_pairs={{0,2},{1,3},{2,0},{3,1},{4,6},{5,7},{6,4},{7,5},{8,10},{9,11},{10,... | collective-permute-start | bytes 9224 | tf_op jit(solution)/shard_map/ppermute | solution.py:526
  23.2 58.2 %collective-permute-start.1 = (bf16[512,1024]{1,0:T(8,128)(2,1)S(1)}, bf16[512,1024]{1,0:T(8,128)(2,1)}, u32[]{:S(2)}, u32[]{:S(2)}) collective-permute-start(bf16[512,1024]{1,0:T(8,128)(2,1)S(1)} %copy-done.7), channel_id=1, source_target_pairs={{0,1},{1,0},{2,3},{3,2},{4,5},{5,4},{6,7},{7,6},{8,9},{9,8},{10,11... | collective-permute-start | bytes 3145736 | tf_op jit(solution)/shard_map/ppermute | solution.py:446
  44.3 81.6 %collective-permute-start.27 = (bf16[256,1024]{1,0:T(8,128)(2,1)}, bf16[256,1024]{1,0:T(8,128)(2,1)}, u32[]{:S(2)}, u32[]{:S(2)}) collective-permute-start(bf16[256,1024]{1,0:T(8,128)(2,1)} %get-tuple-element.101), channel_id=1, source_target_pairs={{0,2},{1,3},{2,0},{3,1},{4,6},{5,7},{6,4},{7,5},{8,10},{9,11},{10,... | collective-permute-start | bytes 1572872 | tf_op jit(solution)/shard_map/ppermute | solution.py:446
  45.5 114.3 %collective-permute-start.28 = (bf16[256,1024]{1,0:T(8,128)(2,1)}, bf16[256,1024]{1,0:T(8,128)(2,1)}, u32[]{:S(2)}, u32[]{:S(2)}) collective-permute-start(bf16[256,1024]{1,0:T(8,128)(2,1)} %get-tuple-element.101), channel_id=1, source_target_pairs={{0,1},{1,0},{2,3},{3,2},{4,5},{5,4},{6,7},{7,6},{8,9},{9,8},{10,11... | collective-permute-start | bytes 1572872 | tf_op jit(solution)/shard_map/ppermute | solution.py:446
  48.3 33.0 %collective-permute-start.2 = (bf16[512,1024]{1,0:T(8,128)(2,1)S(1)}, bf16[512,1024]{1,0:T(8,128)(2,1)S(1)}, u32[]{:S(2)}, u32[]{:S(2)}) collective-permute-start(bf16[512,1024]{1,0:T(8,128)(2,1)S(1)} %collective-permute-done), channel_id=1, source_target_pairs={{0,1},{1,0},{2,3},{3,2},{4,5},{5,4},{6,7},{7,6},{8,9},{9,8},{10,11... | collective-permute-start | bytes 3145736 | tf_op jit(solution)/shard_map/ppermute | solution.py:446
  91.0 20.5 %collective-permute-start.10 = (bf16[512,768]{1,0:T(8,128)(2,1)S(1)}, bf16[512,768]{1,0:T(8,128)(2,1)S(1)}, u32[]{:S(2)}, u32[]{:S(2)}) collective-permute-start(bf16[512,768]{1,0:T(8,128)(2,1)S(1)} %maximum_select_fusion.5), channel_id=1, source_target_pairs={{0,4},{4,0},{8,12},{12,8},{16,20},{20,16},{24,28},{28,24},{1,5},{5... | collective-permute-start | bytes 2359304 | tf_op jit(solution)/shard_map/ppermute | solution.py:467
  125.9 37.2 %collective-permute-start.29 = (bf16[256,1024]{1,0:T(8,128)(2,1)}, bf16[256,1024]{1,0:T(8,128)(2,1)S(1)}, u32[]{:S(2)}, u32[]{:S(2)}) collective-permute-start(bf16[256,1024]{1,0:T(8,128)(2,1)} %collective-permute-done.27), channel_id=1, source_target_pairs={{0,1},{1,0},{2,3},{3,2},{4,5},{5,4},{6,7},{7,6},{8,9},{9,8},{10,11... | collective-permute-start | bytes 1572872 | tf_op jit(solution)/shard_map/ppermute | solution.py:446
  130.7 23.2 %collective-permute-start.25 = (bf16[512,1024]{1,0:T(8,128)(2,1)S(1)}, bf16[512,1024]{1,0:T(8,128)(2,1)S(1)}, u32[]{:S(2)}, u32[]{:S(2)}) collective-permute-start(bf16[512,1024]{1,0:T(8,128)(2,1)S(1)} %maximum_select_fusion.4), channel_id=1, source_target_pairs={{0,4},{4,0},{8,12},{12,8},{16,20},{20,16},{24,28},{28,24},{1,5},{5... | collective-permute-start | bytes 3145736 | tf_op jit(solution)/shard_map/ppermute | solution.py:467
  153.9 25.6 %collective-permute-start.26 = (bf16[512,1024]{1,0:T(8,128)(2,1)S(1)}, bf16[512,1024]{1,0:T(8,128)(2,1)S(1)}, u32[]{:S(2)}, u32[]{:S(2)}) collective-permute-start(bf16[512,1024]{1,0:T(8,128)(2,1)S(1)} %maximum_select_fusion.3), channel_id=1, source_target_pairs={{0,4},{4,0},{8,12},{12,8},{16,20},{20,16},{24,28},{28,24},{1,5},{5... | collective-permute-start | bytes 3145736 | tf_op jit(solution)/shard_map/ppermute | solution.py:467
  158.1 41.4 %collective-permute-start.35 = (bf16[256,1024]{1,0:T(8,128)(2,1)}, bf16[256,1024]{1,0:T(8,128)(2,1)}, u32[]{:S(2)}, u32[]{:S(2)}) collective-permute-start(bf16[256,1024]{1,0:T(8,128)(2,1)} %get-tuple-element.102), channel_id=1, source_target_pairs={{0,2},{1,3},{2,0},{3,1},{4,6},{5,7},{6,4},{7,5},{8,10},{9,11},{10,... | collective-permute-start | bytes 1572872 | tf_op jit(solution)/shard_map/ppermute | solution.py:446
  159.8 70.1 %collective-permute-start.36 = (bf16[256,1024]{1,0:T(8,128)(2,1)}, bf16[256,1024]{1,0:T(8,128)(2,1)}, u32[]{:S(2)}, u32[]{:S(2)}) collective-permute-start(bf16[256,1024]{1,0:T(8,128)(2,1)} %get-tuple-element.102), channel_id=1, source_target_pairs={{0,1},{1,0},{2,3},{3,2},{4,5},{5,4},{6,7},{7,6},{8,9},{9,8},{10,11... | collective-permute-start | bytes 1572872 | tf_op jit(solution)/shard_map/ppermute | solution.py:446
  179.5 20.3 %collective-permute-start.17 = (bf16[256,1024]{1,0:T(8,128)(2,1)}, bf16[256,1024]{1,0:T(8,128)(2,1)}, u32[]{:S(2)}, u32[]{:S(2)}) collective-permute-start(bf16[256,1024]{1,0:T(8,128)(2,1)} %slice.385), channel_id=1, source_target_pairs={{0,2},{1,3},{2,0},{3,1},{4,6},{5,7},{6,4},{7,5},{8,10},{9,11},{10,... | collective-permute-start | bytes 1572872 | tf_op jit(solution)/shard_map/ppermute | solution.py:446
  199.4 37.7 %collective-permute-start.37 = (bf16[256,1024]{1,0:T(8,128)(2,1)}, bf16[256,1024]{1,0:T(8,128)(2,1)}, u32[]{:S(2)}, u32[]{:S(2)}) collective-permute-start(bf16[256,1024]{1,0:T(8,128)(2,1)} %collective-permute-done.35), channel_id=1, source_target_pairs={{0,1},{1,0},{2,3},{3,2},{4,5},{5,4},{6,7},{7,6},{8,9},{9,8},{10,11... | collective-permute-start | bytes 1572872 | tf_op jit(solution)/shard_map/ppermute | solution.py:446
  227.3 30.7 %collective-permute-start.33 = (bf16[256,1024]{1,0:T(8,128)(2,1)S(1)}, bf16[256,1024]{1,0:T(8,128)(2,1)S(1)}, u32[]{:S(2)}, u32[]{:S(2)}) collective-permute-start(bf16[256,1024]{1,0:T(8,128)(2,1)S(1)} %get-tuple-element.116.refs_0_), channel_id=1, source_target_pairs={{0,1},{1,0},{2,3},{3,2},{4,5},{5,4},{6,7},{7,6},{8,9},{9,8},{10,11... | collective-permute-start | bytes 1572872 | tf_op jit(solution)/shard_map/ppermute | solution.py:446
  229.9 26.2 %collective-permute-start.44 = (bf16[256,1024]{1,0:T(8,128)(2,1)}, bf16[256,1024]{1,0:T(8,128)(2,1)}, u32[]{:S(2)}, u32[]{:S(2)}) collective-permute-start(bf16[256,1024]{1,0:T(8,128)(2,1)} %convert_element_type.307), channel_id=1, source_target_pairs={{0,2},{1,3},{2,0},{3,1},{4,6},{5,7},{6,4},{7,5},{8,10},{9,11},{10,... | collective-permute-start | bytes 1572872 | tf_op jit(solution)/shard_map/ppermute | solution.py:446
  233.4 24.6 %collective-permute-start.34 = (bf16[256,1024]{1,0:T(8,128)(2,1)S(1)}, bf16[256,1024]{1,0:T(8,128)(2,1)S(1)}, u32[]{:S(2)}, u32[]{:S(2)}) collective-permute-start(bf16[256,1024]{1,0:T(8,128)(2,1)S(1)} %collective-permute-done.32.refs_1_), channel_id=1, source_target_pairs={{0,1},{1,0},{2,3},{3,2},{4,5},{5,4},{6,7},{7,6},{8,9},{9,8},{10,11... | collective-permute-start | bytes 1572872 | tf_op jit(solution)/shard_map/ppermute | solution.py:446
  242.3 46.2 %collective-permute-start.45 = (bf16[256,1024]{1,0:T(8,128)(2,1)}, bf16[256,1024]{1,0:T(8,128)(2,1)}, u32[]{:S(2)}, u32[]{:S(2)}) collective-permute-start(bf16[256,1024]{1,0:T(8,128)(2,1)} %convert_element_type.307), channel_id=1, source_target_pairs={{0,1},{1,0},{2,3},{3,2},{4,5},{5,4},{6,7},{7,6},{8,9},{9,8},{10,11... | collective-permute-start | bytes 1572872 | tf_op jit(solution)/shard_map/ppermute | solution.py:446
  256.0 32.9 %collective-permute-start.46 = (bf16[256,1024]{1,0:T(8,128)(2,1)}, bf16[256,1024]{1,0:T(8,128)(2,1)}, u32[]{:S(2)}, u32[]{:S(2)}) collective-permute-start(bf16[256,1024]{1,0:T(8,128)(2,1)} %collective-permute-done.44), channel_id=1, source_target_pairs={{0,1},{1,0},{2,3},{3,2},{4,5},{5,4},{6,7},{7,6},{8,9},{9,8},{10,11... | collective-permute-start | bytes 1572872 | tf_op jit(solution)/shard_map/ppermute | solution.py:446
  275.0 65.7 %collective-permute-start.52 = (bf16[512,1024]{1,0:T(8,128)(2,1)S(1)}, bf16[512,1024]{1,0:T(8,128)(2,1)S(1)}, u32[]{:S(2)}, u32[]{:S(2)}) collective-permute-start(bf16[512,1024]{1,0:T(8,128)(2,1)S(1)} %constant_dynamic-slice_fusion.9), channel_id=1, source_target_pairs={{0,4},{4,0},{8,12},{12,8},{16,20},{20,16},{24,28},{28,24},{1,5},{5... | collective-permute-start | bytes 3145736 | tf_op jit(solution)/shard_map/ppermute | solution.py:467
  284.5 37.8 %collective-permute-start.50 = (bf16[512,1024]{1,0:T(8,128)(2,1)S(1)}, bf16[512,1024]{1,0:T(8,128)(2,1)S(1)}, u32[]{:S(2)}, u32[]{:S(2)}) collective-permute-start(bf16[512,1024]{1,0:T(8,128)(2,1)S(1)} %constant_dynamic-slice_fusion.11), channel_id=1, source_target_pairs={{0,4},{4,0},{8,12},{12,8},{16,20},{20,16},{24,28},{28,24},{1,5},{5... | collective-permute-start | bytes 3145736 | tf_op jit(solution)/shard_map/ppermute | solution.py:467
  286.4 39.0 %collective-permute-start.38 = (bf16[512,1024]{1,0:T(8,128)(2,1)S(1)}, bf16[512,1024]{1,0:T(8,128)(2,1)S(1)}, u32[]{:S(2)}, u32[]{:S(2)}) collective-permute-start(bf16[512,1024]{1,0:T(8,128)(2,1)S(1)} %convolution_convert_fusion.6), channel_id=1, source_target_pairs={{0,1},{1,0},{2,3},{3,2},{4,5},{5,4},{6,7},{7,6},{8,9},{9,8},{10,11... | collective-permute-start | bytes 3145736 | tf_op jit(solution)/shard_map/ppermute | solution.py:446
  288.6 34.2 %collective-permute-start.43 = (bf16[256,1024]{1,0:T(8,128)(2,1)S(1)}, bf16[256,1024]{1,0:T(8,128)(2,1)S(1)}, u32[]{:S(2)}, u32[]{:S(2)}) collective-permute-start(bf16[256,1024]{1,0:T(8,128)(2,1)S(1)} %slice.381), channel_id=1, source_target_pairs={{0,2},{1,3},{2,0},{3,1},{4,6},{5,7},{6,4},{7,5},{8,10},{9,11},{10,... | collective-permute-start | bytes 1572872 | tf_op jit(solution)/shard_map/ppermute | solution.py:446
  329.1 127.2 %collective-permute-start.39 = (bf16[256,1024]{1,0:T(8,128)(2,1)}, bf16[256,1024]{1,0:T(8,128)(2,1)}, u32[]{:S(2)}, u32[]{:S(2)}) collective-permute-start(bf16[256,1024]{1,0:T(8,128)(2,1)} %slice.383), channel_id=1, source_target_pairs={{0,2},{1,3},{2,0},{3,1},{4,6},{5,7},{6,4},{7,5},{8,10},{9,11},{10,... | collective-permute-start | bytes 1572872 | tf_op jit(solution)/shard_map/ppermute | solution.py:446
  372.6 48.0 %collective-permute-start.53 = (bf16[1024,1024]{1,0:T(8,128)(2,1)S(1)}, bf16[1024,1024]{1,0:T(8,128)(2,1)S(1)}, u32[]{:S(2)}, u32[]{:S(2)}) collective-permute-start(bf16[1024,1024]{1,0:T(8,128)(2,1)S(1)} %convolution_convert_fusion.2), channel_id=1, source_target_pairs={{0,1},{1,0},{2,3},{3,2},{4,5},{5,4},{6,7},{7,6},{8,9},{9,8},{10,11... | collective-permute-start | bytes 6291464 | tf_op jit(solution)/shard_map/ppermute | solution.py:446
  377.1 23.7 %collective-permute-start.55 = (bf16[512,768]{1,0:T(8,128)(2,1)S(1)}, bf16[512,768]{1,0:T(8,128)(2,1)S(1)}, u32[]{:S(2)}, u32[]{:S(2)}) collective-permute-start(bf16[512,768]{1,0:T(8,128)(2,1)S(1)} %constant_dynamic-slice_fusion.8), channel_id=1, source_target_pairs={{0,4},{4,0},{8,12},{12,8},{16,20},{20,16},{24,28},{28,24},{1,5},{5... | collective-permute-start | bytes 2359304 | tf_op jit(solution)/shard_map/ppermute | solution.py:467
  384.2 26.3 %collective-permute-start.61 = (bf16[256,1024]{1,0:T(8,128)(2,1)S(1)}, bf16[256,1024]{1,0:T(8,128)(2,1)S(1)}, u32[]{:S(2)}, u32[]{:S(2)}) collective-permute-start(bf16[256,1024]{1,0:T(8,128)(2,1)S(1)} %constant_dynamic-slice_fusion.2), channel_id=1, source_target_pairs={{0,8},{4,12},{8,0},{12,4},{16,24},{20,28},{24,16},{28,20},{1,9},{5... | collective-permute-start | bytes 1572872 | tf_op jit(solution)/shard_map/ppermute | solution.py:467
  388.2 53.2 %collective-permute-start.63 = (bf16[128,1024]{1,0:T(8,128)(2,1)S(1)}, bf16[128,1024]{1,0:T(8,128)(2,1)S(1)}, u32[]{:S(2)}, u32[]{:S(2)}) collective-permute-start(bf16[128,1024]{1,0:T(8,128)(2,1)S(1)} %constant_dynamic-slice_fusion), channel_id=1, source_target_pairs={{0,16},{4,20},{8,24},{12,28},{16,0},{20,4},{24,8},{28,12},{1,17},{... | collective-permute-start | bytes 786440 | tf_op jit(solution)/shard_map/ppermute | solution.py:467
  423.8 26.3 %collective-permute-start.54 = (bf16[512,1024]{1,0:T(8,128)(2,1)}, bf16[512,1024]{1,0:T(8,128)(2,1)}, u32[]{:S(2)}, u32[]{:S(2)}) collective-permute-start(bf16[512,1024]{1,0:T(8,128)(2,1)} %slice.380), channel_id=1, source_target_pairs={{0,2},{1,3},{2,0},{3,1},{4,6},{5,7},{6,4},{7,5},{8,10},{9,11},{10,... | collective-permute-start | bytes 3145736 | tf_op jit(solution)/shard_map/ppermute | solution.py:446
  442.2 72.9 %all-to-all-start.1 = ((bf16[8,128,1024]{2,1,0:T(8,128)(2,1)}), bf16[8,128,1024]{2,1,0:T(8,128)(2,1)S(1)}, u32[]{:S(2)}, u32[]{:S(2)}) async-start(bf16[8,128,1024]{2,1,0:T(8,128)(2,1)} %fusion.25), calls=%async_computation.1 | async-start | bytes 4194304 | tf_op jit(solution)/shard_map/all_to_all | solution.py:699
  454.2 42.5 %collective-permute-start.64 = (f32[6144]{0:T(1024)S(1)}, f32[6144]{0:T(1024)S(1)}, u32[]{:S(2)}, u32[]{:S(2)}) collective-permute-start(f32[6144]{0:T(1024)S(1)} %slice_select_fusion), channel_id=1, source_target_pairs={{0,16},{4,20},{8,24},{12,28},{16,0},{20,4},{24,8},{28,12},{1,17},{... | collective-permute-start | bytes 73736 | tf_op jit(solution)/shard_map/ppermute | solution.py:545
  (112 other events, 1338.1 us)

commit v3 on v2

--- a/solution.py
+++ b/solution.py
@@ -100,9 +100,8 @@
             lse_ref[place[half], 0, rows, :] = lse
 
 
-def attend(core, qkv, chunk, chunks):
-    _, seqs, rows, triple = qkv.shape
-    width = triple // 3
+def attend(core, qk, v, chunk, chunks):
+    _, seqs, rows, width = v.shape
     part = rows // chunks
     per = part // TILE
     subs = tuple(range(chunk * per, (chunk + 1) * per))
@@ -114,7 +113,7 @@
             in_specs=[
                 pl.BlockSpec((2, 1, part, width), lambda s, c: (0, s, chunk, 0)),
                 pl.BlockSpec((2, 1, rows, width), lambda s, c: (0, s, 0, 1)),
-                pl.BlockSpec((2, 1, rows, width), lambda s, c: (0, s, 0, 2)),
+                pl.BlockSpec((2, 1, rows, width), lambda s, c: (0, s, 0, 0)),
             ],
             out_specs=[
                 pl.BlockSpec((2, 1, part, width), lambda s, c: (0, s, 0, 0)),
@@ -129,7 +128,7 @@
         cost_estimate=pl.CostEstimate(
             flops=10 * 10**9 // chunks, bytes_accessed=6 * 10**6, transcendentals=0
         ),
-    )(core, qkv, qkv, qkv)
+    )(core, qk, qk, v)
 
 
 def attend_back_kernel(
@@ -138,7 +137,7 @@
     o_refs = refs[0:chunks]
     lse_refs = refs[chunks : 2 * chunks]
     do_refs = refs[2 * chunks : 3 * chunks]
-    out_ref, dk_acc, dv_acc = refs[3 * chunks :]
+    out_ref, v_out_ref, dk_acc, dv_acc = refs[3 * chunks :]
     core = core_ref[0]
     place = (core, 1 - core)
     width = q_ref.shape[-1]
@@ -191,12 +190,11 @@
     for j in range(2 * per_half):
         rows = slice((j % per_half) * TILE, (j % per_half + 1) * TILE)
         out_ref[place[j // per_half], 0, rows, width : 2 * width] = dk_acc[j].astype(BF16)
-        out_ref[place[j // per_half], 0, rows, 2 * width :] = dv_acc[j].astype(BF16)
-
-
-def attend_back(core, qkv, outs, lses, back):
-    _, seqs, rows, triple = qkv.shape
-    width = triple // 3
+        v_out_ref[place[j // per_half], 0, rows, :] = dv_acc[j].astype(BF16)
+
+
+def attend_back(core, qk, v, outs, lses, back):
+    _, seqs, rows, width = v.shape
     chunks = len(outs)
     part = rows // chunks
 
@@ -208,19 +206,19 @@
         grid_spec=pltpu.PrefetchScalarGridSpec(
             num_scalar_prefetch=1,
             grid=(seqs,),
-            in_specs=[block(rows, width, 0), block(rows, width, 1), block(rows, width, 2)]
+            in_specs=[block(rows, width, 0), block(rows, width, 1), block(rows, width, 0)]
             + [block(part, width, 0)] * chunks
             + [block(part, 128, 0)] * chunks
             + [block(part, width, 0)] * chunks,
-            out_specs=block(rows, triple, 0),
+            out_specs=[block(rows, 2 * width, 0), block(rows, width, 0)],
             scratch_shapes=[pltpu.VMEM((2 * rows // TILE, TILE, width), F32)] * 2,
         ),
-        out_shape=jax.ShapeDtypeStruct(qkv.shape, BF16),
+        out_shape=[jax.ShapeDtypeStruct(qk.shape, BF16), jax.ShapeDtypeStruct(v.shape, BF16)],
         compiler_params=pltpu.CompilerParams(vmem_limit_bytes=VMEM_GRANT),
         cost_estimate=pl.CostEstimate(
             flops=25 * 10**9, bytes_accessed=12 * 10**6, transcendentals=0
         ),
-    )(core, qkv, qkv, qkv, *outs, *lses, *back)
+    )(core, qk, qk, v, *outs, *lses, *back)
 
 
 def hidden_kernel(*refs):
@@ -280,14 +278,32 @@
     )(*blocks, weight, bias.reshape(1, -1), dact)
 
 
-def reversed_bits(index, count):
-    out = 0
-    bit = 1
-    while bit < count:
-        out = 2 * out + (index & 1)
-        index //= 2
-        bit *= 2
-    return out
+def mixed_kernel(*refs):
+    blocks = refs[0:4]
+    w_ref, out_ref, all_ref = refs[4:]
+    rows = blocks[0].shape[0]
+    for at in range(4):
+        value = blocks[at][...]
+        out_ref[at * rows : (at + 1) * rows, :] = mm(value, w_ref[...], NT).astype(BF16)
+        all_ref[at * rows : (at + 1) * rows, :] = value
+
+
+def back_mix(blocks, weight):
+    rows, width = blocks[0].shape
+    cols = weight.shape[0]
+    return pl.pallas_call(
+        mixed_kernel,
+        in_specs=[pl.BlockSpec(memory_space=pltpu.VMEM)] * 5,
+        out_specs=[pl.BlockSpec(memory_space=pltpu.VMEM)] * 2,
+        out_shape=[
+            jax.ShapeDtypeStruct((4 * rows, cols), BF16),
+            jax.ShapeDtypeStruct((4 * rows, width), BF16),
+        ],
+        compiler_params=pltpu.CompilerParams(vmem_limit_bytes=VMEM_GRANT),
+        cost_estimate=pl.CostEstimate(
+            flops=8 * rows * width * cols, bytes_accessed=5 * 10**6, transcendentals=0
+        ),
+    )(*blocks, weight)
 
 
 def muon_kernel(
@@ -326,15 +342,13 @@
     def _():
         grad_buf[...] = jnp.zeros_like(grad_buf)
         for src in range(count):
-            at = reversed_bits(src, count)
             piece = landed_ref[src].astype(F32)
-            grad_buf[at * out_rows : (at + 1) * out_rows, :] = piece[:out_rows]
+            grad_buf[src * out_rows : (src + 1) * out_rows, :] = piece[:out_rows]
 
     @pl.when(jnp.logical_not(is_out))
     def _():
         for src in range(count):
-            at = reversed_bits(src, count)
-            grad_buf[at * share : (at + 1) * share, :] = landed_ref[src].astype(F32)
+            grad_buf[src * share : (src + 1) * share, :] = landed_ref[src].astype(F32)
 
     store_grad.start()
     load_mom.wait()
@@ -452,14 +466,19 @@
     return value, far_block, core_block, swap(far_block, 1)
 
 
-def scatter_sum(value, weight, dims):
-    size = value.shape[0] // 4
-    send = mm(value[2 * size :], weight, dims).astype(BF16)
-    arrived = swap(send, 1)
-    keep = mm(value[: 2 * size], weight, dims)
-    part = keep + arrived.astype(F32)
-    far = swap(part[size:].astype(BF16), 2)
-    return part[:size] + far.astype(F32)
+def scatter_begin(values, weights, dims):
+    size = values[0].shape[0] // 4
+
+    def product(first, last):
+        return sum(mm(v[first * size : last * size], w, dims) for v, w in zip(values, weights))
+
+    arrived = swap(product(2, 4).astype(BF16), 1)
+    return product(0, 2) + arrived.astype(F32)
+
+
+def scatter_end(part):
+    size = part.shape[0] // 2
+    return part[:size] + swap(part[size:].astype(BF16), 2).astype(F32)
 
 
 def data_swap(value, bit):
@@ -471,38 +490,50 @@
     return lax.optimization_barrier((value, *others))[0]
 
 
-def gather_kinds(pieces):
-    index = lax.axis_index("dp")
-    before = []
-    results = []
-    for piece in pieces:
-        done = []
-        for at, bit in enumerate(reversed(axis_bits("dp"))):
-            if before:
-                piece = after(piece, before[at])
-            other = data_swap(piece, bit)
-            upper = (index & bit) != 0
-            piece = jnp.where(
-                upper,
-                jnp.concatenate([other, piece], axis=0),
-                jnp.concatenate([piece, other], axis=0),
-            )
-            done.append(other)
-        before = done
-        results.append(piece)
-    return results
+def last_bits(*bits):
+    return [bit for bit in reversed(axis_bits("dp")) if bit not in bits] + list(bits)
+
+
+def bit_axis(bit):
+    return len(axis_bits("dp")) - bit.bit_length()
+
+
+def spread(value):
+    return value.reshape((2,) * len(axis_bits("dp")) + (-1, value.shape[-1]))
+
+
+def double(piece, bit):
+    upper = (lax.axis_index("dp") & bit) != 0
+    other = data_swap(piece, bit)
+    axis = bit_axis(bit)
+    return jnp.where(
+        upper,
+        jnp.concatenate([other, piece], axis=axis),
+        jnp.concatenate([piece, other], axis=axis),
+    )
+
+
+def open_piece(value):
+    return value.reshape((1,) * len(axis_bits("dp")) + value.shape)
+
+
+def gather_by(value, bits):
+    piece = open_piece(value)
+    for bit in bits:
+        piece = double(piece, bit)
+    return rows2(piece)
 
 
 def halve(value, bit):
-    half = value.shape[0] // 2
     upper = ((lax.axis_index("dp") & bit) != 0).astype(jnp.int32)
-    give = lax.dynamic_slice_in_dim(value, (1 - upper) * half, half, 0)
-    keep = lax.dynamic_slice_in_dim(value, upper * half, half, 0)
+    axis = bit_axis(bit)
+    give = lax.dynamic_slice_in_dim(value, 1 - upper, 1, axis)
+    keep = lax.dynamic_slice_in_dim(value, upper, 1, axis)
     return (keep.astype(F32) + data_swap(give, bit).astype(F32)).astype(BF16)
 
 
-def halve_rest(value, done=1):
-    for bit in axis_bits("dp")[done:]:
+def halve_by(value, bits):
+    for bit in bits:
         value = halve(value, bit)
     return value
 
@@ -519,7 +550,7 @@
 
 def small_gather(value):
     piece = value.reshape(1, -1)
-    for name in ("tensor", "dp"):
+    for name, axis in (("dp", 0), ("tensor", 1)):
         index = lax.axis_index(name)
         count = lax.axis_size(name)
         for bit in axis_bits(name):
@@ -527,23 +558,24 @@
             upper = (index & bit) != 0
             piece = jnp.where(
                 upper,
-                jnp.concatenate([other, piece], axis=0),
-                jnp.concatenate([piece, other], axis=0),
+                jnp.concatenate([other, piece], axis=axis),
+                jnp.concatenate([piece, other], axis=axis),
             )
     return piece.reshape(-1)
 
 
 def small_scatter(value):
-    for name in ("dp", "tensor"):
+    value = value.reshape(lax.axis_size("dp"), -1)
+    for name, axis in (("tensor", 1), ("dp", 0)):
         index = lax.axis_index(name)
         count = lax.axis_size(name)
         for bit in reversed(axis_bits(name)):
-            low, high = jnp.split(value, 2)
+            low, high = jnp.split(value, 2, axis=axis)
             upper = (index & bit) != 0
             give = jnp.where(upper, low, high)
             keep = jnp.where(upper, high, low)
             value = keep + lax.ppermute(give, name, [(i, i ^ bit) for i in range(count)])
-    return value
+    return value.reshape(-1)
 
 
 def norm_parts(values):
@@ -579,21 +611,25 @@
     owned = owner_row == data_idx
     slot_value = master_slots[0]
 
-    order = [reversed_bits(i, data_count) for i in range(data_count)]
     slot_low = slot_value.astype(BF16)
     offer_out = jnp.pad(
         slot_low[:head_width].reshape(data_count, share_out, width),
         ((0, 0), (0, share - share_out), (0, 0)),
     )
     offer = jnp.where(owned[1], offer_out, slot_low.reshape(data_count, share, width))
-    shares = lax.all_to_all(jnp.concatenate([offer[i : i + 1] for i in order]), "dp", 0, 0)
+    shares = lax.all_to_all(offer, "dp", 0, 0)
 
     def share_of(kind):
         return lax.dynamic_index_in_dim(shares, owner_row[kind], 0, keepdims=False)
 
-    w_qkv, w_out, w_proj, w_fc = gather_kinds(
-        (share_of(0)[:, : 3 * head_width], share_of(1)[:share_out], share_of(3), share_of(2))
-    )
+    first = share_of(0)
+    w_qk = gather_by(first[:, : 2 * head_width], last_bits(2, 1))
+    w_v = gather_by(first[:, 2 * head_width : 3 * head_width], last_bits(2, 1)[::-1])
+    w_out = gather_by(share_of(1)[:share_out], last_bits(1, 2))
+    bits_proj = last_bits(1, 2)
+    bits_fc = [2] + last_bits(2, 1)[:-2] + [1]
+    w_proj = double(open_piece(after(share_of(3), w_v)), bits_proj[0])
+    w_fc = double(open_piece(after(share_of(2), w_v)), bits_fc[0])
 
     params = small_gather(small_master)
 
@@ -617,82 +653,112 @@
     unit_all, _ = norm_parts(jnp.concatenate(gather_four(inputs)).astype(F32))
     normed_all = (unit_all * gain_one + shift_one).astype(BF16)
     dy_all = [jnp.concatenate(gather_four(out_grad[rows])) for rows in rows_of]
-    bias_qkv = jnp.concatenate([bias_query, jnp.zeros_like(bias_query), bias_value])
-    scale_qkv = jnp.where(jnp.arange(3 * head_width) < head_width, HEAD_DIM**-0.5, 1.0)
-    qkv = ((mm(normed_all, w_qkv) + bias_qkv) * scale_qkv).astype(BF16)
-    qkv = qkv.reshape(2, 2, rows_dev, 3 * head_width)
-    back_act = [mm(dy, w_proj, NT).astype(BF16) for dy in dy_all]
-
-    mixed, log_sums = [], []
+    bias_qk = jnp.concatenate([bias_query, jnp.zeros_like(bias_query)])
+    scale_qk = jnp.where(jnp.arange(2 * head_width) < head_width, HEAD_DIM**-0.5, 1.0)
+    qk = ((mm(normed_all, w_qk) + bias_qk) * scale_qk).astype(BF16)
+    values = (mm(normed_all, w_v) + bias_value).astype(BF16)
+    qk = qk.reshape(2, 2, rows_dev, 2 * head_width)
+    values = values.reshape(2, 2, rows_dev, head_width)
+
+    w_proj, w_fc = after((w_proj, w_fc), qk, values)
+    for bit in bits_proj[1:-1]:
+        w_proj = double(w_proj, bit)
+    for bit in bits_fc[1:-1]:
+        w_fc = double(w_fc, bit)
+
+    mixed, log_sums, parts = [], [], []
     for chunk in range(CHUNKS):
-        mixed_one, sums_one = attend(core, qkv, chunk, CHUNKS)
+        mixed_one, sums_one = attend(core, qk, values, chunk, CHUNKS)
         mixed.append(mixed_one)
         log_sums.append(sums_one)
-    middles, branches, grad_proj, grad_fc, fc_bias_grad = [], [], 0.0, 0.0, 0.0
-    back_normed_two, mine_two = [], []
-    normed_two = None
+        parts.append(scatter_begin([rows2(mixed_one)], [w_out], NN))
+    w_proj = rows2(double(after(w_proj, mixed[-1]), bits_proj[-1]))
+    w_fc = rows2(double(after(w_fc, parts[-1]), bits_fc[-1]))
+    back_act = [mm(after(dy, parts[-1]), w_proj, NT).astype(BF16) for dy in dy_all]
+    middles, mine_two, normed_two = [], [], []
     for chunk in range(CHUNKS):
-        branch = scatter_sum(rows2(mixed[chunk]), w_out, NN)
+        branch = scatter_end(parts[chunk])
         if chunk > 0:
-            branch = after(branch, normed_two)
+            branch = after(branch, normed_two[-1])
         middle = rows_in[rows_of[chunk]] + branch + bias_out
         unit_two, scale_two = norm_parts(middle)
-        normed_two = (unit_two * gain_two + shift_two).astype(BF16)
-        acts, backs, sums, normed_two_all = hidden_layer(
-            gather_four(normed_two), w_fc, bias_fc, back_act[chunk]
-        )
-        fc_bias_grad = fc_bias_grad + sums[0]
-        back_normed_two.append(scatter_sum(backs, w_fc, NT))
-        branches.append(scatter_sum(acts, w_proj, NN))
-        grad_proj = grad_proj + mm(acts, dy_all[chunk], TN)
-        grad_fc = grad_fc + mm(normed_two_all, backs, TN)
+        normed_two.append((unit_two * gain_two + shift_two).astype(BF16))
         middles.append(middle)
         mine_two.append((unit_two, scale_two))
-    middle = jnp.concatenate(middles)
-    block_out = (middle + jnp.concatenate(branches) + bias_proj).astype(BF16)
-    half_proj = halve(halve(grad_proj.astype(BF16), 1), 2)
-    half_fc = halve(grad_fc.astype(BF16), 1)
-
-    back_middles, back_mixed = [], []
+
+    blocks = [gather_four(value) for value in normed_two]
+    acts, backs, wholes, parts = [], [], [], []
+    fc_bias_grad = 0.0
+    for chunk in range(CHUNKS):
+        earlier = parts[-1] if chunk > 0 else normed_two[-1]
+        block = after(blocks[chunk], earlier)
+        act, back, sums, whole = hidden_layer(block, w_fc, bias_fc, back_act[chunk])
+        parts.append(scatter_begin([back], [w_fc], NT))
+        acts.append(act)
+        backs.append(back)
+        wholes.append(whole)
+        fc_bias_grad = fc_bias_grad + sums[0]
+    acts, backs = after((acts, backs), parts[-1])
+    grad_proj = sum(mm(acts[i], dy_all[i], TN) for i in range(CHUNKS)).astype(BF16)
+    grad_fc = sum(mm(wholes[i], backs[i], TN) for i in range(CHUNKS)).astype(BF16)
+    half_proj = halve(spread(grad_proj), 1)
+    half_fc = halve(spread(grad_fc), 2)
+
+    back_middles, back_lows = [], []
     gain_two_grad, shift_two_grad, grad_out = 0.0, 0.0, 0.0
-    back_low = None
     for chunk in range(CHUNKS):
         unit_two, scale_two = mine_two[chunk]
-        grad = back_normed_two[chunk]
+        grad = scatter_end(parts[chunk])
         if chunk > 0:
-            grad = after(grad, back_low)
+            grad = after(grad, back_lows[-1])
         back_middle = out_grad[rows_of[chunk]].astype(F32) + norm_back(
             unit_two, scale_two, gain_two, grad
         )
-        back_low = back_middle.astype(BF16)
-        mid = jnp.concatenate(gather_four(back_low))
-        back_mixed.append(mm(mid, w_out, NT).astype(BF16).reshape(2, 2, part, head_width))
-        grad_out = grad_out + mm(rows2(mixed[chunk]), mid, TN)
+        back_lows.append(back_middle.astype(BF16))
         gain_two_grad = gain_two_grad + jnp.sum(grad * unit_two, axis=0)
         shift_two_grad = shift_two_grad + jnp.sum(grad, axis=0)
         back_middles.append(back_middle)
+    middle = jnp.concatenate(middles)
     back_middle = jnp.concatenate(back_middles)
     proj_bias_grad = jnp.sum(out_grad, axis=0, dtype=F32)
     out_bias_grad = jnp.sum(back_middle, axis=0)
+
+    back_mixed = []
+    for chunk in range(CHUNKS):
+        block = after(gather_four(back_lows[chunk]), parts[-1])
+        mixed_grad, mid = back_mix(block, w_out)
+        back_mixed.append(mixed_grad.reshape(2, 2, part, head_width))
+        grad_out = grad_out + mm(rows2(mixed[chunk]), mid, TN)
+    share_out_grad = halve_by(spread(grad_out.astype(BF16)), last_bits(1, 2)[::-1])
     back_mixed, half_proj, half_fc = lax.optimization_barrier((back_mixed, half_proj, half_fc))
-    share_proj = halve_rest(half_proj, 2)
-    share_fc = halve_rest(half_fc)
-    back_qkv = attend_back(core, qkv, mixed, log_sums, back_mixed)
-    grad_qkv = mm(normed_all, rows2(back_qkv), TN).astype(BF16)
-    qkv_bias_grad = jnp.sum(back_qkv, axis=(0, 1, 2), dtype=F32)
-    share_out_grad = halve_rest(halve(grad_out.astype(BF16), 1))
-    share_qkv = halve_rest(halve(grad_qkv, 1))
-    back_normed = scatter_sum(rows2(after(back_qkv, grad_qkv)), w_qkv, NT)
+    back_qk, back_v = attend_back(core, qk, values, mixed, log_sums, back_mixed)
+    share_proj = halve_by(half_proj, axis_bits("dp")[1:])
+    share_fc = halve_by(half_fc, [1] + axis_bits("dp")[2:])
+    grad_qk = mm(normed_all, rows2(back_qk), TN).astype(BF16)
+    grad_v = mm(normed_all, rows2(back_v), TN).astype(BF16)
+    half_qk = halve(spread(grad_qk), 1)
+    share_qk = halve_by(half_qk, axis_bits("dp")[1:])
+    share_v = halve_by(spread(grad_v), axis_bits("dp")[::-1])
+    query_bias_grad = jnp.sum(back_qk[..., :head_width], axis=(0, 1, 2), dtype=F32)
+    value_bias_grad = jnp.sum(back_v, axis=(0, 1, 2), dtype=F32)
+
+    acts = after(acts, back_lows[-1])
+    branches = [scatter_end(scatter_begin([act], [w_proj], NN)) for act in acts]
+    block_out = (middle + jnp.concatenate(branches) + bias_proj).astype(BF16)
+    back_qk, back_v = after((back_qk, back_v), half_qk, grad_v)
+    back_normed = scatter_end(scatter_begin([rows2(back_qk), rows2(back_v)], [w_qk, w_v], NT))
     input_grad = back_middle + norm_back(unit_one, scale_one, gain_one, back_normed)
     gain_one_grad = jnp.sum(back_normed * unit_one, axis=0)
     shift_one_grad = jnp.sum(back_normed, axis=0)
 
     bundle = jnp.zeros((data_count, share, width), BF16)
     pieces = (
-        jnp.pad(share_qkv, ((0, 0), (0, width - 3 * head_width))),
-        jnp.pad(share_out_grad, ((0, share - share_out), (0, 0))),
-        share_fc,
-        share_proj,
+        jnp.concatenate(
+            [rows2(share_qk), rows2(share_v), jnp.zeros((share, width - 3 * head_width), BF16)], axis=1
+        ),
+        jnp.pad(rows2(share_out_grad), ((0, share - share_out), (0, 0))),
+        rows2(share_fc),
+        rows2(share_proj),
     )
     for kind in range(4):
         bundle = lax.dynamic_update_index_in_dim(bundle, pieces[kind], owner_row[kind], 0)
@@ -710,8 +776,8 @@
         ]
     )
     for grad, start, size in (
-        (qkv_bias_grad[:head_width], 2 * width, head_width),
-        (qkv_bias_grad[2 * head_width :], 3 * width, head_width),
+        (query_bias_grad, 2 * width, head_width),
+        (value_bias_grad, 3 * width, head_width),
         (fc_bias_grad, 7 * width, ff_width),
     ):
         full_grad = lax.dynamic_update_slice_in_dim(full_grad, grad, start + tensor_idx * size, 0)

time: 575 us -> 567 us (0.986)
  the two profiles are of different devices: /device:TPU:13 before, /device:TPU:2 now
where the time goes in v3:
time: 567 us; the launch traced here: 556 us
  waiting for transfers between devices  219 us (39%)
  Pallas kernels  112 us (20%)
  starting transfers between devices  65.8 us (12%)
  other arithmetic  60.2 us (11%)
  matrix products  59.5 us (10%)
  local copies, waits for them, and re-layouts  25.7 us (5%)
  between operations  12.7 us (2%)
    ppermute x30, waiting for transfers between devices, data_swap(): return lax.ppermute(value, 'dp', [(i, i ^ bit) for i in range(count)])  123 us
    dot_general x28, matrix products, mm(): return lax.dot_general(left, right, dims, preferred_element_type=F32)  59.5 us
    pallas_call x1, Pallas kernels, muon_update(): pl.pallas_call(partial(muon_kernel, out_rows=out_rows), in_specs=[pl.Bloc...  49 us
    ppermute x5, waiting for transfers between devices, small_gather(): other = lax.ppermute(piece, name, [(i, i ^ bit) for i in range(count)])  41.2 us
    ppermute x5, waiting for transfers between devices, small_scatter(): lax.ppermute(give, name, [(i, i ^ bit) for i in range(count)])  29.2 us
    ppermute x30, starting transfers between devices, data_swap(): return lax.ppermute(value, 'dp', [(i, i ^ bit) for i in range(count)])  29 us
    ppermute x35, waiting for transfers between devices, swap(): return lax.ppermute(value, 'tensor', [(i, i ^ bit) for i in range(count)])  25.8 us
    pallas_call x2, Pallas kernels, attend(): pl.pallas_call(partial(attend_kernel, subs=subs, heads=width // HEAD_DIM)...  24.4 us
  transfers between devices with their start and end apart: 77, of which 30 were waited for; matrix products, arithmetic and copies ran while one was open for 25% of the time, Pallas kernels for 11%

profile of v3, /device:TPU:2, one launch (start us, length us, event | category | flops | bytes accessed | tf_op | source)
XLA Modules:
  0.0 555.8 jit_solution(3970801247597651228)
XLA Ops:
  13.5 5.0 all-to-all-start
  23.1 31.1 %collective-permute-done.4 = f32[2,384]{1,0:T(2,128)S(1)} collective-permute-done((f32[2,384]{1,0:T(2,128)S(1)}, f32[2,384]{1,0:T(2,128)S(1)}, u32[]{:S(2)}, u32[]{:S(2)}) %collective-permute-start.4) | collective-permute-done | bytes 3104 | tf_op jit(solution)/shard_map/ppermute | solution.py:557
  57.8 9.6 %collective-permute-done.5 = f32[4,384]{1,0:T(4,128)S(1)} collective-permute-done((f32[4,384]{1,0:T(4,128)S(1)}, f32[4,384]{1,0:T(4,128)S(1)}, u32[]{:S(2)}, u32[]{:S(2)}) %collective-permute-start.5) | collective-permute-done | bytes 6176 | tf_op jit(solution)/shard_map/ppermute | solution.py:557
  85.2 5.0 fusion.5
  96.9 6.5 %collective-permute-done.14 = bf16[1,1,1,32,1024]{4,3,0,2,1:T(8,128)(2,1)S(1)} collective-permute-done((bf16[1,1,1,32,1024]{4,3,0,2,1:T(8,128)(2,1)S(1)}, bf16[1,1,1,32,1024]{4,3,0,2,1:T(8,128)(2,1)S(1)}, u32[]{:S(2)}, u32[]{:S(2)}) %collective-permute-start.14) | collective-permute-done | bytes 65568 | tf_op jit(solution)/shard_map/ppermute | solution.py:486
  109.6 9.9 %collective-permute-done.9 = bf16[2,1,1,128,512]{4,3,2,1,0:T(8,128)(2,1)S(1)} collective-permute-done((bf16[2,1,1,128,512]{4,3,2,1,0:T(8,128)(2,1)S(1)}, bf16[2,1,1,128,512]{4,3,2,1,0:T(8,128)(2,1)S(1)}, u32[]{:S(2)}, u32[]{:S(2)}) %collective-permute-start.9) | collective-permute-done | bytes 262176 | tf_op jit(solution)/shard_map/ppermute | solution.py:486
  125.9 5.4 collective-permute-done.25
  136.5 19.8 %shard_map.144 = (bf16[2,2,256,256]{3,2,1,0:T(8,128)(2,1)S(1)}, f32[2,2,256,128]{3,2,1,0:T(8,128)S(1)}) custom-call(s32[1]{0:T(128)} %bitcast.core_ref, bf16[2,2,512,512]{3,2,1,0:T(8,128)(2,1)S(1)} %bitcast.152, bf16[2,2,512,512]{3,2,1,0:T(8,128)(2,1)S(1)} %bitcast.153, bf16[2,2,512,256]{3,2,1,0:T(8,128)(2,1)S(1)} %bitcast.158), custom_call_target="tpu_custom_call" | custom-call | flops 5000000000 | bytes 6000000 | tf_op jit(solution)/shard_map/pallas_call | solution.py:108
  157.1 4.5 shard_map.143
  176.7 4.2 collective-permute-done.31
  183.2 14.4 %collective-permute-done.26 = bf16[1,2,1,128,1024]{4,3,2,1,0:T(8,128)(2,1)S(1)} collective-permute-done((bf16[1,2,1,128,1024]{4,3,2,1,0:T(8,128)(2,1)}, bf16[1,2,1,128,1024]{4,3,2,1,0:T(8,128)(2,1)S(1)}, u32[]{:S(2)}, u32[]{:S(2)}) %collective-permute-start.26) | collective-permute-done | bytes 524320 | tf_op jit(solution)/shard_map/ppermute | solution.py:486
  202.6 11.8 %collective-permute-done.20 = bf16[256,1024]{1,0:T(8,128)(2,1)S(1)} collective-permute-done((bf16[256,1024]{1,0:T(8,128)(2,1)S(1)}, bf16[256,1024]{1,0:T(8,128)(2,1)S(1)}, u32[]{:S(2)}, u32[]{:S(2)}) %collective-permute-start.20) | collective-permute-done | bytes 524320 | tf_op jit(solution)/shard_map/ppermute | solution.py:460
  215.5 6.7 %collective-permute-done.32 = bf16[2,1,2,128,1024]{4,3,2,1,0:T(8,128)(2,1)S(1)} collective-permute-done((bf16[2,1,2,128,1024]{4,3,2,1,0:T(8,128)(2,1)S(1)}, bf16[2,1,2,128,1024]{4,3,2,1,0:T(8,128)(2,1)S(1)}, u32[]{:S(2)}, u32[]{:S(2)}) %collective-permute-start.32) | collective-permute-done | bytes 1048608 | tf_op jit(solution)/shard_map/ppermute | solution.py:486
  222.6 3.7 convolution_convert_fusion.1.refs_6_
  229.5 8.8 %shard_map.145 = (bf16[1024,1024]{1,0:T(8,128)(2,1)S(1)}, bf16[1024,1024]{1,0:T(8,128)(2,1)}, f32[1,1024]{1,0:T(1,128)S(1)}, bf16[1024,1024]{1,0:T(8,128)(2,1)}) custom-call(bf16[256,1024]{1,0:T(8,128)(2,1)S(1)} %add_convert_fusion.9.refs_0_, bf16[256,1024]{1,0:T(8,128)(2,1)S(1)} %collective-permute-done.21.refs_1_, ...), custom_call_target="tpu_custom_call" | custom-call | flops 2147483648 | bytes 12000000 | tf_op jit(solution)/shard_map/pallas_call | solution.py:253
  244.8 3.7 convolution_convert_fusion.refs_6_
  252.8 8.9 %shard_map.146 = (bf16[1024,1024]{1,0:T(8,128)(2,1)S(1)}, bf16[1024,1024]{1,0:T(8,128)(2,1)}, f32[1,1024]{1,0:T(1,128)S(1)}, bf16[1024,1024]{1,0:T(8,128)(2,1)}) custom-call(bf16[256,1024]{1,0:T(8,128)(2,1)S(1)} %add_convert_fusion.8.refs_0_, bf16[256,1024]{1,0:T(8,128)(2,1)S(1)} %collective-permute-done.33.refs_1_, ...), custom_call_target="tpu_custom_call" | custom-call | flops 2147483648 | bytes 12000000 | tf_op jit(solution)/shard_map/pallas_call | solution.py:253
  261.7 4.3 convolution_convert_fusion.4
  284.7 3.9 fusion.38
  288.7 4.2 add_convert_fusion.2
  310.0 9.0 %collective-permute-done.53 = bf16[2,2,1,128,1024]{4,3,2,1,0:T(8,128)(2,1)} collective-permute-done((bf16[2,2,1,128,1024]{4,3,2,1,0:T(8,128)(2,1)}, bf16[2,2,1,128,1024]{4,3,2,1,0:T(8,128)(2,1)}, u32[]{:S(2)}, u32[]{:S(2)}) %collective-permute-start.53) | collective-permute-done | bytes 1048608 | tf_op jit(solution)/shard_map/ppermute | solution.py:486
  330.2 19.9 %shard_map.149 = (bf16[2,2,512,512]{3,2,1,0:T(8,128)(2,1)}, bf16[2,2,512,256]{3,2,1,0:T(8,128)(2,1)S(1)}) custom-call(s32[1]{0:T(128)} %bitcast.core_ref, bf16[2,2,512,512]{3,2,1,0:T(8,128)(2,1)} %bitcast.156, bf16[2,2,512,512]{3,2,1,0:T(8,128)(2,1)} %bitcast.157, bf16[2,2,512,256]{3,2,1,0:T(8,128)(2,1)S(1)} %bitcast.160, ...), custom_call_target="tpu_custom_call" | custom-call | flops 24999999488 | bytes 12000000 | tf_op jit(solution)/shard_map/pallas_call | solution.py:204
  358.2 15.9 %collective-permute-done.63 = bf16[2,1,2,32,1024]{4,3,2,1,0:T(8,128)(2,1)S(1)} collective-permute-done((bf16[2,1,2,32,1024]{4,3,2,1,0:T(8,128)(2,1)S(1)}, bf16[2,1,2,32,1024]{4,3,2,1,0:T(8,128)(2,1)S(1)}, u32[]{:S(2)}, u32[]{:S(2)}) %collective-permute-start.63) | collective-permute-done | bytes 262176 | tf_op jit(solution)/shard_map/ppermute | solution.py:486
  375.9 11.7 %collective-permute-done.60 = bf16[1,2,2,128,256]{4,3,2,1,0:T(8,128)(2,1)S(1)} collective-permute-done((bf16[1,2,2,128,256]{4,3,2,1,0:T(8,128)(2,1)S(1)}, bf16[1,2,2,128,256]{4,3,2,1,0:T(8,128)(2,1)S(1)}, u32[]{:S(2)}, u32[]{:S(2)}) %collective-permute-start.60) | collective-permute-done | bytes 262176 | tf_op jit(solution)/shard_map/ppermute | solution.py:486
  393.0 4.9 collective-permute-done.61
  409.5 8.5 %collective-permute-done.66 = bf16[2,1,1,128,1024]{4,3,2,1,0:T(8,128)(2,1)S(1)} collective-permute-done((bf16[2,1,1,128,1024]{4,3,2,1,0:T(8,128)(2,1)S(1)}, bf16[2,1,1,128,1024]{4,3,2,1,0:T(8,128)(2,1)S(1)}, u32[]{:S(2)}, u32[]{:S(2)}) %collective-permute-start.66) | collective-permute-done | bytes 524320 | tf_op jit(solution)/shard_map/ppermute | solution.py:486
  422.0 12.6 %collective-permute-done.58 = bf16[2,1,1,128,512]{4,3,2,1,0:T(8,128)(2,1)S(1)} collective-permute-done((bf16[2,1,1,128,512]{4,3,2,1,0:T(8,128)(2,1)S(1)}, bf16[2,1,1,128,512]{4,3,2,1,0:T(8,128)(2,1)S(1)}, u32[]{:S(2)}, u32[]{:S(2)}) %collective-permute-start.58) | collective-permute-done | bytes 262176 | tf_op jit(solution)/shard_map/ppermute | solution.py:486
  446.1 4.0 all-to-all-start.1
  450.1 10.3 %collective-permute-done.57 = bf16[512,1024]{1,0:T(8,128)(2,1)} collective-permute-done((bf16[512,1024]{1,0:T(8,128)(2,1)}, bf16[512,1024]{1,0:T(8,128)(2,1)}, u32[]{:S(2)}, u32[]{:S(2)}) %collective-permute-start.57) | collective-permute-done | bytes 1048608 | tf_op jit(solution)/shard_map/ppermute | solution.py:460
  472.8 24.3 %collective-permute-done.72 = f32[4,384]{1,0:T(4,128)S(1)} collective-permute-done((f32[4,384]{1,0:T(4,128)S(1)}, f32[4,384]{1,0:T(4,128)S(1)}, u32[]{:S(2)}, u32[]{:S(2)}) %collective-permute-start.72) | collective-permute-done | bytes 6176 | tf_op jit(solution)/shard_map/ppermute | solution.py:577
  502.2 3.7 maximum_add_fusion.1
  506.6 49.0 %shard_map.150 = (f32[1024,1024]{1,0:T(8,128)}, f32[1024,1024]{1,0:T(8,128)}, f32[1024,1024]{1,0:T(8,128)}) custom-call(s32[3]{0:T(128)S(1)} %pad_add_fusion.limit_ref, bf16[8,128,1024]{2,1,0:T(8,128)(2,1)S(1)} %all-to-all-done.1.landed_ref, f32[1024,1024]{1,0:T(8,128)} %bitcast.210, f32[1024,1024]{1,0:T(8,128)} %bitcast.166), custom_call_target="tpu_custom_call" | custom-call | flops 32212254720 | bytes 23068672 | tf_op jit(solution)/shard_map/pallas_call | solution.py:432
  (433 shorter events, 198.0 us)
Async XLA Ops:
  0.6 57.0 %collective-permute-start = (bf16[512,1024]{1,0:T(8,128)(2,1)}, bf16[512,1024]{1,0:T(8,128)(2,1)S(1)}, u32[]{:S(2)}, u32[]{:S(2)}) collective-permute-start(bf16[512,1024]{1,0:T(8,128)(2,1)} %param.8), channel_id=1, source_target_pairs={{0,2},{1,3},{2,0},{3,1},{4,6},{5,7},{6,4},{7,5},{8,10},{9,11},{10,... | collective-permute-start | bytes 3145736 | tf_op jit(solution)/shard_map/ppermute | solution.py:460
  0.7 78.0 %collective-permute-start.1 = (bf16[512,1024]{1,0:T(8,128)(2,1)}, bf16[512,1024]{1,0:T(8,128)(2,1)}, u32[]{:S(2)}, u32[]{:S(2)}) collective-permute-start(bf16[512,1024]{1,0:T(8,128)(2,1)} %param.8), channel_id=1, source_target_pairs={{0,1},{1,0},{2,3},{3,2},{4,5},{5,4},{6,7},{7,6},{8,9},{9,8},{10,11... | collective-permute-start | bytes 3145736 | tf_op jit(solution)/shard_map/ppermute | solution.py:460
  13.5 76.7 %all-to-all-start = ((bf16[8,128,1024]{2,1,0:T(8,128)(2,1)}), bf16[8,128,1024]{2,1,0:T(8,128)(2,1)}, u32[]{:S(2)}, u32[]{:S(2)}) async-start(bf16[8,128,1024]{2,1,0:T(8,128)(2,1)} %pad_select_fusion), calls=%async_computation | async-start | bytes 4194304 | tf_op jit(solution)/shard_map/all_to_all | solution.py:620
  18.5 35.7 %collective-permute-start.4 = (f32[2,384]{1,0:T(2,128)S(1)}, f32[2,384]{1,0:T(2,128)S(1)}, u32[]{:S(2)}, u32[]{:S(2)}) collective-permute-start(f32[2,384]{1,0:T(2,128)S(1)} %maximum_select_fusion.22), channel_id=1, source_target_pairs={{0,8},{4,12},{8,0},{12,4},{16,24},{20,28},{24,16},{28,20},{1,9},{5... | collective-permute-start | bytes 9224 | tf_op jit(solution)/shard_map/ppermute | solution.py:557
  21.6 87.4 %collective-permute-start.28 = (bf16[256,1024]{1,0:T(8,128)(2,1)}, bf16[256,1024]{1,0:T(8,128)(2,1)}, u32[]{:S(2)}, u32[]{:S(2)}) collective-permute-start(bf16[256,1024]{1,0:T(8,128)(2,1)} %get-tuple-element.161), channel_id=1, source_target_pairs={{0,2},{1,3},{2,0},{3,1},{4,6},{5,7},{6,4},{7,5},{8,10},{9,11},{10,... | collective-permute-start | bytes 1572872 | tf_op jit(solution)/shard_map/ppermute | solution.py:460
  23.1 143.6 %collective-permute-start.29 = (bf16[256,1024]{1,0:T(8,128)(2,1)}, bf16[256,1024]{1,0:T(8,128)(2,1)}, u32[]{:S(2)}, u32[]{:S(2)}) collective-permute-start(bf16[256,1024]{1,0:T(8,128)(2,1)} %get-tuple-element.161), channel_id=1, source_target_pairs={{0,1},{1,0},{2,3},{3,2},{4,5},{5,4},{6,7},{7,6},{8,9},{9,8},{10,11... | collective-permute-start | bytes 1572872 | tf_op jit(solution)/shard_map/ppermute | solution.py:460
  57.6 21.1 %collective-permute-start.2 = (bf16[512,1024]{1,0:T(8,128)(2,1)S(1)}, bf16[512,1024]{1,0:T(8,128)(2,1)S(1)}, u32[]{:S(2)}, u32[]{:S(2)}) collective-permute-start(bf16[512,1024]{1,0:T(8,128)(2,1)S(1)} %collective-permute-done), channel_id=1, source_target_pairs={{0,1},{1,0},{2,3},{3,2},{4,5},{5,4},{6,7},{7,6},{8,9},{9,8},{10,11... | collective-permute-start | bytes 3145736 | tf_op jit(solution)/shard_map/ppermute | solution.py:460
  109.0 65.4 %collective-permute-start.37 = (bf16[256,1024]{1,0:T(8,128)(2,1)}, bf16[256,1024]{1,0:T(8,128)(2,1)}, u32[]{:S(2)}, u32[]{:S(2)}) collective-permute-start(bf16[256,1024]{1,0:T(8,128)(2,1)} %get-tuple-element.160), channel_id=1, source_target_pairs={{0,2},{1,3},{2,0},{3,1},{4,6},{5,7},{6,4},{7,5},{8,10},{9,11},{10,... | collective-permute-start | bytes 1572872 | tf_op jit(solution)/shard_map/ppermute | solution.py:460
  119.5 52.1 %collective-permute-start.30 = (bf16[256,1024]{1,0:T(8,128)(2,1)}, bf16[256,1024]{1,0:T(8,128)(2,1)}, u32[]{:S(2)}, u32[]{:S(2)}) collective-permute-start(bf16[256,1024]{1,0:T(8,128)(2,1)} %collective-permute-done.28), channel_id=1, source_target_pairs={{0,1},{1,0},{2,3},{3,2},{4,5},{5,4},{6,7},{7,6},{8,9},{9,8},{10,11... | collective-permute-start | bytes 1572872 | tf_op jit(solution)/shard_map/ppermute | solution.py:460
  131.3 34.1 %collective-permute-start.24 = (bf16[1,1,1,128,1024]{4,3,2,1,0:T(8,128)(2,1)S(1)}, bf16[1,1,1,128,1024]{4,3,2,1,0:T(8,128)(2,1)S(1)}, u32[]{:S(2)}, u32[]{:S(2)}) collective-permute-start(bf16[1,1,1,128,1024]{4,3,2,1,0:T(8,128)(2,1)S(1)} %bitcast.194), channel_id=1, source_target_pairs={{0,16},{4,20},{8,24},{12,28},{16,0},{20,4},{24,8},{28,12},{1,17},{... | collective-permute-start | bytes 786440 | tf_op jit(solution)/shard_map/ppermute | solution.py:486
  165.4 32.3 %collective-permute-start.19 = (bf16[512,1024]{1,0:T(8,128)(2,1)}, bf16[512,1024]{1,0:T(8,128)(2,1)}, u32[]{:S(2)}, u32[]{:S(2)}) collective-permute-start(bf16[512,1024]{1,0:T(8,128)(2,1)} %convolution_convert_fusion.6), channel_id=1, source_target_pairs={{0,1},{1,0},{2,3},{3,2},{4,5},{5,4},{6,7},{7,6},{8,9},{9,8},{10,11... | collective-permute-start | bytes 3145736 | tf_op jit(solution)/shard_map/ppermute | solution.py:460
  171.6 26.0 %collective-permute-start.26 = (bf16[1,2,1,128,1024]{4,3,2,1,0:T(8,128)(2,1)}, bf16[1,2,1,128,1024]{4,3,2,1,0:T(8,128)(2,1)S(1)}, u32[]{:S(2)}, u32[]{:S(2)}) collective-permute-start(bf16[1,2,1,128,1024]{4,3,2,1,0:T(8,128)(2,1)} %maximum_select_fusion.9), channel_id=1, source_target_pairs={{0,16},{4,20},{8,24},{12,28},{16,0},{20,4},{24,8},{28,12},{1,17},{... | collective-permute-start | bytes 1572872 | tf_op jit(solution)/shard_map/ppermute | solution.py:486
  174.4 68.2 %collective-permute-start.38 = (bf16[256,1024]{1,0:T(8,128)(2,1)}, bf16[256,1024]{1,0:T(8,128)(2,1)}, u32[]{:S(2)}, u32[]{:S(2)}) collective-permute-start(bf16[256,1024]{1,0:T(8,128)(2,1)} %get-tuple-element.160), channel_id=1, source_target_pairs={{0,1},{1,0},{2,3},{3,2},{4,5},{5,4},{6,7},{7,6},{8,9},{9,8},{10,11... | collective-permute-start | bytes 1572872 | tf_op jit(solution)/shard_map/ppermute | solution.py:460
  174.5 68.1 %collective-permute-start.39 = (bf16[256,1024]{1,0:T(8,128)(2,1)}, bf16[256,1024]{1,0:T(8,128)(2,1)}, u32[]{:S(2)}, u32[]{:S(2)}) collective-permute-start(bf16[256,1024]{1,0:T(8,128)(2,1)} %collective-permute-done.37), channel_id=1, source_target_pairs={{0,1},{1,0},{2,3},{3,2},{4,5},{5,4},{6,7},{7,6},{8,9},{9,8},{10,11... | collective-permute-start | bytes 1572872 | tf_op jit(solution)/shard_map/ppermute | solution.py:460
  197.5 24.7 %collective-permute-start.32 = (bf16[2,1,2,128,1024]{4,3,2,1,0:T(8,128)(2,1)S(1)}, bf16[2,1,2,128,1024]{4,3,2,1,0:T(8,128)(2,1)S(1)}, u32[]{:S(2)}, u32[]{:S(2)}) collective-permute-start(bf16[2,1,2,128,1024]{4,3,2,1,0:T(8,128)(2,1)S(1)} %maximum_select_fusion.4), channel_id=1, source_target_pairs={{0,8},{4,12},{8,0},{12,4},{16,24},{20,28},{24,16},{28,20},{1,9},{5... | collective-permute-start | bytes 3145736 | tf_op jit(solution)/shard_map/ppermute | solution.py:486
  199.6 27.6 %collective-permute-start.27 = (bf16[2,2,1,128,1024]{4,3,2,1,0:T(8,128)(2,1)S(1)}, bf16[2,2,1,128,1024]{4,3,2,1,0:T(8,128)(2,1)S(1)}, u32[]{:S(2)}, u32[]{:S(2)}) collective-permute-start(bf16[2,2,1,128,1024]{4,3,2,1,0:T(8,128)(2,1)S(1)} %maximum_select_fusion.3), channel_id=1, source_target_pairs={{0,4},{4,0},{8,12},{12,8},{16,20},{20,16},{24,28},{28,24},{1,5},{5... | collective-permute-start | bytes 3145736 | tf_op jit(solution)/shard_map/ppermute | solution.py:486
  271.7 22.8 %collective-permute-start.47 = (bf16[256,1024]{1,0:T(8,128)(2,1)S(1)}, bf16[256,1024]{1,0:T(8,128)(2,1)S(1)}, u32[]{:S(2)}, u32[]{:S(2)}) collective-permute-start(bf16[256,1024]{1,0:T(8,128)(2,1)S(1)} %convert_element_type.332.refs_0_), channel_id=1, source_target_pairs={{0,2},{1,3},{2,0},{3,1},{4,6},{5,7},{6,4},{7,5},{8,10},{9,11},{10,... | collective-permute-start | bytes 1572872 | tf_op jit(solution)/shard_map/ppermute | solution.py:460
  272.8 32.0 %collective-permute-start.48 = (bf16[256,1024]{1,0:T(8,128)(2,1)S(1)}, bf16[256,1024]{1,0:T(8,128)(2,1)S(1)}, u32[]{:S(2)}, u32[]{:S(2)}) collective-permute-start(bf16[256,1024]{1,0:T(8,128)(2,1)S(1)} %convert_element_type.332.refs_0_), channel_id=1, source_target_pairs={{0,1},{1,0},{2,3},{3,2},{4,5},{5,4},{6,7},{7,6},{8,9},{9,8},{10,11... | collective-permute-start | bytes 1572872 | tf_op jit(solution)/shard_map/ppermute | solution.py:460
  282.0 25.7 %collective-permute-start.54 = (bf16[2,1,2,128,1024]{4,3,2,1,0:T(8,128)(2,1)S(1)}, bf16[2,1,2,128,1024]{4,3,2,1,0:T(8,128)(2,1)}, u32[]{:S(2)}, u32[]{:S(2)}) collective-permute-start(bf16[2,1,2,128,1024]{4,3,2,1,0:T(8,128)(2,1)S(1)} %constant_dynamic-slice_fusion.13), channel_id=1, source_target_pairs={{0,8},{4,12},{8,0},{12,4},{16,24},{20,28},{24,16},{28,20},{1,9},{5... | collective-permute-start | bytes 3145736 | tf_op jit(solution)/shard_map/ppermute | solution.py:486
  294.0 25.1 %collective-permute-start.53 = (bf16[2,2,1,128,1024]{4,3,2,1,0:T(8,128)(2,1)}, bf16[2,2,1,128,1024]{4,3,2,1,0:T(8,128)(2,1)}, u32[]{:S(2)}, u32[]{:S(2)}) collective-permute-start(bf16[2,2,1,128,1024]{4,3,2,1,0:T(8,128)(2,1)} %constant_dynamic-slice_fusion.14), channel_id=1, source_target_pairs={{0,4},{4,0},{8,12},{12,8},{16,20},{20,16},{24,28},{28,24},{1,5},{5... | collective-permute-start | bytes 3145736 | tf_op jit(solution)/shard_map/ppermute | solution.py:486
  305.8 20.3 %collective-permute-start.45 = (bf16[512,1024]{1,0:T(8,128)(2,1)}, bf16[512,1024]{1,0:T(8,128)(2,1)S(1)}, u32[]{:S(2)}, u32[]{:S(2)}) collective-permute-start(bf16[512,1024]{1,0:T(8,128)(2,1)} %convolution_convert_fusion.2), channel_id=1, source_target_pairs={{0,1},{1,0},{2,3},{3,2},{4,5},{5,4},{6,7},{7,6},{8,9},{9,8},{10,11... | collective-permute-start | bytes 3145736 | tf_op jit(solution)/shard_map/ppermute | solution.py:460
  307.7 21.7 %collective-permute-start.51 = (bf16[256,1024]{1,0:T(8,128)(2,1)S(1)}, bf16[256,1024]{1,0:T(8,128)(2,1)S(1)}, u32[]{:S(2)}, u32[]{:S(2)}) collective-permute-start(bf16[256,1024]{1,0:T(8,128)(2,1)S(1)} %convert_element_type.333.refs_0_), channel_id=1, source_target_pairs={{0,1},{1,0},{2,3},{3,2},{4,5},{5,4},{6,7},{7,6},{8,9},{9,8},{10,11... | collective-permute-start | bytes 1572872 | tf_op jit(solution)/shard_map/ppermute | solution.py:460
  325.2 79.9 %collective-permute-start.44 = (bf16[256,1024]{1,0:T(8,128)(2,1)}, bf16[256,1024]{1,0:T(8,128)(2,1)}, u32[]{:S(2)}, u32[]{:S(2)}) collective-permute-start(bf16[256,1024]{1,0:T(8,128)(2,1)} %slice.351), channel_id=1, source_target_pairs={{0,2},{1,3},{2,0},{3,1},{4,6},{5,7},{6,4},{7,5},{8,10},{9,11},{10,... | collective-permute-start | bytes 1572872 | tf_op jit(solution)/shard_map/ppermute | solution.py:460
  328.4 137.0 %collective-permute-start.46 = (bf16[256,1024]{1,0:T(8,128)(2,1)}, bf16[256,1024]{1,0:T(8,128)(2,1)}, u32[]{:S(2)}, u32[]{:S(2)}) collective-permute-start(bf16[256,1024]{1,0:T(8,128)(2,1)} %slice.350), channel_id=1, source_target_pairs={{0,2},{1,3},{2,0},{3,1},{4,6},{5,7},{6,4},{7,5},{8,10},{9,11},{10,... | collective-permute-start | bytes 1572872 | tf_op jit(solution)/shard_map/ppermute | solution.py:460
  354.5 44.7 %collective-permute-start.55 = (bf16[2,2,1,128,512]{4,3,2,1,0:T(8,128)(2,1)S(1)}, bf16[2,2,1,128,512]{4,3,2,1,0:T(8,128)(2,1)S(1)}, u32[]{:S(2)}, u32[]{:S(2)}) collective-permute-start(bf16[2,2,1,128,512]{4,3,2,1,0:T(8,128)(2,1)S(1)} %constant_dynamic-slice_fusion.12), channel_id=1, source_target_pairs={{0,4},{4,0},{8,12},{12,8},{16,20},{20,16},{24,28},{28,24},{1,5},{5... | collective-permute-start | bytes 1572872 | tf_op jit(solution)/shard_map/ppermute | solution.py:486
  354.9 52.4 %collective-permute-start.68 = (bf16[2,1,1,128,1024]{4,3,2,1,0:T(8,128)(2,1)S(1)}, bf16[2,1,1,128,1024]{4,3,2,1,0:T(8,128)(2,1)S(1)}, u32[]{:S(2)}, u32[]{:S(2)}) collective-permute-start(bf16[2,1,1,128,1024]{4,3,2,1,0:T(8,128)(2,1)S(1)} %constant_dynamic-slice_fusion.1), channel_id=1, source_target_pairs={{0,8},{4,12},{8,0},{12,4},{16,24},{20,28},{24,16},{28,20},{1,9},{5... | collective-permute-start | bytes 1572872 | tf_op jit(solution)/shard_map/ppermute | solution.py:486
  403.5 31.3 %collective-permute-start.56 = (bf16[1024,1024]{1,0:T(8,128)(2,1)S(1)}, bf16[1024,1024]{1,0:T(8,128)(2,1)S(1)}, u32[]{:S(2)}, u32[]{:S(2)}) collective-permute-start(bf16[1024,1024]{1,0:T(8,128)(2,1)S(1)} %add_convert_fusion), channel_id=1, source_target_pairs={{0,1},{1,0},{2,3},{3,2},{4,5},{5,4},{6,7},{7,6},{8,9},{9,8},{10,11... | collective-permute-start | bytes 6291464 | tf_op jit(solution)/shard_map/ppermute | solution.py:460
  407.5 37.9 %collective-permute-start.69 = (bf16[1,1,1,128,1024]{4,3,2,1,0:T(8,128)(2,1)S(1)}, bf16[1,1,1,128,1024]{4,3,2,1,0:T(8,128)(2,1)S(1)}, u32[]{:S(2)}, u32[]{:S(2)}) collective-permute-start(bf16[1,1,1,128,1024]{4,3,2,1,0:T(8,128)(2,1)S(1)} %constant_dynamic-slice_fusion), channel_id=1, source_target_pairs={{0,16},{4,20},{8,24},{12,28},{16,0},{20,4},{24,8},{28,12},{1,17},{... | collective-permute-start | bytes 786440 | tf_op jit(solution)/shard_map/ppermute | solution.py:486
  418.2 26.4 %collective-permute-start.67 = (bf16[1,1,1,128,1024]{4,3,2,1,0:T(8,128)(2,1)S(1)}, bf16[1,1,1,128,1024]{4,3,2,1,0:T(8,128)(2,1)S(1)}, u32[]{:S(2)}, u32[]{:S(2)}) collective-permute-start(bf16[1,1,1,128,1024]{4,3,2,1,0:T(8,128)(2,1)S(1)} %constant_dynamic-slice_fusion.2), channel_id=1, source_target_pairs={{0,16},{4,20},{8,24},{12,28},{16,0},{20,4},{24,8},{28,12},{1,17},{... | collective-permute-start | bytes 786440 | tf_op jit(solution)/shard_map/ppermute | solution.py:486
  437.4 23.0 %collective-permute-start.57 = (bf16[512,1024]{1,0:T(8,128)(2,1)}, bf16[512,1024]{1,0:T(8,128)(2,1)}, u32[]{:S(2)}, u32[]{:S(2)}) collective-permute-start(bf16[512,1024]{1,0:T(8,128)(2,1)} %slice.349), channel_id=1, source_target_pairs={{0,2},{1,3},{2,0},{3,1},{4,6},{5,7},{6,4},{7,5},{8,10},{9,11},{10,... | collective-permute-start | bytes 3145736 | tf_op jit(solution)/shard_map/ppermute | solution.py:460
  446.1 60.4 %all-to-all-start.1 = ((bf16[8,128,1024]{2,1,0:T(8,128)(2,1)}), bf16[8,128,1024]{2,1,0:T(8,128)(2,1)S(1)}, u32[]{:S(2)}, u32[]{:S(2)}) async-start(bf16[8,128,1024]{2,1,0:T(8,128)(2,1)} %fusion.24), calls=%async_computation.1 | async-start | bytes 4194304 | tf_op jit(solution)/shard_map/all_to_all | solution.py:765
  471.3 25.8 %collective-permute-start.72 = (f32[4,384]{1,0:T(4,128)S(1)}, f32[4,384]{1,0:T(4,128)S(1)}, u32[]{:S(2)}, u32[]{:S(2)}) collective-permute-start(f32[4,384]{1,0:T(4,128)S(1)} %slice_select_fusion.2), channel_id=1, source_target_pairs={{0,16},{4,20},{8,24},{12,28},{16,0},{20,4},{24,8},{28,12},{1,17},{... | collective-permute-start | bytes 18440 | tf_op jit(solution)/shard_map/ppermute | solution.py:577
  (105 other events, 930.4 us)

commit v4 on v3

--- a/solution.py
+++ b/solution.py
@@ -137,7 +137,7 @@
     o_refs = refs[0:chunks]
     lse_refs = refs[chunks : 2 * chunks]
     do_refs = refs[2 * chunks : 3 * chunks]
-    out_ref, v_out_ref, dk_acc, dv_acc = refs[3 * chunks :]
+    out_ref, v_out_ref, dk_acc, dv_acc = refs[-4:]
     core = core_ref[0]
     place = (core, 1 - core)
     width = q_ref.shape[-1]
@@ -193,37 +193,40 @@
         v_out_ref[place[j // per_half], 0, rows, :] = dv_acc[j].astype(BF16)
 
 
-def attend_back(core, qk, v, outs, lses, back):
-    _, seqs, rows, width = v.shape
+def attend_back(core, qk, v, outs, lses, back, seq, before=()):
+    _, _, rows, width = v.shape
     chunks = len(outs)
     part = rows // chunks
 
     def block(size, cols, at):
-        return pl.BlockSpec((2, 1, size, cols), lambda s, c: (0, s, 0, at))
-
+        return pl.BlockSpec((2, 1, size, cols), lambda s, c: (0, seq, 0, at))
+
+    operands = (core, qk, qk, v, *outs, *lses, *back)
     return pl.pallas_call(
         partial(attend_back_kernel, heads=width // HEAD_DIM, chunks=chunks),
         grid_spec=pltpu.PrefetchScalarGridSpec(
             num_scalar_prefetch=1,
-            grid=(seqs,),
+            grid=(1,),
             in_specs=[block(rows, width, 0), block(rows, width, 1), block(rows, width, 0)]
             + [block(part, width, 0)] * chunks
             + [block(part, 128, 0)] * chunks
-            + [block(part, width, 0)] * chunks,
+            + [block(part, width, 0)] * chunks
+            + [pl.BlockSpec(memory_space=pl.ANY)] * len(before),
             out_specs=[block(rows, 2 * width, 0), block(rows, width, 0)],
             scratch_shapes=[pltpu.VMEM((2 * rows // TILE, TILE, width), F32)] * 2,
         ),
         out_shape=[jax.ShapeDtypeStruct(qk.shape, BF16), jax.ShapeDtypeStruct(v.shape, BF16)],
+        input_output_aliases={len(operands) + i: i for i in range(len(before))},
         compiler_params=pltpu.CompilerParams(vmem_limit_bytes=VMEM_GRANT),
         cost_estimate=pl.CostEstimate(
-            flops=25 * 10**9, bytes_accessed=12 * 10**6, transcendentals=0
-        ),
-    )(core, qk, qk, v, *outs, *lses, *back)
+            flops=12 * 10**9, bytes_accessed=6 * 10**6, transcendentals=0
+        ),
+    )(*operands, *before)
 
 
 def hidden_kernel(*refs):
-    blocks = refs[0:4]
-    w_ref, bias_ref, dact_ref, act_ref, back_ref, sum_ref, all_ref = refs[4:]
+    blocks = refs[:-7]
+    w_ref, bias_ref, dact_ref, act_ref, back_ref, sum_ref, all_ref = refs[-7:]
     rows = blocks[0].shape[0]
     value = jnp.concatenate([block[...] for block in blocks], axis=0)
     hidden = mm(value, w_ref[...]) + bias_ref[...]
@@ -240,20 +243,21 @@
 
     @pl.when(pl.program_id(0) == 0)
     def _():
-        for at in range(4):
+        for at in range(len(blocks)):
             all_ref[at * rows : (at + 1) * rows, :] = blocks[at][...]
 
 
 def hidden_layer(blocks, weight, bias, dact):
     rows, width = blocks[0].shape
     cols = weight.shape[1]
+    total = len(blocks) * rows
     tile = min(256, cols)
     whole = pl.BlockSpec((rows, width), lambda n: (0, 0))
-    column = pl.BlockSpec((4 * rows, tile), lambda n: (0, n))
+    column = pl.BlockSpec((total, tile), lambda n: (0, n))
     return pl.pallas_call(
         hidden_kernel,
         grid=(cols // tile,),
-        in_specs=[whole] * 4
+        in_specs=[whole] * len(blocks)
         + [
             pl.BlockSpec((width, tile), lambda n: (0, n)),
             pl.BlockSpec((1, tile), lambda n: (0, n)),
@@ -263,26 +267,26 @@
             column,
             column,
             pl.BlockSpec((1, tile), lambda n: (0, n)),
-            pl.BlockSpec((4 * rows, width), lambda n: (0, 0)),
+            pl.BlockSpec((total, width), lambda n: (0, 0)),
         ],
         out_shape=[
-            jax.ShapeDtypeStruct((4 * rows, cols), BF16),
-            jax.ShapeDtypeStruct((4 * rows, cols), BF16),
+            jax.ShapeDtypeStruct((total, cols), BF16),
+            jax.ShapeDtypeStruct((total, cols), BF16),
             jax.ShapeDtypeStruct((1, cols), F32),
-            jax.ShapeDtypeStruct((4 * rows, width), BF16),
+            jax.ShapeDtypeStruct((total, width), BF16),
         ],
         compiler_params=pltpu.CompilerParams(vmem_limit_bytes=VMEM_GRANT),
         cost_estimate=pl.CostEstimate(
-            flops=8 * rows * width * cols, bytes_accessed=12 * 10**6, transcendentals=0
+            flops=2 * total * width * cols, bytes_accessed=12 * 10**6, transcendentals=0
         ),
     )(*blocks, weight, bias.reshape(1, -1), dact)
 
 
 def mixed_kernel(*refs):
-    blocks = refs[0:4]
-    w_ref, out_ref, all_ref = refs[4:]
+    blocks = refs[:-3]
+    w_ref, out_ref, all_ref = refs[-3:]
     rows = blocks[0].shape[0]
-    for at in range(4):
+    for at in range(len(blocks)):
         value = blocks[at][...]
         out_ref[at * rows : (at + 1) * rows, :] = mm(value, w_ref[...], NT).astype(BF16)
         all_ref[at * rows : (at + 1) * rows, :] = value
@@ -291,17 +295,18 @@
 def back_mix(blocks, weight):
     rows, width = blocks[0].shape
     cols = weight.shape[0]
+    total = len(blocks) * rows
     return pl.pallas_call(
         mixed_kernel,
-        in_specs=[pl.BlockSpec(memory_space=pltpu.VMEM)] * 5,
+        in_specs=[pl.BlockSpec(memory_space=pltpu.VMEM)] * (len(blocks) + 1),
         out_specs=[pl.BlockSpec(memory_space=pltpu.VMEM)] * 2,
         out_shape=[
-            jax.ShapeDtypeStruct((4 * rows, cols), BF16),
-            jax.ShapeDtypeStruct((4 * rows, width), BF16),
+            jax.ShapeDtypeStruct((total, cols), BF16),
+            jax.ShapeDtypeStruct((total, width), BF16),
         ],
         compiler_params=pltpu.CompilerParams(vmem_limit_bytes=VMEM_GRANT),
         cost_estimate=pl.CostEstimate(
-            flops=8 * rows * width * cols, bytes_accessed=5 * 10**6, transcendentals=0
+            flops=2 * total * width * cols, bytes_accessed=5 * 10**6, transcendentals=0
         ),
     )(*blocks, weight)
 
@@ -342,8 +347,12 @@
     def _():
         grad_buf[...] = jnp.zeros_like(grad_buf)
         for src in range(count):
-            piece = landed_ref[src].astype(F32)
-            grad_buf[src * out_rows : (src + 1) * out_rows, :] = piece[:out_rows]
+            cols = size * out_rows // share
+            piece = landed_ref[src].astype(F32)[:, size - cols :]
+            for at in range(share // out_rows):
+                grad_buf[
+                    src * out_rows : (src + 1) * out_rows, at * cols : (at + 1) * cols
+                ] = piece[at * out_rows : (at + 1) * out_rows]
 
     @pl.when(jnp.logical_not(is_out))
     def _():
@@ -481,6 +490,13 @@
     return part[:size] + swap(part[size:].astype(BF16), 2).astype(F32)
 
 
+def exchange(part):
+    size = part.shape[0] // 2
+    given = part.astype(BF16)
+    given = jnp.concatenate([given[size:], given[:size]])
+    return part + swap(given, 2).astype(F32)
+
+
 def data_swap(value, bit):
     count = lax.axis_size("dp")
     return lax.ppermute(value, "dp", [(i, i ^ bit) for i in range(count)])
@@ -548,20 +564,18 @@
     return bits
 
 
-def small_gather(value):
-    piece = value.reshape(1, -1)
-    for name, axis in (("dp", 0), ("tensor", 1)):
-        index = lax.axis_index(name)
-        count = lax.axis_size(name)
-        for bit in axis_bits(name):
-            other = lax.ppermute(piece, name, [(i, i ^ bit) for i in range(count)])
-            upper = (index & bit) != 0
-            piece = jnp.where(
-                upper,
-                jnp.concatenate([other, piece], axis=axis),
-                jnp.concatenate([piece, other], axis=axis),
-            )
-    return piece.reshape(-1)
+def small_gather(piece, name, axis):
+    index = lax.axis_index(name)
+    count = lax.axis_size(name)
+    for bit in axis_bits(name):
+        other = lax.ppermute(piece, name, [(i, i ^ bit) for i in range(count)])
+        upper = (index & bit) != 0
+        piece = jnp.where(
+            upper,
+            jnp.concatenate([other, piece], axis=axis),
+            jnp.concatenate([piece, other], axis=axis),
+        )
+    return piece
 
 
 def small_scatter(value):
@@ -611,27 +625,14 @@
     owned = owner_row == data_idx
     slot_value = master_slots[0]
 
+    params = small_gather(small_master.reshape(1, -1), "dp", 0)
     slot_low = slot_value.astype(BF16)
-    offer_out = jnp.pad(
-        slot_low[:head_width].reshape(data_count, share_out, width),
-        ((0, 0), (0, share - share_out), (0, 0)),
-    )
+    offer_out = slot_low[:head_width].reshape(data_count, share_out, tensor_count, head_width)
+    offer_out = jnp.swapaxes(offer_out, 1, 2).reshape(data_count, share, head_width)
+    offer_out = jnp.pad(offer_out, ((0, 0), (0, 0), (width - head_width, 0)))
     offer = jnp.where(owned[1], offer_out, slot_low.reshape(data_count, share, width))
-    shares = lax.all_to_all(offer, "dp", 0, 0)
-
-    def share_of(kind):
-        return lax.dynamic_index_in_dim(shares, owner_row[kind], 0, keepdims=False)
-
-    first = share_of(0)
-    w_qk = gather_by(first[:, : 2 * head_width], last_bits(2, 1))
-    w_v = gather_by(first[:, 2 * head_width : 3 * head_width], last_bits(2, 1)[::-1])
-    w_out = gather_by(share_of(1)[:share_out], last_bits(1, 2))
-    bits_proj = last_bits(1, 2)
-    bits_fc = [2] + last_bits(2, 1)[:-2] + [1]
-    w_proj = double(open_piece(after(share_of(3), w_v)), bits_proj[0])
-    w_fc = double(open_piece(after(share_of(2), w_v)), bits_fc[0])
-
-    params = small_gather(small_master)
+    shares = lax.all_to_all(after(offer, params), "dp", 0, 0)
+    params = small_gather(params, "tensor", 1).reshape(-1)
 
     def own_slice(start, size):
         return lax.dynamic_slice_in_dim(params, start + tensor_idx * size, size, 0)
@@ -650,113 +651,149 @@
     rows_of = [slice(chunk * part, (chunk + 1) * part) for chunk in range(CHUNKS)]
     rows_in = inputs.astype(F32)
     unit_one, scale_one = norm_parts(rows_in)
-    unit_all, _ = norm_parts(jnp.concatenate(gather_four(inputs)).astype(F32))
+    inputs_four = gather_four(inputs)
+    unit_all, _ = norm_parts(jnp.concatenate(inputs_four).astype(F32))
     normed_all = (unit_all * gain_one + shift_one).astype(BF16)
-    dy_all = [jnp.concatenate(gather_four(out_grad[rows])) for rows in rows_of]
+    dy_four = [gather_four(out_grad[rows]) for rows in rows_of]
+    dy_all = [jnp.concatenate(four) for four in dy_four]
+
+    shares = after(shares, normed_all, *dy_all)
+
+    def share_of(kind):
+        return lax.dynamic_index_in_dim(shares, owner_row[kind], 0, keepdims=False)
+
+    split = 2 * head_width
+    first = share_of(0)
+    piece_vo = jnp.concatenate(
+        [first[:, split : split + head_width], share_of(1)[:, width - head_width :]], axis=1
+    )
+    w_qk = gather_by(first[:, :split], last_bits(2, 1))
+    w_vo = gather_by(piece_vo, last_bits(1, 2))
+    w_v = w_vo[:, :head_width]
+    w_out = w_vo[:, head_width:].reshape(data_count, tensor_count, share_out, head_width)
+    w_out = jnp.swapaxes(w_out, 1, 2).reshape(head_width, width)
+    bits_proj = last_bits(1, 2)
+    bits_fc = last_bits(2, 1)
+    w_proj = double(open_piece(share_of(3)), bits_proj[0])
+    w_fc = double(open_piece(after(share_of(2), w_proj)), bits_fc[0])
     bias_qk = jnp.concatenate([bias_query, jnp.zeros_like(bias_query)])
-    scale_qk = jnp.where(jnp.arange(2 * head_width) < head_width, HEAD_DIM**-0.5, 1.0)
+    scale_qk = jnp.where(jnp.arange(split) < head_width, HEAD_DIM**-0.5, 1.0)
     qk = ((mm(normed_all, w_qk) + bias_qk) * scale_qk).astype(BF16)
     values = (mm(normed_all, w_v) + bias_value).astype(BF16)
-    qk = qk.reshape(2, 2, rows_dev, 2 * head_width)
+    qk, values = after((qk, values), w_proj, w_fc)
+    qk = qk.reshape(2, 2, rows_dev, split)
     values = values.reshape(2, 2, rows_dev, head_width)
 
-    w_proj, w_fc = after((w_proj, w_fc), qk, values)
     for bit in bits_proj[1:-1]:
         w_proj = double(w_proj, bit)
     for bit in bits_fc[1:-1]:
         w_fc = double(w_fc, bit)
-
     mixed, log_sums, parts = [], [], []
     for chunk in range(CHUNKS):
         mixed_one, sums_one = attend(core, qk, values, chunk, CHUNKS)
+        if chunk > 0:
+            mixed_one = after(mixed_one, w_proj, w_fc)
         mixed.append(mixed_one)
         log_sums.append(sums_one)
         parts.append(scatter_begin([rows2(mixed_one)], [w_out], NN))
     w_proj = rows2(double(after(w_proj, mixed[-1]), bits_proj[-1]))
-    w_fc = rows2(double(after(w_fc, parts[-1]), bits_fc[-1]))
+    w_fc = rows2(double(after(w_fc, mixed[-1]), bits_fc[-1]))
     back_act = [mm(after(dy, parts[-1]), w_proj, NT).astype(BF16) for dy in dy_all]
     middles, mine_two, normed_two = [], [], []
+    branches = [exchange(value) for value in parts]
     for chunk in range(CHUNKS):
-        branch = scatter_end(parts[chunk])
+        rows = rows_of[chunk]
+        branch = branches[chunk]
         if chunk > 0:
             branch = after(branch, normed_two[-1])
-        middle = rows_in[rows_of[chunk]] + branch + bias_out
+        residual = jnp.concatenate([inputs[rows], inputs_four[1][rows]]).astype(F32)
+        middle = residual + branch + bias_out
         unit_two, scale_two = norm_parts(middle)
         normed_two.append((unit_two * gain_two + shift_two).astype(BF16))
-        middles.append(middle)
+        middles.append(middle[:part])
         mine_two.append((unit_two, scale_two))
 
-    blocks = [gather_four(value) for value in normed_two]
     acts, backs, wholes, parts = [], [], [], []
-    fc_bias_grad = 0.0
+    grad_proj, grad_fc, fc_bias_grad = 0.0, 0.0, 0.0
     for chunk in range(CHUNKS):
-        earlier = parts[-1] if chunk > 0 else normed_two[-1]
-        block = after(blocks[chunk], earlier)
+        block = (normed_two[chunk], swap(normed_two[chunk], 1))
+        if chunk > 0:
+            block = after(block, parts[-1])
         act, back, sums, whole = hidden_layer(block, w_fc, bias_fc, back_act[chunk])
-        parts.append(scatter_begin([back], [w_fc], NT))
+        parts.append(scatter_begin([after(back, branches[-1])], [w_fc], NT))
+        act, back, whole = after((act, back, whole), parts[-1])
+        grad_proj = grad_proj + mm(act, dy_all[chunk], TN)
+        grad_fc = grad_fc + mm(whole, back, TN)
         acts.append(act)
-        backs.append(back)
-        wholes.append(whole)
         fc_bias_grad = fc_bias_grad + sums[0]
-    acts, backs = after((acts, backs), parts[-1])
-    grad_proj = sum(mm(acts[i], dy_all[i], TN) for i in range(CHUNKS)).astype(BF16)
-    grad_fc = sum(mm(wholes[i], backs[i], TN) for i in range(CHUNKS)).astype(BF16)
-    half_proj = halve(spread(grad_proj), 1)
-    half_fc = halve(spread(grad_fc), 2)
-
-    back_middles, back_lows = [], []
-    gain_two_grad, shift_two_grad, grad_out = 0.0, 0.0, 0.0
+    half_proj = halve(spread(grad_proj.astype(BF16)), 1)
+    half_fc = halve(spread(grad_fc.astype(BF16)), 2)
+
+    back_middles, back_lows, back_mixed, mids = [], [], [], []
+    gain_two_grad, shift_two_grad = 0.0, 0.0
     for chunk in range(CHUNKS):
         unit_two, scale_two = mine_two[chunk]
-        grad = scatter_end(parts[chunk])
+        grad = exchange(parts[chunk])
         if chunk > 0:
             grad = after(grad, back_lows[-1])
-        back_middle = out_grad[rows_of[chunk]].astype(F32) + norm_back(
-            unit_two, scale_two, gain_two, grad
-        )
+        dy = jnp.concatenate(dy_four[chunk][:2]).astype(F32)
+        back_middle = dy + norm_back(unit_two, scale_two, gain_two, grad)
         back_lows.append(back_middle.astype(BF16))
-        gain_two_grad = gain_two_grad + jnp.sum(grad * unit_two, axis=0)
-        shift_two_grad = shift_two_grad + jnp.sum(grad, axis=0)
-        back_middles.append(back_middle)
+        gain_two_grad = gain_two_grad + jnp.sum(grad[:part] * unit_two[:part], axis=0)
+        shift_two_grad = shift_two_grad + jnp.sum(grad[:part], axis=0)
+        back_middles.append(back_middle[:part])
+        block = after((back_lows[-1], swap(back_lows[-1], 1)), parts[-1])
+        mixed_grad, mid = back_mix(block, w_out)
+        back_mixed.append(mixed_grad.reshape(2, 2, part, head_width))
+        mids.append(mid)
     middle = jnp.concatenate(middles)
     back_middle = jnp.concatenate(back_middles)
     proj_bias_grad = jnp.sum(out_grad, axis=0, dtype=F32)
     out_bias_grad = jnp.sum(back_middle, axis=0)
 
-    back_mixed = []
-    for chunk in range(CHUNKS):
-        block = after(gather_four(back_lows[chunk]), parts[-1])
-        mixed_grad, mid = back_mix(block, w_out)
-        back_mixed.append(mixed_grad.reshape(2, 2, part, head_width))
-        grad_out = grad_out + mm(rows2(mixed[chunk]), mid, TN)
-    share_out_grad = halve_by(spread(grad_out.astype(BF16)), last_bits(1, 2)[::-1])
     back_mixed, half_proj, half_fc = lax.optimization_barrier((back_mixed, half_proj, half_fc))
-    back_qk, back_v = attend_back(core, qk, values, mixed, log_sums, back_mixed)
-    share_proj = halve_by(half_proj, axis_bits("dp")[1:])
-    share_fc = halve_by(half_fc, [1] + axis_bits("dp")[2:])
+    steps = axis_bits("dp")
+    rest_proj, rest_fc = steps[1:], steps[2:] + [1]
+    half_proj = halve(half_proj, rest_proj[0])
+    half_fc = halve(half_fc, rest_fc[0])
+    attend_grad = attend_back(core, qk, values, mixed, log_sums, back_mixed, 0)
+    back_mixed = after(back_mixed, half_proj, half_fc)
+    back_qk, back_v = attend_back(core, qk, values, mixed, log_sums, back_mixed, 1, attend_grad)
+    share_proj = halve_by(half_proj, rest_proj[1:])
+    share_fc = halve_by(half_fc, rest_fc[1:])
+    grad_out = sum(mm(rows2(mixed[i]), mids[i], TN) for i in range(CHUNKS)).astype(BF16)
+    grad_out = grad_out.reshape(data_count, share_out, tensor_count, head_width)
+    grad_out = jnp.swapaxes(grad_out, 1, 2).reshape(width, head_width)
     grad_qk = mm(normed_all, rows2(back_qk), TN).astype(BF16)
     grad_v = mm(normed_all, rows2(back_v), TN).astype(BF16)
+    grad_vo = jnp.concatenate([grad_v, grad_out], axis=1)
     half_qk = halve(spread(grad_qk), 1)
-    share_qk = halve_by(half_qk, axis_bits("dp")[1:])
-    share_v = halve_by(spread(grad_v), axis_bits("dp")[::-1])
-    query_bias_grad = jnp.sum(back_qk[..., :head_width], axis=(0, 1, 2), dtype=F32)
-    value_bias_grad = jnp.sum(back_v, axis=(0, 1, 2), dtype=F32)
+    half_vo = halve(spread(grad_vo), 2)
+    share_qk = halve_by(half_qk, steps[1:])
+    share_vo = halve_by(half_vo, [1] + steps[2:])
 
     acts = after(acts, back_lows[-1])
     branches = [scatter_end(scatter_begin([act], [w_proj], NN)) for act in acts]
     block_out = (middle + jnp.concatenate(branches) + bias_proj).astype(BF16)
-    back_qk, back_v = after((back_qk, back_v), half_qk, grad_v)
-    back_normed = scatter_end(scatter_begin([rows2(back_qk), rows2(back_v)], [w_qk, w_v], NT))
+    late_qk, late_v = after((back_qk, back_v), grad_qk, grad_vo)
+    back_normed = scatter_end(scatter_begin([rows2(late_qk), rows2(late_v)], [w_qk, w_v], NT))
     input_grad = back_middle + norm_back(unit_one, scale_one, gain_one, back_normed)
     gain_one_grad = jnp.sum(back_normed * unit_one, axis=0)
     shift_one_grad = jnp.sum(back_normed, axis=0)
+    query_bias_grad = jnp.sum(late_qk[..., :head_width], axis=(0, 1, 2), dtype=F32)
+    value_bias_grad = jnp.sum(late_v, axis=(0, 1, 2), dtype=F32)
 
     bundle = jnp.zeros((data_count, share, width), BF16)
     pieces = (
         jnp.concatenate(
-            [rows2(share_qk), rows2(share_v), jnp.zeros((share, width - 3 * head_width), BF16)], axis=1
-        ),
-        jnp.pad(rows2(share_out_grad), ((0, share - share_out), (0, 0))),
+            [
+                rows2(share_qk),
+                rows2(share_vo)[:, :head_width],
+                jnp.zeros((share, width - 3 * head_width), BF16),
+            ],
+            axis=1,
+        ),
+        jnp.pad(rows2(share_vo)[:, head_width:], ((0, 0), (width - head_width, 0))),
         rows2(share_fc),
         rows2(share_proj),
     )

time: 567 us -> 565 us (level)
  the two profiles are of different devices: /device:TPU:2 before, /device:TPU:8 now
where the time goes in v4:
time: 565 us; the launch traced here: 555 us
  waiting for transfers between devices  182 us (32%)
  Pallas kernels  101 us (18%)
  starting transfers between devices  90 us (16%)
  other arithmetic  78.1 us (14%)
  matrix products  53.6 us (9%)
  local copies, waits for them, and re-layouts  38.3 us (7%)
  between operations  12.7 us (2%)
    ppermute x24, waiting for transfers between devices, data_swap(): return lax.ppermute(value, 'dp', [(i, i ^ bit) for i in range(count)])  80.7 us
    ppermute x27, waiting for transfers between devices, swap(): return lax.ppermute(value, 'tensor', [(i, i ^ bit) for i in range(count)])  60.2 us
    dot_general x28, matrix products, mm(): return lax.dot_general(left, right, dims, preferred_element_type=F32)  53.6 us
    ppermute x24, starting transfers between devices, data_swap(): return lax.ppermute(value, 'dp', [(i, i ^ bit) for i in range(count)])  50.2 us
    pallas_call x1, Pallas kernels, muon_update(): pl.pallas_call(partial(muon_kernel, out_rows=out_rows), in_specs=[pl.Bloc...  49 us
    pallas_call x2, Pallas kernels, attend_back(): pl.pallas_call(partial(attend_back_kernel, heads=width // HEAD_DIM, chunk...  22 us
    ppermute x5, waiting for transfers between devices, small_gather(): other = lax.ppermute(piece, name, [(i, i ^ bit) for i in range(count)])  21.4 us
    ppermute x5, waiting for transfers between devices, small_scatter(): lax.ppermute(give, name, [(i, i ^ bit) for i in range(count)])  19.8 us
  transfers between devices with their start and end apart: 63, of which 27 were waited for; matrix products, arithmetic and copies ran while one was open for 24% of the time, Pallas kernels for 6%

profile of v4, /device:TPU:8, one launch (start us, length us, event | category | flops | bytes accessed | tf_op | source)
XLA Modules:
  0.0 555.4 jit_solution(15045210358250959175)
XLA Ops:
  6.8 3.8 convert_element_type.294
  15.1 4.2 pad_select_fusion
  19.4 5.8 %all-to-all-start = ((bf16[8,128,1024]{2,1,0:T(8,128)(2,1)}), bf16[8,128,1024]{2,1,0:T(8,128)(2,1)}, u32[]{:S(2)}, u32[]{:S(2)}) async-start(bf16[8,128,1024]{2,1,0:T(8,128)(2,1)} %pad_select_fusion), calls=%async_computation | async-start | bytes 4194304 | tf_op jit(solution)/shard_map/all_to_all | solution.py:634
  30.3 20.4 %collective-permute-done.7 = f32[8,768]{1,0:T(8,128)S(1)} collective-permute-done((f32[8,768]{1,0:T(8,128)S(1)}, f32[8,768]{1,0:T(8,128)S(1)}, u32[]{:S(2)}, u32[]{:S(2)}) %collective-permute-start.7) | collective-permute-done | bytes 24608 | tf_op jit(solution)/shard_map/ppermute | solution.py:571
  73.8 5.4 fusion.5
  86.4 11.2 %collective-permute-done.14 = bf16[1,1,1,128,512]{4,3,2,1,0:T(8,128)(2,1)S(1)} collective-permute-done((bf16[1,1,1,128,512]{4,3,2,1,0:T(8,128)(2,1)S(1)}, bf16[1,1,1,128,512]{4,3,2,1,0:T(8,128)(2,1)S(1)}, u32[]{:S(2)}, u32[]{:S(2)}) %collective-permute-start.14) | collective-permute-done | bytes 131104 | tf_op jit(solution)/shard_map/ppermute | solution.py:502
  102.0 4.1 collective-permute-done.20
  113.8 5.5 collective-permute-done.21
  123.5 4.3 collective-permute-done.19
  134.2 4.5 shard_map.143
  139.4 5.7 %shard_map.144 = (bf16[2,2,256,256]{3,2,1,0:T(8,128)(2,1)S(1)}, f32[2,2,256,128]{3,2,1,0:T(8,128)S(1)}) custom-call(s32[1]{0:T(128)} %bitcast.core_ref, bf16[2,2,512,512]{3,2,1,0:T(8,128)(2,1)S(1)} %bitcast.163, bf16[2,2,512,512]{3,2,1,0:T(8,128)(2,1)S(1)} %bitcast.164, bf16[2,2,512,256]{3,2,1,0:T(8,128)(2,1)S(1)} %bitcast.170), custom_call_target="tpu_custom_call" | custom-call | flops 5000000000 | bytes 6000000 | tf_op jit(solution)/shard_map/pallas_call | solution.py:108
  155.2 17.1 %collective-permute-done.29 = bf16[2,2,1,128,1024]{4,3,2,1,0:T(8,128)(2,1)S(1)} collective-permute-done((bf16[2,2,1,128,1024]{4,3,2,1,0:T(8,128)(2,1)S(1)}, bf16[2,2,1,128,1024]{4,3,2,1,0:T(8,128)(2,1)S(1)}, u32[]{:S(2)}, u32[]{:S(2)}) %collective-permute-start.29) | collective-permute-done | bytes 1048608 | tf_op jit(solution)/shard_map/ppermute | solution.py:502
  183.9 12.5 %collective-permute-done.27 = bf16[512,1024]{1,0:T(8,128)(2,1)S(1)} collective-permute-done((bf16[512,1024]{1,0:T(8,128)(2,1)S(1)}, bf16[512,1024]{1,0:T(8,128)(2,1)S(1)}, u32[]{:S(2)}, u32[]{:S(2)}) %collective-permute-start.27) | collective-permute-done | bytes 1048608 | tf_op jit(solution)/shard_map/ppermute | solution.py:469
  198.2 8.7 %shard_map.145 = (bf16[1024,1024]{1,0:T(8,128)(2,1)S(1)}, bf16[1024,1024]{1,0:T(8,128)(2,1)}, f32[1,1024]{1,0:T(1,128)S(1)}, bf16[1024,1024]{1,0:T(8,128)(2,1)}) custom-call(bf16[512,1024]{1,0:T(8,128)(2,1)S(1)} %get-tuple-element.152.refs_0_, bf16[512,1024]{1,0:T(8,128)(2,1)S(1)} %collective-permute-done.28.refs_1_, bf16[1024,1024]{1,0:T(8,128)(2,1)} %bitcast.204, ...), custom_call_target="tpu_custom_call" | custom-call | flops 2147483648 | bytes 12000000 | tf_op jit(solution)/shard_map/pallas_call | solution.py:257
  222.9 19.4 %collective-permute-done.35 = bf16[512,1024]{1,0:T(8,128)(2,1)} collective-permute-done((bf16[512,1024]{1,0:T(8,128)(2,1)}, bf16[512,1024]{1,0:T(8,128)(2,1)}, u32[]{:S(2)}, u32[]{:S(2)}) %collective-permute-start.35) | collective-permute-done | bytes 1048608 | tf_op jit(solution)/shard_map/ppermute | solution.py:469
  252.5 9.0 %shard_map.146 = (bf16[1024,1024]{1,0:T(8,128)(2,1)S(1)}, bf16[1024,1024]{1,0:T(8,128)(2,1)}, f32[1,1024]{1,0:T(1,128)S(1)}, bf16[1024,1024]{1,0:T(8,128)(2,1)}) custom-call(bf16[512,1024]{1,0:T(8,128)(2,1)S(1)} %get-tuple-element.84.refs_0_, bf16[512,1024]{1,0:T(8,128)(2,1)S(1)} %collective-permute-done.32.refs_1_, bf16[1024,1024]{1,0:T(8,128)(2,1)} %bitcast.205, ...), custom_call_target="tpu_custom_call" | custom-call | flops 2147483648 | bytes 12000000 | tf_op jit(solution)/shard_map/pallas_call | solution.py:257
  288.7 4.0 add_convert_fusion.2
  297.1 12.1 %collective-permute-done.34 = bf16[512,1024]{1,0:T(8,128)(2,1)} collective-permute-done((bf16[512,1024]{1,0:T(8,128)(2,1)}, bf16[512,1024]{1,0:T(8,128)(2,1)}, u32[]{:S(2)}, u32[]{:S(2)}) %collective-permute-start.34) | collective-permute-done | bytes 1048608 | tf_op jit(solution)/shard_map/ppermute | solution.py:469
  338.3 10.9 %shard_map.149 = (bf16[2,2,512,512]{3,2,1,0:T(8,128)(2,1)}, bf16[2,2,512,256]{3,2,1,0:T(8,128)(2,1)S(1)}) custom-call(s32[1]{0:T(128)} %bitcast.core_ref, bf16[2,2,512,512]{3,2,1,0:T(8,128)(2,1)} %bitcast.165, bf16[2,2,512,512]{3,2,1,0:T(8,128)(2,1)} %bitcast.166, bf16[2,2,512,256]{3,2,1,0:T(8,128)(2,1)S(1)} %bitcast.171, ...), custom_call_target="tpu_custom_call" | custom-call | flops 12000000000 | bytes 6000000 | tf_op jit(solution)/shard_map/pallas_call | solution.py:205
  354.2 4.7 collective-permute-done.45
  362.4 11.2 %shard_map.150 = (bf16[2,2,512,512]{3,2,1,0:T(8,128)(2,1)}, bf16[2,2,512,256]{3,2,1,0:T(8,128)(2,1)S(1)}) custom-call(s32[1]{0:T(128)} %bitcast.core_ref, bf16[2,2,512,512]{3,2,1,0:T(8,128)(2,1)} %bitcast.167, bf16[2,2,512,512]{3,2,1,0:T(8,128)(2,1)} %bitcast.168, ...), custom_call_target="tpu_custom_call", output_to_operand_aliasing={{0}: (10, {}), {1}: (11, {})} | custom-call | flops 12000000000 | bytes 6000000 | tf_op jit(solution)/shard_map/pallas_call | solution.py:205
  373.6 4.1 convolution_convert_fusion.8
  390.3 6.3 %collective-permute-done.48 = bf16[2,2,1,128,512]{4,3,2,1,0:T(8,128)(2,1)S(1)} collective-permute-done((bf16[2,2,1,128,512]{4,3,2,1,0:T(8,128)(2,1)S(1)}, bf16[2,2,1,128,512]{4,3,2,1,0:T(8,128)(2,1)S(1)}, u32[]{:S(2)}, u32[]{:S(2)}) %collective-permute-start.48) | collective-permute-done | bytes 524320 | tf_op jit(solution)/shard_map/ppermute | solution.py:502
  405.3 9.4 %collective-permute-done.49 = bf16[2,1,1,128,512]{4,3,2,1,0:T(8,128)(2,1)S(1)} collective-permute-done((bf16[2,1,1,128,512]{4,3,2,1,0:T(8,128)(2,1)S(1)}, bf16[2,1,1,128,512]{4,3,2,1,0:T(8,128)(2,1)S(1)}, u32[]{:S(2)}, u32[]{:S(2)}) %collective-permute-start.49) | collective-permute-done | bytes 262176 | tf_op jit(solution)/shard_map/ppermute | solution.py:502
  415.6 6.1 %collective-permute-done.52 = bf16[2,1,1,128,512]{4,3,2,1,0:T(8,128)(2,1)S(1)} collective-permute-done((bf16[2,1,1,128,512]{4,3,2,1,0:T(8,128)(2,1)S(1)}, bf16[2,1,1,128,512]{4,3,2,1,0:T(8,128)(2,1)S(1)}, u32[]{:S(2)}, u32[]{:S(2)}) %collective-permute-start.52) | collective-permute-done | bytes 262176 | tf_op jit(solution)/shard_map/ppermute | solution.py:502
  421.7 4.3 collective-permute-start.50
  426.2 4.9 collective-permute-done.50
  446.2 6.2 %all-to-all-start.1 = ((bf16[8,128,1024]{2,1,0:T(8,128)(2,1)}), bf16[8,128,1024]{2,1,0:T(8,128)(2,1)S(1)}, u32[]{:S(2)}, u32[]{:S(2)}) async-start(bf16[8,128,1024]{2,1,0:T(8,128)(2,1)} %fusion.44), calls=%async_computation.1 | async-start | bytes 4194304 | tf_op jit(solution)/shard_map/all_to_all | solution.py:802
  452.3 11.4 %collective-permute-done.47 = bf16[512,1024]{1,0:T(8,128)(2,1)} collective-permute-done((bf16[512,1024]{1,0:T(8,128)(2,1)}, bf16[512,1024]{1,0:T(8,128)(2,1)}, u32[]{:S(2)}, u32[]{:S(2)}) %collective-permute-start.47) | collective-permute-done | bytes 1048608 | tf_op jit(solution)/shard_map/ppermute | solution.py:469
  478.1 17.1 %collective-permute-done.58 = f32[4,384]{1,0:T(4,128)S(1)} collective-permute-done((f32[4,384]{1,0:T(4,128)S(1)}, f32[4,384]{1,0:T(4,128)S(1)}, u32[]{:S(2)}, u32[]{:S(2)}) %collective-permute-start.58) | collective-permute-done | bytes 6176 | tf_op jit(solution)/shard_map/ppermute | solution.py:591
  495.2 4.0 collective-permute-start.59
  506.2 49.0 %shard_map.151 = (f32[1024,1024]{1,0:T(8,128)}, f32[1024,1024]{1,0:T(8,128)}, f32[1024,1024]{1,0:T(8,128)}) custom-call(s32[3]{0:T(128)S(1)} %pad_add_fusion.limit_ref, bf16[8,128,1024]{2,1,0:T(8,128)(2,1)S(1)} %all-to-all-done.1.landed_ref, f32[1024,1024]{1,0:T(8,128)} %bitcast.225, f32[1024,1024]{1,0:T(8,128)} %bitcast.182), custom_call_target="tpu_custom_call" | custom-call | flops 32212254720 | bytes 23068672 | tf_op jit(solution)/shard_map/pallas_call | solution.py:441
  (442 shorter events, 235.2 us)
Async XLA Ops:
  2.8 47.8 %collective-permute-start = (bf16[512,1024]{1,0:T(8,128)(2,1)}, bf16[512,1024]{1,0:T(8,128)(2,1)S(1)}, u32[]{:S(2)}, u32[]{:S(2)}) collective-permute-start(bf16[512,1024]{1,0:T(8,128)(2,1)} %param.8), channel_id=1, source_target_pairs={{0,2},{1,3},{2,0},{3,1},{4,6},{5,7},{6,4},{7,5},{8,10},{9,11},{10,... | collective-permute-start | bytes 3145736 | tf_op jit(solution)/shard_map/ppermute | solution.py:469
  19.4 59.9 %all-to-all-start = ((bf16[8,128,1024]{2,1,0:T(8,128)(2,1)}), bf16[8,128,1024]{2,1,0:T(8,128)(2,1)}, u32[]{:S(2)}, u32[]{:S(2)}) async-start(bf16[8,128,1024]{2,1,0:T(8,128)(2,1)} %pad_select_fusion), calls=%async_computation | async-start | bytes 4194304 | tf_op jit(solution)/shard_map/all_to_all | solution.py:634
  26.6 32.7 %collective-permute-start.8 = (bf16[256,1024]{1,0:T(8,128)(2,1)S(1)}, bf16[256,1024]{1,0:T(8,128)(2,1)}, u32[]{:S(2)}, u32[]{:S(2)}) collective-permute-start(bf16[256,1024]{1,0:T(8,128)(2,1)S(1)} %get-tuple-element.184), channel_id=1, source_target_pairs={{0,2},{1,3},{2,0},{3,1},{4,6},{5,7},{6,4},{7,5},{8,10},{9,11},{10,... | collective-permute-start | bytes 1572872 | tf_op jit(solution)/shard_map/ppermute | solution.py:469
  26.6 33.0 %collective-permute-start.11 = (bf16[256,1024]{1,0:T(8,128)(2,1)S(1)}, bf16[256,1024]{1,0:T(8,128)(2,1)}, u32[]{:S(2)}, u32[]{:S(2)}) collective-permute-start(bf16[256,1024]{1,0:T(8,128)(2,1)S(1)} %get-tuple-element.183), channel_id=1, source_target_pairs={{0,2},{1,3},{2,0},{3,1},{4,6},{5,7},{6,4},{7,5},{8,10},{9,11},{10,... | collective-permute-start | bytes 1572872 | tf_op jit(solution)/shard_map/ppermute | solution.py:469
  28.6 31.2 %collective-permute-start.9 = (bf16[256,1024]{1,0:T(8,128)(2,1)S(1)}, bf16[256,1024]{1,0:T(8,128)(2,1)}, u32[]{:S(2)}, u32[]{:S(2)}) collective-permute-start(bf16[256,1024]{1,0:T(8,128)(2,1)S(1)} %get-tuple-element.184), channel_id=1, source_target_pairs={{0,1},{1,0},{2,3},{3,2},{4,5},{5,4},{6,7},{7,6},{8,9},{9,8},{10,11... | collective-permute-start | bytes 1572872 | tf_op jit(solution)/shard_map/ppermute | solution.py:469
  30.2 20.5 %collective-permute-start.7 = (f32[8,768]{1,0:T(8,128)S(1)}, f32[8,768]{1,0:T(8,128)S(1)}, u32[]{:S(2)}, u32[]{:S(2)}) collective-permute-start(f32[8,768]{1,0:T(8,128)S(1)} %maximum_select_fusion.17), channel_id=1, source_target_pairs={{0,2},{1,3},{2,0},{3,1},{4,6},{5,7},{6,4},{7,5},{8,10},{9,11},{10,... | collective-permute-start | bytes 73736 | tf_op jit(solution)/shard_map/ppermute | solution.py:571
  83.3 17.1 %collective-permute-start.17 = (bf16[1,1,1,128,512]{4,3,2,1,0:T(8,128)(2,1)S(1)}, bf16[1,1,1,128,512]{4,3,2,1,0:T(8,128)(2,1)S(1)}, u32[]{:S(2)}, u32[]{:S(2)}) collective-permute-start(bf16[1,1,1,128,512]{4,3,2,1,0:T(8,128)(2,1)S(1)} %get-tuple-element.193), channel_id=1, source_target_pairs={{0,16},{4,20},{8,24},{12,28},{16,0},{20,4},{24,8},{28,12},{1,17},{... | collective-permute-start | bytes 393224 | tf_op jit(solution)/shard_map/ppermute | solution.py:502
  83.8 22.2 %collective-permute-start.20 = (bf16[1,1,1,128,1024]{4,3,2,1,0:T(8,128)(2,1)S(1)}, bf16[1,1,1,128,1024]{4,3,2,1,0:T(8,128)(2,1)S(1)}, u32[]{:S(2)}, u32[]{:S(2)}) collective-permute-start(bf16[1,1,1,128,1024]{4,3,2,1,0:T(8,128)(2,1)S(1)} %get-tuple-element.166), channel_id=1, source_target_pairs={{0,16},{4,20},{8,24},{12,28},{16,0},{20,4},{24,8},{28,12},{1,17},{... | collective-permute-start | bytes 786440 | tf_op jit(solution)/shard_map/ppermute | solution.py:502
  106.1 17.2 %collective-permute-start.24 = (bf16[2,1,1,128,1024]{4,3,2,1,0:T(8,128)(2,1)S(1)}, bf16[2,1,1,128,1024]{4,3,2,1,0:T(8,128)(2,1)S(1)}, u32[]{:S(2)}, u32[]{:S(2)}) collective-permute-start(bf16[2,1,1,128,1024]{4,3,2,1,0:T(8,128)(2,1)S(1)} %maximum_select_fusion.8), channel_id=1, source_target_pairs={{0,4},{4,0},{8,12},{12,8},{16,20},{20,16},{24,28},{28,24},{1,5},{5... | collective-permute-start | bytes 1572872 | tf_op jit(solution)/shard_map/ppermute | solution.py:502
  112.0 19.7 %collective-permute-start.16 = (bf16[2,2,1,128,512]{4,3,2,1,0:T(8,128)(2,1)S(1)}, bf16[2,2,1,128,512]{4,3,2,1,0:T(8,128)(2,1)S(1)}, u32[]{:S(2)}, u32[]{:S(2)}) collective-permute-start(bf16[2,2,1,128,512]{4,3,2,1,0:T(8,128)(2,1)S(1)} %maximum_select_fusion.6), channel_id=1, source_target_pairs={{0,4},{4,0},{8,12},{12,8},{16,20},{20,16},{24,28},{28,24},{1,5},{5... | collective-permute-start | bytes 1572872 | tf_op jit(solution)/shard_map/ppermute | solution.py:502
  119.4 25.6 %collective-permute-start.25 = (bf16[2,1,1,128,1024]{4,3,2,1,0:T(8,128)(2,1)S(1)}, bf16[2,1,1,128,1024]{4,3,2,1,0:T(8,128)(2,1)S(1)}, u32[]{:S(2)}, u32[]{:S(2)}) collective-permute-start(bf16[2,1,1,128,1024]{4,3,2,1,0:T(8,128)(2,1)S(1)} %maximum_select_fusion.9), channel_id=1, source_target_pairs={{0,8},{4,12},{8,0},{12,4},{16,24},{20,28},{24,16},{28,20},{1,9},{5... | collective-permute-start | bytes 1572872 | tf_op jit(solution)/shard_map/ppermute | solution.py:502
  147.2 25.1 %collective-permute-start.29 = (bf16[2,2,1,128,1024]{4,3,2,1,0:T(8,128)(2,1)S(1)}, bf16[2,2,1,128,1024]{4,3,2,1,0:T(8,128)(2,1)S(1)}, u32[]{:S(2)}, u32[]{:S(2)}) collective-permute-start(bf16[2,2,1,128,1024]{4,3,2,1,0:T(8,128)(2,1)S(1)} %maximum_select_fusion.5), channel_id=1, source_target_pairs={{0,4},{4,0},{8,12},{12,8},{16,20},{20,16},{24,28},{28,24},{1,5},{5... | collective-permute-start | bytes 3145736 | tf_op jit(solution)/shard_map/ppermute | solution.py:502
  149.0 26.1 %collective-permute-start.23 = (bf16[512,1024]{1,0:T(8,128)(2,1)S(1)}, bf16[512,1024]{1,0:T(8,128)(2,1)S(1)}, u32[]{:S(2)}, u32[]{:S(2)}) collective-permute-start(bf16[512,1024]{1,0:T(8,128)(2,1)S(1)} %pad_maximum_fusion.3), channel_id=1, source_target_pairs={{0,2},{1,3},{2,0},{3,1},{4,6},{5,7},{6,4},{7,5},{8,10},{9,11},{10,... | collective-permute-start | bytes 3145736 | tf_op jit(solution)/shard_map/ppermute | solution.py:469
  151.0 27.0 %collective-permute-start.30 = (bf16[2,1,2,128,1024]{4,3,2,1,0:T(8,128)(2,1)S(1)}, bf16[2,1,2,128,1024]{4,3,2,1,0:T(8,128)(2,1)S(1)}, u32[]{:S(2)}, u32[]{:S(2)}) collective-permute-start(bf16[2,1,2,128,1024]{4,3,2,1,0:T(8,128)(2,1)S(1)} %maximum_select_fusion.4), channel_id=1, source_target_pairs={{0,8},{4,12},{8,0},{12,4},{16,24},{20,28},{24,16},{28,20},{1,9},{5... | collective-permute-start | bytes 3145736 | tf_op jit(solution)/shard_map/ppermute | solution.py:502
  154.1 42.3 %collective-permute-start.27 = (bf16[512,1024]{1,0:T(8,128)(2,1)S(1)}, bf16[512,1024]{1,0:T(8,128)(2,1)S(1)}, u32[]{:S(2)}, u32[]{:S(2)}) collective-permute-start(bf16[512,1024]{1,0:T(8,128)(2,1)S(1)} %pad_maximum_fusion.4), channel_id=1, source_target_pairs={{0,2},{1,3},{2,0},{3,1},{4,6},{5,7},{6,4},{7,5},{8,10},{9,11},{10,... | collective-permute-start | bytes 3145736 | tf_op jit(solution)/shard_map/ppermute | solution.py:469
  178.0 20.2 %collective-permute-start.28 = (bf16[512,1024]{1,0:T(8,128)(2,1)S(1)}, bf16[512,1024]{1,0:T(8,128)(2,1)S(1)}, u32[]{:S(2)}, u32[]{:S(2)}) collective-permute-start(bf16[512,1024]{1,0:T(8,128)(2,1)S(1)} %get-tuple-element.152.refs_0_), channel_id=1, source_target_pairs={{0,1},{1,0},{2,3},{3,2},{4,5},{5,4},{6,7},{7,6},{8,9},{9,8},{10,11... | collective-permute-start | bytes 3145736 | tf_op jit(solution)/shard_map/ppermute | solution.py:469
  216.7 25.5 %collective-permute-start.35 = (bf16[512,1024]{1,0:T(8,128)(2,1)}, bf16[512,1024]{1,0:T(8,128)(2,1)}, u32[]{:S(2)}, u32[]{:S(2)}) collective-permute-start(bf16[512,1024]{1,0:T(8,128)(2,1)} %pad_maximum_fusion.6), channel_id=1, source_target_pairs={{0,2},{1,3},{2,0},{3,1},{4,6},{5,7},{6,4},{7,5},{8,10},{9,11},{10,... | collective-permute-start | bytes 3145736 | tf_op jit(solution)/shard_map/ppermute | solution.py:469
  280.6 37.0 %collective-permute-start.43 = (bf16[2,1,2,128,1024]{4,3,2,1,0:T(8,128)(2,1)}, bf16[2,1,2,128,1024]{4,3,2,1,0:T(8,128)(2,1)}, u32[]{:S(2)}, u32[]{:S(2)}) collective-permute-start(bf16[2,1,2,128,1024]{4,3,2,1,0:T(8,128)(2,1)} %constant_dynamic-slice_fusion.9), channel_id=1, source_target_pairs={{0,8},{4,12},{8,0},{12,4},{16,24},{20,28},{24,16},{28,20},{1,9},{5... | collective-permute-start | bytes 3145736 | tf_op jit(solution)/shard_map/ppermute | solution.py:502
  284.1 25.1 %collective-permute-start.34 = (bf16[512,1024]{1,0:T(8,128)(2,1)}, bf16[512,1024]{1,0:T(8,128)(2,1)}, u32[]{:S(2)}, u32[]{:S(2)}) collective-permute-start(bf16[512,1024]{1,0:T(8,128)(2,1)} %pad_maximum_fusion.5), channel_id=1, source_target_pairs={{0,2},{1,3},{2,0},{3,1},{4,6},{5,7},{6,4},{7,5},{8,10},{9,11},{10,... | collective-permute-start | bytes 3145736 | tf_op jit(solution)/shard_map/ppermute | solution.py:469
  294.4 26.6 %collective-permute-start.42 = (bf16[2,2,1,128,1024]{4,3,2,1,0:T(8,128)(2,1)}, bf16[2,2,1,128,1024]{4,3,2,1,0:T(8,128)(2,1)}, u32[]{:S(2)}, u32[]{:S(2)}) collective-permute-start(bf16[2,2,1,128,1024]{4,3,2,1,0:T(8,128)(2,1)} %constant_dynamic-slice_fusion.10), channel_id=1, source_target_pairs={{0,4},{4,0},{8,12},{12,8},{16,20},{20,16},{24,28},{28,24},{1,5},{5... | collective-permute-start | bytes 3145736 | tf_op jit(solution)/shard_map/ppermute | solution.py:502
  313.1 18.5 %collective-permute-start.41 = (bf16[512,1024]{1,0:T(8,128)(2,1)S(1)}, bf16[512,1024]{1,0:T(8,128)(2,1)S(1)}, u32[]{:S(2)}, u32[]{:S(2)}) collective-permute-start(bf16[512,1024]{1,0:T(8,128)(2,1)S(1)} %get-tuple-element.100.refs_0_), channel_id=1, source_target_pairs={{0,1},{1,0},{2,3},{3,2},{4,5},{5,4},{6,7},{7,6},{8,9},{9,8},{10,11... | collective-permute-start | bytes 3145736 | tf_op jit(solution)/shard_map/ppermute | solution.py:469
  326.1 58.3 %collective-permute-start.39 = (bf16[256,1024]{1,0:T(8,128)(2,1)}, bf16[256,1024]{1,0:T(8,128)(2,1)}, u32[]{:S(2)}, u32[]{:S(2)}) collective-permute-start(bf16[256,1024]{1,0:T(8,128)(2,1)} %slice.401), channel_id=1, source_target_pairs={{0,2},{1,3},{2,0},{3,1},{4,6},{5,7},{6,4},{7,5},{8,10},{9,11},{10,... | collective-permute-start | bytes 1572872 | tf_op jit(solution)/shard_map/ppermute | solution.py:469
  330.3 138.6 %collective-permute-start.37 = (bf16[256,1024]{1,0:T(8,128)(2,1)}, bf16[256,1024]{1,0:T(8,128)(2,1)}, u32[]{:S(2)}, u32[]{:S(2)}) collective-permute-start(bf16[256,1024]{1,0:T(8,128)(2,1)} %slice.402), channel_id=1, source_target_pairs={{0,2},{1,3},{2,0},{3,1},{4,6},{5,7},{6,4},{7,5},{8,10},{9,11},{10,... | collective-permute-start | bytes 1572872 | tf_op jit(solution)/shard_map/ppermute | solution.py:469
  334.1 24.7 %collective-permute-start.45 = (bf16[1,1,2,128,1024]{4,3,2,1,0:T(8,128)(2,1)}, bf16[1,1,2,128,1024]{4,3,2,1,0:T(8,128)(2,1)}, u32[]{:S(2)}, u32[]{:S(2)}) collective-permute-start(bf16[1,1,2,128,1024]{4,3,2,1,0:T(8,128)(2,1)} %constant_dynamic-slice_fusion.7), channel_id=1, source_target_pairs={{0,16},{4,20},{8,24},{12,28},{16,0},{20,4},{24,8},{28,12},{1,17},{... | collective-permute-start | bytes 1572872 | tf_op jit(solution)/shard_map/ppermute | solution.py:502
  336.5 24.5 %collective-permute-start.44 = (bf16[2,1,1,128,1024]{4,3,2,1,0:T(8,128)(2,1)}, bf16[2,1,1,128,1024]{4,3,2,1,0:T(8,128)(2,1)}, u32[]{:S(2)}, u32[]{:S(2)}) collective-permute-start(bf16[2,1,1,128,1024]{4,3,2,1,0:T(8,128)(2,1)} %constant_dynamic-slice_fusion.8), channel_id=1, source_target_pairs={{0,8},{4,12},{8,0},{12,4},{16,24},{20,28},{24,16},{28,20},{1,9},{5... | collective-permute-start | bytes 1572872 | tf_op jit(solution)/shard_map/ppermute | solution.py:502
  378.1 66.5 %collective-permute-start.54 = (bf16[1,1,1,128,1024]{4,3,2,1,0:T(8,128)(2,1)}, bf16[1,1,1,128,1024]{4,3,2,1,0:T(8,128)(2,1)S(1)}, u32[]{:S(2)}, u32[]{:S(2)}) collective-permute-start(bf16[1,1,1,128,1024]{4,3,2,1,0:T(8,128)(2,1)} %constant_dynamic-slice_fusion.1), channel_id=1, source_target_pairs={{0,4},{4,0},{8,12},{12,8},{16,20},{20,16},{24,28},{28,24},{1,5},{5... | collective-permute-start | bytes 786440 | tf_op jit(solution)/shard_map/ppermute | solution.py:502
  379.3 17.3 %collective-permute-start.48 = (bf16[2,2,1,128,512]{4,3,2,1,0:T(8,128)(2,1)S(1)}, bf16[2,2,1,128,512]{4,3,2,1,0:T(8,128)(2,1)S(1)}, u32[]{:S(2)}, u32[]{:S(2)}) collective-permute-start(bf16[2,2,1,128,512]{4,3,2,1,0:T(8,128)(2,1)S(1)} %constant_dynamic-slice_fusion.6), channel_id=1, source_target_pairs={{0,4},{4,0},{8,12},{12,8},{16,20},{20,16},{24,28},{28,24},{1,5},{5... | collective-permute-start | bytes 1572872 | tf_op jit(solution)/shard_map/ppermute | solution.py:502
  382.9 54.6 %collective-permute-start.46 = (bf16[1024,1024]{1,0:T(8,128)(2,1)S(1)}, bf16[1024,1024]{1,0:T(8,128)(2,1)S(1)}, u32[]{:S(2)}, u32[]{:S(2)}) collective-permute-start(bf16[1024,1024]{1,0:T(8,128)(2,1)S(1)} %add_convert_fusion), channel_id=1, source_target_pairs={{0,1},{1,0},{2,3},{3,2},{4,5},{5,4},{6,7},{7,6},{8,9},{9,8},{10,11... | collective-permute-start | bytes 6291464 | tf_op jit(solution)/shard_map/ppermute | solution.py:469
  396.6 48.8 %collective-permute-start.55 = (bf16[1,1,1,128,1024]{4,3,2,1,0:T(8,128)(2,1)S(1)}, bf16[1,1,1,128,1024]{4,3,2,1,0:T(8,128)(2,1)S(1)}, u32[]{:S(2)}, u32[]{:S(2)}) collective-permute-start(bf16[1,1,1,128,1024]{4,3,2,1,0:T(8,128)(2,1)S(1)} %constant_dynamic-slice_fusion), channel_id=1, source_target_pairs={{0,16},{4,20},{8,24},{12,28},{16,0},{20,4},{24,8},{28,12},{1,17},{... | collective-permute-start | bytes 786440 | tf_op jit(solution)/shard_map/ppermute | solution.py:502
  440.5 23.3 %collective-permute-start.47 = (bf16[512,1024]{1,0:T(8,128)(2,1)}, bf16[512,1024]{1,0:T(8,128)(2,1)}, u32[]{:S(2)}, u32[]{:S(2)}) collective-permute-start(bf16[512,1024]{1,0:T(8,128)(2,1)} %slice.400), channel_id=1, source_target_pairs={{0,2},{1,3},{2,0},{3,1},{4,6},{5,7},{6,4},{7,5},{8,10},{9,11},{10,... | collective-permute-start | bytes 3145736 | tf_op jit(solution)/shard_map/ppermute | solution.py:469
  446.2 60.0 %all-to-all-start.1 = ((bf16[8,128,1024]{2,1,0:T(8,128)(2,1)}), bf16[8,128,1024]{2,1,0:T(8,128)(2,1)S(1)}, u32[]{:S(2)}, u32[]{:S(2)}) async-start(bf16[8,128,1024]{2,1,0:T(8,128)(2,1)} %fusion.44), calls=%async_computation.1 | async-start | bytes 4194304 | tf_op jit(solution)/shard_map/all_to_all | solution.py:802
  475.0 20.3 %collective-permute-start.58 = (f32[4,384]{1,0:T(4,128)S(1)}, f32[4,384]{1,0:T(4,128)S(1)}, u32[]{:S(2)}, u32[]{:S(2)}) collective-permute-start(f32[4,384]{1,0:T(4,128)S(1)} %slice_select_fusion.2), channel_id=1, source_target_pairs={{0,16},{4,20},{8,24},{12,28},{16,0},{20,4},{24,8},{28,12},{1,17},{... | collective-permute-start | bytes 18440 | tf_op jit(solution)/shard_map/ppermute | solution.py:591
  (105 other events, 910.0 us)

commit v5 on v4

--- a/solution.py
+++ b/solution.py
@@ -392,20 +392,22 @@
         now = lax.rem(turn, 2)
         later = 1 - now
 
-        def gram_rows(r, c):
-            rows = at_rows(r, tile)
-            gram[rows, :] = mm(x_buf[now, rows, :], x_buf[now], NT).astype(BF16)
-            return c
-
-        lax.fori_loop(0, tiles, gram_rows, 0)
-
-        def poly_rows(r, c):
-            rows = at_rows(r, tile)
-            mine = gram[rows, :]
-            poly[rows, :] = (ns_b * mine.astype(F32) + ns_c * mm(mine, gram[...])).astype(BF16)
-            return c
-
-        lax.fori_loop(0, tiles, poly_rows, 0)
+        for r in range(size // TILE):
+            rows, rest = slice(r * TILE, (r + 1) * TILE), slice(r * TILE, size)
+            value = mm(x_buf[now, rows, :], x_buf[now, rest, :], NT).astype(BF16)
+            gram[rows, rest] = value
+            for c in range(r + 1, size // TILE):
+                block_rows = slice(c * TILE, (c + 1) * TILE)
+                gram[block_rows, rows] = value[:, (c - r) * TILE : (c - r + 1) * TILE].T
+
+        for r in range(size // TILE):
+            rows, rest = slice(r * TILE, (r + 1) * TILE), slice(r * TILE, size)
+            square = mm(gram[rows, :], gram[:, rest])
+            value = (ns_b * gram[rows, rest].astype(F32) + ns_c * square).astype(BF16)
+            poly[rows, rest] = value
+            for c in range(r + 1, size // TILE):
+                block_rows = slice(c * TILE, (c + 1) * TILE)
+                poly[block_rows, rows] = value[:, (c - r) * TILE : (c - r + 1) * TILE].T
 
         def next_rows(r, c):
             rows = at_rows(r, tile)
@@ -625,14 +627,15 @@
     owned = owner_row == data_idx
     slot_value = master_slots[0]
 
-    params = small_gather(small_master.reshape(1, -1), "dp", 0)
+    group_params = small_gather(small_master.reshape(1, -1), "tensor", 1)
+    params = small_gather(group_params, "dp", 0)
     slot_low = slot_value.astype(BF16)
     offer_out = slot_low[:head_width].reshape(data_count, share_out, tensor_count, head_width)
     offer_out = jnp.swapaxes(offer_out, 1, 2).reshape(data_count, share, head_width)
     offer_out = jnp.pad(offer_out, ((0, 0), (0, 0), (width - head_width, 0)))
     offer = jnp.where(owned[1], offer_out, slot_low.reshape(data_count, share, width))
     shares = lax.all_to_all(after(offer, params), "dp", 0, 0)
-    params = small_gather(params, "tensor", 1).reshape(-1)
+    params = params.reshape(-1)
 
     def own_slice(start, size):
         return lax.dynamic_slice_in_dim(params, start + tensor_idx * size, size, 0)
@@ -651,10 +654,10 @@
     rows_of = [slice(chunk * part, (chunk + 1) * part) for chunk in range(CHUNKS)]
     rows_in = inputs.astype(F32)
     unit_one, scale_one = norm_parts(rows_in)
-    inputs_four = gather_four(inputs)
+    inputs_four = gather_four(after(inputs, group_params))
     unit_all, _ = norm_parts(jnp.concatenate(inputs_four).astype(F32))
     normed_all = (unit_all * gain_one + shift_one).astype(BF16)
-    dy_four = [gather_four(out_grad[rows]) for rows in rows_of]
+    dy_four = [gather_four(after(out_grad[rows], inputs_four[1])) for rows in rows_of]
     dy_all = [jnp.concatenate(four) for four in dy_four]
 
     shares = after(shares, normed_all, *dy_all)
@@ -667,30 +670,38 @@
     piece_vo = jnp.concatenate(
         [first[:, split : split + head_width], share_of(1)[:, width - head_width :]], axis=1
     )
-    w_qk = gather_by(first[:, :split], last_bits(2, 1))
-    w_vo = gather_by(piece_vo, last_bits(1, 2))
+    bits_qk, bits_vo = last_bits(2, 1), last_bits(1, 2)
+    one_qk = double(open_piece(first[:, :split]), bits_qk[0])
+    one_vo = double(open_piece(piece_vo), bits_vo[0])
+    w_qk, w_vo = one_qk, one_vo
+    for bit in bits_qk[1:]:
+        w_qk = double(w_qk, bit)
+    for bit in bits_vo[1:]:
+        w_vo = double(w_vo, bit)
+    w_qk, w_vo = rows2(w_qk), rows2(w_vo)
     w_v = w_vo[:, :head_width]
     w_out = w_vo[:, head_width:].reshape(data_count, tensor_count, share_out, head_width)
     w_out = jnp.swapaxes(w_out, 1, 2).reshape(head_width, width)
     bits_proj = last_bits(1, 2)
     bits_fc = last_bits(2, 1)
-    w_proj = double(open_piece(share_of(3)), bits_proj[0])
+    w_proj = double(open_piece(after(share_of(3), one_qk, one_vo)), bits_proj[0])
     w_fc = double(open_piece(after(share_of(2), w_proj)), bits_fc[0])
     bias_qk = jnp.concatenate([bias_query, jnp.zeros_like(bias_query)])
     scale_qk = jnp.where(jnp.arange(split) < head_width, HEAD_DIM**-0.5, 1.0)
     qk = ((mm(normed_all, w_qk) + bias_qk) * scale_qk).astype(BF16)
     values = (mm(normed_all, w_v) + bias_value).astype(BF16)
-    qk, values = after((qk, values), w_proj, w_fc)
     qk = qk.reshape(2, 2, rows_dev, split)
     values = values.reshape(2, 2, rows_dev, head_width)
 
+    first_steps = (w_proj, w_fc)
     for bit in bits_proj[1:-1]:
         w_proj = double(w_proj, bit)
     for bit in bits_fc[1:-1]:
         w_fc = double(w_fc, bit)
     mixed, log_sums, parts = [], [], []
     for chunk in range(CHUNKS):
-        mixed_one, sums_one = attend(core, qk, values, chunk, CHUNKS)
+        late = (qk, values) if chunk == 0 else after((qk, values), *first_steps)
+        mixed_one, sums_one = attend(core, *late, chunk, CHUNKS)
         if chunk > 0:
             mixed_one = after(mixed_one, w_proj, w_fc)
         mixed.append(mixed_one)
@@ -713,29 +724,24 @@
         middles.append(middle[:part])
         mine_two.append((unit_two, scale_two))
 
-    acts, backs, wholes, parts = [], [], [], []
+    acts, backs, wholes, parts, sums_two = [], [], [], [], []
     grad_proj, grad_fc, fc_bias_grad = 0.0, 0.0, 0.0
     for chunk in range(CHUNKS):
         block = (normed_two[chunk], swap(normed_two[chunk], 1))
         if chunk > 0:
             block = after(block, parts[-1])
         act, back, sums, whole = hidden_layer(block, w_fc, bias_fc, back_act[chunk])
-        parts.append(scatter_begin([after(back, branches[-1])], [w_fc], NT))
-        act, back, whole = after((act, back, whole), parts[-1])
-        grad_proj = grad_proj + mm(act, dy_all[chunk], TN)
-        grad_fc = grad_fc + mm(whole, back, TN)
+        parts.append(scatter_begin([after(back, *sums_two)], [w_fc], NT))
+        sums_two.append(exchange(parts[-1]))
         acts.append(act)
+        backs.append(back)
+        wholes.append(whole)
         fc_bias_grad = fc_bias_grad + sums[0]
-    half_proj = halve(spread(grad_proj.astype(BF16)), 1)
-    half_fc = halve(spread(grad_fc.astype(BF16)), 2)
-
     back_middles, back_lows, back_mixed, mids = [], [], [], []
     gain_two_grad, shift_two_grad = 0.0, 0.0
     for chunk in range(CHUNKS):
         unit_two, scale_two = mine_two[chunk]
-        grad = exchange(parts[chunk])
-        if chunk > 0:
-            grad = after(grad, back_lows[-1])
+        grad = after(sums_two[chunk], parts[-1], *back_lows[-1:])
         dy = jnp.concatenate(dy_four[chunk][:2]).astype(F32)
         back_middle = dy + norm_back(unit_two, scale_two, gain_two, grad)
         back_lows.append(back_middle.astype(BF16))
@@ -743,6 +749,10 @@
         shift_two_grad = shift_two_grad + jnp.sum(grad[:part], axis=0)
         back_middles.append(back_middle[:part])
         block = after((back_lows[-1], swap(back_lows[-1], 1)), parts[-1])
+        grad_rows = (acts[chunk], wholes[chunk], backs[chunk])
+        act, whole, back = after(grad_rows, parts[0] if chunk == 0 else back_lows[0])
+        grad_proj = grad_proj + mm(act, dy_all[chunk], TN)
+        grad_fc = grad_fc + mm(whole, back, TN)
         mixed_grad, mid = back_mix(block, w_out)
         back_mixed.append(mixed_grad.reshape(2, 2, part, head_width))
         mids.append(mid)
@@ -751,6 +761,9 @@
     proj_bias_grad = jnp.sum(out_grad, axis=0, dtype=F32)
     out_bias_grad = jnp.sum(back_middle, axis=0)
 
+    grad_proj, grad_fc = grad_proj.astype(BF16), grad_fc.astype(BF16)
+    half_proj = halve(spread(grad_proj), 1)
+    half_fc = halve(spread(grad_fc), 2)
     back_mixed, half_proj, half_fc = lax.optimization_barrier((back_mixed, half_proj, half_fc))
     steps = axis_bits("dp")
     rest_proj, rest_fc = steps[1:], steps[2:] + [1]
@@ -772,7 +785,7 @@
     share_qk = halve_by(half_qk, steps[1:])
     share_vo = halve_by(half_vo, [1] + steps[2:])
 
-    acts = after(acts, back_lows[-1])
+    acts = after(acts, grad_qk)
     branches = [scatter_end(scatter_begin([act], [w_proj], NN)) for act in acts]
     block_out = (middle + jnp.concatenate(branches) + bias_proj).astype(BF16)
     late_qk, late_v = after((back_qk, back_v), grad_qk, grad_vo)

time: 565 us -> 562 us (level)
  the two profiles are of different devices: /device:TPU:8 before, /device:TPU:6 now
where the time goes in v5:
time: 562 us; the launch traced here: 552 us
  waiting for transfers between devices  232 us (41%)
  Pallas kernels  90.2 us (16%)
  other arithmetic  62.2 us (11%)
  starting transfers between devices  57 us (10%)
  matrix products  53.7 us (10%)
  local copies, waits for them, and re-layouts  44.2 us (8%)
  between operations  13 us (2%)
    ppermute x24, waiting for transfers between devices, data_swap(): return lax.ppermute(value, 'dp', [(i, i ^ bit) for i in range(count)])  116 us
    ppermute x27, waiting for transfers between devices, swap(): return lax.ppermute(value, 'tensor', [(i, i ^ bit) for i in range(count)])  74.5 us
    dot_general x28, matrix products, mm(): return lax.dot_general(left, right, dims, preferred_element_type=F32)  53.7 us
    pallas_call x1, Pallas kernels, muon_update(): pl.pallas_call(partial(muon_kernel, out_rows=out_rows), in_specs=[pl.Bloc...  38.1 us
    ppermute x5, waiting for transfers between devices, small_gather(): other = lax.ppermute(piece, name, [(i, i ^ bit) for i in range(count)])  32.3 us
    ppermute x24, starting transfers between devices, data_swap(): return lax.ppermute(value, 'dp', [(i, i ^ bit) for i in range(count)])  23 us
    pallas_call x2, Pallas kernels, attend_back(): pl.pallas_call(partial(attend_back_kernel, heads=width // HEAD_DIM, chunk...  22 us
    pallas_call x2, Pallas kernels, hidden_layer(): pl.pallas_call(hidden_kernel, grid=(cols // tile,), in_specs=[whole] * le...  18.1 us
  transfers between devices with their start and end apart: 63, of which 27 were waited for; matrix products, arithmetic and copies ran while one was open for 23% of the time, Pallas kernels for 6%

profile of v5, /device:TPU:6, one launch (start us, length us, event | category | flops | bytes accessed | tf_op | source)
XLA Modules:
  0.0 552.0 jit_solution(15521042989124558193)
XLA Ops:
  18.2 6.9 %all-to-all-start = ((bf16[8,128,1024]{2,1,0:T(8,128)(2,1)}), bf16[8,128,1024]{2,1,0:T(8,128)(2,1)}, u32[]{:S(2)}, u32[]{:S(2)}) async-start(bf16[8,128,1024]{2,1,0:T(8,128)(2,1)} %pad_select_fusion), calls=%async_computation | async-start | bytes 4194304 | tf_op jit(solution)/shard_map/all_to_all | solution.py:637
  28.0 30.0 %collective-permute-done.6 = f32[2,1536]{1,0:T(2,128)S(1)} collective-permute-done((f32[2,1536]{1,0:T(2,128)S(1)}, f32[2,1536]{1,0:T(2,128)S(1)}, u32[]{:S(2)}, u32[]{:S(2)}) %collective-permute-start.6) | collective-permute-done | bytes 12320 | tf_op jit(solution)/shard_map/ppermute | solution.py:573
  58.0 4.7 collective-permute-start.7
  74.7 11.6 %collective-permute-done.8 = bf16[256,1024]{1,0:T(8,128)(2,1)} collective-permute-done((bf16[256,1024]{1,0:T(8,128)(2,1)S(1)}, bf16[256,1024]{1,0:T(8,128)(2,1)}, u32[]{:S(2)}, u32[]{:S(2)}) %collective-permute-start.8) | collective-permute-done | bytes 524320 | tf_op jit(solution)/shard_map/ppermute | solution.py:471
  86.3 10.3 %collective-permute-done.11 = bf16[256,1024]{1,0:T(8,128)(2,1)} collective-permute-done((bf16[256,1024]{1,0:T(8,128)(2,1)S(1)}, bf16[256,1024]{1,0:T(8,128)(2,1)}, u32[]{:S(2)}, u32[]{:S(2)}) %collective-permute-start.11) | collective-permute-done | bytes 524320 | tf_op jit(solution)/shard_map/ppermute | solution.py:471
  108.5 5.2 fusion.5
  118.2 8.4 %collective-permute-done.17 = bf16[1,1,1,128,512]{4,3,2,1,0:T(8,128)(2,1)S(1)} collective-permute-done((bf16[1,1,1,128,512]{4,3,2,1,0:T(8,128)(2,1)S(1)}, bf16[1,1,1,128,512]{4,3,2,1,0:T(8,128)(2,1)S(1)}, u32[]{:S(2)}, u32[]{:S(2)}) %collective-permute-start.17) | collective-permute-done | bytes 131104 | tf_op jit(solution)/shard_map/ppermute | solution.py:504
  132.4 10.8 %collective-permute-done.22 = bf16[1,1,1,128,1024]{4,3,2,1,0:T(8,128)(2,1)S(1)} collective-permute-done((bf16[1,1,1,128,1024]{4,3,2,1,0:T(8,128)(2,1)S(1)}, bf16[1,1,1,128,1024]{4,3,2,1,0:T(8,128)(2,1)S(1)}, u32[]{:S(2)}, u32[]{:S(2)}) %collective-permute-start.22) | collective-permute-done | bytes 262176 | tf_op jit(solution)/shard_map/ppermute | solution.py:504
  149.1 8.8 %collective-permute-done.23 = bf16[1,1,1,128,1024]{4,3,2,1,0:T(8,128)(2,1)S(1)} collective-permute-done((bf16[1,1,1,128,1024]{4,3,2,1,0:T(8,128)(2,1)S(1)}, bf16[1,1,1,128,1024]{4,3,2,1,0:T(8,128)(2,1)S(1)}, u32[]{:S(2)}, u32[]{:S(2)}) %collective-permute-start.23) | collective-permute-done | bytes 262176 | tf_op jit(solution)/shard_map/ppermute | solution.py:504
  158.2 6.9 %collective-permute-done.19 = bf16[2,1,2,128,512]{4,3,2,1,0:T(8,128)(2,1)S(1)} collective-permute-done((bf16[2,1,2,128,512]{4,3,2,1,0:T(8,128)(2,1)S(1)}, bf16[2,1,2,128,512]{4,3,2,1,0:T(8,128)(2,1)S(1)}, u32[]{:S(2)}, u32[]{:S(2)}) %collective-permute-start.19) | collective-permute-done | bytes 524320 | tf_op jit(solution)/shard_map/ppermute | solution.py:504
  178.9 5.9 %shard_map.144 = (bf16[2,2,256,256]{3,2,1,0:T(8,128)(2,1)S(1)}, f32[2,2,256,128]{3,2,1,0:T(8,128)S(1)}) custom-call(s32[1]{0:T(128)} %bitcast.core_ref, bf16[2,2,512,512]{3,2,1,0:T(8,128)(2,1)S(1)} %bitcast.165, bf16[2,2,512,512]{3,2,1,0:T(8,128)(2,1)S(1)} %bitcast.166, bf16[2,2,512,256]{3,2,1,0:T(8,128)(2,1)S(1)} %bitcast.172), custom_call_target="tpu_custom_call" | custom-call | flops 5000000000 | bytes 6000000 | tf_op jit(solution)/shard_map/pallas_call | solution.py:108
  191.4 20.5 %collective-permute-done.29 = bf16[2,2,1,128,1024]{4,3,2,1,0:T(8,128)(2,1)S(1)} collective-permute-done((bf16[2,2,1,128,1024]{4,3,2,1,0:T(8,128)(2,1)S(1)}, bf16[2,2,1,128,1024]{4,3,2,1,0:T(8,128)(2,1)S(1)}, u32[]{:S(2)}, u32[]{:S(2)}) %collective-permute-start.29) | collective-permute-done | bytes 1048608 | tf_op jit(solution)/shard_map/ppermute | solution.py:504
  222.5 12.6 %collective-permute-done.27 = bf16[512,1024]{1,0:T(8,128)(2,1)S(1)} collective-permute-done((bf16[512,1024]{1,0:T(8,128)(2,1)S(1)}, bf16[512,1024]{1,0:T(8,128)(2,1)S(1)}, u32[]{:S(2)}, u32[]{:S(2)}) %collective-permute-start.27) | collective-permute-done | bytes 1048608 | tf_op jit(solution)/shard_map/ppermute | solution.py:471
  235.5 8.7 %shard_map.145 = (bf16[1024,1024]{1,0:T(8,128)(2,1)S(1)}, bf16[1024,1024]{1,0:T(8,128)(2,1)}, f32[1,1024]{1,0:T(1,128)S(1)}, bf16[1024,1024]{1,0:T(8,128)(2,1)}) custom-call(bf16[512,1024]{1,0:T(8,128)(2,1)S(1)} %get-tuple-element.157.refs_0_, bf16[512,1024]{1,0:T(8,128)(2,1)S(1)} %collective-permute-done.28.refs_1_, bf16[1024,1024]{1,0:T(8,128)(2,1)} %bitcast.209, ...), custom_call_target="tpu_custom_call" | custom-call | flops 2147483648 | bytes 12000000 | tf_op jit(solution)/shard_map/pallas_call | solution.py:257
  259.1 5.9 %convolution_convert_fusion.refs_4_ = bf16[1024,1024]{1,0:T(8,128)(2,1)} fusion(bf16[1024,1024]{1,0:T(8,128)(2,1)} %copy-done.60, bf16[1024,1024]{1,0:T(8,128)(2,1)} %bitcast.204), kind=kOutput, calls=%fused_computation.63 | convolution fusion | flops 2148532224 | bytes 6291456 | tf_op jit(solution)/shard_map/dot_general | solution.py:44
  265.0 9.4 %shard_map.146 = (bf16[1024,1024]{1,0:T(8,128)(2,1)S(1)}, bf16[1024,1024]{1,0:T(8,128)(2,1)}, f32[1,1024]{1,0:T(1,128)S(1)}, bf16[1024,1024]{1,0:T(8,128)(2,1)}) custom-call(bf16[512,1024]{1,0:T(8,128)(2,1)S(1)} %get-tuple-element.87.refs_0_, bf16[512,1024]{1,0:T(8,128)(2,1)} %collective-permute-done.31.refs_1_, bf16[1024,1024]{1,0:T(8,128)(2,1)} %bitcast.210, ...), custom_call_target="tpu_custom_call" | custom-call | flops 2147483648 | bytes 12000000 | tf_op jit(solution)/shard_map/pallas_call | solution.py:257
  274.4 6.3 %collective-permute-done.33 = bf16[512,1024]{1,0:T(8,128)(2,1)} collective-permute-done((bf16[512,1024]{1,0:T(8,128)(2,1)}, bf16[512,1024]{1,0:T(8,128)(2,1)}, u32[]{:S(2)}, u32[]{:S(2)}) %collective-permute-start.33) | collective-permute-done | bytes 1048608 | tf_op jit(solution)/shard_map/ppermute | solution.py:471
  310.5 8.3 %collective-permute-done.36 = bf16[512,1024]{1,0:T(8,128)(2,1)S(1)} collective-permute-done((bf16[512,1024]{1,0:T(8,128)(2,1)S(1)}, bf16[512,1024]{1,0:T(8,128)(2,1)S(1)}, u32[]{:S(2)}, u32[]{:S(2)}) %collective-permute-start.36) | collective-permute-done | bytes 1048608 | tf_op jit(solution)/shard_map/ppermute | solution.py:471
  328.0 6.3 %collective-permute-done.39 = bf16[2,1,2,128,1024]{4,3,2,1,0:T(8,128)(2,1)} collective-permute-done((bf16[2,1,2,128,1024]{4,3,2,1,0:T(8,128)(2,1)}, bf16[2,1,2,128,1024]{4,3,2,1,0:T(8,128)(2,1)}, u32[]{:S(2)}, u32[]{:S(2)}) %collective-permute-start.39) | collective-permute-done | bytes 1048608 | tf_op jit(solution)/shard_map/ppermute | solution.py:504
  341.2 11.0 %shard_map.149 = (bf16[2,2,512,512]{3,2,1,0:T(8,128)(2,1)}, bf16[2,2,512,256]{3,2,1,0:T(8,128)(2,1)S(1)}) custom-call(s32[1]{0:T(128)} %bitcast.core_ref, bf16[2,2,512,512]{3,2,1,0:T(8,128)(2,1)} %bitcast.167, bf16[2,2,512,512]{3,2,1,0:T(8,128)(2,1)} %bitcast.168, bf16[2,2,512,256]{3,2,1,0:T(8,128)(2,1)S(1)} %bitcast.173, ...), custom_call_target="tpu_custom_call" | custom-call | flops 12000000000 | bytes 6000000 | tf_op jit(solution)/shard_map/pallas_call | solution.py:205
  357.3 7.2 %collective-permute-done.41 = bf16[1,1,2,128,1024]{4,3,2,1,0:T(8,128)(2,1)} collective-permute-done((bf16[1,1,2,128,1024]{4,3,2,1,0:T(8,128)(2,1)}, bf16[1,1,2,128,1024]{4,3,2,1,0:T(8,128)(2,1)}, u32[]{:S(2)}, u32[]{:S(2)}) %collective-permute-start.41) | collective-permute-done | bytes 524320 | tf_op jit(solution)/shard_map/ppermute | solution.py:504
  367.9 11.0 %shard_map.150 = (bf16[2,2,512,512]{3,2,1,0:T(8,128)(2,1)}, bf16[2,2,512,256]{3,2,1,0:T(8,128)(2,1)S(1)}) custom-call(s32[1]{0:T(128)} %bitcast.core_ref, bf16[2,2,512,512]{3,2,1,0:T(8,128)(2,1)} %bitcast.169, bf16[2,2,512,512]{3,2,1,0:T(8,128)(2,1)} %bitcast.170, ...), custom_call_target="tpu_custom_call", output_to_operand_aliasing={{0}: (10, {}), {1}: (11, {})} | custom-call | flops 12000000000 | bytes 6000000 | tf_op jit(solution)/shard_map/pallas_call | solution.py:205
  396.6 9.6 %collective-permute-done.51 = bf16[2,1,2,128,512]{4,3,2,1,0:T(8,128)(2,1)S(1)} collective-permute-done((bf16[2,1,2,128,512]{4,3,2,1,0:T(8,128)(2,1)S(1)}, bf16[2,1,2,128,512]{4,3,2,1,0:T(8,128)(2,1)S(1)}, u32[]{:S(2)}, u32[]{:S(2)}) %collective-permute-start.51) | collective-permute-done | bytes 524320 | tf_op jit(solution)/shard_map/ppermute | solution.py:504
  408.2 6.9 %collective-permute-done.52 = bf16[2,1,1,128,512]{4,3,2,1,0:T(8,128)(2,1)S(1)} collective-permute-done((bf16[2,1,1,128,512]{4,3,2,1,0:T(8,128)(2,1)S(1)}, bf16[2,1,1,128,512]{4,3,2,1,0:T(8,128)(2,1)S(1)}, u32[]{:S(2)}, u32[]{:S(2)}) %collective-permute-start.52) | collective-permute-done | bytes 262176 | tf_op jit(solution)/shard_map/ppermute | solution.py:504
  415.3 7.8 %collective-permute-done.49 = bf16[2,1,1,128,512]{4,3,2,1,0:T(8,128)(2,1)S(1)} collective-permute-done((bf16[2,1,1,128,512]{4,3,2,1,0:T(8,128)(2,1)S(1)}, bf16[2,1,1,128,512]{4,3,2,1,0:T(8,128)(2,1)S(1)}, u32[]{:S(2)}, u32[]{:S(2)}) %collective-permute-start.49) | collective-permute-done | bytes 262176 | tf_op jit(solution)/shard_map/ppermute | solution.py:504
  424.3 6.8 %collective-permute-done.53 = bf16[1,1,1,128,512]{4,3,2,1,0:T(8,128)(2,1)S(1)} collective-permute-done((bf16[1,1,1,128,512]{4,3,2,1,0:T(8,128)(2,1)S(1)}, bf16[1,1,1,128,512]{4,3,2,1,0:T(8,128)(2,1)S(1)}, u32[]{:S(2)}, u32[]{:S(2)}) %collective-permute-start.53) | collective-permute-done | bytes 131104 | tf_op jit(solution)/shard_map/ppermute | solution.py:504
  431.1 8.2 %collective-permute-done.50 = bf16[1,1,1,128,512]{4,3,2,1,0:T(8,128)(2,1)S(1)} collective-permute-done((bf16[1,1,1,128,512]{4,3,2,1,0:T(8,128)(2,1)S(1)}, bf16[1,1,1,128,512]{4,3,2,1,0:T(8,128)(2,1)S(1)}, u32[]{:S(2)}, u32[]{:S(2)}) %collective-permute-start.50) | collective-permute-done | bytes 131104 | tf_op jit(solution)/shard_map/ppermute | solution.py:504
  451.6 5.2 all-to-all-start.1
  463.3 20.1 %collective-permute-done.45 = bf16[256,1024]{1,0:T(8,128)(2,1)} collective-permute-done((bf16[256,1024]{1,0:T(8,128)(2,1)}, bf16[256,1024]{1,0:T(8,128)(2,1)}, u32[]{:S(2)}, u32[]{:S(2)}) %collective-permute-start.45) | collective-permute-done | bytes 524320 | tf_op jit(solution)/shard_map/ppermute | solution.py:471
  489.6 4.8 collective-permute-done.43
  499.5 5.7 %collective-permute-done.58 = f32[4,384]{1,0:T(4,128)S(1)} collective-permute-done((f32[4,384]{1,0:T(4,128)S(1)}, f32[4,384]{1,0:T(4,128)S(1)}, u32[]{:S(2)}, u32[]{:S(2)}) %collective-permute-start.58) | collective-permute-done | bytes 6176 | tf_op jit(solution)/shard_map/ppermute | solution.py:593
  513.6 38.1 %shard_map.151 = (f32[1024,1024]{1,0:T(8,128)}, f32[1024,1024]{1,0:T(8,128)}, f32[1024,1024]{1,0:T(8,128)}) custom-call(s32[3]{0:T(128)S(1)} %pad_add_fusion.limit_ref, bf16[8,128,1024]{2,1,0:T(8,128)(2,1)S(1)} %all-to-all-done.1.landed_ref, f32[1024,1024]{1,0:T(8,128)} %bitcast.230, f32[1024,1024]{1,0:T(8,128)} %bitcast.184), custom_call_target="tpu_custom_call" | custom-call | flops 32212254720 | bytes 23068672 | tf_op jit(solution)/shard_map/pallas_call | solution.py:443
  (453 shorter events, 209.0 us)
Async XLA Ops:
  6.3 56.3 %collective-permute-start.2 = (bf16[512,1024]{1,0:T(8,128)(2,1)}, bf16[512,1024]{1,0:T(8,128)(2,1)S(1)}, u32[]{:S(2)}, u32[]{:S(2)}) collective-permute-start(bf16[512,1024]{1,0:T(8,128)(2,1)} %param.8), channel_id=1, source_target_pairs={{0,2},{1,3},{2,0},{3,1},{4,6},{5,7},{6,4},{7,5},{8,10},{9,11},{10,... | collective-permute-start | bytes 3145736 | tf_op jit(solution)/shard_map/ppermute | solution.py:471
  18.2 95.5 %all-to-all-start = ((bf16[8,128,1024]{2,1,0:T(8,128)(2,1)}), bf16[8,128,1024]{2,1,0:T(8,128)(2,1)}, u32[]{:S(2)}, u32[]{:S(2)}) async-start(bf16[8,128,1024]{2,1,0:T(8,128)(2,1)} %pad_select_fusion), calls=%async_computation | async-start | bytes 4194304 | tf_op jit(solution)/shard_map/all_to_all | solution.py:637
  25.2 32.8 %collective-permute-start.6 = (f32[2,1536]{1,0:T(2,128)S(1)}, f32[2,1536]{1,0:T(2,128)S(1)}, u32[]{:S(2)}, u32[]{:S(2)}) collective-permute-start(f32[2,1536]{1,0:T(2,128)S(1)} %maximum_select_fusion.18), channel_id=1, source_target_pairs={{0,8},{4,12},{8,0},{12,4},{16,24},{20,28},{24,16},{28,20},{1,9},{5... | collective-permute-start | bytes 36872 | tf_op jit(solution)/shard_map/ppermute | solution.py:573
  70.9 29.2 %collective-permute-start.3 = (bf16[512,1024]{1,0:T(8,128)(2,1)S(1)}, bf16[512,1024]{1,0:T(8,128)(2,1)}, u32[]{:S(2)}, u32[]{:S(2)}) collective-permute-start(bf16[512,1024]{1,0:T(8,128)(2,1)S(1)} %copy-done.15), channel_id=1, source_target_pairs={{0,1},{1,0},{2,3},{3,2},{4,5},{5,4},{6,7},{7,6},{8,9},{9,8},{10,11... | collective-permute-start | bytes 3145736 | tf_op jit(solution)/shard_map/ppermute | solution.py:471
  72.9 23.8 %collective-permute-start.11 = (bf16[256,1024]{1,0:T(8,128)(2,1)S(1)}, bf16[256,1024]{1,0:T(8,128)(2,1)}, u32[]{:S(2)}, u32[]{:S(2)}) collective-permute-start(bf16[256,1024]{1,0:T(8,128)(2,1)S(1)} %get-tuple-element.72), channel_id=1, source_target_pairs={{0,2},{1,3},{2,0},{3,1},{4,6},{5,7},{6,4},{7,5},{8,10},{9,11},{10,... | collective-permute-start | bytes 1572872 | tf_op jit(solution)/shard_map/ppermute | solution.py:471
  73.5 28.6 %collective-permute-start.4 = (bf16[512,1024]{1,0:T(8,128)(2,1)S(1)}, bf16[512,1024]{1,0:T(8,128)(2,1)S(1)}, u32[]{:S(2)}, u32[]{:S(2)}) collective-permute-start(bf16[512,1024]{1,0:T(8,128)(2,1)S(1)} %collective-permute-done.2), channel_id=1, source_target_pairs={{0,1},{1,0},{2,3},{3,2},{4,5},{5,4},{6,7},{7,6},{8,9},{9,8},{10,11... | collective-permute-start | bytes 3145736 | tf_op jit(solution)/shard_map/ppermute | solution.py:471
  74.2 25.8 %collective-permute-start.12 = (bf16[256,1024]{1,0:T(8,128)(2,1)S(1)}, bf16[256,1024]{1,0:T(8,128)(2,1)S(1)}, u32[]{:S(2)}, u32[]{:S(2)}) collective-permute-start(bf16[256,1024]{1,0:T(8,128)(2,1)S(1)} %get-tuple-element.72), channel_id=1, source_target_pairs={{0,1},{1,0},{2,3},{3,2},{4,5},{5,4},{6,7},{7,6},{8,9},{9,8},{10,11... | collective-permute-start | bytes 1572872 | tf_op jit(solution)/shard_map/ppermute | solution.py:471
  143.5 21.6 %collective-permute-start.19 = (bf16[2,1,2,128,512]{4,3,2,1,0:T(8,128)(2,1)S(1)}, bf16[2,1,2,128,512]{4,3,2,1,0:T(8,128)(2,1)S(1)}, u32[]{:S(2)}, u32[]{:S(2)}) collective-permute-start(bf16[2,1,2,128,512]{4,3,2,1,0:T(8,128)(2,1)S(1)} %maximum_select_fusion.7), channel_id=1, source_target_pairs={{0,8},{4,12},{8,0},{12,4},{16,24},{20,28},{24,16},{28,20},{1,9},{5... | collective-permute-start | bytes 1572872 | tf_op jit(solution)/shard_map/ppermute | solution.py:504
  146.8 38.0 %collective-permute-start.24 = (bf16[2,1,1,128,1024]{4,3,2,1,0:T(8,128)(2,1)S(1)}, bf16[2,1,1,128,1024]{4,3,2,1,0:T(8,128)(2,1)S(1)}, u32[]{:S(2)}, u32[]{:S(2)}) collective-permute-start(bf16[2,1,1,128,1024]{4,3,2,1,0:T(8,128)(2,1)S(1)} %maximum_select_fusion.8), channel_id=1, source_target_pairs={{0,4},{4,0},{8,12},{12,8},{16,20},{20,16},{24,28},{28,24},{1,5},{5... | collective-permute-start | bytes 1572872 | tf_op jit(solution)/shard_map/ppermute | solution.py:504
  147.3 23.7 %collective-permute-start.16 = (bf16[2,2,1,128,512]{4,3,2,1,0:T(8,128)(2,1)S(1)}, bf16[2,2,1,128,512]{4,3,2,1,0:T(8,128)(2,1)S(1)}, u32[]{:S(2)}, u32[]{:S(2)}) collective-permute-start(bf16[2,2,1,128,512]{4,3,2,1,0:T(8,128)(2,1)S(1)} %maximum_select_fusion.6), channel_id=1, source_target_pairs={{0,4},{4,0},{8,12},{12,8},{16,20},{20,16},{24,28},{28,24},{1,5},{5... | collective-permute-start | bytes 1572872 | tf_op jit(solution)/shard_map/ppermute | solution.py:504
  158.0 27.0 %collective-permute-start.25 = (bf16[2,1,1,128,1024]{4,3,2,1,0:T(8,128)(2,1)S(1)}, bf16[2,1,1,128,1024]{4,3,2,1,0:T(8,128)(2,1)S(1)}, u32[]{:S(2)}, u32[]{:S(2)}) collective-permute-start(bf16[2,1,1,128,1024]{4,3,2,1,0:T(8,128)(2,1)S(1)} %maximum_select_fusion.9), channel_id=1, source_target_pairs={{0,8},{4,12},{8,0},{12,4},{16,24},{20,28},{24,16},{28,20},{1,9},{5... | collective-permute-start | bytes 1572872 | tf_op jit(solution)/shard_map/ppermute | solution.py:504
  186.7 25.1 %collective-permute-start.29 = (bf16[2,2,1,128,1024]{4,3,2,1,0:T(8,128)(2,1)S(1)}, bf16[2,2,1,128,1024]{4,3,2,1,0:T(8,128)(2,1)S(1)}, u32[]{:S(2)}, u32[]{:S(2)}) collective-permute-start(bf16[2,2,1,128,1024]{4,3,2,1,0:T(8,128)(2,1)S(1)} %maximum_select_fusion.5), channel_id=1, source_target_pairs={{0,4},{4,0},{8,12},{12,8},{16,20},{20,16},{24,28},{28,24},{1,5},{5... | collective-permute-start | bytes 3145736 | tf_op jit(solution)/shard_map/ppermute | solution.py:504
  187.7 26.1 %collective-permute-start.21 = (bf16[512,1024]{1,0:T(8,128)(2,1)S(1)}, bf16[512,1024]{1,0:T(8,128)(2,1)S(1)}, u32[]{:S(2)}, u32[]{:S(2)}) collective-permute-start(bf16[512,1024]{1,0:T(8,128)(2,1)S(1)} %pad_maximum_fusion.1), channel_id=1, source_target_pairs={{0,2},{1,3},{2,0},{3,1},{4,6},{5,7},{6,4},{7,5},{8,10},{9,11},{10,... | collective-permute-start | bytes 3145736 | tf_op jit(solution)/shard_map/ppermute | solution.py:471
  189.3 27.3 %collective-permute-start.30 = (bf16[2,1,2,128,1024]{4,3,2,1,0:T(8,128)(2,1)S(1)}, bf16[2,1,2,128,1024]{4,3,2,1,0:T(8,128)(2,1)S(1)}, u32[]{:S(2)}, u32[]{:S(2)}) collective-permute-start(bf16[2,1,2,128,1024]{4,3,2,1,0:T(8,128)(2,1)S(1)} %maximum_select_fusion.4), channel_id=1, source_target_pairs={{0,8},{4,12},{8,0},{12,4},{16,24},{20,28},{24,16},{28,20},{1,9},{5... | collective-permute-start | bytes 3145736 | tf_op jit(solution)/shard_map/ppermute | solution.py:504
  190.3 44.7 %collective-permute-start.27 = (bf16[512,1024]{1,0:T(8,128)(2,1)S(1)}, bf16[512,1024]{1,0:T(8,128)(2,1)S(1)}, u32[]{:S(2)}, u32[]{:S(2)}) collective-permute-start(bf16[512,1024]{1,0:T(8,128)(2,1)S(1)} %pad_maximum_fusion.2), channel_id=1, source_target_pairs={{0,2},{1,3},{2,0},{3,1},{4,6},{5,7},{6,4},{7,5},{8,10},{9,11},{10,... | collective-permute-start | bytes 3145736 | tf_op jit(solution)/shard_map/ppermute | solution.py:471
  216.6 18.9 %collective-permute-start.28 = (bf16[512,1024]{1,0:T(8,128)(2,1)S(1)}, bf16[512,1024]{1,0:T(8,128)(2,1)S(1)}, u32[]{:S(2)}, u32[]{:S(2)}) collective-permute-start(bf16[512,1024]{1,0:T(8,128)(2,1)S(1)} %get-tuple-element.157.refs_0_), channel_id=1, source_target_pairs={{0,1},{1,0},{2,3},{3,2},{4,5},{5,4},{6,7},{7,6},{8,9},{9,8},{10,11... | collective-permute-start | bytes 3145736 | tf_op jit(solution)/shard_map/ppermute | solution.py:471
  254.9 25.9 %collective-permute-start.33 = (bf16[512,1024]{1,0:T(8,128)(2,1)}, bf16[512,1024]{1,0:T(8,128)(2,1)}, u32[]{:S(2)}, u32[]{:S(2)}) collective-permute-start(bf16[512,1024]{1,0:T(8,128)(2,1)} %pad_maximum_fusion.3), channel_id=1, source_target_pairs={{0,2},{1,3},{2,0},{3,1},{4,6},{5,7},{6,4},{7,5},{8,10},{9,11},{10,... | collective-permute-start | bytes 3145736 | tf_op jit(solution)/shard_map/ppermute | solution.py:471
  293.2 25.6 %collective-permute-start.36 = (bf16[512,1024]{1,0:T(8,128)(2,1)S(1)}, bf16[512,1024]{1,0:T(8,128)(2,1)S(1)}, u32[]{:S(2)}, u32[]{:S(2)}) collective-permute-start(bf16[512,1024]{1,0:T(8,128)(2,1)S(1)} %pad_maximum_fusion.4), channel_id=1, source_target_pairs={{0,2},{1,3},{2,0},{3,1},{4,6},{5,7},{6,4},{7,5},{8,10},{9,11},{10,... | collective-permute-start | bytes 3145736 | tf_op jit(solution)/shard_map/ppermute | solution.py:471
  300.7 25.6 %collective-permute-start.38 = (bf16[2,2,1,128,1024]{4,3,2,1,0:T(8,128)(2,1)}, bf16[2,2,1,128,1024]{4,3,2,1,0:T(8,128)(2,1)}, u32[]{:S(2)}, u32[]{:S(2)}) collective-permute-start(bf16[2,2,1,128,1024]{4,3,2,1,0:T(8,128)(2,1)} %constant_dynamic-slice_fusion.10), channel_id=1, source_target_pairs={{0,4},{4,0},{8,12},{12,8},{16,20},{20,16},{24,28},{28,24},{1,5},{5... | collective-permute-start | bytes 3145736 | tf_op jit(solution)/shard_map/ppermute | solution.py:504
  308.7 25.5 %collective-permute-start.39 = (bf16[2,1,2,128,1024]{4,3,2,1,0:T(8,128)(2,1)}, bf16[2,1,2,128,1024]{4,3,2,1,0:T(8,128)(2,1)}, u32[]{:S(2)}, u32[]{:S(2)}) collective-permute-start(bf16[2,1,2,128,1024]{4,3,2,1,0:T(8,128)(2,1)} %constant_dynamic-slice_fusion.9), channel_id=1, source_target_pairs={{0,8},{4,12},{8,0},{12,4},{16,24},{20,28},{24,16},{28,20},{1,9},{5... | collective-permute-start | bytes 3145736 | tf_op jit(solution)/shard_map/ppermute | solution.py:504
  339.1 25.4 %collective-permute-start.41 = (bf16[1,1,2,128,1024]{4,3,2,1,0:T(8,128)(2,1)}, bf16[1,1,2,128,1024]{4,3,2,1,0:T(8,128)(2,1)}, u32[]{:S(2)}, u32[]{:S(2)}) collective-permute-start(bf16[1,1,2,128,1024]{4,3,2,1,0:T(8,128)(2,1)} %constant_dynamic-slice_fusion.7), channel_id=1, source_target_pairs={{0,16},{4,20},{8,24},{12,28},{16,0},{20,4},{24,8},{28,12},{1,17},{... | collective-permute-start | bytes 1572872 | tf_op jit(solution)/shard_map/ppermute | solution.py:504
  339.5 27.1 %collective-permute-start.40 = (bf16[2,1,1,128,1024]{4,3,2,1,0:T(8,128)(2,1)}, bf16[2,1,1,128,1024]{4,3,2,1,0:T(8,128)(2,1)}, u32[]{:S(2)}, u32[]{:S(2)}) collective-permute-start(bf16[2,1,1,128,1024]{4,3,2,1,0:T(8,128)(2,1)} %constant_dynamic-slice_fusion.8), channel_id=1, source_target_pairs={{0,8},{4,12},{8,0},{12,4},{16,24},{20,28},{24,16},{28,20},{1,9},{5... | collective-permute-start | bytes 1572872 | tf_op jit(solution)/shard_map/ppermute | solution.py:504
  383.4 59.0 %collective-permute-start.54 = (bf16[1,1,1,128,1024]{4,3,2,1,0:T(8,128)(2,1)}, bf16[1,1,1,128,1024]{4,3,2,1,0:T(8,128)(2,1)S(1)}, u32[]{:S(2)}, u32[]{:S(2)}) collective-permute-start(bf16[1,1,1,128,1024]{4,3,2,1,0:T(8,128)(2,1)} %constant_dynamic-slice_fusion.1), channel_id=1, source_target_pairs={{0,4},{4,0},{8,12},{12,8},{16,20},{20,16},{24,28},{28,24},{1,5},{5... | collective-permute-start | bytes 786440 | tf_op jit(solution)/shard_map/ppermute | solution.py:504
  385.3 65.6 %collective-permute-start.55 = (bf16[1,1,1,128,1024]{4,3,2,1,0:T(8,128)(2,1)S(1)}, bf16[1,1,1,128,1024]{4,3,2,1,0:T(8,128)(2,1)S(1)}, u32[]{:S(2)}, u32[]{:S(2)}) collective-permute-start(bf16[1,1,1,128,1024]{4,3,2,1,0:T(8,128)(2,1)S(1)} %constant_dynamic-slice_fusion), channel_id=1, source_target_pairs={{0,16},{4,20},{8,24},{12,28},{16,0},{20,4},{24,8},{28,12},{1,17},{... | collective-permute-start | bytes 786440 | tf_op jit(solution)/shard_map/ppermute | solution.py:504
  386.7 19.6 %collective-permute-start.48 = (bf16[2,2,1,128,512]{4,3,2,1,0:T(8,128)(2,1)S(1)}, bf16[2,2,1,128,512]{4,3,2,1,0:T(8,128)(2,1)S(1)}, u32[]{:S(2)}, u32[]{:S(2)}) collective-permute-start(bf16[2,2,1,128,512]{4,3,2,1,0:T(8,128)(2,1)S(1)} %constant_dynamic-slice_fusion.6), channel_id=1, source_target_pairs={{0,4},{4,0},{8,12},{12,8},{16,20},{20,16},{24,28},{28,24},{1,5},{5... | collective-permute-start | bytes 1572872 | tf_op jit(solution)/shard_map/ppermute | solution.py:504
  387.1 19.1 %collective-permute-start.51 = (bf16[2,1,2,128,512]{4,3,2,1,0:T(8,128)(2,1)S(1)}, bf16[2,1,2,128,512]{4,3,2,1,0:T(8,128)(2,1)S(1)}, u32[]{:S(2)}, u32[]{:S(2)}) collective-permute-start(bf16[2,1,2,128,512]{4,3,2,1,0:T(8,128)(2,1)S(1)} %fusion.32), channel_id=1, source_target_pairs={{0,8},{4,12},{8,0},{12,4},{16,24},{20,28},{24,16},{28,20},{1,9},{5... | collective-permute-start | bytes 1572872 | tf_op jit(solution)/shard_map/ppermute | solution.py:504
  393.0 53.6 %collective-permute-start.44 = (bf16[512,1024]{1,0:T(8,128)(2,1)S(1)}, bf16[512,1024]{1,0:T(8,128)(2,1)S(1)}, u32[]{:S(2)}, u32[]{:S(2)}) collective-permute-start(bf16[512,1024]{1,0:T(8,128)(2,1)S(1)} %convolution_convert_fusion.2), channel_id=1, source_target_pairs={{0,1},{1,0},{2,3},{3,2},{4,5},{5,4},{6,7},{7,6},{8,9},{9,8},{10,11... | collective-permute-start | bytes 3145736 | tf_op jit(solution)/shard_map/ppermute | solution.py:471
  406.2 37.1 %collective-permute-start.46 = (bf16[1024,1024]{1,0:T(8,128)(2,1)S(1)}, bf16[1024,1024]{1,0:T(8,128)(2,1)S(1)}, u32[]{:S(2)}, u32[]{:S(2)}) collective-permute-start(bf16[1024,1024]{1,0:T(8,128)(2,1)S(1)} %add_convert_fusion), channel_id=1, source_target_pairs={{0,1},{1,0},{2,3},{3,2},{4,5},{5,4},{6,7},{7,6},{8,9},{9,8},{10,11... | collective-permute-start | bytes 6291464 | tf_op jit(solution)/shard_map/ppermute | solution.py:471
  445.8 39.7 %collective-permute-start.47 = (bf16[512,1024]{1,0:T(8,128)(2,1)}, bf16[512,1024]{1,0:T(8,128)(2,1)}, u32[]{:S(2)}, u32[]{:S(2)}) collective-permute-start(bf16[512,1024]{1,0:T(8,128)(2,1)} %slice.401), channel_id=1, source_target_pairs={{0,2},{1,3},{2,0},{3,1},{4,6},{5,7},{6,4},{7,5},{8,10},{9,11},{10,... | collective-permute-start | bytes 3145736 | tf_op jit(solution)/shard_map/ppermute | solution.py:471
  449.5 33.8 %collective-permute-start.45 = (bf16[256,1024]{1,0:T(8,128)(2,1)}, bf16[256,1024]{1,0:T(8,128)(2,1)}, u32[]{:S(2)}, u32[]{:S(2)}) collective-permute-start(bf16[256,1024]{1,0:T(8,128)(2,1)} %slice.402), channel_id=1, source_target_pairs={{0,2},{1,3},{2,0},{3,1},{4,6},{5,7},{6,4},{7,5},{8,10},{9,11},{10,... | collective-permute-start | bytes 1572872 | tf_op jit(solution)/shard_map/ppermute | solution.py:471
  451.6 62.0 %all-to-all-start.1 = ((bf16[8,128,1024]{2,1,0:T(8,128)(2,1)}), bf16[8,128,1024]{2,1,0:T(8,128)(2,1)S(1)}, u32[]{:S(2)}, u32[]{:S(2)}) async-start(bf16[8,128,1024]{2,1,0:T(8,128)(2,1)} %fusion.44), calls=%async_computation.1 | async-start | bytes 4194304 | tf_op jit(solution)/shard_map/all_to_all | solution.py:815
  462.6 31.9 %collective-permute-start.43 = (bf16[256,1024]{1,0:T(8,128)(2,1)}, bf16[256,1024]{1,0:T(8,128)(2,1)}, u32[]{:S(2)}, u32[]{:S(2)}) collective-permute-start(bf16[256,1024]{1,0:T(8,128)(2,1)} %slice.403), channel_id=1, source_target_pairs={{0,2},{1,3},{2,0},{3,1},{4,6},{5,7},{6,4},{7,5},{8,10},{9,11},{10,... | collective-permute-start | bytes 1572872 | tf_op jit(solution)/shard_map/ppermute | solution.py:471
  (105 other events, 990.3 us)

commit v6 on v5

--- a/solution.py
+++ b/solution.py
@@ -508,6 +508,13 @@
     return lax.optimization_barrier((value, *others))[0]
 
 
+def tie(value, *others):
+    held = False
+    for other in others:
+        held = held | jnp.isinf(other.reshape(-1)[0])
+    return jnp.where(held, jnp.zeros_like(value), value)
+
+
 def last_bits(*bits):
     return [bit for bit in reversed(axis_bits("dp")) if bit not in bits] + list(bits)
 
@@ -634,7 +641,7 @@
     offer_out = jnp.swapaxes(offer_out, 1, 2).reshape(data_count, share, head_width)
     offer_out = jnp.pad(offer_out, ((0, 0), (0, 0), (width - head_width, 0)))
     offer = jnp.where(owned[1], offer_out, slot_low.reshape(data_count, share, width))
-    shares = lax.all_to_all(after(offer, params), "dp", 0, 0)
+    shares = lax.all_to_all(tie(offer, params), "dp", 0, 0)
     params = params.reshape(-1)
 
     def own_slice(start, size):
@@ -667,25 +674,21 @@
 
     split = 2 * head_width
     first = share_of(0)
-    piece_vo = jnp.concatenate(
-        [first[:, split : split + head_width], share_of(1)[:, width - head_width :]], axis=1
+    piece = open_piece(
+        jnp.concatenate([first[:, : split + head_width], share_of(1)[:, width - head_width :]], axis=1)
     )
-    bits_qk, bits_vo = last_bits(2, 1), last_bits(1, 2)
-    one_qk = double(open_piece(first[:, :split]), bits_qk[0])
-    one_vo = double(open_piece(piece_vo), bits_vo[0])
-    w_qk, w_vo = one_qk, one_vo
-    for bit in bits_qk[1:]:
-        w_qk = double(w_qk, bit)
-    for bit in bits_vo[1:]:
-        w_vo = double(w_vo, bit)
-    w_qk, w_vo = rows2(w_qk), rows2(w_vo)
+    for bit in last_bits(2, 1)[:-2]:
+        piece = double(piece, bit)
+    two_qk = double(piece[..., :split], 2)
+    two_vo = double(piece[..., split:], 1)
+    w_qk, w_vo = rows2(double(two_qk, 1)), rows2(double(two_vo, 2))
     w_v = w_vo[:, :head_width]
     w_out = w_vo[:, head_width:].reshape(data_count, tensor_count, share_out, head_width)
     w_out = jnp.swapaxes(w_out, 1, 2).reshape(head_width, width)
     bits_proj = last_bits(1, 2)
     bits_fc = last_bits(2, 1)
-    w_proj = double(open_piece(after(share_of(3), one_qk, one_vo)), bits_proj[0])
-    w_fc = double(open_piece(after(share_of(2), w_proj)), bits_fc[0])
+    w_proj = double(open_piece(tie(share_of(3), two_qk, two_vo)), bits_proj[0])
+    w_fc = double(open_piece(tie(share_of(2), w_proj, w_qk)), bits_fc[0])
     bias_qk = jnp.concatenate([bias_query, jnp.zeros_like(bias_query)])
     scale_qk = jnp.where(jnp.arange(split) < head_width, HEAD_DIM**-0.5, 1.0)
     qk = ((mm(normed_all, w_qk) + bias_qk) * scale_qk).astype(BF16)
@@ -782,14 +785,14 @@
     grad_vo = jnp.concatenate([grad_v, grad_out], axis=1)
     half_qk = halve(spread(grad_qk), 1)
     half_vo = halve(spread(grad_vo), 2)
-    share_qk = halve_by(half_qk, steps[1:])
-    share_vo = halve_by(half_vo, [1] + steps[2:])
-
-    acts = after(acts, grad_qk)
+    share_attend = jnp.concatenate([halve(half_qk, 2), halve(half_vo, 1)], axis=-1)
+    share_attend = rows2(halve_by(share_attend, steps[2:]))
+
+    late_qk, late_v = after((back_qk, back_v), grad_qk, grad_vo)
+    back_normed = scatter_end(scatter_begin([rows2(late_qk), rows2(late_v)], [w_qk, w_v], NT))
+    acts = after(acts, back_normed)
     branches = [scatter_end(scatter_begin([act], [w_proj], NN)) for act in acts]
     block_out = (middle + jnp.concatenate(branches) + bias_proj).astype(BF16)
-    late_qk, late_v = after((back_qk, back_v), grad_qk, grad_vo)
-    back_normed = scatter_end(scatter_begin([rows2(late_qk), rows2(late_v)], [w_qk, w_v], NT))
     input_grad = back_middle + norm_back(unit_one, scale_one, gain_one, back_normed)
     gain_one_grad = jnp.sum(back_normed * unit_one, axis=0)
     shift_one_grad = jnp.sum(back_normed, axis=0)
@@ -798,15 +801,8 @@
 
     bundle = jnp.zeros((data_count, share, width), BF16)
     pieces = (
-        jnp.concatenate(
-            [
-                rows2(share_qk),
-                rows2(share_vo)[:, :head_width],
-                jnp.zeros((share, width - 3 * head_width), BF16),
-            ],
-            axis=1,
-        ),
-        jnp.pad(rows2(share_vo)[:, head_width:], ((0, 0), (width - head_width, 0))),
+        jnp.pad(share_attend[:, : 3 * head_width], ((0, 0), (0, width - 3 * head_width))),
+        jnp.pad(share_attend[:, width - head_width :], ((0, 0), (width - head_width, 0))),
         rows2(share_fc),
         rows2(share_proj),
     )

time: 562 us -> 550 us (0.979)
  the two profiles are of different devices: /device:TPU:6 before, /device:TPU:24 now
where the time goes in v6:
time: 550 us; the launch traced here: 544 us
  waiting for transfers between devices  217 us (39%)
  Pallas kernels  90.7 us (16%)
  other arithmetic  66.8 us (12%)
  starting transfers between devices  59.3 us (11%)
  matrix products  50.8 us (9%)
  local copies, waits for them, and re-layouts  42.9 us (8%)
  between operations  17.1 us (3%)
    ppermute x22, waiting for transfers between devices, data_swap(): return lax.ppermute(value, 'dp', [(i, i ^ bit) for i in range(count)])  95.6 us
    ppermute x27, waiting for transfers between devices, swap(): return lax.ppermute(value, 'tensor', [(i, i ^ bit) for i in range(count)])  73.9 us
    dot_general x28, matrix products, mm(): return lax.dot_general(left, right, dims, preferred_element_type=F32)  50.8 us
    pallas_call x1, Pallas kernels, muon_update(): pl.pallas_call(partial(muon_kernel, out_rows=out_rows), in_specs=[pl.Bloc...  38.1 us
    ppermute x5, waiting for transfers between devices, small_scatter(): lax.ppermute(give, name, [(i, i ^ bit) for i in range(count)])  36.8 us
    ppermute x22, starting transfers between devices, data_swap(): return lax.ppermute(value, 'dp', [(i, i ^ bit) for i in range(count)])  27.1 us
    pallas_call x2, Pallas kernels, attend_back(): pl.pallas_call(partial(attend_back_kernel, heads=width // HEAD_DIM, chunk...  22 us
    pallas_call x2, Pallas kernels, hidden_layer(): pl.pallas_call(hidden_kernel, grid=(cols // tile,), in_specs=[whole] * le...  18.6 us
  transfers between devices with their start and end apart: 61, of which 29 were waited for; matrix products, arithmetic and copies ran while one was open for 24% of the time, Pallas kernels for 6%

profile of v6, /device:TPU:24, one launch (start us, length us, event | category | flops | bytes accessed | tf_op | source)
XLA Modules:
  0.0 544.5 jit_solution(14090594038309921817)
XLA Ops:
  22.2 9.5 %collective-permute-done.2 = bf16[512,1024]{1,0:T(8,128)(2,1)S(1)} collective-permute-done((bf16[512,1024]{1,0:T(8,128)(2,1)}, bf16[512,1024]{1,0:T(8,128)(2,1)S(1)}, u32[]{:S(2)}, u32[]{:S(2)}) %collective-permute-start.2) | collective-permute-done | bytes 1048608 | tf_op jit(solution)/shard_map/ppermute | solution.py:471
  31.7 4.2 select_select_fusion
  35.9 5.5 %all-to-all-start = ((bf16[8,128,1024]{2,1,0:T(8,128)(2,1)}), bf16[8,128,1024]{2,1,0:T(8,128)(2,1)}, u32[]{:S(2)}, u32[]{:S(2)}) async-start(bf16[8,128,1024]{2,1,0:T(8,128)(2,1)} %select_select_fusion), calls=%async_computation | async-start | bytes 4194304 | tf_op jit(solution)/shard_map/all_to_all | solution.py:644
  49.3 7.1 %collective-permute-done.8 = bf16[256,1024]{1,0:T(8,128)(2,1)} collective-permute-done((bf16[256,1024]{1,0:T(8,128)(2,1)S(1)}, bf16[256,1024]{1,0:T(8,128)(2,1)}, u32[]{:S(2)}, u32[]{:S(2)}) %collective-permute-start.8) | collective-permute-done | bytes 524320 | tf_op jit(solution)/shard_map/ppermute | solution.py:471
  56.4 10.2 %collective-permute-done.11 = bf16[256,1024]{1,0:T(8,128)(2,1)} collective-permute-done((bf16[256,1024]{1,0:T(8,128)(2,1)S(1)}, bf16[256,1024]{1,0:T(8,128)(2,1)}, u32[]{:S(2)}, u32[]{:S(2)}) %collective-permute-start.11) | collective-permute-done | bytes 524320 | tf_op jit(solution)/shard_map/ppermute | solution.py:471
  76.2 6.4 %fusion.5 = bf16[2048,1024]{1,0:T(8,128)(2,1)} fusion(f32[1024]{0:T(1024)S(1)} %get-tuple-element.200, f32[1024]{0:T(1024)S(1)} %get-tuple-element.201, f32[2048]{0:T(1024)S(1)} %add_rsqrt_fusion, f32[2048]{0:T(1024)S(1)} %broadcast_multiply_fusion, bf16[512,1024]{1,0:T(8,128)(2,1)S(1)} %collective-permute-done.4, ...), kind=kLoop, calls=%fused_computation.7 | loop fusion | flops 27262976 | bytes 8413184 | tf_op jit(solution)/shard_map/convert_element_type | solution.py:666
  82.6 6.2 %all-to-all-done = bf16[8,128,1024]{2,1,0:T(8,128)(2,1)} async-done(((bf16[8,128,1024]{2,1,0:T(8,128)(2,1)}), bf16[8,128,1024]{2,1,0:T(8,128)(2,1)}, u32[]{:S(2)}, u32[]{:S(2)}) %all-to-all-start) | async-done | bytes 2097184 | tf_op jit(solution)/shard_map/all_to_all | solution.py:644
  90.0 13.0 %collective-permute-done.14 = bf16[1,1,1,128,1024]{4,3,0,2,1:T(8,128)(2,1)S(1)} collective-permute-done((bf16[1,1,1,128,1024]{4,3,0,2,1:T(8,128)(2,1)S(1)}, bf16[1,1,1,128,1024]{4,3,0,2,1:T(8,128)(2,1)S(1)}, u32[]{:S(2)}, u32[]{:S(2)}) %collective-permute-start.14) | collective-permute-done | bytes 262176 | tf_op jit(solution)/shard_map/ppermute | solution.py:504
  106.7 4.7 collective-permute-done.15
  123.9 7.0 %collective-permute-done.21 = bf16[1,1,1,128,1024]{4,3,2,1,0:T(8,128)(2,1)} collective-permute-done((bf16[1,1,1,128,1024]{4,3,2,1,0:T(8,128)(2,1)S(1)}, bf16[1,1,1,128,1024]{4,3,2,1,0:T(8,128)(2,1)}, u32[]{:S(2)}, u32[]{:S(2)}) %collective-permute-start.21) | collective-permute-done | bytes 262176 | tf_op jit(solution)/shard_map/ppermute | solution.py:504
  148.3 4.8 shard_map.143
  157.2 5.7 %shard_map.144 = (bf16[2,2,256,256]{3,2,1,0:T(8,128)(2,1)S(1)}, f32[2,2,256,128]{3,2,1,0:T(8,128)S(1)}) custom-call(s32[1]{0:T(128)} %bitcast.core_ref, bf16[2,2,512,512]{3,2,1,0:T(8,128)(2,1)S(1)} %bitcast.175, bf16[2,2,512,512]{3,2,1,0:T(8,128)(2,1)S(1)} %bitcast.176, bf16[2,2,512,256]{3,2,1,0:T(8,128)(2,1)S(1)} %bitcast.182), custom_call_target="tpu_custom_call" | custom-call | flops 5000000000 | bytes 6000000 | tf_op jit(solution)/shard_map/pallas_call | solution.py:108
  163.0 7.0 %collective-permute-done.24 = bf16[2,1,1,128,1024]{4,3,0,2,1:T(8,128)(2,1)S(1)} collective-permute-done((bf16[2,1,1,128,1024]{4,3,0,2,1:T(8,128)(2,1)S(1)}, bf16[2,1,1,128,1024]{4,3,0,2,1:T(8,128)(2,1)S(1)}, u32[]{:S(2)}, u32[]{:S(2)}) %collective-permute-start.24) | collective-permute-done | bytes 524320 | tf_op jit(solution)/shard_map/ppermute | solution.py:504
  174.5 20.5 %collective-permute-done.28 = bf16[2,2,1,128,1024]{4,3,0,2,1:T(8,128)(2,1)S(1)} collective-permute-done((bf16[2,2,1,128,1024]{4,3,0,2,1:T(8,128)(2,1)S(1)}, bf16[2,2,1,128,1024]{4,3,0,2,1:T(8,128)(2,1)S(1)}, u32[]{:S(2)}, u32[]{:S(2)}) %collective-permute-start.28) | collective-permute-done | bytes 1048608 | tf_op jit(solution)/shard_map/ppermute | solution.py:504
  208.3 13.2 %collective-permute-done.26 = bf16[512,1024]{1,0:T(8,128)(2,1)S(1)} collective-permute-done((bf16[512,1024]{1,0:T(8,128)(2,1)S(1)}, bf16[512,1024]{1,0:T(8,128)(2,1)S(1)}, u32[]{:S(2)}, u32[]{:S(2)}) %collective-permute-start.26) | collective-permute-done | bytes 1048608 | tf_op jit(solution)/shard_map/ppermute | solution.py:471
  222.0 9.2 %shard_map.145 = (bf16[1024,1024]{1,0:T(8,128)(2,1)S(1)}, bf16[1024,1024]{1,0:T(8,128)(2,1)}, f32[1,1024]{1,0:T(1,128)S(1)}, bf16[1024,1024]{1,0:T(8,128)(2,1)}) custom-call(bf16[512,1024]{1,0:T(8,128)(2,1)S(1)} %get-tuple-element.156.refs_0_, bf16[512,1024]{1,0:T(8,128)(2,1)S(1)} %collective-permute-done.27.refs_1_, bf16[1024,1024]{1,0:T(8,128)(2,1)} %bitcast.214, ...), custom_call_target="tpu_custom_call" | custom-call | flops 2147483648 | bytes 12000000 | tf_op jit(solution)/shard_map/pallas_call | solution.py:257
  245.9 5.9 %convolution_convert_fusion.refs_4_ = bf16[1024,1024]{1,0:T(8,128)(2,1)} fusion(bf16[1024,1024]{1,0:T(8,128)(2,1)} %copy-done.58, bf16[1024,1024]{1,0:T(8,128)(2,1)} %bitcast.209), kind=kOutput, calls=%fused_computation.63 | convolution fusion | flops 2148532224 | bytes 6291456 | tf_op jit(solution)/shard_map/dot_general | solution.py:44
  251.8 9.4 %shard_map.146 = (bf16[1024,1024]{1,0:T(8,128)(2,1)S(1)}, bf16[1024,1024]{1,0:T(8,128)(2,1)}, f32[1,1024]{1,0:T(1,128)S(1)}, bf16[1024,1024]{1,0:T(8,128)(2,1)}) custom-call(bf16[512,1024]{1,0:T(8,128)(2,1)S(1)} %get-tuple-element.83.refs_0_, bf16[512,1024]{1,0:T(8,128)(2,1)} %collective-permute-done.30.refs_1_, bf16[1024,1024]{1,0:T(8,128)(2,1)} %bitcast.215, ...), custom_call_target="tpu_custom_call" | custom-call | flops 2147483648 | bytes 12000000 | tf_op jit(solution)/shard_map/pallas_call | solution.py:257
  261.3 6.4 %collective-permute-done.32 = bf16[512,1024]{1,0:T(8,128)(2,1)} collective-permute-done((bf16[512,1024]{1,0:T(8,128)(2,1)}, bf16[512,1024]{1,0:T(8,128)(2,1)}, u32[]{:S(2)}, u32[]{:S(2)}) %collective-permute-start.32) | collective-permute-done | bytes 1048608 | tf_op jit(solution)/shard_map/ppermute | solution.py:471
  297.8 8.0 %collective-permute-done.35 = bf16[512,1024]{1,0:T(8,128)(2,1)S(1)} collective-permute-done((bf16[512,1024]{1,0:T(8,128)(2,1)S(1)}, bf16[512,1024]{1,0:T(8,128)(2,1)S(1)}, u32[]{:S(2)}, u32[]{:S(2)}) %collective-permute-start.35) | collective-permute-done | bytes 1048608 | tf_op jit(solution)/shard_map/ppermute | solution.py:471
  315.0 6.3 %collective-permute-done.38 = bf16[2,1,2,128,1024]{4,3,2,1,0:T(8,128)(2,1)} collective-permute-done((bf16[2,1,2,128,1024]{4,3,2,1,0:T(8,128)(2,1)}, bf16[2,1,2,128,1024]{4,3,2,1,0:T(8,128)(2,1)}, u32[]{:S(2)}, u32[]{:S(2)}) %collective-permute-start.38) | collective-permute-done | bytes 1048608 | tf_op jit(solution)/shard_map/ppermute | solution.py:504
  328.7 11.0 %shard_map.149 = (bf16[2,2,512,512]{3,2,1,0:T(8,128)(2,1)}, bf16[2,2,512,256]{3,2,1,0:T(8,128)(2,1)S(1)}) custom-call(s32[1]{0:T(128)} %bitcast.core_ref, bf16[2,2,512,512]{3,2,1,0:T(8,128)(2,1)} %bitcast.177, bf16[2,2,512,512]{3,2,1,0:T(8,128)(2,1)} %bitcast.178, bf16[2,2,512,256]{3,2,1,0:T(8,128)(2,1)S(1)} %bitcast.183, ...), custom_call_target="tpu_custom_call" | custom-call | flops 12000000000 | bytes 6000000 | tf_op jit(solution)/shard_map/pallas_call | solution.py:205
  344.9 4.9 collective-permute-done.39
  353.2 11.0 %shard_map.150 = (bf16[2,2,512,512]{3,2,1,0:T(8,128)(2,1)}, bf16[2,2,512,256]{3,2,1,0:T(8,128)(2,1)S(1)}) custom-call(s32[1]{0:T(128)} %bitcast.core_ref, bf16[2,2,512,512]{3,2,1,0:T(8,128)(2,1)} %bitcast.179, bf16[2,2,512,512]{3,2,1,0:T(8,128)(2,1)} %bitcast.180, ...), custom_call_target="tpu_custom_call", output_to_operand_aliasing={{0}: (10, {}), {1}: (11, {})} | custom-call | flops 12000000000 | bytes 6000000 | tf_op jit(solution)/shard_map/pallas_call | solution.py:205
  376.4 10.1 %collective-permute-done.47 = bf16[2,2,1,128,512]{4,3,2,1,0:T(8,128)(2,1)S(1)} collective-permute-done((bf16[2,2,1,128,512]{4,3,2,1,0:T(8,128)(2,1)S(1)}, bf16[2,2,1,128,512]{4,3,2,1,0:T(8,128)(2,1)S(1)}, u32[]{:S(2)}, u32[]{:S(2)}) %collective-permute-start.47) | collective-permute-done | bytes 524320 | tf_op jit(solution)/shard_map/ppermute | solution.py:504
  390.1 4.8 collective-permute-done.48
  404.3 11.4 %collective-permute-done.51 = bf16[1,1,1,128,1024]{4,3,2,1,0:T(8,128)(2,1)S(1)} collective-permute-done((bf16[1,1,1,128,1024]{4,3,2,1,0:T(8,128)(2,1)S(1)}, bf16[1,1,1,128,1024]{4,3,2,1,0:T(8,128)(2,1)S(1)}, u32[]{:S(2)}, u32[]{:S(2)}) %collective-permute-start.51) | collective-permute-done | bytes 262176 | tf_op jit(solution)/shard_map/ppermute | solution.py:504
  422.0 5.9 %all-to-all-start.1 = ((bf16[8,128,1024]{2,1,0:T(8,128)(2,1)}), bf16[8,128,1024]{2,1,0:T(8,128)(2,1)S(1)}, u32[]{:S(2)}, u32[]{:S(2)}) async-start(bf16[8,128,1024]{2,1,0:T(8,128)(2,1)} %fusion.54), calls=%async_computation.1 | async-start | bytes 4194304 | tf_op jit(solution)/shard_map/all_to_all | solution.py:811
  440.8 34.2 %collective-permute-done.56 = f32[4,384]{1,0:T(4,128)S(1)} collective-permute-done((f32[4,384]{1,0:T(4,128)S(1)}, f32[4,384]{1,0:T(4,128)S(1)}, u32[]{:S(2)}, u32[]{:S(2)}) %collective-permute-start.56) | collective-permute-done | bytes 6176 | tf_op jit(solution)/shard_map/ppermute | solution.py:600
  485.0 10.7 %collective-permute-done.46 = bf16[256,1024]{1,0:T(8,128)(2,1)S(1)} collective-permute-done((bf16[256,1024]{1,0:T(8,128)(2,1)S(1)}, bf16[256,1024]{1,0:T(8,128)(2,1)S(1)}, u32[]{:S(2)}, u32[]{:S(2)}) %collective-permute-start.46) | collective-permute-done | bytes 524320 | tf_op jit(solution)/shard_map/ppermute | solution.py:471
  495.8 8.7 %collective-permute-done.44 = bf16[256,1024]{1,0:T(8,128)(2,1)S(1)} collective-permute-done((bf16[256,1024]{1,0:T(8,128)(2,1)S(1)}, bf16[256,1024]{1,0:T(8,128)(2,1)S(1)}, u32[]{:S(2)}, u32[]{:S(2)}) %collective-permute-start.44) | collective-permute-done | bytes 524320 | tf_op jit(solution)/shard_map/ppermute | solution.py:471
  506.2 38.1 %shard_map.151 = (f32[1024,1024]{1,0:T(8,128)}, f32[1024,1024]{1,0:T(8,128)}, f32[1024,1024]{1,0:T(8,128)}) custom-call(s32[3]{0:T(128)S(1)} %pad_add_fusion.limit_ref, bf16[8,128,1024]{2,1,0:T(8,128)(2,1)S(1)} %all-to-all-done.1.landed_ref, f32[1024,1024]{1,0:T(8,128)} %bitcast.241, f32[1024,1024]{1,0:T(8,128)} %bitcast.195), custom_call_target="tpu_custom_call" | custom-call | flops 32212254720 | bytes 23068672 | tf_op jit(solution)/shard_map/pallas_call | solution.py:443
  (456 shorter events, 206.3 us)
Async XLA Ops:
  7.7 24.0 %collective-permute-start.2 = (bf16[512,1024]{1,0:T(8,128)(2,1)}, bf16[512,1024]{1,0:T(8,128)(2,1)S(1)}, u32[]{:S(2)}, u32[]{:S(2)}) collective-permute-start(bf16[512,1024]{1,0:T(8,128)(2,1)} %param.8), channel_id=1, source_target_pairs={{0,2},{1,3},{2,0},{3,1},{4,6},{5,7},{6,4},{7,5},{8,10},{9,11},{10,... | collective-permute-start | bytes 3145736 | tf_op jit(solution)/shard_map/ppermute | solution.py:471
  35.9 52.9 %all-to-all-start = ((bf16[8,128,1024]{2,1,0:T(8,128)(2,1)}), bf16[8,128,1024]{2,1,0:T(8,128)(2,1)}, u32[]{:S(2)}, u32[]{:S(2)}) async-start(bf16[8,128,1024]{2,1,0:T(8,128)(2,1)} %select_select_fusion), calls=%async_computation | async-start | bytes 4194304 | tf_op jit(solution)/shard_map/all_to_all | solution.py:644
  42.9 23.6 %collective-permute-start.11 = (bf16[256,1024]{1,0:T(8,128)(2,1)S(1)}, bf16[256,1024]{1,0:T(8,128)(2,1)}, u32[]{:S(2)}, u32[]{:S(2)}) collective-permute-start(bf16[256,1024]{1,0:T(8,128)(2,1)S(1)} %get-tuple-element.70), channel_id=1, source_target_pairs={{0,2},{1,3},{2,0},{3,1},{4,6},{5,7},{6,4},{7,5},{8,10},{9,11},{10,... | collective-permute-start | bytes 1572872 | tf_op jit(solution)/shard_map/ppermute | solution.py:471
  48.0 22.0 %collective-permute-start.3 = (bf16[512,1024]{1,0:T(8,128)(2,1)S(1)}, bf16[512,1024]{1,0:T(8,128)(2,1)S(1)}, u32[]{:S(2)}, u32[]{:S(2)}) collective-permute-start(bf16[512,1024]{1,0:T(8,128)(2,1)S(1)} %copy-done.15), channel_id=1, source_target_pairs={{0,1},{1,0},{2,3},{3,2},{4,5},{5,4},{6,7},{7,6},{8,9},{9,8},{10,11... | collective-permute-start | bytes 3145736 | tf_op jit(solution)/shard_map/ppermute | solution.py:471
  48.0 23.9 %collective-permute-start.4 = (bf16[512,1024]{1,0:T(8,128)(2,1)S(1)}, bf16[512,1024]{1,0:T(8,128)(2,1)S(1)}, u32[]{:S(2)}, u32[]{:S(2)}) collective-permute-start(bf16[512,1024]{1,0:T(8,128)(2,1)S(1)} %collective-permute-done.2), channel_id=1, source_target_pairs={{0,1},{1,0},{2,3},{3,2},{4,5},{5,4},{6,7},{7,6},{8,9},{9,8},{10,11... | collective-permute-start | bytes 3145736 | tf_op jit(solution)/shard_map/ppermute | solution.py:471
  49.1 20.7 %collective-permute-start.12 = (bf16[256,1024]{1,0:T(8,128)(2,1)S(1)}, bf16[256,1024]{1,0:T(8,128)(2,1)S(1)}, u32[]{:S(2)}, u32[]{:S(2)}) collective-permute-start(bf16[256,1024]{1,0:T(8,128)(2,1)S(1)} %get-tuple-element.70), channel_id=1, source_target_pairs={{0,1},{1,0},{2,3},{3,2},{4,5},{5,4},{6,7},{7,6},{8,9},{9,8},{10,11... | collective-permute-start | bytes 1572872 | tf_op jit(solution)/shard_map/ppermute | solution.py:471
  111.6 22.7 %collective-permute-start.16 = (bf16[2,2,1,128,512]{4,3,0,2,1:T(8,128)(2,1)S(1)}, bf16[2,2,1,128,512]{4,3,0,2,1:T(8,128)(2,1)}, u32[]{:S(2)}, u32[]{:S(2)}) collective-permute-start(bf16[2,2,1,128,512]{4,3,0,2,1:T(8,128)(2,1)S(1)} %maximum_select_fusion.7), channel_id=1, source_target_pairs={{0,4},{4,0},{8,12},{12,8},{16,20},{20,16},{24,28},{28,24},{1,5},{5... | collective-permute-start | bytes 1572872 | tf_op jit(solution)/shard_map/ppermute | solution.py:504
  114.3 21.5 %collective-permute-start.18 = (bf16[2,1,2,128,512]{4,3,0,2,1:T(8,128)(2,1)S(1)}, bf16[2,1,2,128,512]{4,3,0,2,1:T(8,128)(2,1)}, u32[]{:S(2)}, u32[]{:S(2)}) collective-permute-start(bf16[2,1,2,128,512]{4,3,0,2,1:T(8,128)(2,1)S(1)} %maximum_select_fusion.8), channel_id=1, source_target_pairs={{0,8},{4,12},{8,0},{12,4},{16,24},{20,28},{24,16},{28,20},{1,9},{5... | collective-permute-start | bytes 1572872 | tf_op jit(solution)/shard_map/ppermute | solution.py:504
  132.0 23.6 %collective-permute-start.23 = (bf16[2,1,1,128,1024]{4,3,0,2,1:T(8,128)(2,1)S(1)}, bf16[2,1,1,128,1024]{4,3,0,2,1:T(8,128)(2,1)}, u32[]{:S(2)}, u32[]{:S(2)}) collective-permute-start(bf16[2,1,1,128,1024]{4,3,0,2,1:T(8,128)(2,1)S(1)} %fusion.44), channel_id=1, source_target_pairs={{0,4},{4,0},{8,12},{12,8},{16,20},{20,16},{24,28},{28,24},{1,5},{5... | collective-permute-start | bytes 1572872 | tf_op jit(solution)/shard_map/ppermute | solution.py:504
  170.1 24.8 %collective-permute-start.28 = (bf16[2,2,1,128,1024]{4,3,0,2,1:T(8,128)(2,1)S(1)}, bf16[2,2,1,128,1024]{4,3,0,2,1:T(8,128)(2,1)S(1)}, u32[]{:S(2)}, u32[]{:S(2)}) collective-permute-start(bf16[2,2,1,128,1024]{4,3,0,2,1:T(8,128)(2,1)S(1)} %maximum_select_fusion.5), channel_id=1, source_target_pairs={{0,4},{4,0},{8,12},{12,8},{16,20},{20,16},{24,28},{28,24},{1,5},{5... | collective-permute-start | bytes 3145736 | tf_op jit(solution)/shard_map/ppermute | solution.py:504
  171.8 25.2 %collective-permute-start.25 = (bf16[512,1024]{1,0:T(8,128)(2,1)S(1)}, bf16[512,1024]{1,0:T(8,128)(2,1)S(1)}, u32[]{:S(2)}, u32[]{:S(2)}) collective-permute-start(bf16[512,1024]{1,0:T(8,128)(2,1)S(1)} %convolution_convert_fusion.6), channel_id=1, source_target_pairs={{0,1},{1,0},{2,3},{3,2},{4,5},{5,4},{6,7},{7,6},{8,9},{9,8},{10,11... | collective-permute-start | bytes 3145736 | tf_op jit(solution)/shard_map/ppermute | solution.py:471
  172.5 26.6 %collective-permute-start.20 = (bf16[512,1024]{1,0:T(8,128)(2,1)S(1)}, bf16[512,1024]{1,0:T(8,128)(2,1)S(1)}, u32[]{:S(2)}, u32[]{:S(2)}) collective-permute-start(bf16[512,1024]{1,0:T(8,128)(2,1)S(1)} %pad_maximum_fusion.1), channel_id=1, source_target_pairs={{0,2},{1,3},{2,0},{3,1},{4,6},{5,7},{6,4},{7,5},{8,10},{9,11},{10,... | collective-permute-start | bytes 3145736 | tf_op jit(solution)/shard_map/ppermute | solution.py:471
  174.2 27.8 %collective-permute-start.29 = (bf16[2,1,2,128,1024]{4,3,0,2,1:T(8,128)(2,1)S(1)}, bf16[2,1,2,128,1024]{4,3,0,2,1:T(8,128)(2,1)S(1)}, u32[]{:S(2)}, u32[]{:S(2)}) collective-permute-start(bf16[2,1,2,128,1024]{4,3,0,2,1:T(8,128)(2,1)S(1)} %maximum_select_fusion.4), channel_id=1, source_target_pairs={{0,8},{4,12},{8,0},{12,4},{16,24},{20,28},{24,16},{28,20},{1,9},{5... | collective-permute-start | bytes 3145736 | tf_op jit(solution)/shard_map/ppermute | solution.py:504
  197.6 24.0 %collective-permute-start.26 = (bf16[512,1024]{1,0:T(8,128)(2,1)S(1)}, bf16[512,1024]{1,0:T(8,128)(2,1)S(1)}, u32[]{:S(2)}, u32[]{:S(2)}) collective-permute-start(bf16[512,1024]{1,0:T(8,128)(2,1)S(1)} %pad_maximum_fusion.2), channel_id=1, source_target_pairs={{0,2},{1,3},{2,0},{3,1},{4,6},{5,7},{6,4},{7,5},{8,10},{9,11},{10,... | collective-permute-start | bytes 3145736 | tf_op jit(solution)/shard_map/ppermute | solution.py:471
  201.9 20.1 %collective-permute-start.27 = (bf16[512,1024]{1,0:T(8,128)(2,1)S(1)}, bf16[512,1024]{1,0:T(8,128)(2,1)S(1)}, u32[]{:S(2)}, u32[]{:S(2)}) collective-permute-start(bf16[512,1024]{1,0:T(8,128)(2,1)S(1)} %get-tuple-element.156.refs_0_), channel_id=1, source_target_pairs={{0,1},{1,0},{2,3},{3,2},{4,5},{5,4},{6,7},{7,6},{8,9},{9,8},{10,11... | collective-permute-start | bytes 3145736 | tf_op jit(solution)/shard_map/ppermute | solution.py:471
  241.9 25.9 %collective-permute-start.32 = (bf16[512,1024]{1,0:T(8,128)(2,1)}, bf16[512,1024]{1,0:T(8,128)(2,1)}, u32[]{:S(2)}, u32[]{:S(2)}) collective-permute-start(bf16[512,1024]{1,0:T(8,128)(2,1)} %pad_maximum_fusion.3), channel_id=1, source_target_pairs={{0,2},{1,3},{2,0},{3,1},{4,6},{5,7},{6,4},{7,5},{8,10},{9,11},{10,... | collective-permute-start | bytes 3145736 | tf_op jit(solution)/shard_map/ppermute | solution.py:471
  280.0 17.8 %collective-permute-start.34 = (bf16[512,1024]{1,0:T(8,128)(2,1)S(1)}, bf16[512,1024]{1,0:T(8,128)(2,1)S(1)}, u32[]{:S(2)}, u32[]{:S(2)}) collective-permute-start(bf16[512,1024]{1,0:T(8,128)(2,1)S(1)} %get-tuple-element.92.refs_0_), channel_id=1, source_target_pairs={{0,1},{1,0},{2,3},{3,2},{4,5},{5,4},{6,7},{7,6},{8,9},{9,8},{10,11... | collective-permute-start | bytes 3145736 | tf_op jit(solution)/shard_map/ppermute | solution.py:471
  280.2 25.6 %collective-permute-start.35 = (bf16[512,1024]{1,0:T(8,128)(2,1)S(1)}, bf16[512,1024]{1,0:T(8,128)(2,1)S(1)}, u32[]{:S(2)}, u32[]{:S(2)}) collective-permute-start(bf16[512,1024]{1,0:T(8,128)(2,1)S(1)} %pad_maximum_fusion.4), channel_id=1, source_target_pairs={{0,2},{1,3},{2,0},{3,1},{4,6},{5,7},{6,4},{7,5},{8,10},{9,11},{10,... | collective-permute-start | bytes 3145736 | tf_op jit(solution)/shard_map/ppermute | solution.py:471
  287.7 25.6 %collective-permute-start.37 = (bf16[2,2,1,128,1024]{4,3,2,1,0:T(8,128)(2,1)}, bf16[2,2,1,128,1024]{4,3,2,1,0:T(8,128)(2,1)}, u32[]{:S(2)}, u32[]{:S(2)}) collective-permute-start(bf16[2,2,1,128,1024]{4,3,2,1,0:T(8,128)(2,1)} %constant_dynamic-slice_fusion.8), channel_id=1, source_target_pairs={{0,4},{4,0},{8,12},{12,8},{16,20},{20,16},{24,28},{28,24},{1,5},{5... | collective-permute-start | bytes 3145736 | tf_op jit(solution)/shard_map/ppermute | solution.py:504
  295.6 25.6 %collective-permute-start.38 = (bf16[2,1,2,128,1024]{4,3,2,1,0:T(8,128)(2,1)}, bf16[2,1,2,128,1024]{4,3,2,1,0:T(8,128)(2,1)}, u32[]{:S(2)}, u32[]{:S(2)}) collective-permute-start(bf16[2,1,2,128,1024]{4,3,2,1,0:T(8,128)(2,1)} %constant_dynamic-slice_fusion.7), channel_id=1, source_target_pairs={{0,8},{4,12},{8,0},{12,4},{16,24},{20,28},{24,16},{28,20},{1,9},{5... | collective-permute-start | bytes 3145736 | tf_op jit(solution)/shard_map/ppermute | solution.py:504
  326.1 25.7 %collective-permute-start.40 = (bf16[1,1,2,128,1024]{4,3,2,1,0:T(8,128)(2,1)}, bf16[1,1,2,128,1024]{4,3,2,1,0:T(8,128)(2,1)}, u32[]{:S(2)}, u32[]{:S(2)}) collective-permute-start(bf16[1,1,2,128,1024]{4,3,2,1,0:T(8,128)(2,1)} %constant_dynamic-slice_fusion.5), channel_id=1, source_target_pairs={{0,16},{4,20},{8,24},{12,28},{16,0},{20,4},{24,8},{28,12},{1,17},{... | collective-permute-start | bytes 1572872 | tf_op jit(solution)/shard_map/ppermute | solution.py:504
  327.4 22.3 %collective-permute-start.39 = (bf16[2,1,1,128,1024]{4,3,2,1,0:T(8,128)(2,1)}, bf16[2,1,1,128,1024]{4,3,2,1,0:T(8,128)(2,1)}, u32[]{:S(2)}, u32[]{:S(2)}) collective-permute-start(bf16[2,1,1,128,1024]{4,3,2,1,0:T(8,128)(2,1)} %constant_dynamic-slice_fusion.6), channel_id=1, source_target_pairs={{0,8},{4,12},{8,0},{12,4},{16,24},{20,28},{24,16},{28,20},{1,9},{5... | collective-permute-start | bytes 1572872 | tf_op jit(solution)/shard_map/ppermute | solution.py:504
  372.0 25.7 %collective-permute-start.41 = (bf16[1024,1024]{1,0:T(8,128)(2,1)S(1)}, bf16[1024,1024]{1,0:T(8,128)(2,1)S(1)}, u32[]{:S(2)}, u32[]{:S(2)}) collective-permute-start(bf16[1024,1024]{1,0:T(8,128)(2,1)S(1)} %add_convert_fusion), channel_id=1, source_target_pairs={{0,1},{1,0},{2,3},{3,2},{4,5},{5,4},{6,7},{7,6},{8,9},{9,8},{10,11... | collective-permute-start | bytes 6291464 | tf_op jit(solution)/shard_map/ppermute | solution.py:471
  396.7 19.1 %collective-permute-start.51 = (bf16[1,1,1,128,1024]{4,3,2,1,0:T(8,128)(2,1)S(1)}, bf16[1,1,1,128,1024]{4,3,2,1,0:T(8,128)(2,1)S(1)}, u32[]{:S(2)}, u32[]{:S(2)}) collective-permute-start(bf16[1,1,1,128,1024]{4,3,2,1,0:T(8,128)(2,1)S(1)} %fusion.55), channel_id=1, source_target_pairs={{0,16},{4,20},{8,24},{12,28},{16,0},{20,4},{24,8},{28,12},{1,17},{... | collective-permute-start | bytes 786440 | tf_op jit(solution)/shard_map/ppermute | solution.py:504
  400.3 27.6 %collective-permute-start.42 = (bf16[512,1024]{1,0:T(8,128)(2,1)}, bf16[512,1024]{1,0:T(8,128)(2,1)}, u32[]{:S(2)}, u32[]{:S(2)}) collective-permute-start(bf16[512,1024]{1,0:T(8,128)(2,1)} %slice.422), channel_id=1, source_target_pairs={{0,2},{1,3},{2,0},{3,1},{4,6},{5,7},{6,4},{7,5},{8,10},{9,11},{10,... | collective-permute-start | bytes 3145736 | tf_op jit(solution)/shard_map/ppermute | solution.py:471
  400.9 17.9 %collective-permute-start.52 = (bf16[1,1,1,128,1024]{4,3,2,1,0:T(8,128)(2,1)S(1)}, bf16[1,1,1,128,1024]{4,3,2,1,0:T(8,128)(2,1)S(1)}, u32[]{:S(2)}, u32[]{:S(2)}) collective-permute-start(bf16[1,1,1,128,1024]{4,3,2,1,0:T(8,128)(2,1)S(1)} %constant_dynamic-slice_fusion.1), channel_id=1, source_target_pairs={{0,4},{4,0},{8,12},{12,8},{16,20},{20,16},{24,28},{28,24},{1,5},{5... | collective-permute-start | bytes 786440 | tf_op jit(solution)/shard_map/ppermute | solution.py:504
  401.9 19.3 %collective-permute-start.53 = (bf16[1,1,1,128,1024]{4,3,2,1,0:T(8,128)(2,1)S(1)}, bf16[1,1,1,128,1024]{4,3,2,1,0:T(8,128)(2,1)S(1)}, u32[]{:S(2)}, u32[]{:S(2)}) collective-permute-start(bf16[1,1,1,128,1024]{4,3,2,1,0:T(8,128)(2,1)S(1)} %constant_dynamic-slice_fusion), channel_id=1, source_target_pairs={{0,16},{4,20},{8,24},{12,28},{16,0},{20,4},{24,8},{28,12},{1,17},{... | collective-permute-start | bytes 786440 | tf_op jit(solution)/shard_map/ppermute | solution.py:504
  422.0 84.2 %all-to-all-start.1 = ((bf16[8,128,1024]{2,1,0:T(8,128)(2,1)}), bf16[8,128,1024]{2,1,0:T(8,128)(2,1)S(1)}, u32[]{:S(2)}, u32[]{:S(2)}) async-start(bf16[8,128,1024]{2,1,0:T(8,128)(2,1)} %fusion.54), calls=%async_computation.1 | async-start | bytes 4194304 | tf_op jit(solution)/shard_map/all_to_all | solution.py:811
  439.7 35.3 %collective-permute-start.56 = (f32[4,384]{1,0:T(4,128)S(1)}, f32[4,384]{1,0:T(4,128)S(1)}, u32[]{:S(2)}, u32[]{:S(2)}) collective-permute-start(f32[4,384]{1,0:T(4,128)S(1)} %slice_select_fusion.2), channel_id=1, source_target_pairs={{0,16},{4,20},{8,24},{12,28},{16,0},{20,4},{24,8},{28,12},{1,17},{... | collective-permute-start | bytes 18440 | tf_op jit(solution)/shard_map/ppermute | solution.py:600
  440.3 39.1 %collective-permute-start.45 = (bf16[512,1024]{1,0:T(8,128)(2,1)S(1)}, bf16[512,1024]{1,0:T(8,128)(2,1)S(1)}, u32[]{:S(2)}, u32[]{:S(2)}) collective-permute-start(bf16[512,1024]{1,0:T(8,128)(2,1)S(1)} %convolution_convert_fusion.2), channel_id=1, source_target_pairs={{0,1},{1,0},{2,3},{3,2},{4,5},{5,4},{6,7},{7,6},{8,9},{9,8},{10,11... | collective-permute-start | bytes 3145736 | tf_op jit(solution)/shard_map/ppermute | solution.py:471
  440.3 41.1 %collective-permute-start.43 = (bf16[512,1024]{1,0:T(8,128)(2,1)S(1)}, bf16[512,1024]{1,0:T(8,128)(2,1)S(1)}, u32[]{:S(2)}, u32[]{:S(2)}) collective-permute-start(bf16[512,1024]{1,0:T(8,128)(2,1)S(1)} %convolution_convert_fusion.3), channel_id=1, source_target_pairs={{0,1},{1,0},{2,3},{3,2},{4,5},{5,4},{6,7},{7,6},{8,9},{9,8},{10,11... | collective-permute-start | bytes 3145736 | tf_op jit(solution)/shard_map/ppermute | solution.py:471
  482.8 21.7 %collective-permute-start.44 = (bf16[256,1024]{1,0:T(8,128)(2,1)S(1)}, bf16[256,1024]{1,0:T(8,128)(2,1)S(1)}, u32[]{:S(2)}, u32[]{:S(2)}) collective-permute-start(bf16[256,1024]{1,0:T(8,128)(2,1)S(1)} %slice.424), channel_id=1, source_target_pairs={{0,2},{1,3},{2,0},{3,1},{4,6},{5,7},{6,4},{7,5},{8,10},{9,11},{10,... | collective-permute-start | bytes 1572872 | tf_op jit(solution)/shard_map/ppermute | solution.py:471
  (102 other events, 944.9 us)

commit v7 on v6

--- a/solution.py
+++ b/solution.py
@@ -641,7 +641,8 @@
     offer_out = jnp.swapaxes(offer_out, 1, 2).reshape(data_count, share, head_width)
     offer_out = jnp.pad(offer_out, ((0, 0), (0, 0), (width - head_width, 0)))
     offer = jnp.where(owned[1], offer_out, slot_low.reshape(data_count, share, width))
-    shares = lax.all_to_all(tie(offer, params), "dp", 0, 0)
+    offer = tie(offer, params)
+    shares = lax.all_to_all(offer, "dp", 0, 0)
     params = params.reshape(-1)
 
     def own_slice(start, size):
@@ -661,7 +662,7 @@
     rows_of = [slice(chunk * part, (chunk + 1) * part) for chunk in range(CHUNKS)]
     rows_in = inputs.astype(F32)
     unit_one, scale_one = norm_parts(rows_in)
-    inputs_four = gather_four(after(inputs, group_params))
+    inputs_four = gather_four(tie(inputs, offer))
     unit_all, _ = norm_parts(jnp.concatenate(inputs_four).astype(F32))
     normed_all = (unit_all * gain_one + shift_one).astype(BF16)
     dy_four = [gather_four(after(out_grad[rows], inputs_four[1])) for rows in rows_of]
@@ -773,7 +774,9 @@
     half_proj = halve(half_proj, rest_proj[0])
     half_fc = halve(half_fc, rest_fc[0])
     attend_grad = attend_back(core, qk, values, mixed, log_sums, back_mixed, 0)
-    back_mixed = after(back_mixed, half_proj, half_fc)
+    acts = after(acts, attend_grad[0])
+    branch_parts = [scatter_begin([act], [w_proj], NN) for act in acts]
+    back_mixed = after(back_mixed, half_proj, half_fc, *branch_parts)
     back_qk, back_v = attend_back(core, qk, values, mixed, log_sums, back_mixed, 1, attend_grad)
     share_proj = halve_by(half_proj, rest_proj[1:])
     share_fc = halve_by(half_fc, rest_fc[1:])
@@ -790,8 +793,7 @@
 
     late_qk, late_v = after((back_qk, back_v), grad_qk, grad_vo)
     back_normed = scatter_end(scatter_begin([rows2(late_qk), rows2(late_v)], [w_qk, w_v], NT))
-    acts = after(acts, back_normed)
-    branches = [scatter_end(scatter_begin([act], [w_proj], NN)) for act in acts]
+    branches = [scatter_end(value) for value in branch_parts]
     block_out = (middle + jnp.concatenate(branches) + bias_proj).astype(BF16)
     input_grad = back_middle + norm_back(unit_one, scale_one, gain_one, back_normed)
     gain_one_grad = jnp.sum(back_normed * unit_one, axis=0)

time: 550 us -> 549 us (level)
  the two profiles are of different devices: /device:TPU:24 before, /device:TPU:8 now
where the time goes in v7:
time: 549 us; the launch traced here: 542 us
  waiting for transfers between devices  189 us (34%)
  Pallas kernels  90.7 us (17%)
  other arithmetic  74.4 us (14%)
  starting transfers between devices  65.3 us (12%)
  matrix products  54.5 us (10%)
  local copies, waits for them, and re-layouts  50 us (9%)
  between operations  17.9 us (3%)
    ppermute x27, waiting for transfers between devices, swap(): return lax.ppermute(value, 'tensor', [(i, i ^ bit) for i in range(count)])  89.2 us
    ppermute x22, waiting for transfers between devices, data_swap(): return lax.ppermute(value, 'dp', [(i, i ^ bit) for i in range(count)])  72 us
    dot_general x28, matrix products, mm(): return lax.dot_general(left, right, dims, preferred_element_type=F32)  54.5 us
    pallas_call x1, Pallas kernels, muon_update(): pl.pallas_call(partial(muon_kernel, out_rows=out_rows), in_specs=[pl.Bloc...  38.1 us
    ppermute x22, starting transfers between devices, data_swap(): return lax.ppermute(value, 'dp', [(i, i ^ bit) for i in range(count)])  29.4 us
    pallas_call x2, Pallas kernels, attend_back(): pl.pallas_call(partial(attend_back_kernel, heads=width // HEAD_DIM, chunk...  22.1 us
    pallas_call x2, Pallas kernels, hidden_layer(): pl.pallas_call(hidden_kernel, grid=(cols // tile,), in_specs=[whole] * le...  18.3 us
    unnamed x162, local copies, waits for them, and re-layouts  18 us
  transfers between devices with their start and end apart: 61, of which 28 were waited for; matrix products, arithmetic and copies ran while one was open for 27% of the time, Pallas kernels for 8%

profile of v7, /device:TPU:8, one launch (start us, length us, event | category | flops | bytes accessed | tf_op | source)
XLA Modules:
  0.0 541.8 jit_solution(4511221947063468628)
XLA Ops:
  31.1 19.0 %collective-permute-done.5 = bf16[512,1024]{1,0:T(8,128)(2,1)S(1)} collective-permute-done((bf16[512,1024]{1,0:T(8,128)(2,1)S(1)}, bf16[512,1024]{1,0:T(8,128)(2,1)S(1)}, u32[]{:S(2)}, u32[]{:S(2)}) %collective-permute-start.5) | collective-permute-done | bytes 1048608 | tf_op jit(solution)/shard_map/ppermute | solution.py:471
  50.1 5.0 all-to-all-start
  64.1 6.2 %collective-permute-done.8 = bf16[256,1024]{1,0:T(8,128)(2,1)} collective-permute-done((bf16[256,1024]{1,0:T(8,128)(2,1)}, bf16[256,1024]{1,0:T(8,128)(2,1)}, u32[]{:S(2)}, u32[]{:S(2)}) %collective-permute-start.8) | collective-permute-done | bytes 524320 | tf_op jit(solution)/shard_map/ppermute | solution.py:471
  71.4 9.4 %collective-permute-done.11 = bf16[256,1024]{1,0:T(8,128)(2,1)} collective-permute-done((bf16[256,1024]{1,0:T(8,128)(2,1)}, bf16[256,1024]{1,0:T(8,128)(2,1)}, u32[]{:S(2)}, u32[]{:S(2)}) %collective-permute-start.11) | collective-permute-done | bytes 524320 | tf_op jit(solution)/shard_map/ppermute | solution.py:471
  90.5 6.4 %fusion.5 = bf16[2048,1024]{1,0:T(8,128)(2,1)} fusion(f32[1024]{0:T(1024)S(1)} %get-tuple-element.197, f32[1024]{0:T(1024)S(1)} %get-tuple-element.198, f32[2048]{0:T(1024)S(1)} %add_rsqrt_fusion, f32[2048]{0:T(1024)S(1)} %broadcast_multiply_fusion, bf16[512,1024]{1,0:T(8,128)(2,1)S(1)} %collective-permute-done.7, ...), kind=kLoop, calls=%fused_computation.7 | loop fusion | flops 27262976 | bytes 8413184 | tf_op jit(solution)/shard_map/convert_element_type | solution.py:667
  96.8 5.0 all-to-all-done
  106.4 10.0 %collective-permute-done.14 = bf16[1,1,1,128,1024]{4,3,0,2,1:T(8,128)(2,1)S(1)} collective-permute-done((bf16[1,1,1,128,1024]{4,3,0,2,1:T(8,128)(2,1)S(1)}, bf16[1,1,1,128,1024]{4,3,0,2,1:T(8,128)(2,1)S(1)}, u32[]{:S(2)}, u32[]{:S(2)}) %collective-permute-start.14) | collective-permute-done | bytes 262176 | tf_op jit(solution)/shard_map/ppermute | solution.py:504
  116.5 3.7 collective-permute-start.15
  122.8 3.9 collective-permute-done.15
  138.3 9.9 %collective-permute-done.21 = bf16[1,1,1,128,1024]{4,3,2,1,0:T(8,128)(2,1)} collective-permute-done((bf16[1,1,1,128,1024]{4,3,2,1,0:T(8,128)(2,1)S(1)}, bf16[1,1,1,128,1024]{4,3,2,1,0:T(8,128)(2,1)}, u32[]{:S(2)}, u32[]{:S(2)}) %collective-permute-start.21) | collective-permute-done | bytes 262176 | tf_op jit(solution)/shard_map/ppermute | solution.py:504
  162.0 4.8 shard_map.143
  172.5 6.0 %shard_map.144 = (bf16[2,2,256,256]{3,2,1,0:T(8,128)(2,1)S(1)}, f32[2,2,256,128]{3,2,1,0:T(8,128)S(1)}) custom-call(s32[1]{0:T(128)} %bitcast.7.core_ref, bf16[2,2,512,512]{3,2,1,0:T(8,128)(2,1)S(1)} %bitcast.178, bf16[2,2,512,512]{3,2,1,0:T(8,128)(2,1)S(1)} %bitcast.179, bf16[2,2,512,256]{3,2,1,0:T(8,128)(2,1)S(1)} %bitcast.185), custom_call_target="tpu_custom_call" | custom-call | flops 5000000000 | bytes 6000000 | tf_op jit(solution)/shard_map/pallas_call | solution.py:108
  178.5 6.3 %collective-permute-done.24 = bf16[2,1,1,128,1024]{4,3,0,2,1:T(8,128)(2,1)S(1)} collective-permute-done((bf16[2,1,1,128,1024]{4,3,0,2,1:T(8,128)(2,1)S(1)}, bf16[2,1,1,128,1024]{4,3,0,2,1:T(8,128)(2,1)S(1)}, u32[]{:S(2)}, u32[]{:S(2)}) %collective-permute-start.24) | collective-permute-done | bytes 524320 | tf_op jit(solution)/shard_map/ppermute | solution.py:504
  190.6 19.4 %collective-permute-done.28 = bf16[2,2,1,128,1024]{4,3,0,2,1:T(8,128)(2,1)S(1)} collective-permute-done((bf16[2,2,1,128,1024]{4,3,0,2,1:T(8,128)(2,1)S(1)}, bf16[2,2,1,128,1024]{4,3,0,2,1:T(8,128)(2,1)S(1)}, u32[]{:S(2)}, u32[]{:S(2)}) %collective-permute-start.28) | collective-permute-done | bytes 1048608 | tf_op jit(solution)/shard_map/ppermute | solution.py:504
  219.7 3.7 convolution_convert_fusion.1.refs_4_
  223.4 13.4 %collective-permute-done.26 = bf16[512,1024]{1,0:T(8,128)(2,1)S(1)} collective-permute-done((bf16[512,1024]{1,0:T(8,128)(2,1)S(1)}, bf16[512,1024]{1,0:T(8,128)(2,1)S(1)}, u32[]{:S(2)}, u32[]{:S(2)}) %collective-permute-start.26) | collective-permute-done | bytes 1048608 | tf_op jit(solution)/shard_map/ppermute | solution.py:471
  237.3 8.9 %shard_map.145 = (bf16[1024,1024]{1,0:T(8,128)(2,1)S(1)}, bf16[1024,1024]{1,0:T(8,128)(2,1)}, f32[1,1024]{1,0:T(1,128)S(1)}, bf16[1024,1024]{1,0:T(8,128)(2,1)}) custom-call(bf16[512,1024]{1,0:T(8,128)(2,1)S(1)} %get-tuple-element.153.refs_0_, bf16[512,1024]{1,0:T(8,128)(2,1)S(1)} %collective-permute-done.27.refs_1_, bf16[1024,1024]{1,0:T(8,128)(2,1)} %bitcast.217, ...), custom_call_target="tpu_custom_call" | custom-call | flops 2147483648 | bytes 12000000 | tf_op jit(solution)/shard_map/pallas_call | solution.py:257
  260.9 5.9 %convolution_convert_fusion.refs_4_ = bf16[1024,1024]{1,0:T(8,128)(2,1)} fusion(bf16[1024,1024]{1,0:T(8,128)(2,1)} %copy-done.58, bf16[1024,1024]{1,0:T(8,128)(2,1)} %bitcast.212), kind=kOutput, calls=%fused_computation.63 | convolution fusion | flops 2148532224 | bytes 6291456 | tf_op jit(solution)/shard_map/dot_general | solution.py:44
  266.8 9.5 %shard_map.146 = (bf16[1024,1024]{1,0:T(8,128)(2,1)S(1)}, bf16[1024,1024]{1,0:T(8,128)(2,1)}, f32[1,1024]{1,0:T(1,128)S(1)}, bf16[1024,1024]{1,0:T(8,128)(2,1)}) custom-call(bf16[512,1024]{1,0:T(8,128)(2,1)S(1)} %get-tuple-element.81.refs_0_, bf16[512,1024]{1,0:T(8,128)(2,1)} %collective-permute-done.30.refs_1_, bf16[1024,1024]{1,0:T(8,128)(2,1)} %bitcast.218, ...), custom_call_target="tpu_custom_call" | custom-call | flops 2147483648 | bytes 12000000 | tf_op jit(solution)/shard_map/pallas_call | solution.py:257
  276.3 6.4 %collective-permute-done.32 = bf16[512,1024]{1,0:T(8,128)(2,1)} collective-permute-done((bf16[512,1024]{1,0:T(8,128)(2,1)}, bf16[512,1024]{1,0:T(8,128)(2,1)}, u32[]{:S(2)}, u32[]{:S(2)}) %collective-permute-start.32) | collective-permute-done | bytes 1048608 | tf_op jit(solution)/shard_map/ppermute | solution.py:471
  313.2 7.3 %collective-permute-done.35 = bf16[512,1024]{1,0:T(8,128)(2,1)S(1)} collective-permute-done((bf16[512,1024]{1,0:T(8,128)(2,1)S(1)}, bf16[512,1024]{1,0:T(8,128)(2,1)S(1)}, u32[]{:S(2)}, u32[]{:S(2)}) %collective-permute-start.35) | collective-permute-done | bytes 1048608 | tf_op jit(solution)/shard_map/ppermute | solution.py:471
  331.3 4.8 collective-permute-done.38
  345.4 11.0 %shard_map.149 = (bf16[2,2,512,512]{3,2,1,0:T(8,128)(2,1)}, bf16[2,2,512,256]{3,2,1,0:T(8,128)(2,1)S(1)}) custom-call(s32[1]{0:T(128)} %bitcast.7.core_ref, bf16[2,2,512,512]{3,2,1,0:T(8,128)(2,1)} %bitcast.180, bf16[2,2,512,512]{3,2,1,0:T(8,128)(2,1)} %bitcast.181, bf16[2,2,512,256]{3,2,1,0:T(8,128)(2,1)S(1)} %bitcast.186, ...), custom_call_target="tpu_custom_call" | custom-call | flops 12000000000 | bytes 6000000 | tf_op jit(solution)/shard_map/pallas_call | solution.py:205
  375.0 3.8 convert_add_fusion.1
  381.4 11.0 %shard_map.150 = (bf16[2,2,512,512]{3,2,1,0:T(8,128)(2,1)}, bf16[2,2,512,256]{3,2,1,0:T(8,128)(2,1)S(1)}) custom-call(s32[1]{0:T(128)} %bitcast.7.core_ref, bf16[2,2,512,512]{3,2,1,0:T(8,128)(2,1)} %bitcast.182, bf16[2,2,512,512]{3,2,1,0:T(8,128)(2,1)} %bitcast.183, ...), custom_call_target="tpu_custom_call", output_to_operand_aliasing={{0}: (10, {}), {1}: (11, {})} | custom-call | flops 12000000000 | bytes 6000000 | tf_op jit(solution)/shard_map/pallas_call | solution.py:205
  401.6 8.4 %collective-permute-done.47 = bf16[2,2,1,128,512]{4,3,2,1,0:T(8,128)(2,1)S(1)} collective-permute-done((bf16[2,2,1,128,512]{4,3,2,1,0:T(8,128)(2,1)S(1)}, bf16[2,2,1,128,512]{4,3,2,1,0:T(8,128)(2,1)S(1)}, u32[]{:S(2)}, u32[]{:S(2)}) %collective-permute-start.47) | collective-permute-done | bytes 524320 | tf_op jit(solution)/shard_map/ppermute | solution.py:504
  410.3 5.0 collective-permute-done.49
  427.6 7.7 %collective-permute-done.42 = bf16[256,1024]{1,0:T(8,128)(2,1)S(1)} collective-permute-done((bf16[256,1024]{1,0:T(8,128)(2,1)S(1)}, bf16[256,1024]{1,0:T(8,128)(2,1)S(1)}, u32[]{:S(2)}, u32[]{:S(2)}) %collective-permute-start.42) | collective-permute-done | bytes 524320 | tf_op jit(solution)/shard_map/ppermute | solution.py:471
  443.6 4.6 all-to-all-start.1
  448.2 19.6 %collective-permute-done.46 = bf16[512,1024]{1,0:T(8,128)(2,1)} collective-permute-done((bf16[512,1024]{1,0:T(8,128)(2,1)}, bf16[512,1024]{1,0:T(8,128)(2,1)}, u32[]{:S(2)}, u32[]{:S(2)}) %collective-permute-start.46) | collective-permute-done | bytes 1048608 | tf_op jit(solution)/shard_map/ppermute | solution.py:471
  480.3 12.6 %collective-permute-done.56 = f32[4,384]{1,0:T(4,128)S(1)} collective-permute-done((f32[4,384]{1,0:T(4,128)S(1)}, f32[4,384]{1,0:T(4,128)S(1)}, u32[]{:S(2)}, u32[]{:S(2)}) %collective-permute-start.56) | collective-permute-done | bytes 6176 | tf_op jit(solution)/shard_map/ppermute | solution.py:600
  503.2 38.1 %shard_map.151 = (f32[1024,1024]{1,0:T(8,128)}, f32[1024,1024]{1,0:T(8,128)}, f32[1024,1024]{1,0:T(8,128)}) custom-call(s32[3]{0:T(128)S(1)} %pad_add_fusion.limit_ref, bf16[8,128,1024]{2,1,0:T(8,128)(2,1)S(1)} %all-to-all-done.1.landed_ref, f32[1024,1024]{1,0:T(8,128)} %bitcast.245, f32[1024,1024]{1,0:T(8,128)} %bitcast.198), custom_call_target="tpu_custom_call" | custom-call | flops 32212254720 | bytes 23068672 | tf_op jit(solution)/shard_map/pallas_call | solution.py:443
  (459 shorter events, 227.1 us)
Async XLA Ops:
  28.5 21.6 %collective-permute-start.5 = (bf16[512,1024]{1,0:T(8,128)(2,1)S(1)}, bf16[512,1024]{1,0:T(8,128)(2,1)S(1)}, u32[]{:S(2)}, u32[]{:S(2)}) collective-permute-start(bf16[512,1024]{1,0:T(8,128)(2,1)S(1)} %broadcast_select_fusion), channel_id=1, source_target_pairs={{0,2},{1,3},{2,0},{3,1},{4,6},{5,7},{6,4},{7,5},{8,10},{9,11},{10,... | collective-permute-start | bytes 3145736 | tf_op jit(solution)/shard_map/ppermute | solution.py:471
  50.1 51.7 %all-to-all-start = ((bf16[8,128,1024]{2,1,0:T(8,128)(2,1)}), bf16[8,128,1024]{2,1,0:T(8,128)(2,1)}, u32[]{:S(2)}, u32[]{:S(2)}) async-start(bf16[8,128,1024]{2,1,0:T(8,128)(2,1)} %select_select_fusion), calls=%async_computation | async-start | bytes 4194304 | tf_op jit(solution)/shard_map/all_to_all | solution.py:645
  55.2 15.1 %collective-permute-start.8 = (bf16[256,1024]{1,0:T(8,128)(2,1)}, bf16[256,1024]{1,0:T(8,128)(2,1)}, u32[]{:S(2)}, u32[]{:S(2)}) collective-permute-start(bf16[256,1024]{1,0:T(8,128)(2,1)} %get-tuple-element.67), channel_id=1, source_target_pairs={{0,2},{1,3},{2,0},{3,1},{4,6},{5,7},{6,4},{7,5},{8,10},{9,11},{10,... | collective-permute-start | bytes 1572872 | tf_op jit(solution)/shard_map/ppermute | solution.py:471
  56.7 24.1 %collective-permute-start.11 = (bf16[256,1024]{1,0:T(8,128)(2,1)}, bf16[256,1024]{1,0:T(8,128)(2,1)}, u32[]{:S(2)}, u32[]{:S(2)}) collective-permute-start(bf16[256,1024]{1,0:T(8,128)(2,1)} %get-tuple-element.68), channel_id=1, source_target_pairs={{0,2},{1,3},{2,0},{3,1},{4,6},{5,7},{6,4},{7,5},{8,10},{9,11},{10,... | collective-permute-start | bytes 1572872 | tf_op jit(solution)/shard_map/ppermute | solution.py:471
  61.7 22.5 %collective-permute-start.6 = (bf16[512,1024]{1,0:T(8,128)(2,1)S(1)}, bf16[512,1024]{1,0:T(8,128)(2,1)S(1)}, u32[]{:S(2)}, u32[]{:S(2)}) collective-permute-start(bf16[512,1024]{1,0:T(8,128)(2,1)S(1)} %broadcast_select_fusion), channel_id=1, source_target_pairs={{0,1},{1,0},{2,3},{3,2},{4,5},{5,4},{6,7},{7,6},{8,9},{9,8},{10,11... | collective-permute-start | bytes 3145736 | tf_op jit(solution)/shard_map/ppermute | solution.py:471
  61.8 24.4 %collective-permute-start.7 = (bf16[512,1024]{1,0:T(8,128)(2,1)S(1)}, bf16[512,1024]{1,0:T(8,128)(2,1)S(1)}, u32[]{:S(2)}, u32[]{:S(2)}) collective-permute-start(bf16[512,1024]{1,0:T(8,128)(2,1)S(1)} %collective-permute-done.5), channel_id=1, source_target_pairs={{0,1},{1,0},{2,3},{3,2},{4,5},{5,4},{6,7},{7,6},{8,9},{9,8},{10,11... | collective-permute-start | bytes 3145736 | tf_op jit(solution)/shard_map/ppermute | solution.py:471
  62.9 21.2 %collective-permute-start.12 = (bf16[256,1024]{1,0:T(8,128)(2,1)}, bf16[256,1024]{1,0:T(8,128)(2,1)S(1)}, u32[]{:S(2)}, u32[]{:S(2)}) collective-permute-start(bf16[256,1024]{1,0:T(8,128)(2,1)} %get-tuple-element.68), channel_id=1, source_target_pairs={{0,1},{1,0},{2,3},{3,2},{4,5},{5,4},{6,7},{7,6},{8,9},{9,8},{10,11... | collective-permute-start | bytes 1572872 | tf_op jit(solution)/shard_map/ppermute | solution.py:471
  126.9 24.8 %collective-permute-start.16 = (bf16[2,2,1,128,512]{4,3,0,2,1:T(8,128)(2,1)S(1)}, bf16[2,2,1,128,512]{4,3,0,2,1:T(8,128)(2,1)}, u32[]{:S(2)}, u32[]{:S(2)}) collective-permute-start(bf16[2,2,1,128,512]{4,3,0,2,1:T(8,128)(2,1)S(1)} %maximum_select_fusion.7), channel_id=1, source_target_pairs={{0,4},{4,0},{8,12},{12,8},{16,20},{20,16},{24,28},{28,24},{1,5},{5... | collective-permute-start | bytes 1572872 | tf_op jit(solution)/shard_map/ppermute | solution.py:504
  129.4 23.7 %collective-permute-start.18 = (bf16[2,1,2,128,512]{4,3,0,2,1:T(8,128)(2,1)S(1)}, bf16[2,1,2,128,512]{4,3,0,2,1:T(8,128)(2,1)}, u32[]{:S(2)}, u32[]{:S(2)}) collective-permute-start(bf16[2,1,2,128,512]{4,3,0,2,1:T(8,128)(2,1)S(1)} %maximum_select_fusion.8), channel_id=1, source_target_pairs={{0,8},{4,12},{8,0},{12,4},{16,24},{20,28},{24,16},{28,20},{1,9},{5... | collective-permute-start | bytes 1572872 | tf_op jit(solution)/shard_map/ppermute | solution.py:504
  149.4 22.9 %collective-permute-start.23 = (bf16[2,1,1,128,1024]{4,3,0,2,1:T(8,128)(2,1)S(1)}, bf16[2,1,1,128,1024]{4,3,0,2,1:T(8,128)(2,1)S(1)}, u32[]{:S(2)}, u32[]{:S(2)}) collective-permute-start(bf16[2,1,1,128,1024]{4,3,0,2,1:T(8,128)(2,1)S(1)} %fusion.44), channel_id=1, source_target_pairs={{0,4},{4,0},{8,12},{12,8},{16,20},{20,16},{24,28},{28,24},{1,5},{5... | collective-permute-start | bytes 1572872 | tf_op jit(solution)/shard_map/ppermute | solution.py:504
  168.1 18.4 %collective-permute-start.19 = (bf16[512,1024]{1,0:T(8,128)(2,1)S(1)}, bf16[512,1024]{1,0:T(8,128)(2,1)S(1)}, u32[]{:S(2)}, u32[]{:S(2)}) collective-permute-start(bf16[512,1024]{1,0:T(8,128)(2,1)S(1)} %convolution_convert_fusion.7), channel_id=1, source_target_pairs={{0,1},{1,0},{2,3},{3,2},{4,5},{5,4},{6,7},{7,6},{8,9},{9,8},{10,11... | collective-permute-start | bytes 3145736 | tf_op jit(solution)/shard_map/ppermute | solution.py:471
  169.4 15.4 %collective-permute-start.24 = (bf16[2,1,1,128,1024]{4,3,0,2,1:T(8,128)(2,1)S(1)}, bf16[2,1,1,128,1024]{4,3,0,2,1:T(8,128)(2,1)S(1)}, u32[]{:S(2)}, u32[]{:S(2)}) collective-permute-start(bf16[2,1,1,128,1024]{4,3,0,2,1:T(8,128)(2,1)S(1)} %maximum_select_fusion.9), channel_id=1, source_target_pairs={{0,8},{4,12},{8,0},{12,4},{16,24},{20,28},{24,16},{28,20},{1,9},{5... | collective-permute-start | bytes 1572872 | tf_op jit(solution)/shard_map/ppermute | solution.py:504
  185.0 25.0 %collective-permute-start.28 = (bf16[2,2,1,128,1024]{4,3,0,2,1:T(8,128)(2,1)S(1)}, bf16[2,2,1,128,1024]{4,3,0,2,1:T(8,128)(2,1)S(1)}, u32[]{:S(2)}, u32[]{:S(2)}) collective-permute-start(bf16[2,2,1,128,1024]{4,3,0,2,1:T(8,128)(2,1)S(1)} %maximum_select_fusion.5), channel_id=1, source_target_pairs={{0,4},{4,0},{8,12},{12,8},{16,20},{20,16},{24,28},{28,24},{1,5},{5... | collective-permute-start | bytes 3145736 | tf_op jit(solution)/shard_map/ppermute | solution.py:504
  186.5 25.6 %collective-permute-start.25 = (bf16[512,1024]{1,0:T(8,128)(2,1)S(1)}, bf16[512,1024]{1,0:T(8,128)(2,1)S(1)}, u32[]{:S(2)}, u32[]{:S(2)}) collective-permute-start(bf16[512,1024]{1,0:T(8,128)(2,1)S(1)} %convolution_convert_fusion.6), channel_id=1, source_target_pairs={{0,1},{1,0},{2,3},{3,2},{4,5},{5,4},{6,7},{7,6},{8,9},{9,8},{10,11... | collective-permute-start | bytes 3145736 | tf_op jit(solution)/shard_map/ppermute | solution.py:471
  187.2 27.1 %collective-permute-start.20 = (bf16[512,1024]{1,0:T(8,128)(2,1)S(1)}, bf16[512,1024]{1,0:T(8,128)(2,1)S(1)}, u32[]{:S(2)}, u32[]{:S(2)}) collective-permute-start(bf16[512,1024]{1,0:T(8,128)(2,1)S(1)} %pad_maximum_fusion.1), channel_id=1, source_target_pairs={{0,2},{1,3},{2,0},{3,1},{4,6},{5,7},{6,4},{7,5},{8,10},{9,11},{10,... | collective-permute-start | bytes 3145736 | tf_op jit(solution)/shard_map/ppermute | solution.py:471
  188.8 28.2 %collective-permute-start.29 = (bf16[2,1,2,128,1024]{4,3,0,2,1:T(8,128)(2,1)S(1)}, bf16[2,1,2,128,1024]{4,3,0,2,1:T(8,128)(2,1)S(1)}, u32[]{:S(2)}, u32[]{:S(2)}) collective-permute-start(bf16[2,1,2,128,1024]{4,3,0,2,1:T(8,128)(2,1)S(1)} %maximum_select_fusion.4), channel_id=1, source_target_pairs={{0,8},{4,12},{8,0},{12,4},{16,24},{20,28},{24,16},{28,20},{1,9},{5... | collective-permute-start | bytes 3145736 | tf_op jit(solution)/shard_map/ppermute | solution.py:504
  212.7 24.2 %collective-permute-start.26 = (bf16[512,1024]{1,0:T(8,128)(2,1)S(1)}, bf16[512,1024]{1,0:T(8,128)(2,1)S(1)}, u32[]{:S(2)}, u32[]{:S(2)}) collective-permute-start(bf16[512,1024]{1,0:T(8,128)(2,1)S(1)} %pad_maximum_fusion.2), channel_id=1, source_target_pairs={{0,2},{1,3},{2,0},{3,1},{4,6},{5,7},{6,4},{7,5},{8,10},{9,11},{10,... | collective-permute-start | bytes 3145736 | tf_op jit(solution)/shard_map/ppermute | solution.py:471
  217.0 20.3 %collective-permute-start.27 = (bf16[512,1024]{1,0:T(8,128)(2,1)S(1)}, bf16[512,1024]{1,0:T(8,128)(2,1)S(1)}, u32[]{:S(2)}, u32[]{:S(2)}) collective-permute-start(bf16[512,1024]{1,0:T(8,128)(2,1)S(1)} %get-tuple-element.153.refs_0_), channel_id=1, source_target_pairs={{0,1},{1,0},{2,3},{3,2},{4,5},{5,4},{6,7},{7,6},{8,9},{9,8},{10,11... | collective-permute-start | bytes 3145736 | tf_op jit(solution)/shard_map/ppermute | solution.py:471
  256.8 25.9 %collective-permute-start.32 = (bf16[512,1024]{1,0:T(8,128)(2,1)}, bf16[512,1024]{1,0:T(8,128)(2,1)}, u32[]{:S(2)}, u32[]{:S(2)}) collective-permute-start(bf16[512,1024]{1,0:T(8,128)(2,1)} %pad_maximum_fusion.3), channel_id=1, source_target_pairs={{0,2},{1,3},{2,0},{3,1},{4,6},{5,7},{6,4},{7,5},{8,10},{9,11},{10,... | collective-permute-start | bytes 3145736 | tf_op jit(solution)/shard_map/ppermute | solution.py:471
  294.7 18.5 %collective-permute-start.34 = (bf16[512,1024]{1,0:T(8,128)(2,1)S(1)}, bf16[512,1024]{1,0:T(8,128)(2,1)S(1)}, u32[]{:S(2)}, u32[]{:S(2)}) collective-permute-start(bf16[512,1024]{1,0:T(8,128)(2,1)S(1)} %get-tuple-element.90.refs_0_), channel_id=1, source_target_pairs={{0,1},{1,0},{2,3},{3,2},{4,5},{5,4},{6,7},{7,6},{8,9},{9,8},{10,11... | collective-permute-start | bytes 3145736 | tf_op jit(solution)/shard_map/ppermute | solution.py:471
  294.9 25.6 %collective-permute-start.35 = (bf16[512,1024]{1,0:T(8,128)(2,1)S(1)}, bf16[512,1024]{1,0:T(8,128)(2,1)S(1)}, u32[]{:S(2)}, u32[]{:S(2)}) collective-permute-start(bf16[512,1024]{1,0:T(8,128)(2,1)S(1)} %pad_maximum_fusion.4), channel_id=1, source_target_pairs={{0,2},{1,3},{2,0},{3,1},{4,6},{5,7},{6,4},{7,5},{8,10},{9,11},{10,... | collective-permute-start | bytes 3145736 | tf_op jit(solution)/shard_map/ppermute | solution.py:471
  302.4 26.1 %collective-permute-start.37 = (bf16[2,2,1,128,1024]{4,3,2,1,0:T(8,128)(2,1)}, bf16[2,2,1,128,1024]{4,3,2,1,0:T(8,128)(2,1)}, u32[]{:S(2)}, u32[]{:S(2)}) collective-permute-start(bf16[2,2,1,128,1024]{4,3,2,1,0:T(8,128)(2,1)} %constant_dynamic-slice_fusion.8), channel_id=1, source_target_pairs={{0,4},{4,0},{8,12},{12,8},{16,20},{20,16},{24,28},{28,24},{1,5},{5... | collective-permute-start | bytes 3145736 | tf_op jit(solution)/shard_map/ppermute | solution.py:504
  310.5 25.6 %collective-permute-start.38 = (bf16[2,1,2,128,1024]{4,3,2,1,0:T(8,128)(2,1)}, bf16[2,1,2,128,1024]{4,3,2,1,0:T(8,128)(2,1)}, u32[]{:S(2)}, u32[]{:S(2)}) collective-permute-start(bf16[2,1,2,128,1024]{4,3,2,1,0:T(8,128)(2,1)} %constant_dynamic-slice_fusion.7), channel_id=1, source_target_pairs={{0,8},{4,12},{8,0},{12,4},{16,24},{20,28},{24,16},{28,20},{1,9},{5... | collective-permute-start | bytes 3145736 | tf_op jit(solution)/shard_map/ppermute | solution.py:504
  343.3 23.7 %collective-permute-start.44 = (bf16[1,1,2,128,1024]{4,3,2,1,0:T(8,128)(2,1)}, bf16[1,1,2,128,1024]{4,3,2,1,0:T(8,128)(2,1)}, u32[]{:S(2)}, u32[]{:S(2)}) collective-permute-start(bf16[1,1,2,128,1024]{4,3,2,1,0:T(8,128)(2,1)} %constant_dynamic-slice_fusion.5), channel_id=1, source_target_pairs={{0,16},{4,20},{8,24},{12,28},{16,0},{20,4},{24,8},{28,12},{1,17},{... | collective-permute-start | bytes 1572872 | tf_op jit(solution)/shard_map/ppermute | solution.py:504
  344.7 25.2 %collective-permute-start.43 = (bf16[2,1,1,128,1024]{4,3,2,1,0:T(8,128)(2,1)}, bf16[2,1,1,128,1024]{4,3,2,1,0:T(8,128)(2,1)}, u32[]{:S(2)}, u32[]{:S(2)}) collective-permute-start(bf16[2,1,1,128,1024]{4,3,2,1,0:T(8,128)(2,1)} %constant_dynamic-slice_fusion.6), channel_id=1, source_target_pairs={{0,8},{4,12},{8,0},{12,4},{16,24},{20,28},{24,16},{28,20},{1,9},{5... | collective-permute-start | bytes 1572872 | tf_op jit(solution)/shard_map/ppermute | solution.py:504
  358.7 16.3 %collective-permute-start.41 = (bf16[512,1024]{1,0:T(8,128)(2,1)}, bf16[512,1024]{1,0:T(8,128)(2,1)}, u32[]{:S(2)}, u32[]{:S(2)}) collective-permute-start(bf16[512,1024]{1,0:T(8,128)(2,1)} %convolution_convert_fusion.2), channel_id=1, source_target_pairs={{0,1},{1,0},{2,3},{3,2},{4,5},{5,4},{6,7},{7,6},{8,9},{9,8},{10,11... | collective-permute-start | bytes 3145736 | tf_op jit(solution)/shard_map/ppermute | solution.py:471
  368.6 71.5 %collective-permute-start.52 = (bf16[1,1,1,128,1024]{4,3,2,1,0:T(8,128)(2,1)S(1)}, bf16[1,1,1,128,1024]{4,3,2,1,0:T(8,128)(2,1)}, u32[]{:S(2)}, u32[]{:S(2)}) collective-permute-start(bf16[1,1,1,128,1024]{4,3,2,1,0:T(8,128)(2,1)S(1)} %constant_dynamic-slice_fusion.1), channel_id=1, source_target_pairs={{0,4},{4,0},{8,12},{12,8},{16,20},{20,16},{24,28},{28,24},{1,5},{5... | collective-permute-start | bytes 786440 | tf_op jit(solution)/shard_map/ppermute | solution.py:504
  371.9 70.0 %collective-permute-start.53 = (bf16[1,1,1,128,1024]{4,3,2,1,0:T(8,128)(2,1)}, bf16[1,1,1,128,1024]{4,3,2,1,0:T(8,128)(2,1)}, u32[]{:S(2)}, u32[]{:S(2)}) collective-permute-start(bf16[1,1,1,128,1024]{4,3,2,1,0:T(8,128)(2,1)} %constant_dynamic-slice_fusion), channel_id=1, source_target_pairs={{0,16},{4,20},{8,24},{12,28},{16,0},{20,4},{24,8},{28,12},{1,17},{... | collective-permute-start | bytes 786440 | tf_op jit(solution)/shard_map/ppermute | solution.py:504
  400.3 23.4 %collective-permute-start.45 = (bf16[1024,1024]{1,0:T(8,128)(2,1)S(1)}, bf16[1024,1024]{1,0:T(8,128)(2,1)S(1)}, u32[]{:S(2)}, u32[]{:S(2)}) collective-permute-start(bf16[1024,1024]{1,0:T(8,128)(2,1)S(1)} %add_convert_fusion), channel_id=1, source_target_pairs={{0,1},{1,0},{2,3},{3,2},{4,5},{5,4},{6,7},{7,6},{8,9},{9,8},{10,11... | collective-permute-start | bytes 6291464 | tf_op jit(solution)/shard_map/ppermute | solution.py:471
  423.0 49.5 %collective-permute-start.40 = (bf16[256,1024]{1,0:T(8,128)(2,1)}, bf16[256,1024]{1,0:T(8,128)(2,1)}, u32[]{:S(2)}, u32[]{:S(2)}) collective-permute-start(bf16[256,1024]{1,0:T(8,128)(2,1)} %slice.439), channel_id=1, source_target_pairs={{0,2},{1,3},{2,0},{3,1},{4,6},{5,7},{6,4},{7,5},{8,10},{9,11},{10,... | collective-permute-start | bytes 1572872 | tf_op jit(solution)/shard_map/ppermute | solution.py:471
  435.3 32.5 %collective-permute-start.46 = (bf16[512,1024]{1,0:T(8,128)(2,1)}, bf16[512,1024]{1,0:T(8,128)(2,1)}, u32[]{:S(2)}, u32[]{:S(2)}) collective-permute-start(bf16[512,1024]{1,0:T(8,128)(2,1)} %slice.437), channel_id=1, source_target_pairs={{0,2},{1,3},{2,0},{3,1},{4,6},{5,7},{6,4},{7,5},{8,10},{9,11},{10,... | collective-permute-start | bytes 3145736 | tf_op jit(solution)/shard_map/ppermute | solution.py:471
  443.6 59.6 %all-to-all-start.1 = ((bf16[8,128,1024]{2,1,0:T(8,128)(2,1)}), bf16[8,128,1024]{2,1,0:T(8,128)(2,1)S(1)}, u32[]{:S(2)}, u32[]{:S(2)}) async-start(bf16[8,128,1024]{2,1,0:T(8,128)(2,1)} %fusion.54), calls=%async_computation.1 | async-start | bytes 4194304 | tf_op jit(solution)/shard_map/all_to_all | solution.py:813
  (102 other events, 796.9 us)
